TPU v7x, 32 devices: a whole 2x2x4 slice. The times are simulated.
32 devices in a mesh: ctx: 8 (over z, y), tp: 4 (over x, core).
Axes of the slice: x: 2, y: 2, z: 4, core: 2. Of those that a mesh axis runs over, the one named last changes fastest.
Arguments:
- queries: bfloat16 [2048, 1024], P('ctx', 'tp'), may hold values from -18 to 18
- keys: bfloat16 [2048, 1024], P('ctx', 'tp'), may hold values from -6 to 6
- values: bfloat16 [2048, 1024], P('ctx', 'tp'), may hold values from -6 to 6
- cross_queries: bfloat16 [2048, 1024], P('ctx', 'tp'), may hold values from -18 to 18
- nbr_keys: bfloat16 [64, 128, 1024], P('ctx', None, 'tp'), may hold values from -6 to 6
- nbr_values: bfloat16 [64, 128, 1024], P('ctx', None, 'tp'), may hold values from -6 to 6
- nbr_slot: int32 [64], P('ctx'), may hold values from 0 to 63, as said below
- w_cross: bfloat16 [1024, 8192], P('tp'), may hold values from -0.25 to 0.25
Outputs:
- attended: bfloat16 [2048, 1024], P('ctx', 'tp')
- crossed: bfloat16 [2048, 8192], P('ctx', 'tp')
Inputs may be any that keep to these rules, and one draw needn't show every extreme that they name: `nbr_slot`: every slot appears exactly once. The 8 neighbours held by one index of ctx go to 8 different owners, and no index of ctx holds two neighbours of one owner, where the owner of slot g is the index of ctx holding the tokens of block g // 2.
All inputs are finite; a program needn't handle non-finite values.
Results may differ from a plain program's by a relative error of at most 0.009.
Values may be sent and summed in bfloat16 or wider, within the bound.
No kernel may reach another device: no remote copies, remote signals or barrier semaphores. Data moves between devices by JAX's collectives and lax.ppermute only.
A program may use at most 64 MiB of HBM per device.

v0:
```python
import jax
import jax.numpy as jnp
from jax import lax
from jax.sharding import PartitionSpec as P

HD = 128
BLOCK = 64


NEGATIVE = -1e30


def from_behind(value, axis, steps):
    count = lax.axis_size(axis)
    first, last = (max(0, -steps), min(count, count - steps))
    return lax.ppermute(value, axis, [(source, source + steps) for source in range(first, last)])


def fresh_state(heads, rows, width):
    return (
        jnp.full((heads, rows), NEGATIVE, jnp.float32),
        jnp.zeros((heads, rows), jnp.float32),
        jnp.zeros((heads, rows, width), jnp.float32),
    )


def absorb(state, queries, block, allowed):
    peak, total, accum = state
    heads = peak.shape[0]
    rows = queries.shape[0]
    width = queries.shape[1] // heads
    count = block.shape[0]
    query_heads = queries.reshape(rows, heads, width)
    key_heads = block[:, : heads * width].reshape(count, heads, width)
    value_heads = block[:, heads * width :].reshape(count, heads, width)
    scores = jnp.einsum(
        "qhd,khd->hqk", query_heads, key_heads, preferred_element_type=jnp.float32
    ) * HD ** (-0.5)
    scores = jnp.where(allowed, scores, NEGATIVE)
    new_peak = jnp.maximum(peak, jnp.max(scores, axis=-1))
    weights = jnp.where(allowed, jnp.exp(scores - new_peak[:, :, None]), 0.0)
    factor = jnp.exp(peak - new_peak)
    total = total * factor + jnp.sum(weights, axis=-1)
    accum = accum * factor[:, :, None] + jnp.einsum(
        "hqk,khd->hqd",
        weights.astype(jnp.bfloat16),
        value_heads,
        preferred_element_type=jnp.float32,
    )
    return (new_peak, total, accum)


def finish(state):
    peak, total, accum = state
    heads, rows, width = accum.shape
    result = accum / total[:, :, None]
    return result.transpose(1, 0, 2).reshape(rows, heads * width).astype(jnp.bfloat16)


def block_attend(query_blocks, kv_blocks):
    count, length, width = query_blocks.shape
    heads = width // HD
    keys_len = kv_blocks.shape[1]
    query_heads = query_blocks.reshape(count, length, heads, HD)
    key_heads = kv_blocks[:, :, :width].reshape(count, keys_len, heads, HD)
    value_heads = kv_blocks[:, :, width:].reshape(count, keys_len, heads, HD)
    scores = jnp.einsum(
        "bqhd,bkhd->bhqk", query_heads, key_heads, preferred_element_type=jnp.float32
    ) * HD ** (-0.5)
    peak = jnp.max(scores, axis=-1, keepdims=True)
    weights = jnp.exp(scores - peak)
    total = jnp.sum(weights, axis=-1)
    mixed = jnp.einsum(
        "bhqk,bkhd->bqhd",
        weights.astype(jnp.bfloat16),
        value_heads,
        preferred_element_type=jnp.float32,
    )
    result = mixed / jnp.transpose(total, (0, 2, 1))[..., None]
    return result.reshape(count, length, width).astype(jnp.bfloat16)


def shards(queries, keys, values, cross_queries, nbr_keys, nbr_values, nbr_slot, w_cross):
    rank = lax.axis_index("ctx")
    devices_ctx = lax.axis_size("ctx")
    rows = queries.shape[0]
    local_width = queries.shape[1]
    heads = local_width // HD
    positions = jnp.arange(rows)
    lower = positions[None, :] <= positions[:, None]
    bundle = jnp.concatenate([keys, values], axis=1)
    state = absorb(fresh_state(heads, rows, HD), queries, bundle, lower)

    def turn_one(turn, carry):
        moving, acc_state = carry
        moving = from_behind(moving, "ctx", 1)
        return (moving, absorb(acc_state, queries, moving, turn <= rank))

    attended = finish(lax.fori_loop(1, devices_ctx, turn_one, (bundle, state))[1])
    nb_dev = nbr_keys.shape[0]
    nb_len = nbr_keys.shape[1]
    block_count = nb_dev // 2
    held = jnp.concatenate([nbr_keys, nbr_values], axis=2)
    channels = held.shape[2]
    owner = nbr_slot // nb_dev
    position = nbr_slot % nb_dev
    matched = owner[None, :] == jnp.arange(devices_ctx)[:, None]
    outgoing = jnp.einsum(
        "dn,nlc->dlc", matched.astype(jnp.bfloat16), held, preferred_element_type=jnp.float32
    ).astype(jnp.bfloat16)
    labels = jnp.max(jnp.where(matched, position[None, :], -1), axis=1)
    incoming, sources = (
        lax.all_to_all(outgoing, "ctx", split_axis=0, concat_axis=0, tiled=True),
        lax.all_to_all(labels, "ctx", split_axis=0, concat_axis=0, tiled=True),
    )
    placed = sources[None, :] == jnp.arange(nb_dev)[:, None]
    owned = jnp.einsum(
        "pn,nlc->plc", placed.astype(jnp.bfloat16), incoming, preferred_element_type=jnp.float32
    ).astype(jnp.bfloat16)
    blocks = owned.reshape(block_count, 2 * nb_len, channels)
    earlier = from_behind(blocks[block_count - 1], "ctx", 1)
    extended_blocks = jnp.concatenate([earlier[None], blocks], axis=0)
    padded = jnp.concatenate(
        [
            jnp.zeros((1, local_width), jnp.bfloat16),
            cross_queries,
            jnp.zeros((BLOCK - 1, local_width), jnp.bfloat16),
        ],
        axis=0,
    )
    padded = padded.reshape(block_count + 1, BLOCK, local_width)
    cross_heads = block_attend(padded, extended_blocks).reshape(
        (block_count + 1) * BLOCK, local_width
    )[1 : rows + 1]
    term = jnp.dot(cross_heads, w_cross, preferred_element_type=jnp.float32)
    crossed = lax.psum_scatter(term.astype(jnp.bfloat16), "tp", scatter_dimension=1, tiled=True)
    return (attended, crossed)


def solution(mesh):
    in_specs = (
        P("ctx", "tp"),
        P("ctx", "tp"),
        P("ctx", "tp"),
        P("ctx", "tp"),
        P("ctx", None, "tp"),
        P("ctx", None, "tp"),
        P("ctx"),
        P("tp", None),
    )
    out_specs = (P("ctx", "tp"), P("ctx", "tp"))
    return jax.shard_map(shards, mesh=mesh, in_specs=in_specs, out_specs=out_specs, check_vma=False)
```

profile of v0, /device:TPU:0, one launch (start us, length us, event | category | flops | bytes accessed | tf_op | source)
XLA Modules:
  0.0 146.3 jit_solution(10596930536150166413)
XLA Ops:
  7.2 0.7 and_select_fusion
  7.8 0.1 select_reduce_fusion
  8.0 0.7 copy.71
  8.6 7.3 %all-to-all-start = ((s32[8,1,1]{2,1,0:T(1,128)}), s32[8,1,1]{2,1,0:T(1,128)S(1)}, u32[]{:S(2)}, u32[]{:S(2)}) async-start(s32[8,1,1]{2,1,0:T(1,128)} %copy.71), calls=%async_computation | async-start | bytes 8192 | tf_op jit(solution)/shard_map/all_to_all | solution.py:114
  15.9 1.3 copy.72
  17.2 1.3 copy.73
  18.6 0.4 convolution_convert_fusion.2
  19.0 1.3 copy.74
  20.3 2.0 %all-to-all-done = s32[8,1,1]{2,1,0:T(1,128)S(1)} async-done(((s32[8,1,1]{2,1,0:T(1,128)}), s32[8,1,1]{2,1,0:T(1,128)S(1)}, u32[]{:S(2)}, u32[]{:S(2)}) %all-to-all-start) | async-done | bytes 64 | tf_op jit(solution)/shard_map/all_to_all | solution.py:114
  22.3 4.2 %all-to-all-start.1 = ((bf16[8,128,512]{2,1,0:T(8,128)(2,1)}), bf16[8,128,512]{2,1,0:T(8,128)(2,1)S(1)}, u32[]{:S(2)}, u32[]{:S(2)}) async-start(bf16[8,128,512]{2,1,0:T(8,128)(2,1)} %copy.74), calls=%async_computation.1 | async-start | bytes 2097152 | tf_op jit(solution)/shard_map/all_to_all | solution.py:113
  26.8 0.2 maximum_maximum_fusion
  27.1 0.2 fusion.48
  27.3 0.2 reduce
  27.6 24.3 %all-to-all-done.1 = bf16[8,128,512]{2,1,0:T(8,128)(2,1)S(1)} async-done(((bf16[8,128,512]{2,1,0:T(8,128)(2,1)}), bf16[8,128,512]{2,1,0:T(8,128)(2,1)S(1)}, u32[]{:S(2)}, u32[]{:S(2)}) %all-to-all-start.1) | async-done | bytes 1048608 | tf_op jit(solution)/shard_map/all_to_all | solution.py:113
  51.9 0.7 convolution_convert_fusion.1
  52.6 0.3 slice.33
  52.9 3.1 %collective-permute-start.1 = (bf16[256,512]{1,0:T(8,128)(2,1)S(1)}, bf16[256,512]{1,0:T(8,128)(2,1)S(1)}, u32[]{:S(2)}, u32[]{:S(2)}) collective-permute-start(bf16[256,512]{1,0:T(8,128)(2,1)S(1)} %bitcast.92), channel_id=1, source_target_pairs={{0,4},{4,8},{8,12},{12,16},{16,20},{20,24},{24,28},{1,5},{5,9},{9,... | collective-permute-start | bytes 786440 | tf_op jit(solution)/shard_map/ppermute | solution.py:16
  56.1 0.7 pad_maximum_fusion.1
  56.8 0.1 fusion.21
  56.9 0.3 copy.77
  57.2 3.6 %collective-permute-done.1 = bf16[256,512]{1,0:T(8,128)(2,1)S(1)} collective-permute-done((bf16[256,512]{1,0:T(8,128)(2,1)S(1)}, bf16[256,512]{1,0:T(8,128)(2,1)S(1)}, u32[]{:S(2)}, u32[]{:S(2)}) %collective-permute-start.1) | collective-permute-done | bytes 262176 | tf_op jit(solution)/shard_map/ppermute | solution.py:16
  60.9 0.2 copy.79
  61.1 1.1 copy.78
  62.2 0.3 fusion.49
  62.6 0.3 fusion.18
  62.9 0.4 copy-done.2
  63.3 0.4 fusion.12
  63.7 0.2 copy.83
  63.9 0.7 copy-done
  64.6 3.2 %convolution_convert_fusion = bf16[256,8192]{1,0:T(8,128)(2,1)} fusion(bf16[256,8192]{1,0:T(8,128)(2,1)S(1)} %copy-done, bf16[320,256]{1,0:T(8,128)(2,1)S(1)} %bitcast.90), kind=kOutput, calls=%fused_computation.14 | convolution fusion | flops 1075838976 | bytes 8519680 | tf_op jit(solution)/shard_map/dot_general | solution.py:135
  67.8 0.3 convolution_add_fusion.1
  68.2 0.6 copy-done.4
  68.8 69.9 %while.19 = (s32[]{:T(128)}, bf16[256,512]{0,1:T(8,128)(2,1)S(1)}, f32[2,256]{1,0:T(2,128)S(1)}, f32[2,256]{1,0:T(2,128)S(1)}, f32[2,256,128]{2,1,0:T(8,128)S(1)...) while((s32[]{:T(128)}, bf16[256,512]{0,1:T(8,128)(2,1)S(1)}, f32[2,256]{1,0:T(2,128)S(1)}, ...), condition=%wide.region_5.6_spmd, body=%wide.region_2.5_spmd.sunk | while | flops 68420608 | bytes 4620425 | solution.py:99
  68.8 4.4 %collective-permute-start = (bf16[256,512]{0,1:T(8,128)(2,1)S(1)}, bf16[256,512]{0,1:T(8,128)(2,1)S(1)}, u32[]{:S(2)}, u32[]{:S(2)}) collective-permute-start(bf16[256,512]{0,1:T(8,128)(2,1)S(1)} %get-tuple-element.223), channel_id=1, source_target_pairs={{0,4},{4,8},{8,12},{12,16},{16,20},{20,24},{24,28},{1,5},{5,9},{9,... | collective-permute-start | bytes 786440 | tf_op jit(solution)/shard_map/while/body/eval_jaxpr/ppermute | solution.py:16
  73.2 3.9 %collective-permute-done = bf16[256,512]{0,1:T(8,128)(2,1)S(1)} collective-permute-done((bf16[256,512]{0,1:T(8,128)(2,1)S(1)}, bf16[256,512]{0,1:T(8,128)(2,1)S(1)}, u32[]{:S(2)}, u32[]{:S(2)}) %collective-permute-start) | collective-permute-done | bytes 262176 | tf_op jit(solution)/shard_map/while/body/eval_jaxpr/ppermute | solution.py:16
  77.0 0.3 fusion.72
  77.3 0.1 fusion.73
  77.5 0.3 convolution_add_fusion.3
  77.8 4.4 %collective-permute-start = (bf16[256,512]{0,1:T(8,128)(2,1)S(1)}, bf16[256,512]{0,1:T(8,128)(2,1)S(1)}, u32[]{:S(2)}, u32[]{:S(2)}) collective-permute-start(bf16[256,512]{0,1:T(8,128)(2,1)S(1)} %get-tuple-element.223), channel_id=1, source_target_pairs={{0,4},{4,8},{8,12},{12,16},{16,20},{20,24},{24,28},{1,5},{5,9},{9,... | collective-permute-start | bytes 786440 | tf_op jit(solution)/shard_map/while/body/eval_jaxpr/ppermute | solution.py:16
  82.3 3.9 %collective-permute-done = bf16[256,512]{0,1:T(8,128)(2,1)S(1)} collective-permute-done((bf16[256,512]{0,1:T(8,128)(2,1)S(1)}, bf16[256,512]{0,1:T(8,128)(2,1)S(1)}, u32[]{:S(2)}, u32[]{:S(2)}) %collective-permute-start) | collective-permute-done | bytes 262176 | tf_op jit(solution)/shard_map/while/body/eval_jaxpr/ppermute | solution.py:16
  86.1 0.3 fusion.72
  86.6 0.3 convolution_add_fusion.3
  86.9 4.4 %collective-permute-start = (bf16[256,512]{0,1:T(8,128)(2,1)S(1)}, bf16[256,512]{0,1:T(8,128)(2,1)S(1)}, u32[]{:S(2)}, u32[]{:S(2)}) collective-permute-start(bf16[256,512]{0,1:T(8,128)(2,1)S(1)} %get-tuple-element.223), channel_id=1, source_target_pairs={{0,4},{4,8},{8,12},{12,16},{16,20},{20,24},{24,28},{1,5},{5,9},{9,... | collective-permute-start | bytes 786440 | tf_op jit(solution)/shard_map/while/body/eval_jaxpr/ppermute | solution.py:16
  91.4 3.9 %collective-permute-done = bf16[256,512]{0,1:T(8,128)(2,1)S(1)} collective-permute-done((bf16[256,512]{0,1:T(8,128)(2,1)S(1)}, bf16[256,512]{0,1:T(8,128)(2,1)S(1)}, u32[]{:S(2)}, u32[]{:S(2)}) %collective-permute-start) | collective-permute-done | bytes 262176 | tf_op jit(solution)/shard_map/while/body/eval_jaxpr/ppermute | solution.py:16
  95.2 0.3 fusion.72
  95.7 0.3 convolution_add_fusion.3
  96.1 5.2 %collective-permute-start = (bf16[256,512]{0,1:T(8,128)(2,1)S(1)}, bf16[256,512]{0,1:T(8,128)(2,1)S(1)}, u32[]{:S(2)}, u32[]{:S(2)}) collective-permute-start(bf16[256,512]{0,1:T(8,128)(2,1)S(1)} %get-tuple-element.223), channel_id=1, source_target_pairs={{0,4},{4,8},{8,12},{12,16},{16,20},{20,24},{24,28},{1,5},{5,9},{9,... | collective-permute-start | bytes 786440 | tf_op jit(solution)/shard_map/while/body/eval_jaxpr/ppermute | solution.py:16
  101.2 3.9 %collective-permute-done = bf16[256,512]{0,1:T(8,128)(2,1)S(1)} collective-permute-done((bf16[256,512]{0,1:T(8,128)(2,1)S(1)}, bf16[256,512]{0,1:T(8,128)(2,1)S(1)}, u32[]{:S(2)}, u32[]{:S(2)}) %collective-permute-start) | collective-permute-done | bytes 262176 | tf_op jit(solution)/shard_map/while/body/eval_jaxpr/ppermute | solution.py:16
  105.1 0.3 fusion.72
  105.5 0.3 convolution_add_fusion.3
  105.9 5.3 %collective-permute-start = (bf16[256,512]{0,1:T(8,128)(2,1)S(1)}, bf16[256,512]{0,1:T(8,128)(2,1)S(1)}, u32[]{:S(2)}, u32[]{:S(2)}) collective-permute-start(bf16[256,512]{0,1:T(8,128)(2,1)S(1)} %get-tuple-element.223), channel_id=1, source_target_pairs={{0,4},{4,8},{8,12},{12,16},{16,20},{20,24},{24,28},{1,5},{5,9},{9,... | collective-permute-start | bytes 786440 | tf_op jit(solution)/shard_map/while/body/eval_jaxpr/ppermute | solution.py:16
  111.2 4.4 %collective-permute-done = bf16[256,512]{0,1:T(8,128)(2,1)S(1)} collective-permute-done((bf16[256,512]{0,1:T(8,128)(2,1)S(1)}, bf16[256,512]{0,1:T(8,128)(2,1)S(1)}, u32[]{:S(2)}, u32[]{:S(2)}) %collective-permute-start) | collective-permute-done | bytes 262176 | tf_op jit(solution)/shard_map/while/body/eval_jaxpr/ppermute | solution.py:16
  115.6 0.3 fusion.72
  115.9 0.1 fusion.73
  116.1 0.3 convolution_add_fusion.3
  116.4 5.6 %collective-permute-start = (bf16[256,512]{0,1:T(8,128)(2,1)S(1)}, bf16[256,512]{0,1:T(8,128)(2,1)S(1)}, u32[]{:S(2)}, u32[]{:S(2)}) collective-permute-start(bf16[256,512]{0,1:T(8,128)(2,1)S(1)} %get-tuple-element.223), channel_id=1, source_target_pairs={{0,4},{4,8},{8,12},{12,16},{16,20},{20,24},{24,28},{1,5},{5,9},{9,... | collective-permute-start | bytes 786440 | tf_op jit(solution)/shard_map/while/body/eval_jaxpr/ppermute | solution.py:16
  122.0 5.5 %collective-permute-done = bf16[256,512]{0,1:T(8,128)(2,1)S(1)} collective-permute-done((bf16[256,512]{0,1:T(8,128)(2,1)S(1)}, bf16[256,512]{0,1:T(8,128)(2,1)S(1)}, u32[]{:S(2)}, u32[]{:S(2)}) %collective-permute-start) | collective-permute-done | bytes 262176 | tf_op jit(solution)/shard_map/while/body/eval_jaxpr/ppermute | solution.py:16
  127.5 0.3 fusion.72
  128.0 0.3 convolution_add_fusion.3
  128.4 5.6 %collective-permute-start = (bf16[256,512]{0,1:T(8,128)(2,1)S(1)}, bf16[256,512]{0,1:T(8,128)(2,1)S(1)}, u32[]{:S(2)}, u32[]{:S(2)}) collective-permute-start(bf16[256,512]{0,1:T(8,128)(2,1)S(1)} %get-tuple-element.223), channel_id=1, source_target_pairs={{0,4},{4,8},{8,12},{12,16},{16,20},{20,24},{24,28},{1,5},{5,9},{9,... | collective-permute-start | bytes 786440 | tf_op jit(solution)/shard_map/while/body/eval_jaxpr/ppermute | solution.py:16
  134.0 3.9 %collective-permute-done = bf16[256,512]{0,1:T(8,128)(2,1)S(1)} collective-permute-done((bf16[256,512]{0,1:T(8,128)(2,1)S(1)}, bf16[256,512]{0,1:T(8,128)(2,1)S(1)}, u32[]{:S(2)}, u32[]{:S(2)}) %collective-permute-start) | collective-permute-done | bytes 262176 | tf_op jit(solution)/shard_map/while/body/eval_jaxpr/ppermute | solution.py:16
  137.9 0.3 fusion.72
  138.3 0.3 convolution_add_fusion.3
  138.7 0.8 copy_bitcast_fusion.1
  (66 shorter events, 1.6 us)
Async XLA Ops:
  8.6 13.7 %all-to-all-start = ((s32[8,1,1]{2,1,0:T(1,128)}), s32[8,1,1]{2,1,0:T(1,128)S(1)}, u32[]{:S(2)}, u32[]{:S(2)}) async-start(s32[8,1,1]{2,1,0:T(1,128)} %copy.71), calls=%async_computation | async-start | bytes 8192 | tf_op jit(solution)/shard_map/all_to_all | solution.py:114
  19.0 7.6 %copy-start.6 = (bf16[256,256]{1,0:T(8,128)(2,1)S(1)}, bf16[256,256]{1,0:T(8,128)(2,1)}, u32[]{:S(2)}) copy-start(bf16[256,256]{1,0:T(8,128)(2,1)} %param.11) | copy-start | bytes 393220
  19.0 7.7 %copy-start.3 = (bf16[256,256]{1,0:T(8,128)(2,1)S(1)}, bf16[256,256]{1,0:T(8,128)(2,1)}, u32[]{:S(2)}) copy-start(bf16[256,256]{1,0:T(8,128)(2,1)} %param.12) | copy-start | bytes 393220
  19.0 7.8 %copy-start.5 = (bf16[256,256]{1,0:T(8,128)(2,1)S(1)}, bf16[256,256]{1,0:T(8,128)(2,1)}, u32[]{:S(2)}) copy-start(bf16[256,256]{1,0:T(8,128)(2,1)} %param.13) | copy-start | bytes 393220
  20.3 6.8 %copy-start.1 = (bf16[256,256]{1,0:T(8,128)(2,1)S(1)}, bf16[256,256]{1,0:T(8,128)(2,1)}, u32[]{:S(2)}) copy-start(bf16[256,256]{1,0:T(8,128)(2,1)} %param.10) | copy-start | bytes 393220
  22.3 29.6 %all-to-all-start.1 = ((bf16[8,128,512]{2,1,0:T(8,128)(2,1)}), bf16[8,128,512]{2,1,0:T(8,128)(2,1)S(1)}, u32[]{:S(2)}, u32[]{:S(2)}) async-start(bf16[8,128,512]{2,1,0:T(8,128)(2,1)} %copy.74), calls=%async_computation.1 | async-start | bytes 2097152 | tf_op jit(solution)/shard_map/all_to_all | solution.py:113
  26.5 113.0 %reduce-scatter.2.cloned.1.call-start = ((), (), s32[]{:S(2)}) async-start(), calls=%async_computation.3 | async-start | bytes 5242880 | tf_op jit(solution)/shard_map/reduce_scatter | solution.py:136
  52.9 7.9 %collective-permute-start.1 = (bf16[256,512]{1,0:T(8,128)(2,1)S(1)}, bf16[256,512]{1,0:T(8,128)(2,1)S(1)}, u32[]{:S(2)}, u32[]{:S(2)}) collective-permute-start(bf16[256,512]{1,0:T(8,128)(2,1)S(1)} %bitcast.92), channel_id=1, source_target_pairs={{0,4},{4,8},{8,12},{12,16},{16,20},{20,24},{24,28},{1,5},{5,9},{9,... | collective-permute-start | bytes 786440 | tf_op jit(solution)/shard_map/ppermute | solution.py:16
  62.2 1.1 copy-start.2
  62.2 2.4 %copy-start = (bf16[256,8192]{1,0:T(8,128)(2,1)S(1)}, bf16[256,8192]{1,0:T(8,128)(2,1)}, u32[]{:S(2)}) copy-start(bf16[256,8192]{1,0:T(8,128)(2,1)} %param.17) | copy-start | bytes 12582916
  67.8 0.9 copy-start.4
  68.8 8.3 %collective-permute-start = (bf16[256,512]{0,1:T(8,128)(2,1)S(1)}, bf16[256,512]{0,1:T(8,128)(2,1)S(1)}, u32[]{:S(2)}, u32[]{:S(2)}) collective-permute-start(bf16[256,512]{0,1:T(8,128)(2,1)S(1)} %get-tuple-element.223), channel_id=1, source_target_pairs={{0,4},{4,8},{8,12},{12,16},{16,20},{20,24},{24,28},{1,5},{5,9},{9,... | collective-permute-start | bytes 786440 | tf_op jit(solution)/shard_map/while/body/eval_jaxpr/ppermute | solution.py:16
  77.8 8.3 %collective-permute-start = (bf16[256,512]{0,1:T(8,128)(2,1)S(1)}, bf16[256,512]{0,1:T(8,128)(2,1)S(1)}, u32[]{:S(2)}, u32[]{:S(2)}) collective-permute-start(bf16[256,512]{0,1:T(8,128)(2,1)S(1)} %get-tuple-element.223), channel_id=1, source_target_pairs={{0,4},{4,8},{8,12},{12,16},{16,20},{20,24},{24,28},{1,5},{5,9},{9,... | collective-permute-start | bytes 786440 | tf_op jit(solution)/shard_map/while/body/eval_jaxpr/ppermute | solution.py:16
  86.9 8.3 %collective-permute-start = (bf16[256,512]{0,1:T(8,128)(2,1)S(1)}, bf16[256,512]{0,1:T(8,128)(2,1)S(1)}, u32[]{:S(2)}, u32[]{:S(2)}) collective-permute-start(bf16[256,512]{0,1:T(8,128)(2,1)S(1)} %get-tuple-element.223), channel_id=1, source_target_pairs={{0,4},{4,8},{8,12},{12,16},{16,20},{20,24},{24,28},{1,5},{5,9},{9,... | collective-permute-start | bytes 786440 | tf_op jit(solution)/shard_map/while/body/eval_jaxpr/ppermute | solution.py:16
  96.1 9.0 %collective-permute-start = (bf16[256,512]{0,1:T(8,128)(2,1)S(1)}, bf16[256,512]{0,1:T(8,128)(2,1)S(1)}, u32[]{:S(2)}, u32[]{:S(2)}) collective-permute-start(bf16[256,512]{0,1:T(8,128)(2,1)S(1)} %get-tuple-element.223), channel_id=1, source_target_pairs={{0,4},{4,8},{8,12},{12,16},{16,20},{20,24},{24,28},{1,5},{5,9},{9,... | collective-permute-start | bytes 786440 | tf_op jit(solution)/shard_map/while/body/eval_jaxpr/ppermute | solution.py:16
  105.9 9.7 %collective-permute-start = (bf16[256,512]{0,1:T(8,128)(2,1)S(1)}, bf16[256,512]{0,1:T(8,128)(2,1)S(1)}, u32[]{:S(2)}, u32[]{:S(2)}) collective-permute-start(bf16[256,512]{0,1:T(8,128)(2,1)S(1)} %get-tuple-element.223), channel_id=1, source_target_pairs={{0,4},{4,8},{8,12},{12,16},{16,20},{20,24},{24,28},{1,5},{5,9},{9,... | collective-permute-start | bytes 786440 | tf_op jit(solution)/shard_map/while/body/eval_jaxpr/ppermute | solution.py:16
  116.4 11.1 %collective-permute-start = (bf16[256,512]{0,1:T(8,128)(2,1)S(1)}, bf16[256,512]{0,1:T(8,128)(2,1)S(1)}, u32[]{:S(2)}, u32[]{:S(2)}) collective-permute-start(bf16[256,512]{0,1:T(8,128)(2,1)S(1)} %get-tuple-element.223), channel_id=1, source_target_pairs={{0,4},{4,8},{8,12},{12,16},{16,20},{20,24},{24,28},{1,5},{5,9},{9,... | collective-permute-start | bytes 786440 | tf_op jit(solution)/shard_map/while/body/eval_jaxpr/ppermute | solution.py:16
  128.4 9.5 %collective-permute-start = (bf16[256,512]{0,1:T(8,128)(2,1)S(1)}, bf16[256,512]{0,1:T(8,128)(2,1)S(1)}, u32[]{:S(2)}, u32[]{:S(2)}) collective-permute-start(bf16[256,512]{0,1:T(8,128)(2,1)S(1)} %get-tuple-element.223), channel_id=1, source_target_pairs={{0,4},{4,8},{8,12},{12,16},{16,20},{20,24},{24,28},{1,5},{5,9},{9,... | collective-permute-start | bytes 786440 | tf_op jit(solution)/shard_map/while/body/eval_jaxpr/ppermute | solution.py:16
Sparse Core Ops, SparseCore 0:
  68.0 45.5 reduce-scatter.1
where the time goes:
time: 149 us; the launch traced here: 146 us
  waiting for transfers between devices  59 us (40%)
  starting transfers between devices  49.5 us (33%)
  between operations  14.2 us (10%)
  matrix products  9.94 us (7%)
  local copies, waits for them, and re-layouts  9.09 us (6%)
  other arithmetic  4.16 us (3%)
    ppermute x8, starting transfers between devices, from_behind(): lax.ppermute(value, axis, [(source, source + steps) for source in range(f...  38 us
    ppermute x8, waiting for transfers between devices, from_behind(): lax.ppermute(value, axis, [(source, source + steps) for source in range(f...  32.7 us
    all_to_all x1, waiting for transfers between devices, shards(): lax.all_to_all(outgoing, 'ctx', split_axis=0, concat_axis=0, tiled=True)  24.3 us
    all_to_all x1, starting transfers between devices, shards(): lax.all_to_all(labels, 'ctx', split_axis=0, concat_axis=0, tiled=True)  7.28 us
    unnamed x19, local copies, waits for them, and re-layouts  4.62 us
    all_to_all x1, starting transfers between devices, shards(): lax.all_to_all(outgoing, 'ctx', split_axis=0, concat_axis=0, tiled=True)  4.16 us
    dot_general x1, matrix products, shards(): term = jnp.dot(cross_heads, w_cross, preferred_element_type=jnp.float32)  3.19 us
  transfers between devices with their start and end apart: 11, of which 10 were waited for; matrix products, arithmetic and copies ran while one was open for 9% of the time, Pallas kernels for 0%

commit v1 on v0

v1 whole, which is shorter than its diff:
```python
import functools
import math

import jax
import jax.numpy as jnp
from jax import lax
from jax.experimental import pallas as pl
from jax.experimental.pallas import tpu as pltpu
from jax.sharding import PartitionSpec as P

HD = 128
BLOCK = 64
NEGATIVE = -1e30
SCALE = HD ** -0.5 * math.log2(math.e)
VMEM = pl.BlockSpec(memory_space=pltpu.VMEM)
SMEM = pl.BlockSpec(memory_space=pltpu.SMEM)
ANY = pl.BlockSpec(memory_space=pl.ANY)
PARAMS = pltpu.CompilerParams(vmem_limit_bytes=40 * 1024 * 1024)


def dot(a, b):
    return jnp.dot(a, b, preferred_element_type=jnp.float32)


def dot_t(a, b):
    return lax.dot_general(a, b, (((1,), (1,)), ((), ())), preferred_element_type=jnp.float32)


def arrange_kernel(slot_ref, keys_ref, values_ref, out_ref, label_ref, sems):
    count = keys_ref.shape[0]
    copies = []
    for owner in range(label_ref.shape[0]):
        label_ref[owner] = -1
    for n in range(count):
        slot = slot_ref[n]
        owner = slot // count
        label_ref[owner] = slot - owner * count
        copies.append(pltpu.make_async_copy(keys_ref.at[n], out_ref.at[owner, 0], sems.at[2 * n]))
        copies.append(pltpu.make_async_copy(values_ref.at[n], out_ref.at[owner, 1], sems.at[2 * n + 1]))
    for copy in copies:
        copy.start()
    for copy in copies:
        copy.wait()


def arrange(slots, keys, values, owners):
    count, length, width = keys.shape
    return pl.pallas_call(
        arrange_kernel,
        out_shape=(
            jax.ShapeDtypeStruct((owners, 2, length, width), keys.dtype),
            jax.ShapeDtypeStruct((owners,), jnp.int32),
        ),
        in_specs=[SMEM, ANY, ANY],
        out_specs=(ANY, SMEM),
        scratch_shapes=[pltpu.SemaphoreType.DMA((2 * count,))],
    )(slots, keys, values)


def cross_kernel(label_ref, queries_ref, incoming_ref, out_ref, order_ref):
    sources = label_ref.shape[0]
    for source in range(sources):
        label = label_ref[source]

        @pl.when(label >= 0)
        def _():
            order_ref[label] = source

    rows, width = queries_ref.shape
    for block in range(rows // BLOCK):
        at = pl.ds(block * BLOCK, BLOCK)
        first = order_ref[2 * block]
        second = order_ref[2 * block + 1]
        for head in range(width // HD):
            feats = pl.ds(head * HD, HD)
            q = queries_ref[at, feats]
            s1 = dot_t(q, incoming_ref[first, 0, :, feats])
            s2 = dot_t(q, incoming_ref[second, 0, :, feats])
            peak = jnp.maximum(
                jnp.max(s1, axis=1, keepdims=True), jnp.max(s2, axis=1, keepdims=True)
            )
            p1 = jnp.exp2((s1 - peak) * SCALE)
            p2 = jnp.exp2((s2 - peak) * SCALE)
            total = jnp.sum(p1, axis=1, keepdims=True) + jnp.sum(p2, axis=1, keepdims=True)
            mixed = dot(p1.astype(jnp.bfloat16), incoming_ref[first, 1, :, feats])
            mixed += dot(p2.astype(jnp.bfloat16), incoming_ref[second, 1, :, feats])
            out_ref[at, feats] = (mixed / total).astype(out_ref.dtype)


def cross_attend(labels, queries, incoming):
    return pl.pallas_call(
        cross_kernel,
        out_shape=jax.ShapeDtypeStruct(queries.shape, queries.dtype),
        in_specs=[SMEM, VMEM, VMEM],
        out_specs=VMEM,
        scratch_shapes=[pltpu.SMEM((2 * queries.shape[0] // BLOCK,), jnp.int32)],
        compiler_params=PARAMS,
    )(labels, queries, incoming)


def self_kernel(first, last, step, pair_ref, q_ref, kv_ref, *refs):
    if not first:
        peak_in, total_in, accum_in = refs[:3]
        refs = refs[3:]
    rows = q_ref.shape[0]
    tile = rows // 2
    for part in range(2):
        at = pl.ds(part * tile, tile)

        def emit(peak, total, accum):
            if last:
                refs[0][at, :] = (accum / total).astype(jnp.bfloat16)
            else:
                refs[0][at, :] = jnp.broadcast_to(peak, (tile, HD))
                refs[1][at, :] = jnp.broadcast_to(total, (tile, HD))
                refs[2][at, :] = accum

        def work():
            q = q_ref[at, :]
            count = (part + 1) * tile if first else rows
            s = dot_t(q, kv_ref[:count, :HD])
            if first:
                row = lax.broadcasted_iota(jnp.int32, (tile, count), 0) + part * tile
                col = lax.broadcasted_iota(jnp.int32, (tile, count), 1)
                s = jnp.where(col <= row, s, NEGATIVE)
            peak = jnp.max(s, axis=1, keepdims=True)
            if not first:
                old = peak_in[at, :1]
                peak = jnp.maximum(peak, old)
                factor = jnp.exp2((old - peak) * SCALE)
            p = jnp.exp2((s - peak) * SCALE)
            total = jnp.sum(p, axis=1, keepdims=True)
            accum = dot(p.astype(jnp.bfloat16), kv_ref[:count, HD:])
            if not first:
                total += total_in[at, :1] * factor
                accum += accum_in[at, :] * factor
            emit(peak, total, accum)

        if first:
            work()
        else:
            pl.when(pair_ref[0] >= step)(work)

            @pl.when(pair_ref[0] < step)
            def _():
                emit(peak_in[at, :1], total_in[at, :1], accum_in[at, :])


def self_step(pair, q, kv, state, step, last):
    rows = q.shape[0]
    first = state is None
    held = jax.ShapeDtypeStruct((rows, HD), jnp.float32)
    out_shape = jax.ShapeDtypeStruct((rows, HD), jnp.bfloat16) if last else (held,) * 3
    return pl.pallas_call(
        functools.partial(self_kernel, first, last, step),
        out_shape=out_shape,
        in_specs=[SMEM] + [VMEM] * (2 if first else 5),
        out_specs=VMEM if last else (VMEM,) * 3,
        compiler_params=PARAMS,
    )(pair, q, kv, *(() if first else state))


def project_kernel(groups, column_ref, *refs):
    crossed_ref = refs[-1]
    total = dot(refs[0][...], refs[groups][...])
    for group in range(1, groups):
        total += dot(refs[group][...], refs[groups + group][...])
    crossed_ref[...] = total.astype(crossed_ref.dtype)


def project(column, terms, weights, own_weight):
    groups = len(terms)
    rows, depth = terms[0].shape
    width = own_weight.shape[1] // groups
    tile = min(512, width)
    per = width // tile
    whole = pl.BlockSpec((rows, depth), lambda j, c: (0, 0))
    moved = pl.BlockSpec((depth, tile), lambda j, c: (0, j))
    own = pl.BlockSpec((depth, tile), lambda j, c: (0, c[0] * per + j))
    return pl.pallas_call(
        functools.partial(project_kernel, groups),
        out_shape=jax.ShapeDtypeStruct((rows, width), jnp.bfloat16),
        grid_spec=pltpu.PrefetchScalarGridSpec(
            num_scalar_prefetch=1,
            grid=(per,),
            in_specs=[whole] * groups + [own] + [moved] * (groups - 1),
            out_specs=pl.BlockSpec((rows, tile), lambda j, c: (0, j)),
        ),
        compiler_params=PARAMS,
    )(column, *terms, own_weight, *weights)


def shards(queries, keys, values, cross_queries, nbr_keys, nbr_values, nbr_slot, w_cross):
    ctx = lax.axis_index("ctx")
    count = lax.axis_size("ctx")
    tp = lax.axis_index("tp")
    groups = lax.axis_size("tp")
    side = ctx % 2
    pair = (ctx // 2).reshape(1)
    rows = queries.shape[0]
    width = w_cross.shape[1] // groups

    outgoing, labels = arrange(nbr_slot, nbr_keys, nbr_values, count)
    incoming = lax.all_to_all(outgoing, "ctx", split_axis=0, concat_axis=0, tiled=True)

    swap = [(i, i ^ 1) for i in range(count)]
    self_all = jnp.stack([queries, keys, values])
    lower, upper = self_all[:, :, :HD], self_all[:, :, HD:]
    mine = jnp.where(side == 0, lower, upper)
    other = lax.ppermute(jnp.where(side == 0, upper, lower), "ctx", swap)
    spill = lax.ppermute(cross_queries[: BLOCK - 1], "ctx", [(i + 1, i) for i in range(count - 1)])

    weights = []
    for step in range(1, groups):
        block = lax.dynamic_slice_in_dim(w_cross, (tp ^ step) * width, width, axis=1)
        weights.append(lax.ppermute(block, "tp", [(i, i ^ step) for i in range(groups)]))
    labels = lax.all_to_all(labels, "ctx", split_axis=0, concat_axis=0, tiled=True)

    joint = jnp.where(
        side == 0, jnp.concatenate([mine, other], 1), jnp.concatenate([other, mine], 1)
    )
    q = joint[0]
    kv = jnp.concatenate([joint[1], joint[2]], axis=1)
    forward = [(i, i + 2) for i in range(count - 2)]
    pairs = count // 2
    state = None
    for step in range(pairs):
        following = lax.ppermute(kv, "ctx", forward) if step < pairs - 1 else None
        state = self_step(pair, q, kv, state, step, step == pairs - 1)
        kv = following
    near = jnp.where(side == 0, state[:rows], state[rows:])
    far = lax.ppermute(jnp.where(side == 0, state[rows:], state[:rows]), "ctx", swap)
    attended = jnp.where(
        side == 0, jnp.concatenate([near, far], 1), jnp.concatenate([far, near], 1)
    )

    shifted = jnp.concatenate([cross_queries[BLOCK - 1 :], spill], axis=0)
    answers = cross_attend(labels, shifted, incoming)
    back = lax.ppermute(
        answers[rows - BLOCK + 1 :], "ctx", [(i, i + 1) for i in range(count - 1)]
    )
    cca = jnp.concatenate([back, answers[: rows - BLOCK + 1]], axis=0)
    terms = [cca]
    for step in range(1, groups):
        terms.append(lax.ppermute(cca, "tp", [(i, i ^ step) for i in range(groups)]))
    crossed = project(tp.reshape(1), terms, weights, w_cross)
    return (attended, crossed)


def solution(mesh):
    in_specs = (
        P("ctx", "tp"),
        P("ctx", "tp"),
        P("ctx", "tp"),
        P("ctx", "tp"),
        P("ctx", None, "tp"),
        P("ctx", None, "tp"),
        P("ctx"),
        P("tp", None),
    )
    out_specs = (P("ctx", "tp"), P("ctx", "tp"))
    return jax.shard_map(shards, mesh=mesh, in_specs=in_specs, out_specs=out_specs, check_vma=False)
```

time: 149 us -> 137 us (0.919)
  Pallas kernels: 0 us -> 44.6 us
  waiting for transfers between devices: 59 us -> 32.6 us
  between operations: 14.2 us -> 0.83 us
  matrix products: 9.94 us -> 0 us
  starting transfers between devices: 49.5 us -> 39.6 us
  local copies, waits for them, and re-layouts: 9.09 us -> 12.6 us
    pallas_call x0 -> x7, Pallas kernels: none -> 44.6 us  [the longest x1 34.2 us: arrange(): pl.pallas_call(arrange_kernel, out_shape=(jax.ShapeDtypeStruct((owners, 2...]
    all_to_all x1, waiting for transfers between devices: 24.3 us -> 0.01 us  [shards(): lax.all_to_all(outgoing, 'ctx', split_axis=0, concat_axis=0, tiled=True)]
    dot_general x21 -> x0, matrix products: 9.94 us -> none  [the longest x1 3.19 us: shards(): term = jnp.dot(cross_heads, w_cross, preferred_element_type=jnp.float32)]
    ppermute x8 -> x13, starting transfers between devices: 38 us -> 28.7 us  [the longest x3 15.9 us: shards(): following = lax.ppermute(kv, 'ctx', forward) if step < pairs - 1 else None]
    ppermute x8 -> x13, waiting for transfers between devices: 32.7 us -> 27.3 us  [the longest x1 12.8 us: shards(): other = lax.ppermute(jnp.where(side == 0, upper, lower), 'ctx', swap)]
    dynamic_slice x0 -> x1, local copies, waits for them, and re-layouts: none -> 3.64 us  [shards(): lax.dynamic_slice_in_dim(w_cross, (tp ^ step) * width, width, axis=1)]
    all_to_all x1, waiting for transfers between devices: 1.97 us -> 5.31 us  [shards(): lax.all_to_all(labels, 'ctx', split_axis=0, concat_axis=0, tiled=True)]
    convert_element_type x3 -> x0, local copies, waits for them, and re-layouts: 1.77 us -> none  [the longest x1 1.28 us: shards(): outgoing = jnp.einsum('dn,nlc->dlc', matched.astype(jnp.bfloat16), held,...]
  transfers between devices with their start and end apart: 11 -> 15, of which waited for: 10 -> 9; matrix products, arithmetic and copies ran while one was open for 9% -> 8% of each run, Pallas kernels for 0% -> 5%
where the time goes in v1:
time: 137 us; the launch traced here: 134 us
  Pallas kernels  44.6 us (33%)
  starting transfers between devices  39.6 us (29%)
  waiting for transfers between devices  32.6 us (24%)
  local copies, waits for them, and re-layouts  12.6 us (9%)
  other arithmetic  3.8 us (3%)
    pallas_call x1, Pallas kernels, arrange(): pl.pallas_call(arrange_kernel, out_shape=(jax.ShapeDtypeStruct((owners, 2...  34.2 us
    ppermute x3, starting transfers between devices, shards(): following = lax.ppermute(kv, 'ctx', forward) if step < pairs - 1 else None  15.9 us
    ppermute x1, waiting for transfers between devices, shards(): other = lax.ppermute(jnp.where(side == 0, upper, lower), 'ctx', swap)  12.8 us
    all_to_all x1, starting transfers between devices, shards(): lax.all_to_all(labels, 'ctx', split_axis=0, concat_axis=0, tiled=True)  7.28 us
    ppermute x3, waiting for transfers between devices, shards(): lax.ppermute(cca, 'tp', [(i, i ^ step) for i in range(groups)])  5.58 us
    all_to_all x1, waiting for transfers between devices, shards(): lax.all_to_all(labels, 'ctx', split_axis=0, concat_axis=0, tiled=True)  5.31 us
    ppermute x1, starting transfers between devices, shards(): lax.ppermute(answers[rows - BLOCK + 1:], 'ctx', [(i, i + 1) for i in rang...  4.82 us
    unnamed x8, local copies, waits for them, and re-layouts  4.74 us
  transfers between devices with their start and end apart: 15, of which 9 were waited for; matrix products, arithmetic and copies ran while one was open for 8% of the time, Pallas kernels for 5%

profile of v1, /device:TPU:0, one launch (start us, length us, event | category | flops | bytes accessed | tf_op | source)
XLA Modules:
  0.0 134.1 jit_solution(1836265528843203895)
XLA Ops:
  0.6 34.2 %shard_map.99 = (bf16[8,2,128,256]{3,2,1,0:T(8,128)(2,1)}, s32[8]{0:T(128)}) custom-call(s32[8]{0:T(128)} %slot_ref.1, bf16[8,128,256]{2,1,0:T(8,128)(2,1)} %keys_ref.1, bf16[8,128,256]{2,1,0:T(8,128)(2,1)} %values_ref.1), custom_call_target="tpu_custom_call" | custom-call | tf_op jit(solution)/shard_map/pallas_call | solution.py:48
  34.9 1.3 copy.11
  36.1 7.3 %all-to-all-start = ((s32[8,1,1]{2,1,0:T(1,128)}), s32[8,1,1]{2,1,0:T(1,128)S(1)}, u32[]{:S(2)}, u32[]{:S(2)}) async-start(s32[8,1,1]{2,1,0:T(1,128)} %copy.11), calls=%async_computation | async-start | bytes 8192 | tf_op jit(solution)/shard_map/all_to_all | solution.py:217
  43.4 1.1 pad_maximum_fusion
  44.5 5.3 %all-to-all-done = s32[8,1,1]{2,1,0:T(1,128)S(1)} async-done(((s32[8,1,1]{2,1,0:T(1,128)}), s32[8,1,1]{2,1,0:T(1,128)S(1)}, u32[]{:S(2)}, u32[]{:S(2)}) %all-to-all-start) | async-done | bytes 64 | tf_op jit(solution)/shard_map/all_to_all | solution.py:217
  49.8 3.6 %all-to-all-start.1 = ((bf16[8,2,128,256]{3,2,1,0:T(8,128)(2,1)}), bf16[8,2,128,256]{3,2,1,0:T(8,128)(2,1)S(1)}, u32[]{:S(2)}, u32[]{:S(2)}) async-start(bf16[8,2,128,256]{3,2,1,0:T(8,128)(2,1)} %get-tuple-element.23), calls=%async_computation.1 | async-start | bytes 2097152 | tf_op jit(solution)/shard_map/all_to_all | solution.py:204
  53.4 2.0 %collective-permute-start = (bf16[3,256,128]{2,1,0:T(8,128)(2,1)S(1)}, bf16[3,256,128]{2,1,0:T(8,128)(2,1)S(1)}, u32[]{:S(2)}, u32[]{:S(2)}) collective-permute-start(bf16[3,256,128]{2,1,0:T(8,128)(2,1)S(1)} %get-tuple-element.31), channel_id=1, source_target_pairs={{0,4},{4,0},{8,12},{12,8},{16,20},{20,16},{24,28},{28,24},{1,5},{5... | collective-permute-start | bytes 589832 | tf_op jit(solution)/shard_map/ppermute | solution.py:210
  55.4 12.8 %collective-permute-done = bf16[3,256,128]{2,1,0:T(8,128)(2,1)S(1)} collective-permute-done((bf16[3,256,128]{2,1,0:T(8,128)(2,1)S(1)}, bf16[3,256,128]{2,1,0:T(8,128)(2,1)S(1)}, u32[]{:S(2)}, u32[]{:S(2)}) %collective-permute-start) | collective-permute-done | bytes 196640 | tf_op jit(solution)/shard_map/ppermute | solution.py:210
  68.2 0.1 maximum_select_fusion
  68.4 1.9 %collective-permute-start.1 = (bf16[512,256]{1,0:T(8,128)(2,1)S(1)}, bf16[512,256]{1,0:T(8,128)(2,1)S(1)}, u32[]{:S(2)}, u32[]{:S(2)}) collective-permute-start(bf16[512,256]{1,0:T(8,128)(2,1)S(1)} %pad_maximum_fusion.1.kv_ref), channel_id=1, source_target_pairs={{0,8},{4,12},{8,16},{12,20},{16,24},{20,28},{1,9},{5,13},{9,17},{1... | collective-permute-start | bytes 786440 | tf_op jit(solution)/shard_map/ppermute | solution.py:228
  70.2 3.6 %constant_dynamic-slice_fusion = (bf16[256,2048]{1,0:T(8,128)(2,1)}, bf16[256,2048]{1,0:T(8,128)(2,1)}, bf16[256,2048]{1,0:T(8,128)(2,1)}) fusion(bf16[256,8192]{1,0:T(8,128)(2,1)} %refs_4_.1, s32[]{:T(128)S(6)} %select_n.74, s32[]{:T(128)S(6)} %select_n.73, s32[]{:T(128)S(6)} %select_n.72), kind=kLoop, calls=%fused_computation.13 | loop fusion | bytes 6291468 | tf_op jit(solution)/shard_map/dynamic_slice | solution.py:215
  73.9 0.0 collective-permute-start.12
  73.9 1.5 %collective-permute-start.11 = (bf16[256,2048]{1,0:T(8,128)(2,1)}, bf16[256,2048]{1,0:T(8,128)(2,1)S(1)}, u32[]{:S(2)}, u32[]{:S(2)}) collective-permute-start(bf16[256,2048]{1,0:T(8,128)(2,1)} %get-tuple-element.25), channel_id=1, source_target_pairs={{0,2},{1,3},{2,0},{3,1},{4,6},{5,7},{6,4},{7,5},{8,10},{9,11},{10,... | collective-permute-start | bytes 3145736 | tf_op jit(solution)/shard_map/ppermute | solution.py:216
  75.4 0.3 collective-permute-start.10
  75.7 0.0 collective-permute-done.1.kv_ref
  75.7 8.8 %collective-permute-start.2 = (bf16[512,256]{1,0:T(8,128)(2,1)S(1)}, bf16[512,256]{1,0:T(8,128)(2,1)}, u32[]{:S(2)}, u32[]{:S(2)}) collective-permute-start(bf16[512,256]{1,0:T(8,128)(2,1)S(1)} %collective-permute-done.1.kv_ref), channel_id=1, source_target_pairs={{0,8},{4,12},{8,16},{12,20},{16,24},{20,28},{1,9},{5,13},{9,17},{1... | collective-permute-start | bytes 786440 | tf_op jit(solution)/shard_map/ppermute | solution.py:228
  84.6 0.0 copy-start.2
  84.6 0.7 copy-done.2
  85.3 3.2 %collective-permute-done.2.kv_ref = bf16[512,256]{1,0:T(8,128)(2,1)} collective-permute-done((bf16[512,256]{1,0:T(8,128)(2,1)S(1)}, bf16[512,256]{1,0:T(8,128)(2,1)}, u32[]{:S(2)}, u32[]{:S(2)}) %collective-permute-start.2) | collective-permute-done | bytes 262176 | tf_op jit(solution)/shard_map/ppermute | solution.py:228
  88.4 5.2 %collective-permute-start.3 = (bf16[512,256]{1,0:T(8,128)(2,1)}, bf16[512,256]{1,0:T(8,128)(2,1)}, u32[]{:S(2)}, u32[]{:S(2)}) collective-permute-start(bf16[512,256]{1,0:T(8,128)(2,1)} %collective-permute-done.2.kv_ref), channel_id=1, source_target_pairs={{0,8},{4,12},{8,16},{12,20},{16,24},{20,28},{1,9},{5,13},{9,17},{1... | collective-permute-start | bytes 786440 | tf_op jit(solution)/shard_map/ppermute | solution.py:228
  93.6 1.4 %slice.43 = bf16[63,256]{1,0:T(8,128)(2,1)} slice(bf16[256,256]{1,0:T(8,128)(2,1)} %param.11), slice={[0:63], [0:256]} | slice | bytes 64512 | tf_op jit(solution)/shard_map/slice | solution.py:211
  95.0 1.3 collective-permute-start.5
  96.3 1.6 %slice.42 = bf16[193,256]{1,0:T(8,128)(2,1)} slice(bf16[256,256]{1,0:T(8,128)(2,1)} %param.11), slice={[63:256], [0:256]} | slice | bytes 197632 | tf_op jit(solution)/shard_map/slice | solution.py:237
  97.8 0.2 reduce.label_ref
  98.1 3.9 %collective-permute-done.5 = bf16[63,256]{1,0:T(8,128)(2,1)} collective-permute-done((bf16[63,256]{1,0:T(8,128)(2,1)}, bf16[63,256]{1,0:T(8,128)(2,1)}, u32[]{:S(2)}, u32[]{:S(2)}) %collective-permute-start.5) | collective-permute-done | bytes 32288 | tf_op jit(solution)/shard_map/ppermute | solution.py:211
  102.0 1.6 %pad_maximum_fusion.2.queries_ref = bf16[256,256]{1,0:T(8,128)(2,1)} fusion(bf16[63,256]{1,0:T(8,128)(2,1)} %collective-permute-done.5, bf16[193,256]{1,0:T(8,128)(2,1)} %slice.42), kind=kLoop, calls=%fused_computation.9 | loop fusion | flops 262144 | bytes 262144 | tf_op jit(solution)/shard_map/concatenate | solution.py:237
  103.6 0.7 shard_map.95
  104.3 0.0 copy-start.3
  104.3 0.9 copy-done.3
  105.3 0.3 shard_map.96
  105.5 1.2 shard_map.97
  106.7 0.0 collective-permute-done.3.kv_ref
  106.8 1.2 shard_map.98
  107.9 0.0 all-to-all-done.1.incoming_ref
  107.9 0.0 copy-start.1
  108.0 0.9 copy-done.1
  108.9 2.7 %shard_map.100 = bf16[256,256]{1,0:T(8,128)(2,1)S(1)} custom-call(s32[8]{0:T(128)S(1)} %reduce.label_ref, bf16[256,256]{1,0:T(8,128)(2,1)S(1)} %copy-done.1, bf16[8,2,128,256]{3,2,1,0:T(8,128)(2,1)S(1)} %all-to-all-done.1.incoming_ref), custom_call_target="tpu_custom_call" | custom-call | tf_op jit(solution)/shard_map/pallas_call | solution.py:91
  111.6 4.8 %collective-permute-start.6 = (bf16[63,256]{1,0:T(8,128)(2,1)S(1)}, bf16[63,256]{1,0:T(8,128)(2,1)S(1)}, u32[]{:S(2)}, u32[]{:S(2)}) collective-permute-start(bf16[63,256]{1,0:T(8,128)(2,1)S(1)} %slice.53), channel_id=1, source_target_pairs={{0,4},{4,8},{8,12},{12,16},{16,20},{20,24},{24,28},{1,5},{5,9},{9,... | collective-permute-start | bytes 96776 | tf_op jit(solution)/shard_map/ppermute | solution.py:239
  116.5 1.3 collective-permute-start.4
  117.7 0.3 collective-permute-done.6
  118.0 0.1 collective-permute-start.9
  118.1 0.0 collective-permute-done.12.refs_7_
  118.1 1.6 %collective-permute-start.8 = (bf16[256,256]{1,0:T(8,128)(2,1)S(1)}, bf16[256,256]{1,0:T(8,128)(2,1)S(1)}, u32[]{:S(2)}, u32[]{:S(2)}) collective-permute-start(bf16[256,256]{1,0:T(8,128)(2,1)S(1)} %pad_maximum_fusion.3.refs_0_), channel_id=1, source_target_pairs={{0,2},{1,3},{2,0},{3,1},{4,6},{5,7},{6,4},{7,5},{8,10},{9,11},{10,... | collective-permute-start | bytes 393224 | tf_op jit(solution)/shard_map/ppermute | solution.py:245
  119.7 1.1 collective-permute-done.4
  120.8 0.0 collective-permute-start.7
  120.8 0.7 maximum_select_fusion.1
  121.5 0.6 collective-permute-done.11.refs_6_
  122.0 0.0 collective-permute-done.10.refs_5_
  122.1 2.7 %collective-permute-done.9.refs_3_ = bf16[256,256]{1,0:T(8,128)(2,1)S(1)} collective-permute-done((bf16[256,256]{1,0:T(8,128)(2,1)S(1)}, bf16[256,256]{1,0:T(8,128)(2,1)S(1)}, u32[]{:S(2)}, u32[]{:S(2)}) %collective-permute-start.9) | collective-permute-done | bytes 131104 | tf_op jit(solution)/shard_map/ppermute | solution.py:245
  124.8 2.9 %collective-permute-done.8.refs_2_ = bf16[256,256]{1,0:T(8,128)(2,1)S(1)} collective-permute-done((bf16[256,256]{1,0:T(8,128)(2,1)S(1)}, bf16[256,256]{1,0:T(8,128)(2,1)S(1)}, u32[]{:S(2)}, u32[]{:S(2)}) %collective-permute-start.8) | collective-permute-done | bytes 131104 | tf_op jit(solution)/shard_map/ppermute | solution.py:245
  127.6 0.0 collective-permute-done.7.refs_1_
  127.6 0.0 copy-start
  127.6 2.2 %copy-done = bf16[256,8192]{1,0:T(8,128)(2,1)S(1)} copy-done((bf16[256,8192]{1,0:T(8,128)(2,1)S(1)}, bf16[256,8192]{1,0:T(8,128)(2,1)}, u32[]{:S(2)}) %copy-start) | copy-done | bytes 4194328
  129.8 4.2 %shard_map.101 = bf16[256,2048]{1,0:T(8,128)(2,1)} custom-call(s32[1]{0:T(128)} %bitcast.7.column_ref, bf16[256,256]{1,0:T(8,128)(2,1)S(1)} %pad_maximum_fusion.3.refs_0_, bf16[256,256]{1,0:T(8,128)(2,1)S(1)} %collective-permute-done.7.refs_1_, bf16[256,256]{1,0:T(8,128)(2,1)S(1)} %collective-permute-done.8.refs_2_, ...), custom_call_target="tpu_custom_call" | custom-call | tf_op jit(solution)/shard_map/pallas_call | solution.py:180
  (7 shorter events, 0.2 us)
Async XLA Ops:
  36.1 13.7 %all-to-all-start = ((s32[8,1,1]{2,1,0:T(1,128)}), s32[8,1,1]{2,1,0:T(1,128)S(1)}, u32[]{:S(2)}, u32[]{:S(2)}) async-start(s32[8,1,1]{2,1,0:T(1,128)} %copy.11), calls=%async_computation | async-start | bytes 8192 | tf_op jit(solution)/shard_map/all_to_all | solution.py:217
  49.8 58.1 %all-to-all-start.1 = ((bf16[8,2,128,256]{3,2,1,0:T(8,128)(2,1)}), bf16[8,2,128,256]{3,2,1,0:T(8,128)(2,1)S(1)}, u32[]{:S(2)}, u32[]{:S(2)}) async-start(bf16[8,2,128,256]{3,2,1,0:T(8,128)(2,1)} %get-tuple-element.23), calls=%async_computation.1 | async-start | bytes 2097152 | tf_op jit(solution)/shard_map/all_to_all | solution.py:204
  53.4 14.8 %collective-permute-start = (bf16[3,256,128]{2,1,0:T(8,128)(2,1)S(1)}, bf16[3,256,128]{2,1,0:T(8,128)(2,1)S(1)}, u32[]{:S(2)}, u32[]{:S(2)}) collective-permute-start(bf16[3,256,128]{2,1,0:T(8,128)(2,1)S(1)} %get-tuple-element.31), channel_id=1, source_target_pairs={{0,4},{4,0},{8,12},{12,8},{16,20},{20,16},{24,28},{28,24},{1,5},{5... | collective-permute-start | bytes 589832 | tf_op jit(solution)/shard_map/ppermute | solution.py:210
  68.4 7.4 %collective-permute-start.1 = (bf16[512,256]{1,0:T(8,128)(2,1)S(1)}, bf16[512,256]{1,0:T(8,128)(2,1)S(1)}, u32[]{:S(2)}, u32[]{:S(2)}) collective-permute-start(bf16[512,256]{1,0:T(8,128)(2,1)S(1)} %pad_maximum_fusion.1.kv_ref), channel_id=1, source_target_pairs={{0,8},{4,12},{8,16},{12,20},{16,24},{20,28},{1,9},{5,13},{9,17},{1... | collective-permute-start | bytes 786440 | tf_op jit(solution)/shard_map/ppermute | solution.py:228
  73.9 44.2 %collective-permute-start.12 = (bf16[256,2048]{1,0:T(8,128)(2,1)}, bf16[256,2048]{1,0:T(8,128)(2,1)S(1)}, u32[]{:S(2)}, u32[]{:S(2)}) collective-permute-start(bf16[256,2048]{1,0:T(8,128)(2,1)} %get-tuple-element.24), channel_id=1, source_target_pairs={{0,3},{1,2},{2,1},{3,0},{4,7},{5,6},{6,5},{7,4},{8,11},{9,10},{10,... | collective-permute-start | bytes 3145736 | tf_op jit(solution)/shard_map/ppermute | solution.py:216
  73.9 48.2 %collective-permute-start.11 = (bf16[256,2048]{1,0:T(8,128)(2,1)}, bf16[256,2048]{1,0:T(8,128)(2,1)S(1)}, u32[]{:S(2)}, u32[]{:S(2)}) collective-permute-start(bf16[256,2048]{1,0:T(8,128)(2,1)} %get-tuple-element.25), channel_id=1, source_target_pairs={{0,2},{1,3},{2,0},{3,1},{4,6},{5,7},{6,4},{7,5},{8,10},{9,11},{10,... | collective-permute-start | bytes 3145736 | tf_op jit(solution)/shard_map/ppermute | solution.py:216
  75.4 46.7 %collective-permute-start.10 = (bf16[256,2048]{1,0:T(8,128)(2,1)}, bf16[256,2048]{1,0:T(8,128)(2,1)}, u32[]{:S(2)}, u32[]{:S(2)}) collective-permute-start(bf16[256,2048]{1,0:T(8,128)(2,1)} %get-tuple-element.26), channel_id=1, source_target_pairs={{0,1},{1,0},{2,3},{3,2},{4,5},{5,4},{6,7},{7,6},{8,9},{9,8},{10,11... | collective-permute-start | bytes 3145736 | tf_op jit(solution)/shard_map/ppermute | solution.py:216
  75.7 12.7 %collective-permute-start.2 = (bf16[512,256]{1,0:T(8,128)(2,1)S(1)}, bf16[512,256]{1,0:T(8,128)(2,1)}, u32[]{:S(2)}, u32[]{:S(2)}) collective-permute-start(bf16[512,256]{1,0:T(8,128)(2,1)S(1)} %collective-permute-done.1.kv_ref), channel_id=1, source_target_pairs={{0,8},{4,12},{8,16},{12,20},{16,24},{20,28},{1,9},{5,13},{9,17},{1... | collective-permute-start | bytes 786440 | tf_op jit(solution)/shard_map/ppermute | solution.py:228
  84.6 0.7 copy-start.2
  88.4 18.3 %collective-permute-start.3 = (bf16[512,256]{1,0:T(8,128)(2,1)}, bf16[512,256]{1,0:T(8,128)(2,1)}, u32[]{:S(2)}, u32[]{:S(2)}) collective-permute-start(bf16[512,256]{1,0:T(8,128)(2,1)} %collective-permute-done.2.kv_ref), channel_id=1, source_target_pairs={{0,8},{4,12},{8,16},{12,20},{16,24},{20,28},{1,9},{5,13},{9,17},{1... | collective-permute-start | bytes 786440 | tf_op jit(solution)/shard_map/ppermute | solution.py:228
  95.0 7.0 %collective-permute-start.5 = (bf16[63,256]{1,0:T(8,128)(2,1)}, bf16[63,256]{1,0:T(8,128)(2,1)}, u32[]{:S(2)}, u32[]{:S(2)}) collective-permute-start(bf16[63,256]{1,0:T(8,128)(2,1)} %slice.43), channel_id=1, source_target_pairs={{4,0},{8,4},{12,8},{16,12},{20,16},{24,20},{28,24},{5,1},{9,5},{13... | collective-permute-start | bytes 96776 | tf_op jit(solution)/shard_map/ppermute | solution.py:211
  104.3 1.0 copy-start.3
  107.9 0.9 copy-start.1
  111.6 6.4 %collective-permute-start.6 = (bf16[63,256]{1,0:T(8,128)(2,1)S(1)}, bf16[63,256]{1,0:T(8,128)(2,1)S(1)}, u32[]{:S(2)}, u32[]{:S(2)}) collective-permute-start(bf16[63,256]{1,0:T(8,128)(2,1)S(1)} %slice.53), channel_id=1, source_target_pairs={{0,4},{4,8},{8,12},{12,16},{16,20},{20,24},{24,28},{1,5},{5,9},{9,... | collective-permute-start | bytes 96776 | tf_op jit(solution)/shard_map/ppermute | solution.py:239
  116.5 4.3 %collective-permute-start.4 = (bf16[256,128]{1,0:T(8,128)(2,1)S(1)}, bf16[256,128]{1,0:T(8,128)(2,1)S(1)}, u32[]{:S(2)}, u32[]{:S(2)}) collective-permute-start(bf16[256,128]{1,0:T(8,128)(2,1)S(1)} %get-tuple-element.33), channel_id=1, source_target_pairs={{0,4},{4,0},{8,12},{12,8},{16,20},{20,16},{24,28},{28,24},{1,5},{5... | collective-permute-start | bytes 196616 | tf_op jit(solution)/shard_map/ppermute | solution.py:232
  118.0 6.7 %collective-permute-start.9 = (bf16[256,256]{1,0:T(8,128)(2,1)S(1)}, bf16[256,256]{1,0:T(8,128)(2,1)S(1)}, u32[]{:S(2)}, u32[]{:S(2)}) collective-permute-start(bf16[256,256]{1,0:T(8,128)(2,1)S(1)} %pad_maximum_fusion.3.refs_0_), channel_id=1, source_target_pairs={{0,3},{1,2},{2,1},{3,0},{4,7},{5,6},{6,5},{7,4},{8,11},{9,10},{10,... | collective-permute-start | bytes 393224 | tf_op jit(solution)/shard_map/ppermute | solution.py:245
  118.1 9.5 %collective-permute-start.8 = (bf16[256,256]{1,0:T(8,128)(2,1)S(1)}, bf16[256,256]{1,0:T(8,128)(2,1)S(1)}, u32[]{:S(2)}, u32[]{:S(2)}) collective-permute-start(bf16[256,256]{1,0:T(8,128)(2,1)S(1)} %pad_maximum_fusion.3.refs_0_), channel_id=1, source_target_pairs={{0,2},{1,3},{2,0},{3,1},{4,6},{5,7},{6,4},{7,5},{8,10},{9,11},{10,... | collective-permute-start | bytes 393224 | tf_op jit(solution)/shard_map/ppermute | solution.py:245
  120.8 6.9 %collective-permute-start.7 = (bf16[256,256]{1,0:T(8,128)(2,1)S(1)}, bf16[256,256]{1,0:T(8,128)(2,1)S(1)}, u32[]{:S(2)}, u32[]{:S(2)}) collective-permute-start(bf16[256,256]{1,0:T(8,128)(2,1)S(1)} %pad_maximum_fusion.3.refs_0_), channel_id=1, source_target_pairs={{0,1},{1,0},{2,3},{3,2},{4,5},{5,4},{6,7},{7,6},{8,9},{9,8},{10,11... | collective-permute-start | bytes 393224 | tf_op jit(solution)/shard_map/ppermute | solution.py:245
  127.6 2.2 %copy-start = (bf16[256,8192]{1,0:T(8,128)(2,1)S(1)}, bf16[256,8192]{1,0:T(8,128)(2,1)}, u32[]{:S(2)}) copy-start(bf16[256,8192]{1,0:T(8,128)(2,1)} %refs_4_.1) | copy-start | bytes 12582916

commit v2 on v1

v2 whole, which is shorter than its diff:
```python
import functools
import math

import jax
import jax.numpy as jnp
from jax import lax
from jax.experimental import pallas as pl
from jax.experimental.pallas import tpu as pltpu
from jax.sharding import PartitionSpec as P

HD = 128
BLOCK = 64
LEAD = 16
NEGATIVE = -1e30
SCALE = HD ** -0.5 * math.log2(math.e)
VMEM = pl.BlockSpec(memory_space=pltpu.VMEM)
SMEM = pl.BlockSpec(memory_space=pltpu.SMEM)
ANY = pl.BlockSpec(memory_space=pl.ANY)
PARAMS = pltpu.CompilerParams(vmem_limit_bytes=40 * 1024 * 1024)


def dot(a, b):
    return jnp.dot(a, b, preferred_element_type=jnp.float32)


def dot_t(a, b):
    return lax.dot_general(a, b, (((1,), (1,)), ((), ())), preferred_element_type=jnp.float32)


def prepare_kernel(groups, side_ref, tp_ref, slot_ref, *refs):
    queries, keys, values, nbr_keys, nbr_values, weight = refs[:6]
    away, mine, outgoing, label_ref = refs[6:10]
    blocks = refs[10 : 10 + groups]
    sems = refs[10 + groups]
    side = side_ref[0]
    tp = tp_ref[0]
    count = nbr_keys.shape[0]
    width = blocks[0].shape[1]
    pieces = []
    for at, source in enumerate((queries, keys, values)):
        lane = pl.multiple_of((1 - side) * HD, HD)
        pieces.append((source.at[:, pl.ds(lane, HD)], away.at[at]))
    for step in range(1, groups):
        column = pl.multiple_of((tp ^ step) * width, HD)
        pieces.append((weight.at[:, pl.ds(column, width)], blocks[step]))
    for owner in range(label_ref.shape[0]):
        label_ref[owner] = -1
    for n in range(count):
        slot = slot_ref[n]
        owner = slot // count
        label_ref[owner] = slot - owner * count
        pieces.append((nbr_keys.at[n], outgoing.at[owner, 0]))
        pieces.append((nbr_values.at[n], outgoing.at[owner, 1]))
    for at, source in enumerate((queries, keys, values)):
        lane = pl.multiple_of(side * HD, HD)
        pieces.append((source.at[:, pl.ds(lane, HD)], mine.at[at]))
    column = pl.multiple_of(tp * width, HD)
    pieces.append((weight.at[:, pl.ds(column, width)], blocks[0]))
    copies = [
        pltpu.make_async_copy(source, target, sems.at[at])
        for at, (source, target) in enumerate(pieces)
    ]
    for copy in copies:
        copy.start()
    for copy in copies:
        copy.wait()


def prepare(side, tp, slots, queries, keys, values, nbr_keys, nbr_values, weight, owners, groups):
    count, length, features = nbr_keys.shape
    rows = queries.shape[0]
    depth = weight.shape[0]
    width = weight.shape[1] // groups
    dtype = queries.dtype
    half = jax.ShapeDtypeStruct((3, rows, HD), dtype)
    result = pl.pallas_call(
        functools.partial(prepare_kernel, groups),
        out_shape=(
            half,
            half,
            jax.ShapeDtypeStruct((owners, 2, length, features), dtype),
            jax.ShapeDtypeStruct((owners,), jnp.int32),
        )
        + (jax.ShapeDtypeStruct((depth, width), dtype),) * groups,
        in_specs=[SMEM] * 3 + [ANY] * 6,
        out_specs=(VMEM, VMEM, VMEM, SMEM) + (VMEM,) * groups,
        scratch_shapes=[pltpu.SemaphoreType.DMA((6 + groups + 2 * count,))],
        compiler_params=PARAMS,
    )(side, tp, slots, queries, keys, values, nbr_keys, nbr_values, weight)
    return result[0], result[1], result[2], result[3], result[4:]


def find_sources(label_ref, order_ref):
    for source in range(label_ref.shape[0]):
        label = label_ref[source]

        @pl.when(label >= 0)
        def _():
            order_ref[label] = source


def block_answer(order_ref, incoming_ref, block, feats, q):
    first = order_ref[2 * block]
    second = order_ref[2 * block + 1]
    s1 = dot_t(q, incoming_ref[first, 0, :, feats])
    s2 = dot_t(q, incoming_ref[second, 0, :, feats])
    peak = jnp.maximum(jnp.max(s1, axis=1, keepdims=True), jnp.max(s2, axis=1, keepdims=True))
    p1 = jnp.exp2((s1 - peak) * SCALE)
    p2 = jnp.exp2((s2 - peak) * SCALE)
    total = jnp.sum(p1, axis=1, keepdims=True) + jnp.sum(p2, axis=1, keepdims=True)
    mixed = dot(p1.astype(jnp.bfloat16), incoming_ref[first, 1, :, feats])
    mixed += dot(p2.astype(jnp.bfloat16), incoming_ref[second, 1, :, feats])
    return (mixed / total).astype(jnp.bfloat16)


def last_kernel(label_ref, queries_ref, spill_ref, incoming_ref, tail_ref, next_ref, order_ref):
    find_sources(label_ref, order_ref)
    rows, width = queries_ref.shape
    last = rows // BLOCK - 1
    for head in range(width // HD):
        feats = pl.ds(head * HD, HD)
        q = jnp.concatenate([queries_ref[rows - LEAD :, feats], spill_ref[:, feats]], axis=0)
        answer = block_answer(order_ref, incoming_ref, last, feats, q)
        tail_ref[:, feats] = answer[:LEAD]
        next_ref[:, feats] = answer[LEAD:]


def other_kernel(label_ref, queries_ref, tail_ref, incoming_ref, out_ref, order_ref):
    find_sources(label_ref, order_ref)
    rows, width = queries_ref.shape
    blocks = rows // BLOCK
    row = lax.broadcasted_iota(jnp.int32, (LEAD, HD), 0)
    for head in range(width // HD):
        feats = pl.ds(head * HD, HD)
        before = jnp.zeros((LEAD, HD), jnp.bfloat16)
        out_ref[: BLOCK - LEAD, feats] = jnp.zeros((BLOCK - LEAD, HD), jnp.bfloat16)
        for block in range(blocks):
            start = (block + 1) * BLOCK - LEAD
            if block < blocks - 1:
                q = queries_ref[start : start + BLOCK + LEAD, feats]
                answer = block_answer(order_ref, incoming_ref, block, feats, q)
                head_rows = answer[:LEAD]
                out_ref[start + LEAD : start + BLOCK, feats] = answer[LEAD:BLOCK]
            else:
                head_rows = tail_ref[:, feats]
            out_ref[start : start + LEAD, feats] = jnp.where(row == LEAD - 1, head_rows, before)
            if block < blocks - 1:
                before = answer[BLOCK:]


def order_scratch(rows):
    return [pltpu.SMEM((2 * rows // BLOCK,), jnp.int32)]


def last_attend(labels, queries, spill, incoming):
    rows, width = queries.shape
    return pl.pallas_call(
        last_kernel,
        out_shape=(
            jax.ShapeDtypeStruct((LEAD, width), queries.dtype),
            jax.ShapeDtypeStruct((BLOCK, width), queries.dtype),
        ),
        in_specs=[SMEM, VMEM, VMEM, VMEM],
        out_specs=(VMEM, VMEM),
        scratch_shapes=order_scratch(rows),
        compiler_params=PARAMS,
    )(labels, queries, spill, incoming)


def other_attend(labels, queries, tail, incoming):
    return pl.pallas_call(
        other_kernel,
        out_shape=jax.ShapeDtypeStruct(queries.shape, queries.dtype),
        in_specs=[SMEM, VMEM, VMEM, VMEM],
        out_specs=VMEM,
        scratch_shapes=order_scratch(queries.shape[0]),
        compiler_params=PARAMS,
    )(labels, queries, tail, incoming)


def self_kernel(first, last, step, pair_ref, q_ref, kv_ref, *refs):
    if not first:
        peak_in, total_in, accum_in = refs[:3]
        refs = refs[3:]
    rows = q_ref.shape[0]
    tile = rows // 2
    for part in range(2):
        at = pl.ds(part * tile, tile)

        def emit(peak, total, accum):
            if last:
                refs[0][at, :] = (accum / total).astype(jnp.bfloat16)
            else:
                refs[0][at, :] = jnp.broadcast_to(peak, (tile, HD))
                refs[1][at, :] = jnp.broadcast_to(total, (tile, HD))
                refs[2][at, :] = accum

        def work():
            q = q_ref[at, :]
            count = (part + 1) * tile if first else rows
            s = dot_t(q, kv_ref[:count, :HD])
            if first:
                row = lax.broadcasted_iota(jnp.int32, (tile, count), 0) + part * tile
                col = lax.broadcasted_iota(jnp.int32, (tile, count), 1)
                s = jnp.where(col <= row, s, NEGATIVE)
            peak = jnp.max(s, axis=1, keepdims=True)
            if not first:
                old = peak_in[at, :1]
                peak = jnp.maximum(peak, old)
                factor = jnp.exp2((old - peak) * SCALE)
            p = jnp.exp2((s - peak) * SCALE)
            total = jnp.sum(p, axis=1, keepdims=True)
            accum = dot(p.astype(jnp.bfloat16), kv_ref[:count, HD:])
            if not first:
                total += total_in[at, :1] * factor
                accum += accum_in[at, :] * factor
            emit(peak, total, accum)

        if first:
            work()
        else:
            pl.when(pair_ref[0] >= step)(work)

            @pl.when(pair_ref[0] < step)
            def _():
                emit(peak_in[at, :1], total_in[at, :1], accum_in[at, :])


def self_step(pair, q, kv, state, step, last):
    rows = q.shape[0]
    first = state is None
    held = jax.ShapeDtypeStruct((rows, HD), jnp.float32)
    out_shape = jax.ShapeDtypeStruct((rows, HD), jnp.bfloat16) if last else (held,) * 3
    return pl.pallas_call(
        functools.partial(self_kernel, first, last, step),
        out_shape=out_shape,
        in_specs=[SMEM] + [VMEM] * (2 if first else 5),
        out_specs=VMEM if last else (VMEM,) * 3,
        compiler_params=PARAMS,
    )(pair, q, kv, *(() if first else state))


def project_kernel(groups, *refs):
    crossed_ref = refs[-1]
    width = crossed_ref.shape[1]
    tile = min(512, width)
    for column in range(0, width, tile):
        at = pl.ds(column, tile)
        total = dot(refs[0][...], refs[groups][:, at])
        for group in range(1, groups):
            total += dot(refs[group][...], refs[groups + group][:, at])
        crossed_ref[:, at] = total.astype(crossed_ref.dtype)


def project(terms, weights):
    groups = len(terms)
    rows, width = terms[0].shape[0], weights[0].shape[1]
    return pl.pallas_call(
        functools.partial(project_kernel, groups),
        out_shape=jax.ShapeDtypeStruct((rows, width), jnp.bfloat16),
        in_specs=[VMEM] * (2 * groups),
        out_specs=VMEM,
        compiler_params=PARAMS,
    )(*terms, *weights)


def shards(queries, keys, values, cross_queries, nbr_keys, nbr_values, nbr_slot, w_cross):
    ctx = lax.axis_index("ctx")
    count = lax.axis_size("ctx")
    tp = lax.axis_index("tp")
    groups = lax.axis_size("tp")
    side = ctx & 1
    pair = (ctx >> 1).reshape(1)
    rows = queries.shape[0]

    away, mine, outgoing, labels, blocks = prepare(
        side.reshape(1), tp.reshape(1), nbr_slot, queries, keys, values, nbr_keys, nbr_values,
        w_cross, count, groups,
    )
    swap = [(i, i ^ 1) for i in range(count)]
    other = lax.ppermute(away, "ctx", swap)
    weights = [blocks[0]]
    for step in range(1, groups):
        weights.append(lax.ppermute(blocks[step], "tp", [(i, i ^ step) for i in range(groups)]))
    spill = lax.ppermute(cross_queries[:BLOCK], "ctx", [(i + 1, i) for i in range(count - 1)])
    incoming = lax.all_to_all(outgoing, "ctx", split_axis=0, concat_axis=0, tiled=True)
    labels = lax.all_to_all(labels, "ctx", split_axis=0, concat_axis=0, tiled=True)

    joint = jnp.where(
        side == 0, jnp.concatenate([mine, other], 1), jnp.concatenate([other, mine], 1)
    )
    q = joint[0]
    kv = jnp.concatenate([joint[1], joint[2]], axis=1)
    forward = [(i, i + 2) for i in range(count - 2)]
    pairs = count // 2
    state = None
    for step in range(pairs):
        following = lax.ppermute(kv, "ctx", forward) if step < pairs - 1 else None
        state = self_step(pair, q, kv, state, step, step == pairs - 1)
        kv = following
    near = jnp.where(side == 0, state[:rows], state[rows:])
    far = lax.ppermute(jnp.where(side == 0, state[rows:], state[:rows]), "ctx", swap)
    attended = jnp.where(
        side == 0, jnp.concatenate([near, far], 1), jnp.concatenate([far, near], 1)
    )

    tail, onward = last_attend(labels, cross_queries, spill, incoming)
    back = lax.ppermute(onward, "ctx", [(i, i + 1) for i in range(count - 1)])
    answers = other_attend(labels, cross_queries, tail, incoming)
    early = jnp.arange(BLOCK)[:, None] < BLOCK - 1
    cca = jnp.concatenate([jnp.where(early, back, answers[:BLOCK]), answers[BLOCK:]], axis=0)
    terms = [cca]
    for step in range(1, groups):
        terms.append(lax.ppermute(cca, "tp", [(i, i ^ step) for i in range(groups)]))
    crossed = project(terms, weights)
    return (attended, crossed)


def solution(mesh):
    in_specs = (
        P("ctx", "tp"),
        P("ctx", "tp"),
        P("ctx", "tp"),
        P("ctx", "tp"),
        P("ctx", None, "tp"),
        P("ctx", None, "tp"),
        P("ctx"),
        P("tp", None),
    )
    out_specs = (P("ctx", "tp"), P("ctx", "tp"))
    return jax.shard_map(shards, mesh=mesh, in_specs=in_specs, out_specs=out_specs, check_vma=False)
```

time: 137 us -> 122 us (0.89); the launches traced: 134 us -> 122 us
  Pallas kernels: 44.6 us -> 14.5 us
  blocking collectives: 0 us -> 13.5 us
  waiting for transfers between devices: 32.6 us -> 41.3 us
  starting transfers between devices: 39.6 us -> 35.5 us
  other arithmetic: 3.8 us -> 1.18 us
  local copies, waits for them, and re-layouts: 12.6 us -> 14.6 us
    pallas_call x2 -> x3, Pallas kernels: 37 us -> 7.32 us  [the longest x1 4.02 us: prepare(): pl.pallas_call(functools.partial(prepare_kernel, groups), out_shape=(half...]
    all_to_all x0 -> x1, blocking collectives: none -> 13.5 us  [shards(): lax.all_to_all(labels, 'ctx', split_axis=0, concat_axis=0, tiled=True)]
    ppermute x6, waiting for transfers between devices: 17.5 us -> 29.8 us  [the longest x3 15.9 us: shards(): lax.ppermute(blocks[step], 'tp', [(i, i ^ step) for i in range(groups)])]
    unnamed x8 -> x28, local copies, waits for them, and re-layouts: 4.74 us -> 13.2 us
    all_to_all x1 -> x0, starting transfers between devices: 7.28 us -> none  [shards(): lax.all_to_all(labels, 'ctx', split_axis=0, concat_axis=0, tiled=True)]
    all_to_all x1 -> x0, waiting for transfers between devices: 5.31 us -> none  [shards(): lax.all_to_all(labels, 'ctx', split_axis=0, concat_axis=0, tiled=True)]
    dynamic_slice x1 -> x0, local copies, waits for them, and re-layouts: 3.64 us -> none  [shards(): lax.dynamic_slice_in_dim(w_cross, (tp ^ step) * width, width, axis=1)]
    ppermute x3, waiting for transfers between devices: 3.16 us -> 5.99 us  [shards(): following = lax.ppermute(kv, 'ctx', forward) if step < pairs - 1 else None]
  transfers between devices with their start and end apart: 15 -> 14, of which waited for: 9 -> 7; matrix products, arithmetic and copies ran while one was open for 8% -> 2% of each run, Pallas kernels for 5% -> 6%
where the time goes in v2:
time: 122 us
  waiting for transfers between devices  41.3 us (34%)
  starting transfers between devices  35.5 us (29%)
  local copies, waits for them, and re-layouts  14.6 us (12%)
  Pallas kernels  14.5 us (12%)
  blocking collectives  13.5 us (11%)
    ppermute x3, starting transfers between devices, shards(): following = lax.ppermute(kv, 'ctx', forward) if step < pairs - 1 else None  16.7 us
    ppermute x3, waiting for transfers between devices, shards(): lax.ppermute(blocks[step], 'tp', [(i, i ^ step) for i in range(groups)])  15.9 us
    all_to_all x1, blocking collectives, shards(): lax.all_to_all(labels, 'ctx', split_axis=0, concat_axis=0, tiled=True)  13.5 us
    unnamed x28, local copies, waits for them, and re-layouts  13.2 us
    ppermute x1, waiting for transfers between devices, shards(): other = lax.ppermute(away, 'ctx', swap)  12.9 us
    ppermute x3, waiting for transfers between devices, shards(): following = lax.ppermute(kv, 'ctx', forward) if step < pairs - 1 else None  5.99 us
    ppermute x3, waiting for transfers between devices, shards(): lax.ppermute(cca, 'tp', [(i, i ^ step) for i in range(groups)])  5.51 us
    ppermute x1, starting transfers between devices, shards(): back = lax.ppermute(onward, 'ctx', [(i, i + 1) for i in range(count - 1)])  4.82 us
  transfers between devices with their start and end apart: 14, of which 7 were waited for; matrix products, arithmetic and copies ran while one was open for 2% of the time, Pallas kernels for 6%

profile of v2, /device:TPU:0, one launch (start us, length us, event | category | flops | bytes accessed | tf_op | source)
XLA Modules:
  0.0 121.6 jit_solution(7345027784439209081)
XLA Ops:
  0.6 0.0 copy-start
  0.6 2.2 %copy-done = bf16[256,8192]{1,0:T(8,128)(2,1)S(1)} copy-done((bf16[256,8192]{1,0:T(8,128)(2,1)S(1)}, bf16[256,8192]{1,0:T(8,128)(2,1)}, u32[]{:S(2)}) %copy-start) | copy-done | bytes 4194328
  2.8 0.0 copy-start.3
  2.8 1.0 copy-done.3
  3.9 0.0 copy-start.4
  3.9 1.0 copy-done.4
  4.9 0.0 copy-start.7
  4.9 0.9 copy-done.7
  5.8 0.9 copy-done.8
  6.7 0.9 copy-done.9
  7.6 0.7 copy-done.10
  8.3 4.0 %shard_map.95 = (bf16[3,256,128]{2,1,0:T(8,128)(2,1)S(1)}, bf16[3,256,128]{2,1,0:T(8,128)(2,1)S(1)}, bf16[8,2,128,256]{3,2,1,0:T(8,128)(2,1)}, s32[8]{0:T(128)S(...) custom-call(s32[1]{0:T(128)} %bitcast.1.side_ref, ...), custom_call_target="tpu_custom_call" | custom-call | tf_op jit(solution)/shard_map/pallas_call | solution.py:76
  12.3 0.0 copy-start.11
  12.3 1.0 copy-done.11
  13.3 1.0 copy-done.12
  14.3 1.0 copy-done.13
  15.2 0.1 copy.11
  15.3 13.5 %all_to_all.16 = s32[8,1,1]{2,1,0:T(1,128)S(1)} all-to-all(s32[8,1,1]{2,1,0:T(1,128)S(1)} %copy.11), channel_id=1, replica_groups=mesh['ctx'=8,'tp'=4] {'ctx'}, dimensions={0} | all-to-all | bytes 64 | tf_op jit(solution)/shard_map/all_to_all | solution.py:287
  28.9 3.6 %all-to-all-start.1 = ((bf16[8,2,128,256]{3,2,1,0:T(8,128)(2,1)}), bf16[8,2,128,256]{3,2,1,0:T(8,128)(2,1)S(1)}, u32[]{:S(2)}, u32[]{:S(2)}) async-start(bf16[8,2,128,256]{3,2,1,0:T(8,128)(2,1)} %get-tuple-element.33), calls=%async_computation.1 | async-start | bytes 2097152 | tf_op jit(solution)/shard_map/all_to_all | solution.py:286
  32.4 1.9 %collective-permute-start = (bf16[3,256,128]{2,1,0:T(8,128)(2,1)S(1)}, bf16[3,256,128]{2,1,0:T(8,128)(2,1)S(1)}, u32[]{:S(2)}, u32[]{:S(2)}) collective-permute-start(bf16[3,256,128]{2,1,0:T(8,128)(2,1)S(1)} %get-tuple-element.22), channel_id=1, source_target_pairs={{0,4},{4,0},{8,12},{12,8},{16,20},{20,16},{24,28},{28,24},{1,5},{5... | collective-permute-start | bytes 589832 | tf_op jit(solution)/shard_map/ppermute | solution.py:281
  34.3 12.9 %collective-permute-done = bf16[3,256,128]{2,1,0:T(8,128)(2,1)S(1)} collective-permute-done((bf16[3,256,128]{2,1,0:T(8,128)(2,1)S(1)}, bf16[3,256,128]{2,1,0:T(8,128)(2,1)S(1)}, u32[]{:S(2)}, u32[]{:S(2)}) %collective-permute-start) | collective-permute-done | bytes 196640 | tf_op jit(solution)/shard_map/ppermute | solution.py:281
  47.2 0.1 maximum_select_fusion
  47.4 1.9 %collective-permute-start.1 = (bf16[512,256]{1,0:T(8,128)(2,1)S(1)}, bf16[512,256]{1,0:T(8,128)(2,1)S(1)}, u32[]{:S(2)}, u32[]{:S(2)}) collective-permute-start(bf16[512,256]{1,0:T(8,128)(2,1)S(1)} %pad_maximum_fusion.kv_ref), channel_id=1, source_target_pairs={{0,8},{4,12},{8,16},{12,20},{16,24},{20,28},{1,9},{5,13},{9,17},{1... | collective-permute-start | bytes 786440 | tf_op jit(solution)/shard_map/ppermute | solution.py:298
  49.3 4.7 %collective-permute-done.1.kv_ref = bf16[512,256]{1,0:T(8,128)(2,1)S(1)} collective-permute-done((bf16[512,256]{1,0:T(8,128)(2,1)S(1)}, bf16[512,256]{1,0:T(8,128)(2,1)S(1)}, u32[]{:S(2)}, u32[]{:S(2)}) %collective-permute-start.1) | collective-permute-done | bytes 262176 | tf_op jit(solution)/shard_map/ppermute | solution.py:298
  54.0 9.6 %collective-permute-start.2 = (bf16[512,256]{1,0:T(8,128)(2,1)S(1)}, bf16[512,256]{1,0:T(8,128)(2,1)}, u32[]{:S(2)}, u32[]{:S(2)}) collective-permute-start(bf16[512,256]{1,0:T(8,128)(2,1)S(1)} %collective-permute-done.1.kv_ref), channel_id=1, source_target_pairs={{0,8},{4,12},{8,16},{12,20},{16,24},{20,28},{1,9},{5,13},{9,17},{1... | collective-permute-start | bytes 786440 | tf_op jit(solution)/shard_map/ppermute | solution.py:298
  63.6 0.7 copy-done.5
  64.3 0.0 collective-permute-start.10
  64.3 1.5 %collective-permute-start.11 = (bf16[256,2048]{1,0:T(8,128)(2,1)}, bf16[256,2048]{1,0:T(8,128)(2,1)}, u32[]{:S(2)}, u32[]{:S(2)}) collective-permute-start(bf16[256,2048]{1,0:T(8,128)(2,1)} %copy-done.12), channel_id=1, source_target_pairs={{0,2},{1,3},{2,0},{3,1},{4,6},{5,7},{6,4},{7,5},{8,10},{9,11},{10,... | collective-permute-start | bytes 3145736 | tf_op jit(solution)/shard_map/ppermute | solution.py:284
  65.8 0.4 collective-permute-start.12
  66.2 1.3 %collective-permute-done.2.kv_ref = bf16[512,256]{1,0:T(8,128)(2,1)} collective-permute-done((bf16[512,256]{1,0:T(8,128)(2,1)S(1)}, bf16[512,256]{1,0:T(8,128)(2,1)}, u32[]{:S(2)}, u32[]{:S(2)}) %collective-permute-start.2) | collective-permute-done | bytes 262176 | tf_op jit(solution)/shard_map/ppermute | solution.py:298
  67.4 5.2 %collective-permute-start.3 = (bf16[512,256]{1,0:T(8,128)(2,1)}, bf16[512,256]{1,0:T(8,128)(2,1)}, u32[]{:S(2)}, u32[]{:S(2)}) collective-permute-start(bf16[512,256]{1,0:T(8,128)(2,1)} %collective-permute-done.2.kv_ref), channel_id=1, source_target_pairs={{0,8},{4,12},{8,16},{12,20},{16,24},{20,28},{1,9},{5,13},{9,17},{1... | collective-permute-start | bytes 786440 | tf_op jit(solution)/shard_map/ppermute | solution.py:298
  72.7 1.4 %slice.31 = bf16[64,256]{1,0:T(8,128)(2,1)} slice(bf16[256,256]{1,0:T(8,128)(2,1)} %queries_ref.3), slice={[0:64], [0:256]} | slice | bytes 65536 | tf_op jit(solution)/shard_map/slice | solution.py:285
  74.0 1.3 %collective-permute-start.5 = (bf16[64,256]{1,0:T(8,128)(2,1)}, bf16[64,256]{1,0:T(8,128)(2,1)}, u32[]{:S(2)}, u32[]{:S(2)}) collective-permute-start(bf16[64,256]{1,0:T(8,128)(2,1)} %slice.31), channel_id=1, source_target_pairs={{4,0},{8,4},{12,8},{16,12},{20,16},{24,20},{28,24},{5,1},{9,5},{13... | collective-permute-start | bytes 98312 | tf_op jit(solution)/shard_map/ppermute | solution.py:285
  75.3 0.2 reduce.label_ref
  75.6 0.8 shard_map.96
  76.3 0.0 copy-start.2
  76.3 0.0 copy-start.6
  76.3 1.0 copy-done.6
  77.3 0.3 shard_map.97
  77.6 1.2 shard_map.98
  78.8 0.0 collective-permute-done.3.kv_ref
  78.8 1.2 shard_map.99
  80.0 1.0 collective-permute-done.5.spill_ref
  81.0 0.0 all-to-all-done.1.incoming_ref
  81.0 0.9 copy-done.1
  81.9 1.2 %shard_map.100 = (bf16[16,256]{1,0:T(8,128)(2,1)S(1)}, bf16[64,256]{1,0:T(8,128)(2,1)S(1)}) custom-call(s32[8]{0:T(128)S(1)} %reduce.label_ref, bf16[256,256]{1,0:T(8,128)(2,1)S(1)} %copy-done.1, bf16[64,256]{1,0:T(8,128)(2,1)} %collective-permute-done.5.spill_ref, bf16[8,2,128,256]{3,2,1,0:T(8,128)(2,1)S(1)} %all-to-all-done.1.incoming_ref), custom_call_target="tpu_custom_call" | custom-call | tf_op jit(solution)/shard_map/pallas_call | solution.py:157
  83.2 4.8 %collective-permute-start.6 = (bf16[64,256]{1,0:T(8,128)(2,1)S(1)}, bf16[64,256]{1,0:T(8,128)(2,1)S(1)}, u32[]{:S(2)}, u32[]{:S(2)}) collective-permute-start(bf16[64,256]{1,0:T(8,128)(2,1)S(1)} %get-tuple-element.34), channel_id=1, source_target_pairs={{0,4},{4,8},{8,12},{12,16},{16,20},{20,24},{24,28},{1,5},{5,9},{9,... | collective-permute-start | bytes 98312 | tf_op jit(solution)/shard_map/ppermute | solution.py:308
  88.0 3.5 %collective-permute-start.4 = (bf16[256,128]{1,0:T(8,128)(2,1)S(1)}, bf16[256,128]{1,0:T(8,128)(2,1)S(1)}, u32[]{:S(2)}, u32[]{:S(2)}) collective-permute-start(bf16[256,128]{1,0:T(8,128)(2,1)S(1)} %get-tuple-element.44), channel_id=1, source_target_pairs={{0,4},{4,0},{8,12},{12,8},{16,20},{20,16},{24,28},{28,24},{1,5},{5... | collective-permute-start | bytes 196616 | tf_op jit(solution)/shard_map/ppermute | solution.py:302
  91.5 0.0 copy-done.2
  91.5 2.1 %shard_map.101 = bf16[256,256]{1,0:T(8,128)(2,1)S(1)} custom-call(s32[8]{0:T(128)S(1)} %reduce.label_ref, bf16[256,256]{1,0:T(8,128)(2,1)S(1)} %copy-done.2, bf16[16,256]{1,0:T(8,128)(2,1)S(1)} %get-tuple-element.35.tail_ref, bf16[8,2,128,256]{3,2,1,0:T(8,128)(2,1)S(1)} %all-to-all-done.1.incoming_ref), custom_call_target="tpu_custom_call" | custom-call | tf_op jit(solution)/shard_map/pallas_call | solution.py:171
  93.6 0.0 collective-permute-done.6
  93.6 0.1 slice_select_fusion
  93.7 0.1 collective-permute-start.7
  93.8 0.0 collective-permute-done.10.refs_5_
  93.8 1.6 %collective-permute-start.8 = (bf16[256,256]{1,0:T(8,128)(2,1)S(1)}, bf16[256,256]{1,0:T(8,128)(2,1)S(1)}, u32[]{:S(2)}, u32[]{:S(2)}) collective-permute-start(bf16[256,256]{1,0:T(8,128)(2,1)S(1)} %pad_maximum_fusion.1.refs_0_), channel_id=1, source_target_pairs={{0,2},{1,3},{2,0},{3,1},{4,6},{5,7},{6,4},{7,5},{8,10},{9,11},{10,... | collective-permute-start | bytes 393224 | tf_op jit(solution)/shard_map/ppermute | solution.py:314
  95.3 0.0 collective-permute-done.4
  95.3 0.3 collective-permute-start.9
  95.6 0.7 maximum_select_fusion.1
  96.3 0.0 collective-permute-done.11.refs_6_
  96.3 15.9 %collective-permute-done.12.refs_7_ = bf16[256,2048]{1,0:T(8,128)(2,1)} collective-permute-done((bf16[256,2048]{1,0:T(8,128)(2,1)}, bf16[256,2048]{1,0:T(8,128)(2,1)}, u32[]{:S(2)}, u32[]{:S(2)}) %collective-permute-start.12) | collective-permute-done | bytes 1048608 | tf_op jit(solution)/shard_map/ppermute | solution.py:284
  112.3 0.0 collective-permute-done.7.refs_1_
  112.3 3.5 %collective-permute-done.8.refs_2_ = bf16[256,256]{1,0:T(8,128)(2,1)S(1)} collective-permute-done((bf16[256,256]{1,0:T(8,128)(2,1)S(1)}, bf16[256,256]{1,0:T(8,128)(2,1)S(1)}, u32[]{:S(2)}, u32[]{:S(2)}) %collective-permute-start.8) | collective-permute-done | bytes 131104 | tf_op jit(solution)/shard_map/ppermute | solution.py:314
  115.8 2.0 %collective-permute-done.9.refs_3_ = bf16[256,256]{1,0:T(8,128)(2,1)S(1)} collective-permute-done((bf16[256,256]{1,0:T(8,128)(2,1)S(1)}, bf16[256,256]{1,0:T(8,128)(2,1)S(1)}, u32[]{:S(2)}, u32[]{:S(2)}) %collective-permute-start.9) | collective-permute-done | bytes 131104 | tf_op jit(solution)/shard_map/ppermute | solution.py:314
  117.8 3.8 %shard_map.102 = bf16[256,2048]{1,0:T(8,128)(2,1)} custom-call(bf16[256,256]{1,0:T(8,128)(2,1)S(1)} %pad_maximum_fusion.1.refs_0_, bf16[256,256]{1,0:T(8,128)(2,1)S(1)} %collective-permute-done.7.refs_1_, bf16[256,256]{1,0:T(8,128)(2,1)S(1)} %collective-permute-done.8.refs_2_, bf16[256,256]{1,0:T(8,128)(2,1)S(1)} %collective-permute-done.9.refs_3_, ...), custom_call_target="tpu_custom_call" | custom-call | tf_op jit(solution)/shard_map/pallas_call | solution.py:258
  (13 shorter events, 0.1 us)
Async XLA Ops:
  0.6 2.2 %copy-start = (bf16[256,8192]{1,0:T(8,128)(2,1)S(1)}, bf16[256,8192]{1,0:T(8,128)(2,1)}, u32[]{:S(2)}) copy-start(bf16[256,8192]{1,0:T(8,128)(2,1)} %refs_5_.1) | copy-start | bytes 12582916
  2.8 1.0 copy-start.3
  3.9 1.0 copy-start.4
  4.9 0.9 copy-start.7
  5.8 0.9 copy-start.8
  6.7 0.9 copy-start.9
  7.6 0.7 copy-start.10
  12.3 1.0 copy-start.11
  13.3 1.0 copy-start.12
  14.3 1.0 copy-start.13
  28.9 52.2 %all-to-all-start.1 = ((bf16[8,2,128,256]{3,2,1,0:T(8,128)(2,1)}), bf16[8,2,128,256]{3,2,1,0:T(8,128)(2,1)S(1)}, u32[]{:S(2)}, u32[]{:S(2)}) async-start(bf16[8,2,128,256]{3,2,1,0:T(8,128)(2,1)} %get-tuple-element.33), calls=%async_computation.1 | async-start | bytes 2097152 | tf_op jit(solution)/shard_map/all_to_all | solution.py:286
  32.4 14.8 %collective-permute-start = (bf16[3,256,128]{2,1,0:T(8,128)(2,1)S(1)}, bf16[3,256,128]{2,1,0:T(8,128)(2,1)S(1)}, u32[]{:S(2)}, u32[]{:S(2)}) collective-permute-start(bf16[3,256,128]{2,1,0:T(8,128)(2,1)S(1)} %get-tuple-element.22), channel_id=1, source_target_pairs={{0,4},{4,0},{8,12},{12,8},{16,20},{20,16},{24,28},{28,24},{1,5},{5... | collective-permute-start | bytes 589832 | tf_op jit(solution)/shard_map/ppermute | solution.py:281
  47.4 6.6 %collective-permute-start.1 = (bf16[512,256]{1,0:T(8,128)(2,1)S(1)}, bf16[512,256]{1,0:T(8,128)(2,1)S(1)}, u32[]{:S(2)}, u32[]{:S(2)}) collective-permute-start(bf16[512,256]{1,0:T(8,128)(2,1)S(1)} %pad_maximum_fusion.kv_ref), channel_id=1, source_target_pairs={{0,8},{4,12},{8,16},{12,20},{16,24},{20,28},{1,9},{5,13},{9,17},{1... | collective-permute-start | bytes 786440 | tf_op jit(solution)/shard_map/ppermute | solution.py:298
  54.0 13.5 %collective-permute-start.2 = (bf16[512,256]{1,0:T(8,128)(2,1)S(1)}, bf16[512,256]{1,0:T(8,128)(2,1)}, u32[]{:S(2)}, u32[]{:S(2)}) collective-permute-start(bf16[512,256]{1,0:T(8,128)(2,1)S(1)} %collective-permute-done.1.kv_ref), channel_id=1, source_target_pairs={{0,8},{4,12},{8,16},{12,20},{16,24},{20,28},{1,9},{5,13},{9,17},{1... | collective-permute-start | bytes 786440 | tf_op jit(solution)/shard_map/ppermute | solution.py:298
  63.6 0.7 copy-start.5
  64.3 29.5 %collective-permute-start.10 = (bf16[256,2048]{1,0:T(8,128)(2,1)}, bf16[256,2048]{1,0:T(8,128)(2,1)S(1)}, u32[]{:S(2)}, u32[]{:S(2)}) collective-permute-start(bf16[256,2048]{1,0:T(8,128)(2,1)} %copy-done.13), channel_id=1, source_target_pairs={{0,1},{1,0},{2,3},{3,2},{4,5},{5,4},{6,7},{7,6},{8,9},{9,8},{10,11... | collective-permute-start | bytes 3145736 | tf_op jit(solution)/shard_map/ppermute | solution.py:284
  64.3 32.0 %collective-permute-start.11 = (bf16[256,2048]{1,0:T(8,128)(2,1)}, bf16[256,2048]{1,0:T(8,128)(2,1)}, u32[]{:S(2)}, u32[]{:S(2)}) collective-permute-start(bf16[256,2048]{1,0:T(8,128)(2,1)} %copy-done.12), channel_id=1, source_target_pairs={{0,2},{1,3},{2,0},{3,1},{4,6},{5,7},{6,4},{7,5},{8,10},{9,11},{10,... | collective-permute-start | bytes 3145736 | tf_op jit(solution)/shard_map/ppermute | solution.py:284
  65.8 46.5 %collective-permute-start.12 = (bf16[256,2048]{1,0:T(8,128)(2,1)}, bf16[256,2048]{1,0:T(8,128)(2,1)}, u32[]{:S(2)}, u32[]{:S(2)}) collective-permute-start(bf16[256,2048]{1,0:T(8,128)(2,1)} %copy-done.11), channel_id=1, source_target_pairs={{0,3},{1,2},{2,1},{3,0},{4,7},{5,6},{6,5},{7,4},{8,11},{9,10},{10,... | collective-permute-start | bytes 3145736 | tf_op jit(solution)/shard_map/ppermute | solution.py:284
  67.4 11.4 %collective-permute-start.3 = (bf16[512,256]{1,0:T(8,128)(2,1)}, bf16[512,256]{1,0:T(8,128)(2,1)}, u32[]{:S(2)}, u32[]{:S(2)}) collective-permute-start(bf16[512,256]{1,0:T(8,128)(2,1)} %collective-permute-done.2.kv_ref), channel_id=1, source_target_pairs={{0,8},{4,12},{8,16},{12,20},{16,24},{20,28},{1,9},{5,13},{9,17},{1... | collective-permute-start | bytes 786440 | tf_op jit(solution)/shard_map/ppermute | solution.py:298
  74.0 7.0 %collective-permute-start.5 = (bf16[64,256]{1,0:T(8,128)(2,1)}, bf16[64,256]{1,0:T(8,128)(2,1)}, u32[]{:S(2)}, u32[]{:S(2)}) collective-permute-start(bf16[64,256]{1,0:T(8,128)(2,1)} %slice.31), channel_id=1, source_target_pairs={{4,0},{8,4},{12,8},{16,12},{20,16},{24,20},{28,24},{5,1},{9,5},{13... | collective-permute-start | bytes 98312 | tf_op jit(solution)/shard_map/ppermute | solution.py:285
  76.3 15.2 %copy-start.2 = (bf16[256,256]{1,0:T(8,128)(2,1)S(1)}, bf16[256,256]{1,0:T(8,128)(2,1)}, u32[]{:S(2)}) copy-start(bf16[256,256]{1,0:T(8,128)(2,1)} %queries_ref.3) | copy-start | bytes 393220
  76.3 1.0 copy-start.6
  81.0 0.9 copy-start.1
  83.2 10.4 %collective-permute-start.6 = (bf16[64,256]{1,0:T(8,128)(2,1)S(1)}, bf16[64,256]{1,0:T(8,128)(2,1)S(1)}, u32[]{:S(2)}, u32[]{:S(2)}) collective-permute-start(bf16[64,256]{1,0:T(8,128)(2,1)S(1)} %get-tuple-element.34), channel_id=1, source_target_pairs={{0,4},{4,8},{8,12},{12,16},{16,20},{20,24},{24,28},{1,5},{5,9},{9,... | collective-permute-start | bytes 98312 | tf_op jit(solution)/shard_map/ppermute | solution.py:308
  88.0 7.3 %collective-permute-start.4 = (bf16[256,128]{1,0:T(8,128)(2,1)S(1)}, bf16[256,128]{1,0:T(8,128)(2,1)S(1)}, u32[]{:S(2)}, u32[]{:S(2)}) collective-permute-start(bf16[256,128]{1,0:T(8,128)(2,1)S(1)} %get-tuple-element.44), channel_id=1, source_target_pairs={{0,4},{4,0},{8,12},{12,8},{16,20},{20,16},{24,28},{28,24},{1,5},{5... | collective-permute-start | bytes 196616 | tf_op jit(solution)/shard_map/ppermute | solution.py:302
  93.7 18.6 %collective-permute-start.7 = (bf16[256,256]{1,0:T(8,128)(2,1)S(1)}, bf16[256,256]{1,0:T(8,128)(2,1)S(1)}, u32[]{:S(2)}, u32[]{:S(2)}) collective-permute-start(bf16[256,256]{1,0:T(8,128)(2,1)S(1)} %pad_maximum_fusion.1.refs_0_), channel_id=1, source_target_pairs={{0,1},{1,0},{2,3},{3,2},{4,5},{5,4},{6,7},{7,6},{8,9},{9,8},{10,11... | collective-permute-start | bytes 393224 | tf_op jit(solution)/shard_map/ppermute | solution.py:314
  93.8 22.0 %collective-permute-start.8 = (bf16[256,256]{1,0:T(8,128)(2,1)S(1)}, bf16[256,256]{1,0:T(8,128)(2,1)S(1)}, u32[]{:S(2)}, u32[]{:S(2)}) collective-permute-start(bf16[256,256]{1,0:T(8,128)(2,1)S(1)} %pad_maximum_fusion.1.refs_0_), channel_id=1, source_target_pairs={{0,2},{1,3},{2,0},{3,1},{4,6},{5,7},{6,4},{7,5},{8,10},{9,11},{10,... | collective-permute-start | bytes 393224 | tf_op jit(solution)/shard_map/ppermute | solution.py:314
  95.3 22.4 %collective-permute-start.9 = (bf16[256,256]{1,0:T(8,128)(2,1)S(1)}, bf16[256,256]{1,0:T(8,128)(2,1)S(1)}, u32[]{:S(2)}, u32[]{:S(2)}) collective-permute-start(bf16[256,256]{1,0:T(8,128)(2,1)S(1)} %pad_maximum_fusion.1.refs_0_), channel_id=1, source_target_pairs={{0,3},{1,2},{2,1},{3,0},{4,7},{5,6},{6,5},{7,4},{8,11},{9,10},{10,... | collective-permute-start | bytes 393224 | tf_op jit(solution)/shard_map/ppermute | solution.py:314

commit v3 on v2

v3 whole, which is shorter than its diff:
```python
import functools
import math

import jax
import jax.numpy as jnp
from jax import lax
from jax.experimental import pallas as pl
from jax.experimental.pallas import tpu as pltpu
from jax.sharding import PartitionSpec as P

HD = 128
BLOCK = 64
LEAD = 16
NEGATIVE = -1e30
SCALE = HD ** -0.5 * math.log2(math.e)
VMEM = pl.BlockSpec(memory_space=pltpu.VMEM)
SMEM = pl.BlockSpec(memory_space=pltpu.SMEM)
ANY = pl.BlockSpec(memory_space=pl.ANY)
PARAMS = pltpu.CompilerParams(vmem_limit_bytes=24 * 1024 * 1024)


def dot(a, b):
    return jnp.dot(a, b, preferred_element_type=jnp.float32)


def dot_t(a, b):
    return lax.dot_general(a, b, (((1,), (1,)), ((), ())), preferred_element_type=jnp.float32)


def fetch(pieces, sems):
    copies = [
        pltpu.make_async_copy(source, target, sems.at[at])
        for at, (source, target) in enumerate(pieces)
    ]
    for copy in copies:
        copy.start()
    for copy in copies:
        copy.wait()


def columns_kernel(groups, side_ref, tp_ref, *refs):
    sources, weight = refs[:3], refs[3]
    away, mine = refs[4:6]
    blocks, sems = refs[6:-1], refs[-1]
    parts = len(blocks) // groups
    side = side_ref[0]
    tp = tp_ref[0]
    width = blocks[0].shape[1]
    pieces = []
    for at in range(3):
        lane = pl.multiple_of((1 - side) * HD, HD)
        pieces.append((sources[at].at[:, pl.ds(lane, HD)], away.at[at]))
        lane = pl.multiple_of(side * HD, HD)
        pieces.append((sources[at].at[:, pl.ds(lane, HD)], mine.at[at]))
    for part in range(parts):
        for step in range(groups):
            column = pl.multiple_of(((tp ^ step) * parts + part) * width, HD)
            block = blocks[part * groups + step]
            pieces.append((weight.at[:, pl.ds(column, width)], block))
    fetch(pieces, sems)


def cut_columns(side, tp, queries, keys, values, weight, groups, parts):
    rows = queries.shape[0]
    depth = weight.shape[0]
    width = weight.shape[1] // groups // parts
    dtype = queries.dtype
    half = jax.ShapeDtypeStruct((3, rows, HD), dtype)
    block = jax.ShapeDtypeStruct((depth, width), dtype)
    result = pl.pallas_call(
        functools.partial(columns_kernel, groups),
        out_shape=(half, half) + (block,) * (groups * parts),
        in_specs=[SMEM] * 2 + [ANY] * 4,
        out_specs=(VMEM,) * (2 + groups * parts),
        scratch_shapes=[pltpu.SemaphoreType.DMA((6 + groups * parts,))],
    )(side, tp, queries, keys, values, weight)
    blocks = [result[2 + part * groups : 2 + (part + 1) * groups] for part in range(parts)]
    return result[0], result[1], blocks


def arrange_kernel(slot_ref, keys_ref, values_ref, out_ref, sems):
    count, length, width = keys_ref.shape
    pieces = []
    for n in range(count):
        owner = slot_ref[n] // count
        pieces.append((keys_ref.at[n], out_ref.at[owner, pl.ds(0, length)]))
        pieces.append((values_ref.at[n], out_ref.at[owner, pl.ds(length, length)]))
    for owner in range(out_ref.shape[0]):
        out_ref[owner, 2 * length :, :] = jnp.full((LEAD, width), -1, out_ref.dtype)
    for n in range(count):
        slot = slot_ref[n]
        owner = slot // count
        place = (slot - owner * count).astype(jnp.float32)
        out_ref[owner, 2 * length :, :] = jnp.full((LEAD, width), place).astype(out_ref.dtype)
    fetch(pieces, sems)


def arrange(slots, keys, values, owners):
    count, length, width = keys.shape
    return pl.pallas_call(
        arrange_kernel,
        out_shape=jax.ShapeDtypeStruct((owners, 2 * length + LEAD, width), keys.dtype),
        in_specs=[SMEM, ANY, ANY],
        out_specs=VMEM,
        scratch_shapes=[pltpu.SemaphoreType.DMA((2 * count,))],
    )(slots, keys, values)


def find_sources(incoming_ref, order_ref):
    rows = incoming_ref.shape[1]
    for source in range(incoming_ref.shape[0]):
        place = incoming_ref[source, rows - LEAD :, :HD].astype(jnp.float32)
        place = jnp.max(place).astype(jnp.int32)

        @pl.when(place >= 0)
        def _():
            order_ref[place] = source


def block_answer(order_ref, incoming_ref, block, feats, q):
    first = order_ref[2 * block]
    second = order_ref[2 * block + 1]
    length = (incoming_ref.shape[1] - LEAD) // 2
    s1 = dot_t(q, incoming_ref[first, :length, feats])
    s2 = dot_t(q, incoming_ref[second, :length, feats])
    peak = jnp.maximum(jnp.max(s1, axis=1, keepdims=True), jnp.max(s2, axis=1, keepdims=True))
    p1 = jnp.exp2((s1 - peak) * SCALE)
    p2 = jnp.exp2((s2 - peak) * SCALE)
    total = jnp.sum(p1, axis=1, keepdims=True) + jnp.sum(p2, axis=1, keepdims=True)
    mixed = dot(p1.astype(jnp.bfloat16), incoming_ref[first, length : 2 * length, feats])
    mixed += dot(p2.astype(jnp.bfloat16), incoming_ref[second, length : 2 * length, feats])
    return (mixed / total).astype(jnp.bfloat16)


def last_kernel(queries_ref, spill_ref, incoming_ref, tail_ref, next_ref, order_ref):
    find_sources(incoming_ref, order_ref)
    rows, width = queries_ref.shape
    last = rows // BLOCK - 1
    for head in range(width // HD):
        feats = pl.ds(head * HD, HD)
        q = jnp.concatenate([queries_ref[rows - LEAD :, feats], spill_ref[:BLOCK, feats]], axis=0)
        answer = block_answer(order_ref, incoming_ref, last, feats, q)
        tail_ref[:, feats] = answer[:LEAD]
        next_ref[:, feats] = answer[LEAD:]


def other_kernel(queries_ref, tail_ref, incoming_ref, out_ref, order_ref):
    find_sources(incoming_ref, order_ref)
    rows, width = queries_ref.shape
    blocks = rows // BLOCK
    row = lax.broadcasted_iota(jnp.int32, (LEAD, HD), 0)
    for head in range(width // HD):
        feats = pl.ds(head * HD, HD)
        before = jnp.zeros((LEAD, HD), jnp.bfloat16)
        out_ref[: BLOCK - LEAD, feats] = jnp.zeros((BLOCK - LEAD, HD), jnp.bfloat16)
        for block in range(blocks):
            start = (block + 1) * BLOCK - LEAD
            if block < blocks - 1:
                q = queries_ref[start : start + BLOCK + LEAD, feats]
                answer = block_answer(order_ref, incoming_ref, block, feats, q)
                head_rows = answer[:LEAD]
                out_ref[start + LEAD : start + BLOCK, feats] = answer[LEAD:BLOCK]
            else:
                head_rows = tail_ref[:, feats]
            out_ref[start : start + LEAD, feats] = jnp.where(row == LEAD - 1, head_rows, before)
            if block < blocks - 1:
                before = answer[BLOCK:]


def order_scratch(rows):
    return [pltpu.SMEM((2 * rows // BLOCK,), jnp.int32)]


def last_attend(queries, spill, incoming):
    rows, width = queries.shape
    return pl.pallas_call(
        last_kernel,
        out_shape=(
            jax.ShapeDtypeStruct((LEAD, width), queries.dtype),
            jax.ShapeDtypeStruct((BLOCK, width), queries.dtype),
        ),
        in_specs=[VMEM] * 3,
        out_specs=(VMEM, VMEM),
        scratch_shapes=order_scratch(rows),
        compiler_params=PARAMS,
    )(queries, spill, incoming)


def other_attend(queries, tail, incoming):
    return pl.pallas_call(
        other_kernel,
        out_shape=jax.ShapeDtypeStruct(queries.shape, queries.dtype),
        in_specs=[VMEM] * 3,
        out_specs=VMEM,
        scratch_shapes=order_scratch(queries.shape[0]),
        compiler_params=PARAMS,
    )(queries, tail, incoming)


def self_kernel(first, last, step, pair_ref, q_ref, kv_ref, *refs):
    if not first:
        peak_in, total_in, accum_in = refs[:3]
        refs = refs[3:]
    rows = q_ref.shape[0]
    tile = rows // 2
    for part in range(2):
        at = pl.ds(part * tile, tile)

        def emit(peak, total, accum):
            if last:
                refs[0][at, :] = (accum / total).astype(jnp.bfloat16)
            else:
                refs[0][at, :] = jnp.broadcast_to(peak, (tile, HD))
                refs[1][at, :] = jnp.broadcast_to(total, (tile, HD))
                refs[2][at, :] = accum

        def work():
            q = q_ref[at, :]
            count = (part + 1) * tile if first else rows
            s = dot_t(q, kv_ref[:count, :HD])
            if first:
                row = lax.broadcasted_iota(jnp.int32, (tile, count), 0) + part * tile
                col = lax.broadcasted_iota(jnp.int32, (tile, count), 1)
                s = jnp.where(col <= row, s, NEGATIVE)
            peak = jnp.max(s, axis=1, keepdims=True)
            if not first:
                old = peak_in[at, :1]
                peak = jnp.maximum(peak, old)
                factor = jnp.exp2((old - peak) * SCALE)
            p = jnp.exp2((s - peak) * SCALE)
            total = jnp.sum(p, axis=1, keepdims=True)
            accum = dot(p.astype(jnp.bfloat16), kv_ref[:count, HD:])
            if not first:
                total += total_in[at, :1] * factor
                accum += accum_in[at, :] * factor
            emit(peak, total, accum)

        if first:
            work()
        else:
            pl.when(pair_ref[0] >= step)(work)

            @pl.when(pair_ref[0] < step)
            def _():
                emit(peak_in[at, :1], total_in[at, :1], accum_in[at, :])


def self_step(pair, q, kv, state, step, last):
    rows = q.shape[0]
    first = state is None
    held = jax.ShapeDtypeStruct((rows, HD), jnp.float32)
    out_shape = jax.ShapeDtypeStruct((rows, HD), jnp.bfloat16) if last else (held,) * 3
    return pl.pallas_call(
        functools.partial(self_kernel, first, last, step),
        out_shape=out_shape,
        in_specs=[SMEM] + [VMEM] * (2 if first else 5),
        out_specs=VMEM if last else (VMEM,) * 3,
        compiler_params=PARAMS,
    )(pair, q, kv, *(() if first else state))


def project_kernel(groups, *refs):
    crossed_ref = refs[-1]
    at = 0
    for part in range(len(refs) // groups - 1):
        blocks = refs[(part + 1) * groups : (part + 2) * groups]
        width = blocks[0].shape[1]
        tile = min(512, width)
        for column in range(0, width, tile):
            total = dot(refs[0][...], blocks[0][:, column : column + tile])
            for group in range(1, groups):
                total += dot(refs[group][...], blocks[group][:, column : column + tile])
            crossed_ref[:, at : at + tile] = total.astype(crossed_ref.dtype)
            at += tile


def project(terms, weights):
    groups = len(terms)
    rows = terms[0].shape[0]
    width = sum(part[0].shape[1] for part in weights)
    return pl.pallas_call(
        functools.partial(project_kernel, groups),
        out_shape=jax.ShapeDtypeStruct((rows, width), jnp.bfloat16),
        in_specs=[VMEM] * (groups * (1 + len(weights))),
        out_specs=VMEM,
        compiler_params=PARAMS,
    )(*terms, *(block for part in weights for block in part))


def shards(queries, keys, values, cross_queries, nbr_keys, nbr_values, nbr_slot, w_cross):
    ctx = lax.axis_index("ctx")
    count = lax.axis_size("ctx")
    tp = lax.axis_index("tp")
    groups = lax.axis_size("tp")
    side = ctx & 1
    pair = (ctx >> 1).reshape(1)
    rows = queries.shape[0]
    swap = [(i, i ^ 1) for i in range(count)]
    across = [[(i, i ^ step) for i in range(groups)] for step in range(groups)]

    away, mine, blocks = cut_columns(
        side.reshape(1), tp.reshape(1), queries, keys, values, w_cross, groups, 2
    )
    other = lax.ppermute(away, "ctx", swap)
    weights = [
        [part[0]] + [lax.ppermute(part[step], "tp", across[step]) for step in range(1, groups)]
        for part in blocks
    ]
    spill = lax.ppermute(cross_queries[:BLOCK], "ctx", [(i + 1, i) for i in range(count - 1)])
    outgoing = arrange(nbr_slot, nbr_keys, nbr_values, count)
    other, outgoing = lax.optimization_barrier((other, outgoing))
    incoming = lax.all_to_all(outgoing, "ctx", split_axis=0, concat_axis=0, tiled=True)

    joint = jnp.where(
        side == 0, jnp.concatenate([mine, other], 1), jnp.concatenate([other, mine], 1)
    )
    q = joint[0]
    kv = jnp.concatenate([joint[1], joint[2]], axis=1)
    forward = [(i, i + 2) for i in range(count - 2)]
    pairs = count // 2
    state = None
    for step in range(pairs):
        if step == 2:
            kv, weights[0] = lax.optimization_barrier((kv, weights[0]))
        following = lax.ppermute(kv, "ctx", forward) if step < pairs - 1 else None
        state = self_step(pair, q, kv, state, step, step == pairs - 1)
        kv = following
    near = jnp.where(side == 0, state[:rows], state[rows:])
    far = lax.ppermute(jnp.where(side == 0, state[rows:], state[:rows]), "ctx", swap)
    attended = jnp.where(
        side == 0, jnp.concatenate([near, far], 1), jnp.concatenate([far, near], 1)
    )

    tail, onward = last_attend(cross_queries, spill, incoming)
    back = lax.ppermute(onward, "ctx", [(i, i + 1) for i in range(count - 1)])
    answers = other_attend(cross_queries, tail, incoming)
    early = jnp.arange(BLOCK)[:, None] < BLOCK - 1
    cca = jnp.concatenate([jnp.where(early, back, answers[:BLOCK]), answers[BLOCK:]], axis=0)
    terms = [cca]
    for step in range(1, groups):
        terms.append(lax.ppermute(cca, "tp", across[step]))
    crossed = project(terms, weights)
    return (attended, crossed)


def solution(mesh):
    in_specs = (
        P("ctx", "tp"),
        P("ctx", "tp"),
        P("ctx", "tp"),
        P("ctx", "tp"),
        P("ctx", None, "tp"),
        P("ctx", None, "tp"),
        P("ctx"),
        P("tp", None),
    )
    out_specs = (P("ctx", "tp"), P("ctx", "tp"))
    return jax.shard_map(shards, mesh=mesh, in_specs=in_specs, out_specs=out_specs, check_vma=False)
```

time: 122 us -> 100 us (0.82)
  the two profiles are of different devices: /device:TPU:0 before, /device:TPU:16 now
where the time goes in v3:
time: 100 us; the launch traced here: 99.9 us
  waiting for transfers between devices  47.6 us (48%)
  starting transfers between devices  31 us (31%)
  Pallas kernels  17.8 us (18%)
  local copies, waits for them, and re-layouts  1.74 us (2%)
    ppermute x3, waiting for transfers between devices, shards(): following = lax.ppermute(kv, 'ctx', forward) if step < pairs - 1 else None  30.8 us
    ppermute x6, waiting for transfers between devices, shards(): lax.ppermute(part[step], 'tp', across[step])  8.27 us
    ppermute x3, starting transfers between devices, shards(): following = lax.ppermute(kv, 'ctx', forward) if step < pairs - 1 else None  7.47 us
    all_to_all x1, starting transfers between devices, shards(): lax.all_to_all(outgoing, 'ctx', split_axis=0, concat_axis=0, tiled=True)  6.17 us
    ppermute x3, waiting for transfers between devices, shards(): terms.append(lax.ppermute(cca, 'tp', across[step]))  5.97 us
    ppermute x1, starting transfers between devices, shards(): lax.ppermute(cross_queries[:BLOCK], 'ctx', [(i + 1, i) for i in range(cou...  5.62 us
    pallas_call x1, Pallas kernels, cut_columns(): pl.pallas_call(functools.partial(columns_kernel, groups), out_shape=(half...  4.63 us
    pallas_call x4, Pallas kernels, self_step(): pl.pallas_call(functools.partial(self_kernel, first, last, step), out_sha...  4.22 us
  transfers between devices with their start and end apart: 17, of which 7 were waited for; matrix products, arithmetic and copies ran while one was open for 1% of the time, Pallas kernels for 10%

profile of v3, /device:TPU:16, one launch (start us, length us, event | category | flops | bytes accessed | tf_op | source)
XLA Modules:
  0.0 99.9 jit_solution(9324654142864760169)
XLA Ops:
  0.6 4.6 %shard_map.95 = (bf16[3,256,128]{2,1,0:T(8,128)(2,1)}, bf16[3,256,128]{2,1,0:T(8,128)(2,1)}, bf16[256,1024]{1,0:T(8,128)(2,1)}, bf16[256,1024]{1,0:T(8,128)(2,1)...) custom-call(s32[1]{0:T(128)} %bitcast.1.side_ref, ...), custom_call_target="tpu_custom_call" | custom-call | tf_op jit(solution)/shard_map/pallas_call | solution.py:70
  5.3 1.6 %collective-permute-start = (bf16[3,256,128]{2,1,0:T(8,128)(2,1)}, bf16[3,256,128]{2,1,0:T(8,128)(2,1)S(1)}, u32[]{:S(2)}, u32[]{:S(2)}) collective-permute-start(bf16[3,256,128]{2,1,0:T(8,128)(2,1)} %get-tuple-element.31), channel_id=1, source_target_pairs={{0,4},{4,0},{8,12},{12,8},{16,20},{20,16},{24,28},{28,24},{1,5},{5... | collective-permute-start | bytes 589832 | tf_op jit(solution)/shard_map/ppermute | solution.py:304
  6.9 3.1 %shard_map.96 = bf16[8,272,256]{2,1,0:T(8,128)(2,1)} custom-call(s32[8]{0:T(128)} %slot_ref.1, bf16[8,128,256]{2,1,0:T(8,128)(2,1)} %keys_ref.1, bf16[8,128,256]{2,1,0:T(8,128)(2,1)} %values_ref.1), custom_call_target="tpu_custom_call" | custom-call | tf_op jit(solution)/shard_map/pallas_call | solution.py:100
  10.0 0.0 copy-start.5
  10.0 2.2 %collective-permute-done = bf16[3,256,128]{2,1,0:T(8,128)(2,1)S(1)} collective-permute-done((bf16[3,256,128]{2,1,0:T(8,128)(2,1)}, bf16[3,256,128]{2,1,0:T(8,128)(2,1)S(1)}, u32[]{:S(2)}, u32[]{:S(2)}) %collective-permute-start) | collective-permute-done | bytes 196640 | tf_op jit(solution)/shard_map/ppermute | solution.py:304
  12.2 6.2 %all-to-all-start = ((bf16[8,272,256]{2,1,0:T(8,128)(2,1)}), bf16[8,272,256]{2,1,0:T(8,128)(2,1)S(1)}, u32[]{:S(2)}, u32[]{:S(2)}) async-start(bf16[8,272,256]{2,1,0:T(8,128)(2,1)} %shard_map.96), calls=%async_computation | async-start | bytes 2228224 | tf_op jit(solution)/shard_map/all_to_all | solution.py:312
  18.4 0.0 copy-start
  18.4 0.0 collective-permute-start.3
  18.4 1.6 %collective-permute-start.4 = (bf16[256,1024]{1,0:T(8,128)(2,1)}, bf16[256,1024]{1,0:T(8,128)(2,1)S(1)}, u32[]{:S(2)}, u32[]{:S(2)}) collective-permute-start(bf16[256,1024]{1,0:T(8,128)(2,1)} %get-tuple-element.35), channel_id=1, source_target_pairs={{0,2},{1,3},{2,0},{3,1},{4,6},{5,7},{6,4},{7,5},{8,10},{9,11},{10,... | collective-permute-start | bytes 1572872 | tf_op jit(solution)/shard_map/ppermute | solution.py:306
  19.9 0.0 copy-done.5
  19.9 0.1 maximum_select_fusion
  20.1 3.4 %collective-permute-start.1 = (bf16[512,256]{1,0:T(8,128)(2,1)S(1)}, bf16[512,256]{1,0:T(8,128)(2,1)S(1)}, u32[]{:S(2)}, u32[]{:S(2)}) collective-permute-start(bf16[512,256]{1,0:T(8,128)(2,1)S(1)} %pad_maximum_fusion.kv_ref), channel_id=1, source_target_pairs={{0,8},{4,12},{8,16},{12,20},{16,24},{20,28},{1,9},{5,13},{9,17},{1... | collective-permute-start | bytes 786440 | tf_op jit(solution)/shard_map/ppermute | solution.py:325
  23.5 0.1 collective-permute-start.5
  23.6 24.0 %collective-permute-done.1.kv_ref = bf16[512,256]{1,0:T(8,128)(2,1)S(1)} collective-permute-done((bf16[512,256]{1,0:T(8,128)(2,1)S(1)}, bf16[512,256]{1,0:T(8,128)(2,1)S(1)}, u32[]{:S(2)}, u32[]{:S(2)}) %collective-permute-start.1) | collective-permute-done | bytes 262176 | tf_op jit(solution)/shard_map/ppermute | solution.py:325
  47.6 1.9 %collective-permute-start.2 = (bf16[512,256]{1,0:T(8,128)(2,1)S(1)}, bf16[512,256]{1,0:T(8,128)(2,1)}, u32[]{:S(2)}, u32[]{:S(2)}) collective-permute-start(bf16[512,256]{1,0:T(8,128)(2,1)S(1)} %collective-permute-done.1.kv_ref), channel_id=1, source_target_pairs={{0,8},{4,12},{8,16},{12,20},{16,24},{20,28},{1,9},{5,13},{9,17},{1... | collective-permute-start | bytes 786440 | tf_op jit(solution)/shard_map/ppermute | solution.py:325
  49.5 0.0 copy-start.3
  49.5 0.7 copy-done.3
  50.3 0.0 collective-permute-done.3.refs_5_
  50.3 0.0 collective-permute-done.4.refs_6_
  50.3 0.0 collective-permute-done.5.refs_7_
  50.3 6.8 %collective-permute-done.2.kv_ref = bf16[512,256]{1,0:T(8,128)(2,1)} collective-permute-done((bf16[512,256]{1,0:T(8,128)(2,1)S(1)}, bf16[512,256]{1,0:T(8,128)(2,1)}, u32[]{:S(2)}, u32[]{:S(2)}) %collective-permute-start.2) | collective-permute-done | bytes 262176 | tf_op jit(solution)/shard_map/ppermute | solution.py:325
  57.0 2.2 %collective-permute-start.6 = (bf16[512,256]{1,0:T(8,128)(2,1)}, bf16[512,256]{1,0:T(8,128)(2,1)S(1)}, u32[]{:S(2)}, u32[]{:S(2)}) collective-permute-start(bf16[512,256]{1,0:T(8,128)(2,1)} %collective-permute-done.2.kv_ref), channel_id=1, source_target_pairs={{0,8},{4,12},{8,16},{12,20},{16,24},{20,28},{1,9},{5,13},{9,17},{1... | collective-permute-start | bytes 786440 | tf_op jit(solution)/shard_map/ppermute | solution.py:325
  59.2 0.0 copy-done
  59.2 5.6 %collective-permute-start.8 = (bf16[64,256]{1,0:T(8,128)(2,1)S(1)}, bf16[64,256]{1,0:T(8,128)(2,1)S(1)}, u32[]{:S(2)}, u32[]{:S(2)}) collective-permute-start(bf16[64,256]{1,0:T(8,128)(2,1)S(1)} %slice.31), channel_id=1, source_target_pairs={{4,0},{8,4},{12,8},{16,12},{20,16},{24,20},{28,24},{5,1},{9,5},{13... | collective-permute-start | bytes 98312 | tf_op jit(solution)/shard_map/ppermute | solution.py:309
  64.9 0.1 collective-permute-start.13
  64.9 1.6 %collective-permute-start.14 = (bf16[256,1024]{1,0:T(8,128)(2,1)}, bf16[256,1024]{1,0:T(8,128)(2,1)}, u32[]{:S(2)}, u32[]{:S(2)}) collective-permute-start(bf16[256,1024]{1,0:T(8,128)(2,1)} %get-tuple-element.56), channel_id=1, source_target_pairs={{0,2},{1,3},{2,0},{3,1},{4,6},{5,7},{6,4},{7,5},{8,10},{9,11},{10,... | collective-permute-start | bytes 1572872 | tf_op jit(solution)/shard_map/ppermute | solution.py:306
  66.5 0.3 collective-permute-start.15
  66.8 0.7 shard_map.97
  67.6 0.0 copy-start.4
  67.6 0.9 copy-done.4
  68.5 1.1 %shard_map.98 = (f32[512,128]{1,0:T(8,128)S(1)}, f32[512,128]{1,0:T(8,128)S(1)}, f32[512,128]{1,0:T(8,128)S(1)}) custom-call(s32[1]{0:T(128)} %bitcast.pair_ref, bf16[512,128]{1,0:T(8,128)(2,1)S(1)} %get-tuple-element.60.q_ref, bf16[512,256]{1,0:T(8,128)(2,1)S(1)} %copy-done.4, f32[512,128]{1,0:T(8,128)S(1)} %get-tuple-element.38.refs_0_, ...), custom_call_target="tpu_custom_call" | custom-call | tf_op jit(solution)/shard_map/pallas_call | solution.py:253
  69.7 2.1 %shard_map.99 = (f32[512,128]{1,0:T(8,128)S(1)}, f32[512,128]{1,0:T(8,128)S(1)}, f32[512,128]{1,0:T(8,128)S(1)}) custom-call(s32[1]{0:T(128)} %bitcast.pair_ref, bf16[512,128]{1,0:T(8,128)(2,1)S(1)} %get-tuple-element.60.q_ref, bf16[512,256]{1,0:T(8,128)(2,1)} %collective-permute-done.2.kv_ref, f32[512,128]{1,0:T(8,128)S(1)} %get-tuple-element.41.refs_0_, ...), custom_call_target="tpu_custom_call" | custom-call | tf_op jit(solution)/shard_map/pallas_call | solution.py:253
  71.8 0.0 collective-permute-done.6.kv_ref
  71.8 0.2 shard_map.100
  72.0 0.0 collective-permute-done.8.spill_ref
  72.0 0.0 all-to-all-done.incoming_ref
  72.0 0.6 shard_map.101
  72.6 1.9 %collective-permute-start.9 = (bf16[64,256]{1,0:T(8,128)(2,1)S(1)}, bf16[64,256]{1,0:T(8,128)(2,1)S(1)}, u32[]{:S(2)}, u32[]{:S(2)}) collective-permute-start(bf16[64,256]{1,0:T(8,128)(2,1)S(1)} %get-tuple-element.48), channel_id=1, source_target_pairs={{0,4},{4,8},{8,12},{12,16},{16,20},{20,24},{24,28},{1,5},{5,9},{9,... | collective-permute-start | bytes 98312 | tf_op jit(solution)/shard_map/ppermute | solution.py:335
  74.6 0.0 copy-start.1
  74.6 0.0 copy-start.2
  74.6 2.7 %collective-permute-start.7 = (bf16[256,128]{1,0:T(8,128)(2,1)S(1)}, bf16[256,128]{1,0:T(8,128)(2,1)S(1)}, u32[]{:S(2)}, u32[]{:S(2)}) collective-permute-start(bf16[256,128]{1,0:T(8,128)(2,1)S(1)} %get-tuple-element.62), channel_id=1, source_target_pairs={{0,4},{4,0},{8,12},{12,8},{16,20},{20,16},{24,28},{28,24},{1,5},{5... | collective-permute-start | bytes 196616 | tf_op jit(solution)/shard_map/ppermute | solution.py:329
  77.3 1.6 %shard_map.102 = bf16[256,256]{1,0:T(8,128)(2,1)S(1)} custom-call(bf16[256,256]{1,0:T(8,128)(2,1)S(1)} %copy-done, bf16[16,256]{1,0:T(8,128)(2,1)S(1)} %get-tuple-element.49.tail_ref, bf16[8,272,256]{2,1,0:T(8,128)(2,1)S(1)} %all-to-all-done.incoming_ref), custom_call_target="tpu_custom_call" | custom-call | tf_op jit(solution)/shard_map/pallas_call | solution.py:190
  79.0 0.4 collective-permute-done.9
  79.4 0.1 slice_select_fusion
  79.5 0.6 collective-permute-start.12
  80.1 0.0 collective-permute-done.13.refs_9_
  80.1 1.1 %collective-permute-start.11 = (bf16[256,256]{1,0:T(8,128)(2,1)S(1)}, bf16[256,256]{1,0:T(8,128)(2,1)S(1)}, u32[]{:S(2)}, u32[]{:S(2)}) collective-permute-start(bf16[256,256]{1,0:T(8,128)(2,1)S(1)} %pad_maximum_fusion.1.refs_0_), channel_id=1, source_target_pairs={{0,2},{1,3},{2,0},{3,1},{4,6},{5,7},{6,4},{7,5},{8,10},{9,11},{10,... | collective-permute-start | bytes 393224 | tf_op jit(solution)/shard_map/ppermute | solution.py:341
  81.1 0.0 collective-permute-done.7
  81.1 0.3 collective-permute-start.10
  81.4 0.7 maximum_select_fusion.1
  82.1 0.0 collective-permute-done.14.refs_10_
  82.1 8.3 %collective-permute-done.15.refs_11_ = bf16[256,1024]{1,0:T(8,128)(2,1)} collective-permute-done((bf16[256,1024]{1,0:T(8,128)(2,1)}, bf16[256,1024]{1,0:T(8,128)(2,1)}, u32[]{:S(2)}, u32[]{:S(2)}) %collective-permute-start.15) | collective-permute-done | bytes 524320 | tf_op jit(solution)/shard_map/ppermute | solution.py:306
  90.4 2.7 %collective-permute-done.12.refs_3_ = bf16[256,256]{1,0:T(8,128)(2,1)S(1)} collective-permute-done((bf16[256,256]{1,0:T(8,128)(2,1)S(1)}, bf16[256,256]{1,0:T(8,128)(2,1)S(1)}, u32[]{:S(2)}, u32[]{:S(2)}) %collective-permute-start.12) | collective-permute-done | bytes 131104 | tf_op jit(solution)/shard_map/ppermute | solution.py:341
  93.1 3.3 %collective-permute-done.11.refs_2_ = bf16[256,256]{1,0:T(8,128)(2,1)S(1)} collective-permute-done((bf16[256,256]{1,0:T(8,128)(2,1)S(1)}, bf16[256,256]{1,0:T(8,128)(2,1)S(1)}, u32[]{:S(2)}, u32[]{:S(2)}) %collective-permute-start.11) | collective-permute-done | bytes 131104 | tf_op jit(solution)/shard_map/ppermute | solution.py:341
  96.3 0.0 collective-permute-done.10.refs_1_
  96.3 0.0 copy-done.1
  96.3 0.0 copy-done.2
  96.4 3.6 %shard_map.103 = bf16[256,2048]{1,0:T(8,128)(2,1)} custom-call(bf16[256,256]{1,0:T(8,128)(2,1)S(1)} %pad_maximum_fusion.1.refs_0_, bf16[256,256]{1,0:T(8,128)(2,1)S(1)} %collective-permute-done.10.refs_1_, bf16[256,256]{1,0:T(8,128)(2,1)S(1)} %collective-permute-done.11.refs_2_, bf16[256,256]{1,0:T(8,128)(2,1)S(1)} %collective-permute-done.12.refs_3_, ...), custom_call_target="tpu_custom_call" | custom-call | tf_op jit(solution)/shard_map/pallas_call | solution.py:281
  (7 shorter events, 0.1 us)
Async XLA Ops:
  5.3 6.9 %collective-permute-start = (bf16[3,256,128]{2,1,0:T(8,128)(2,1)}, bf16[3,256,128]{2,1,0:T(8,128)(2,1)S(1)}, u32[]{:S(2)}, u32[]{:S(2)}) collective-permute-start(bf16[3,256,128]{2,1,0:T(8,128)(2,1)} %get-tuple-element.31), channel_id=1, source_target_pairs={{0,4},{4,0},{8,12},{12,8},{16,20},{20,16},{24,28},{28,24},{1,5},{5... | collective-permute-start | bytes 589832 | tf_op jit(solution)/shard_map/ppermute | solution.py:304
  10.0 9.9 %copy-start.5 = (bf16[3,256,128]{2,1,0:T(8,128)(2,1)S(1)}, bf16[3,256,128]{2,1,0:T(8,128)(2,1)}, u32[]{:S(2)}) copy-start(bf16[3,256,128]{2,1,0:T(8,128)(2,1)} %get-tuple-element.30) | copy-start | bytes 589828
  12.2 59.8 %all-to-all-start = ((bf16[8,272,256]{2,1,0:T(8,128)(2,1)}), bf16[8,272,256]{2,1,0:T(8,128)(2,1)S(1)}, u32[]{:S(2)}, u32[]{:S(2)}) async-start(bf16[8,272,256]{2,1,0:T(8,128)(2,1)} %shard_map.96), calls=%async_computation | async-start | bytes 2228224 | tf_op jit(solution)/shard_map/all_to_all | solution.py:312
  18.4 40.9 %copy-start = (bf16[256,256]{1,0:T(8,128)(2,1)S(1)}, bf16[256,256]{1,0:T(8,128)(2,1)}, u32[]{:S(2)}) copy-start(bf16[256,256]{1,0:T(8,128)(2,1)} %queries_ref.3) | copy-start | bytes 393220
  18.4 31.9 %collective-permute-start.3 = (bf16[256,1024]{1,0:T(8,128)(2,1)}, bf16[256,1024]{1,0:T(8,128)(2,1)S(1)}, u32[]{:S(2)}, u32[]{:S(2)}) collective-permute-start(bf16[256,1024]{1,0:T(8,128)(2,1)} %get-tuple-element.34), channel_id=1, source_target_pairs={{0,1},{1,0},{2,3},{3,2},{4,5},{5,4},{6,7},{7,6},{8,9},{9,8},{10,11... | collective-permute-start | bytes 1572872 | tf_op jit(solution)/shard_map/ppermute | solution.py:306
  18.4 31.9 %collective-permute-start.4 = (bf16[256,1024]{1,0:T(8,128)(2,1)}, bf16[256,1024]{1,0:T(8,128)(2,1)S(1)}, u32[]{:S(2)}, u32[]{:S(2)}) collective-permute-start(bf16[256,1024]{1,0:T(8,128)(2,1)} %get-tuple-element.35), channel_id=1, source_target_pairs={{0,2},{1,3},{2,0},{3,1},{4,6},{5,7},{6,4},{7,5},{8,10},{9,11},{10,... | collective-permute-start | bytes 1572872 | tf_op jit(solution)/shard_map/ppermute | solution.py:306
  20.1 27.5 %collective-permute-start.1 = (bf16[512,256]{1,0:T(8,128)(2,1)S(1)}, bf16[512,256]{1,0:T(8,128)(2,1)S(1)}, u32[]{:S(2)}, u32[]{:S(2)}) collective-permute-start(bf16[512,256]{1,0:T(8,128)(2,1)S(1)} %pad_maximum_fusion.kv_ref), channel_id=1, source_target_pairs={{0,8},{4,12},{8,16},{12,20},{16,24},{20,28},{1,9},{5,13},{9,17},{1... | collective-permute-start | bytes 786440 | tf_op jit(solution)/shard_map/ppermute | solution.py:325
  23.5 26.8 %collective-permute-start.5 = (bf16[256,1024]{1,0:T(8,128)(2,1)}, bf16[256,1024]{1,0:T(8,128)(2,1)S(1)}, u32[]{:S(2)}, u32[]{:S(2)}) collective-permute-start(bf16[256,1024]{1,0:T(8,128)(2,1)} %get-tuple-element.36), channel_id=1, source_target_pairs={{0,3},{1,2},{2,1},{3,0},{4,7},{5,6},{6,5},{7,4},{8,11},{9,10},{10,... | collective-permute-start | bytes 1572872 | tf_op jit(solution)/shard_map/ppermute | solution.py:306
  47.6 9.4 %collective-permute-start.2 = (bf16[512,256]{1,0:T(8,128)(2,1)S(1)}, bf16[512,256]{1,0:T(8,128)(2,1)}, u32[]{:S(2)}, u32[]{:S(2)}) collective-permute-start(bf16[512,256]{1,0:T(8,128)(2,1)S(1)} %collective-permute-done.1.kv_ref), channel_id=1, source_target_pairs={{0,8},{4,12},{8,16},{12,20},{16,24},{20,28},{1,9},{5,13},{9,17},{1... | collective-permute-start | bytes 786440 | tf_op jit(solution)/shard_map/ppermute | solution.py:325
  49.5 0.7 copy-start.3
  57.0 14.7 %collective-permute-start.6 = (bf16[512,256]{1,0:T(8,128)(2,1)}, bf16[512,256]{1,0:T(8,128)(2,1)S(1)}, u32[]{:S(2)}, u32[]{:S(2)}) collective-permute-start(bf16[512,256]{1,0:T(8,128)(2,1)} %collective-permute-done.2.kv_ref), channel_id=1, source_target_pairs={{0,8},{4,12},{8,16},{12,20},{16,24},{20,28},{1,9},{5,13},{9,17},{1... | collective-permute-start | bytes 786440 | tf_op jit(solution)/shard_map/ppermute | solution.py:325
  59.2 12.8 %collective-permute-start.8 = (bf16[64,256]{1,0:T(8,128)(2,1)S(1)}, bf16[64,256]{1,0:T(8,128)(2,1)S(1)}, u32[]{:S(2)}, u32[]{:S(2)}) collective-permute-start(bf16[64,256]{1,0:T(8,128)(2,1)S(1)} %slice.31), channel_id=1, source_target_pairs={{4,0},{8,4},{12,8},{16,12},{20,16},{24,20},{28,24},{5,1},{9,5},{13... | collective-permute-start | bytes 98312 | tf_op jit(solution)/shard_map/ppermute | solution.py:309
  64.9 15.2 %collective-permute-start.13 = (bf16[256,1024]{1,0:T(8,128)(2,1)}, bf16[256,1024]{1,0:T(8,128)(2,1)}, u32[]{:S(2)}, u32[]{:S(2)}) collective-permute-start(bf16[256,1024]{1,0:T(8,128)(2,1)} %get-tuple-element.55), channel_id=1, source_target_pairs={{0,1},{1,0},{2,3},{3,2},{4,5},{5,4},{6,7},{7,6},{8,9},{9,8},{10,11... | collective-permute-start | bytes 1572872 | tf_op jit(solution)/shard_map/ppermute | solution.py:306
  64.9 17.2 %collective-permute-start.14 = (bf16[256,1024]{1,0:T(8,128)(2,1)}, bf16[256,1024]{1,0:T(8,128)(2,1)}, u32[]{:S(2)}, u32[]{:S(2)}) collective-permute-start(bf16[256,1024]{1,0:T(8,128)(2,1)} %get-tuple-element.56), channel_id=1, source_target_pairs={{0,2},{1,3},{2,0},{3,1},{4,6},{5,7},{6,4},{7,5},{8,10},{9,11},{10,... | collective-permute-start | bytes 1572872 | tf_op jit(solution)/shard_map/ppermute | solution.py:306
  66.5 23.9 %collective-permute-start.15 = (bf16[256,1024]{1,0:T(8,128)(2,1)}, bf16[256,1024]{1,0:T(8,128)(2,1)}, u32[]{:S(2)}, u32[]{:S(2)}) collective-permute-start(bf16[256,1024]{1,0:T(8,128)(2,1)} %get-tuple-element.57), channel_id=1, source_target_pairs={{0,3},{1,2},{2,1},{3,0},{4,7},{5,6},{6,5},{7,4},{8,11},{9,10},{10,... | collective-permute-start | bytes 1572872 | tf_op jit(solution)/shard_map/ppermute | solution.py:306
  67.6 1.0 copy-start.4
  72.6 6.8 %collective-permute-start.9 = (bf16[64,256]{1,0:T(8,128)(2,1)S(1)}, bf16[64,256]{1,0:T(8,128)(2,1)S(1)}, u32[]{:S(2)}, u32[]{:S(2)}) collective-permute-start(bf16[64,256]{1,0:T(8,128)(2,1)S(1)} %get-tuple-element.48), channel_id=1, source_target_pairs={{0,4},{4,8},{8,12},{12,16},{16,20},{20,24},{24,28},{1,5},{5,9},{9,... | collective-permute-start | bytes 98312 | tf_op jit(solution)/shard_map/ppermute | solution.py:335
  74.6 21.8 %copy-start.1 = (bf16[256,1024]{1,0:T(8,128)(2,1)S(1)}, bf16[256,1024]{1,0:T(8,128)(2,1)}, u32[]{:S(2)}) copy-start(bf16[256,1024]{1,0:T(8,128)(2,1)} %get-tuple-element.50.refs_4_) | copy-start | bytes 1572868
  74.6 21.7 %copy-start.2 = (bf16[256,1024]{1,0:T(8,128)(2,1)S(1)}, bf16[256,1024]{1,0:T(8,128)(2,1)}, u32[]{:S(2)}) copy-start(bf16[256,1024]{1,0:T(8,128)(2,1)} %get-tuple-element.54.refs_8_) | copy-start | bytes 1572868
  74.6 6.5 %collective-permute-start.7 = (bf16[256,128]{1,0:T(8,128)(2,1)S(1)}, bf16[256,128]{1,0:T(8,128)(2,1)S(1)}, u32[]{:S(2)}, u32[]{:S(2)}) collective-permute-start(bf16[256,128]{1,0:T(8,128)(2,1)S(1)} %get-tuple-element.62), channel_id=1, source_target_pairs={{0,4},{4,0},{8,12},{12,8},{16,20},{20,16},{24,28},{28,24},{1,5},{5... | collective-permute-start | bytes 196616 | tf_op jit(solution)/shard_map/ppermute | solution.py:329
  79.5 13.6 %collective-permute-start.12 = (bf16[256,256]{1,0:T(8,128)(2,1)S(1)}, bf16[256,256]{1,0:T(8,128)(2,1)S(1)}, u32[]{:S(2)}, u32[]{:S(2)}) collective-permute-start(bf16[256,256]{1,0:T(8,128)(2,1)S(1)} %pad_maximum_fusion.1.refs_0_), channel_id=1, source_target_pairs={{0,3},{1,2},{2,1},{3,0},{4,7},{5,6},{6,5},{7,4},{8,11},{9,10},{10,... | collective-permute-start | bytes 393224 | tf_op jit(solution)/shard_map/ppermute | solution.py:341
  80.1 16.3 %collective-permute-start.11 = (bf16[256,256]{1,0:T(8,128)(2,1)S(1)}, bf16[256,256]{1,0:T(8,128)(2,1)S(1)}, u32[]{:S(2)}, u32[]{:S(2)}) collective-permute-start(bf16[256,256]{1,0:T(8,128)(2,1)S(1)} %pad_maximum_fusion.1.refs_0_), channel_id=1, source_target_pairs={{0,2},{1,3},{2,0},{3,1},{4,6},{5,7},{6,4},{7,5},{8,10},{9,11},{10,... | collective-permute-start | bytes 393224 | tf_op jit(solution)/shard_map/ppermute | solution.py:341
  81.1 15.2 %collective-permute-start.10 = (bf16[256,256]{1,0:T(8,128)(2,1)S(1)}, bf16[256,256]{1,0:T(8,128)(2,1)S(1)}, u32[]{:S(2)}, u32[]{:S(2)}) collective-permute-start(bf16[256,256]{1,0:T(8,128)(2,1)S(1)} %pad_maximum_fusion.1.refs_0_), channel_id=1, source_target_pairs={{0,1},{1,0},{2,3},{3,2},{4,5},{5,4},{6,7},{7,6},{8,9},{9,8},{10,11... | collective-permute-start | bytes 393224 | tf_op jit(solution)/shard_map/ppermute | solution.py:341

commit v4 on v1

v4 whole, which is shorter than its diff:
```python
import functools
import math

import jax
import jax.numpy as jnp
from jax import lax
from jax.experimental import pallas as pl
from jax.experimental.pallas import tpu as pltpu
from jax.sharding import PartitionSpec as P

HD = 128
BLOCK = 64
LEAD = 16
WINDOW = BLOCK + LEAD
ENTRY = WINDOW + LEAD
ENTRIES = 6
NEGATIVE = -1e30
SCALE = HD ** -0.5 * math.log2(math.e)
VMEM = pl.BlockSpec(memory_space=pltpu.VMEM)
SMEM = pl.BlockSpec(memory_space=pltpu.SMEM)
ANY = pl.BlockSpec(memory_space=pl.ANY)
PARAMS = pltpu.CompilerParams(vmem_limit_bytes=16 * 1024 * 1024)


def dot(a, b):
    return jnp.dot(a, b, preferred_element_type=jnp.float32)


def dot_t(a, b):
    return lax.dot_general(a, b, (((1,), (1,)), ((), ())), preferred_element_type=jnp.float32)


def fetch(pieces, sems):
    copies = [
        pltpu.make_async_copy(source, target, sems.at[at])
        for at, (source, target) in enumerate(pieces)
    ]
    for copy in copies:
        copy.start()
    for copy in copies:
        copy.wait()


def cut_kernel(plan, side_ref, tp_ref, *refs):
    sems, refs = refs[-1], refs[:-1]
    sources, outs = refs[: len(refs) - len(plan)], refs[len(refs) - len(plan) :]
    pieces = []
    for out, parts in zip(outs, plan):
        for at, (index, step, start, width) in enumerate(parts):
            source = sources[index]
            if start is None:
                lane = pl.multiple_of((side_ref[0] ^ step) * HD, HD)
            else:
                total, offset = start
                lane = pl.multiple_of((tp_ref[0] ^ step) * total + offset, HD)
            lanes = pl.ds(lane, width)
            piece = source.at[:, lanes] if len(source.shape) == 2 else source.at[:, :, lanes]
            pieces.append((piece, out.at[at] if len(parts) > 1 else out))
    fetch(pieces, sems)


def cut(side, tp, sources, plan):
    shapes = []
    for parts in plan:
        source = sources[parts[0][0]]
        stack = (len(parts),) if len(parts) > 1 else ()
        shape = stack + source.shape[:-1] + (parts[0][3],)
        shapes.append(jax.ShapeDtypeStruct(shape, source.dtype))
    return pl.pallas_call(
        functools.partial(cut_kernel, plan),
        out_shape=tuple(shapes),
        in_specs=[SMEM] * 2 + [ANY] * len(sources),
        out_specs=(VMEM,) * len(plan),
        scratch_shapes=[pltpu.SemaphoreType.DMA((sum(len(parts) for parts in plan),))],
    )(side, tp, *sources)


def hold_kernel(pair_ref, own_ref, other_ref, kv_own, kv_other, *refs):
    pairs = (len(refs) - 2) // 2
    queries, outs, (all_ref, back_ref) = refs[:pairs], refs[pairs : 2 * pairs], refs[2 * pairs :]
    pair = pair_ref[0]
    rows = queries[0].shape[0]
    blocks = rows // BLOCK
    for step in range(pairs):
        at = pl.multiple_of(lax.rem(pair - step + pairs, pairs) * rows, BLOCK)
        all_ref[pl.ds(at, rows), :] = queries[step][...]
    all_ref[pairs * rows :, :] = jnp.zeros((BLOCK, HD), all_ref.dtype)
    row = lax.broadcasted_iota(jnp.int32, (LEAD, WINDOW), 0)
    for half, (slot_ref, kv) in enumerate(((own_ref, kv_own), (other_ref, kv_other))):
        count = slot_ref.shape[0]
        for n in range(count):
            slot = slot_ref[n]
            block = slot // 2
            owner = block // blocks
            step = lax.rem(owner - pair + pairs, pairs)
            entry = 2 * half + lax.rem(slot // count, 2)
            start = pl.multiple_of(block * BLOCK + BLOCK - LEAD, LEAD)
            s = dot_t(kv[0, n], all_ref[pl.ds(start, WINDOW), :])
            peak = jnp.max(s, axis=0, keepdims=True).astype(jnp.bfloat16).astype(jnp.float32)
            p = jnp.exp2((s - peak) * SCALE)
            total = jnp.sum(p, axis=0, keepdims=True)
            mixed = lax.dot_general(
                p.astype(jnp.bfloat16),
                kv[1, n],
                (((0,), (0,)), ((), ())),
                preferred_element_type=jnp.float32,
            ).astype(jnp.bfloat16)
            high = total.astype(jnp.bfloat16).astype(jnp.float32)
            stats = jnp.where(row == 0, peak, jnp.where(row == 1, high, total - high))
            stats = stats.astype(jnp.bfloat16)
            at = pl.multiple_of(entry * ENTRY, LEAD)
            back_ref[step, pl.ds(at, WINDOW), :] = mixed
            back_ref[step, pl.ds(at + WINDOW, LEAD), :WINDOW] = stats

            @pl.when(lax.rem(block, blocks) == blocks - 1)
            def _():
                after = lax.rem(step + 1, pairs)
                spill = (4 + half) * ENTRY
                back_ref[after, spill : spill + WINDOW, :] = mixed
                back_ref[after, spill + WINDOW : spill + ENTRY, :WINDOW] = stats

    for step in range(pairs):
        outs[step][...] = back_ref[step]


def hold(pair, slots, other_slots, kv, other_kv, queries):
    pairs = len(queries)
    rows = queries[0].shape[0]
    dtype = queries[0].dtype
    return pl.pallas_call(
        hold_kernel,
        out_shape=(jax.ShapeDtypeStruct((ENTRIES * ENTRY, HD), dtype),) * pairs,
        in_specs=[SMEM] * 3 + [VMEM] * (2 + pairs),
        out_specs=(VMEM,) * pairs,
        scratch_shapes=[
            pltpu.VMEM((pairs * rows + BLOCK, HD), dtype),
            pltpu.VMEM((pairs, ENTRIES * ENTRY, HD), dtype),
        ],
        compiler_params=PARAMS,
    )(pair, slots, other_slots, kv, other_kv, *queries)


def table_kernel(blocks, pair_ref, *refs):
    slots, table_ref = refs[:-1], refs[-1]
    pair = pair_ref[0]
    places = 2 * blocks
    for place in range(places + 2):
        table_ref[place] = 0
    for step, slot_ref in enumerate(slots):
        count = slot_ref.shape[0] // 2

        def look(n, carry):
            slot = slot_ref[n]
            owner = slot // places
            place = slot - owner * places
            half = n // count

            @pl.when(owner == pair)
            def _():
                table_ref[place] = step * ENTRIES + 2 * half + lax.rem(slot // count, 2)

            @pl.when((owner == pair - 1) & (place >= places - 2))
            def _():
                table_ref[place + 2] = step * ENTRIES + 4 + half

            return carry

        lax.fori_loop(0, 2 * count, look, 0)


def find_parts(pair, slots, blocks):
    return pl.pallas_call(
        functools.partial(table_kernel, blocks),
        out_shape=jax.ShapeDtypeStruct((2 * blocks + 2,), jnp.int32),
        in_specs=[SMEM] * (1 + len(slots)),
        out_specs=SMEM,
        compiler_params=PARAMS,
    )(pair, *slots)


def combine_kernel(pair_ref, side_ref, table_ref, *refs):
    keep_ref, give_ref, all_ref, factor_ref, cca_ref = refs[-5:]
    parts = refs[:-5]
    length = ENTRIES * ENTRY
    for step, part in enumerate(parts):
        all_ref[step * length : (step + 1) * length, :] = part[...]
    rows = cca_ref.shape[0]
    blocks = rows // BLOCK

    def at(place):
        return pl.multiple_of(table_ref[place] * ENTRY, LEAD)

    def stats(place):
        held = all_ref[pl.ds(at(place) + WINDOW, LEAD), :].astype(jnp.float32)
        return held[0:1], held[1:2] + held[2:3]

    for block in range(blocks + 1):
        peak1, total1 = stats(2 * block)
        peak2, total2 = stats(2 * block + 1)
        peak = jnp.maximum(peak1, peak2)
        weight1 = jnp.exp2((peak1 - peak) * SCALE)
        weight2 = jnp.exp2((peak2 - peak) * SCALE)
        total = weight1 * total1 + weight2 * total2
        factor_ref[2 * block : 2 * block + 1, :] = weight1 / total
        factor_ref[2 * block + 1 : 2 * block + 2, :] = weight2 / total
    factors = factor_ref[...].T

    def answer(block):
        result = None
        for place in (2 * block, 2 * block + 1):
            held = all_ref[pl.ds(at(place), WINDOW), :].astype(jnp.float32)
            held = held * factors[:WINDOW, place : place + 1]
            result = held if result is None else result + held
        return result.astype(jnp.bfloat16)

    row = lax.broadcasted_iota(jnp.int32, (LEAD, HD), 0)
    before = answer(blocks)
    before = jnp.where(pair_ref[0] == 0, jnp.zeros_like(before), before)
    for block in range(blocks):
        now = answer(block)
        top = block * BLOCK
        cca_ref[top : top + BLOCK - LEAD, :] = before[LEAD:BLOCK]
        cca_ref[top + BLOCK - LEAD : top + BLOCK, :] = jnp.where(
            row == LEAD - 1, now[:LEAD], before[BLOCK:]
        )
        before = now
    half = rows // 2
    side = side_ref[0]
    keep_ref[...] = cca_ref[pl.ds(pl.multiple_of(side * half, half), half), :]
    give_ref[...] = cca_ref[pl.ds(pl.multiple_of((1 - side) * half, half), half), :]


def combine(pair, side, table, parts, rows):
    dtype = parts[0].dtype
    half = jax.ShapeDtypeStruct((rows // 2, HD), dtype)
    return pl.pallas_call(
        combine_kernel,
        out_shape=(half, half),
        in_specs=[SMEM] * 3 + [VMEM] * len(parts),
        out_specs=(VMEM, VMEM),
        scratch_shapes=[
            pltpu.VMEM((len(parts) * ENTRIES * ENTRY, HD), dtype),
            pltpu.VMEM((HD, HD), jnp.float32),
            pltpu.VMEM((rows, HD), dtype),
        ],
        compiler_params=PARAMS,
    )(pair, side, table, *parts)


def self_kernel(first, last, step, pair_ref, q_ref, kv_ref, *refs):
    if not first:
        peak_in, total_in, accum_in = refs[:3]
        refs = refs[3:]
    rows = q_ref.shape[0]
    tile = rows // 2
    for part in range(2):
        at = pl.ds(part * tile, tile)

        def emit(peak, total, accum):
            if last:
                refs[0][at, :] = (accum / total).astype(jnp.bfloat16)
            else:
                refs[0][at, :] = jnp.broadcast_to(peak, (tile, HD))
                refs[1][at, :] = jnp.broadcast_to(total, (tile, HD))
                refs[2][at, :] = accum

        def work():
            q = q_ref[at, :]
            count = (part + 1) * tile if first else rows
            s = dot_t(q, kv_ref[:count, :HD])
            if first:
                row = lax.broadcasted_iota(jnp.int32, (tile, count), 0) + part * tile
                col = lax.broadcasted_iota(jnp.int32, (tile, count), 1)
                s = jnp.where(col <= row, s, NEGATIVE)
            peak = jnp.max(s, axis=1, keepdims=True)
            if not first:
                old = peak_in[at, :1]
                peak = jnp.maximum(peak, old)
                factor = jnp.exp2((old - peak) * SCALE)
            p = jnp.exp2((s - peak) * SCALE)
            total = jnp.sum(p, axis=1, keepdims=True)
            accum = dot(p.astype(jnp.bfloat16), kv_ref[:count, HD:])
            if not first:
                total += total_in[at, :1] * factor
                accum += accum_in[at, :] * factor
            emit(peak, total, accum)

        if first:
            work()
        else:
            pl.when(pair_ref[0] >= step)(work)

            @pl.when(pair_ref[0] < step)
            def _():
                emit(peak_in[at, :1], total_in[at, :1], accum_in[at, :])


def self_step(pair, q, kv, state, step, last):
    rows = q.shape[0]
    first = state is None
    held = jax.ShapeDtypeStruct((rows, HD), jnp.float32)
    out_shape = jax.ShapeDtypeStruct((rows, HD), jnp.bfloat16) if last else (held,) * 3
    return pl.pallas_call(
        functools.partial(self_kernel, first, last, step),
        out_shape=out_shape,
        in_specs=[SMEM] + [VMEM] * (2 if first else 5),
        out_specs=VMEM if last else (VMEM,) * 3,
        compiler_params=PARAMS,
    )(pair, q, kv, *(() if first else state))


def project_kernel(groups, *refs):
    crossed_ref = refs[-1]
    at = 0
    for part in range(len(refs) // groups - 1):
        blocks = refs[(part + 1) * groups : (part + 2) * groups]
        width = blocks[0].shape[1]
        tile = min(512, width)
        for column in range(0, width, tile):
            total = dot(refs[0][...], blocks[0][:, column : column + tile])
            for group in range(1, groups):
                total += dot(refs[group][...], blocks[group][:, column : column + tile])
            crossed_ref[:, at : at + tile] = total.astype(crossed_ref.dtype)
            at += tile


def project(terms, weights):
    groups = len(terms)
    rows = terms[0].shape[0]
    width = sum(part[0].shape[1] for part in weights)
    return pl.pallas_call(
        functools.partial(project_kernel, groups),
        out_shape=jax.ShapeDtypeStruct((rows, width), jnp.bfloat16),
        in_specs=[VMEM] * (groups * (1 + len(weights))),
        out_specs=VMEM,
        compiler_params=PARAMS,
    )(*terms, *(block for part in weights for block in part))


def shards(queries, keys, values, cross_queries, nbr_keys, nbr_values, nbr_slot, w_cross):
    ctx = lax.axis_index("ctx")
    count = lax.axis_size("ctx")
    tp = lax.axis_index("tp").reshape(1)
    groups = lax.axis_size("tp")
    side = (ctx & 1).reshape(1)
    pair = (ctx >> 1).reshape(1)
    left = ctx & 1 == 0
    pairs = count // 2
    rows = queries.shape[0]
    swap = [(i, i ^ 1) for i in range(count)]
    across = [[(i, i ^ step) for i in range(groups)] for step in range(groups)]
    around = [[(i, (i + 2 * step) % count) for i in range(count)] for step in range(pairs)]

    def both(mine, other, axis):
        return jnp.where(
            left,
            jnp.concatenate([mine, other], axis),
            jnp.concatenate([other, mine], axis),
        )

    width = w_cross.shape[1] // groups
    halves = ((0, width // 2), (width // 2, width // 2))

    def columns(index, step, part):
        return [(index, step, (width, halves[part][0]), halves[part][1])]

    steps = range(1, groups)
    far_steps = [step for step in steps if step > 1]
    away, mine, *first = cut(
        side, tp, (queries, keys, values, cross_queries, w_cross),
        [[(at, 1, None, HD) for at in range(4)], [(at, 0, None, HD) for at in range(4)]]
        + [columns(4, step, 0) for step in far_steps],
    )
    other = lax.ppermute(away, "ctx", swap)
    moved = {}
    for step, block in zip(far_steps, first):
        moved[step, 0] = lax.ppermute(block, "tp", across[step])
    nbr_away, nbr_mine = cut(
        side, tp, (nbr_keys, nbr_values),
        [[(0, 1, None, HD), (1, 1, None, HD)], [(0, 0, None, HD), (1, 0, None, HD)]],
    )
    nbr_other = lax.ppermute(nbr_away, "ctx", swap)
    slot_other = lax.ppermute(nbr_slot, "ctx", swap)
    later = [(0, 0), (0, 1), (1, 0)] + [(step, 1) for step in steps]
    rest = cut(side, tp, (w_cross,), [columns(0, step, part) for step, part in later])
    for (step, part), block in zip(later, rest):
        moved[step, part] = lax.ppermute(block, "tp", across[step]) if step else block
    weights = [[moved[step, part] for step in range(groups)] for part in range(2)]

    joint = both(mine, other, 1)
    asked = [joint[3]]
    slots = [jnp.concatenate([nbr_slot, slot_other])]
    for step in range(1, pairs):
        asked.append(lax.ppermute(joint[3], "ctx", around[step]))
    answers = hold(pair, nbr_slot, slot_other, nbr_mine, nbr_other, asked)
    slots[0], answers = lax.optimization_barrier((slots[0], answers))
    parts = [answers[0]]
    for step in range(1, pairs):
        parts.append(lax.ppermute(answers[step], "ctx", around[step]))
        slots.append(lax.ppermute(slots[0], "ctx", around[step]))
    table = find_parts(pair, slots, 2 * rows // BLOCK)

    q = joint[0]
    kv = jnp.concatenate([joint[1], joint[2]], axis=1)
    forward = [(i, i + 2) for i in range(count - 2)]
    state = None
    for step in range(pairs):
        if step == 2:
            kv, weights[0] = lax.optimization_barrier((kv, weights[0]))
        following = lax.ppermute(kv, "ctx", forward) if step < pairs - 1 else None
        state = self_step(pair, q, kv, state, step, step == pairs - 1)
        kv = following
    near = jnp.where(left, state[:rows], state[rows:])
    far = lax.ppermute(jnp.where(left, state[rows:], state[:rows]), "ctx", swap)
    attended = both(near, far, 1)

    keep, give = combine(pair, side, table, parts, 2 * rows)
    cca = both(keep, lax.ppermute(give, "ctx", swap), 1)
    terms = [cca]
    for step in range(1, groups):
        terms.append(lax.ppermute(cca, "tp", across[step]))
    crossed = project(terms, weights)
    return (attended, crossed)


def solution(mesh):
    in_specs = (
        P("ctx", "tp"),
        P("ctx", "tp"),
        P("ctx", "tp"),
        P("ctx", "tp"),
        P("ctx", None, "tp"),
        P("ctx", None, "tp"),
        P("ctx"),
        P("tp", None),
    )
    out_specs = (P("ctx", "tp"), P("ctx", "tp"))
    return jax.shard_map(shards, mesh=mesh, in_specs=in_specs, out_specs=out_specs, check_vma=False)
```

time: 137 us -> 115 us (0.84); the launches traced: 134 us -> 115 us
  Pallas kernels: 44.6 us -> 24.5 us
  local copies, waits for them, and re-layouts: 12.6 us -> 3.8 us
  waiting for transfers between devices: 32.6 us -> 38.1 us
  starting transfers between devices: 39.6 us -> 44.2 us
    ppermute x10 -> x23, starting transfers between devices: 12.9 us -> 33.9 us  [the longest x3 11 us: shards(): slots.append(lax.ppermute(slots[0], 'ctx', around[step]))]
    pallas_call x2 -> x6, Pallas kernels: 37 us -> 18.5 us  [the longest x3 8.45 us: cut(): pl.pallas_call(functools.partial(cut_kernel, plan), out_shape=tuple(shape...]
    all_to_all x2 -> x0, starting transfers between devices: 10.8 us -> none  [the longest x1 7.28 us: shards(): lax.all_to_all(labels, 'ctx', split_axis=0, concat_axis=0, tiled=True)]
    ppermute x10 -> x23, waiting for transfers between devices: 24.2 us -> 33.1 us  [the longest x4 8.2 us: shards(): lax.ppermute(block, 'tp', across[step])]
    ppermute x3, starting transfers between devices: 15.9 us -> 10.3 us  [shards(): following = lax.ppermute(kv, 'ctx', forward) if step < pairs - 1 else None]
    all_to_all x2 -> x0, waiting for transfers between devices: 5.31 us -> none  [the longest x1 5.31 us: shards(): lax.all_to_all(labels, 'ctx', split_axis=0, concat_axis=0, tiled=True)]
    dynamic_slice x1 -> x0, local copies, waits for them, and re-layouts: 3.64 us -> none  [shards(): lax.dynamic_slice_in_dim(w_cross, (tp ^ step) * width, width, axis=1)]
    slice x4 -> x0, local copies, waits for them, and re-layouts: 2.96 us -> none  [the longest x1 1.57 us: shards(): shifted = jnp.concatenate([cross_queries[BLOCK - 1:], spill], axis=0)]
  transfers between devices with their start and end apart: 15 -> 26, of which waited for: 9 -> 11; matrix products, arithmetic and copies ran while one was open for 8% -> 1% of each run, Pallas kernels for 5% -> 19%
where the time goes in v4:
time: 115 us
  starting transfers between devices  44.2 us (38%)
  waiting for transfers between devices  38.1 us (33%)
  Pallas kernels  24.5 us (21%)
  local copies, waits for them, and re-layouts  3.8 us (3%)
  other arithmetic  2.93 us (3%)
    ppermute x3, starting transfers between devices, shards(): slots.append(lax.ppermute(slots[0], 'ctx', around[step]))  11 us
    ppermute x3, starting transfers between devices, shards(): following = lax.ppermute(kv, 'ctx', forward) if step < pairs - 1 else None  10.3 us
    pallas_call x3, Pallas kernels, cut(): pl.pallas_call(functools.partial(cut_kernel, plan), out_shape=tuple(shape...  8.45 us
    ppermute x4, waiting for transfers between devices, shards(): lax.ppermute(block, 'tp', across[step])  8.2 us
    ppermute x3, waiting for transfers between devices, shards(): slots.append(lax.ppermute(slots[0], 'ctx', around[step]))  7.34 us
    pallas_call x1, Pallas kernels, hold(): pl.pallas_call(hold_kernel, out_shape=(jax.ShapeDtypeStruct((ENTRIES * EN...  6.53 us
    ppermute x1, waiting for transfers between devices, shards(): other = lax.ppermute(away, 'ctx', swap)  6.52 us
    ppermute x1, waiting for transfers between devices, shards(): slot_other = lax.ppermute(nbr_slot, 'ctx', swap)  6.17 us
  transfers between devices with their start and end apart: 26, of which 11 were waited for; matrix products, arithmetic and copies ran while one was open for 1% of the time, Pallas kernels for 19%

profile of v4, /device:TPU:0, one launch (start us, length us, event | category | flops | bytes accessed | tf_op | source)
XLA Modules:
  0.0 114.5 jit_solution(3424356098026216978)
XLA Ops:
  0.6 2.7 %shard_map.95 = (bf16[4,256,128]{2,1,0:T(8,128)(2,1)}, bf16[4,256,128]{2,1,0:T(8,128)(2,1)}, bf16[256,1024]{1,0:T(8,128)(2,1)}, bf16[256,1024]{1,0:T(8,128)(2,1)}) custom-call(s32[1]{0:T(128)} %bitcast.1.side_ref, s32[1]{0:T(128)} %bitcast.2.tp_ref, bf16[256,256]{1,0:T(8,128)(2,1)} %refs_0_.3, bf16[256,256]{1,0:T(8,128)(2,1)} %refs_1_.2, ...), custom_call_target="tpu_custom_call" | custom-call | tf_op jit(solution)/shard_map/pallas_call | solution.py:69
  3.3 3.0 %collective-permute-start = (bf16[4,256,128]{2,1,0:T(8,128)(2,1)}, bf16[4,256,128]{2,1,0:T(8,128)(2,1)S(1)}, u32[]{:S(2)}, u32[]{:S(2)}) collective-permute-start(bf16[4,256,128]{2,1,0:T(8,128)(2,1)} %get-tuple-element.40), channel_id=1, source_target_pairs={{0,4},{4,0},{8,12},{12,8},{16,20},{20,16},{24,28},{28,24},{1,5},{5... | collective-permute-start | bytes 786440 | tf_op jit(solution)/shard_map/ppermute | solution.py:374
  6.4 6.5 %collective-permute-done = bf16[4,256,128]{2,1,0:T(8,128)(2,1)S(1)} collective-permute-done((bf16[4,256,128]{2,1,0:T(8,128)(2,1)}, bf16[4,256,128]{2,1,0:T(8,128)(2,1)S(1)}, u32[]{:S(2)}, u32[]{:S(2)}) %collective-permute-start) | collective-permute-done | bytes 262176 | tf_op jit(solution)/shard_map/ppermute | solution.py:374
  12.9 1.2 %maximum_select_fusion = bf16[4,512,128]{2,1,0:T(8,128)(2,1)S(1)} fusion(bf16[4,256,128]{2,1,0:T(8,128)(2,1)S(1)} %collective-permute-done, bf16[4,256,128]{2,1,0:T(8,128)(2,1)} %get-tuple-element.39, pred[]{:T(512)S(6)} %eq.3), kind=kLoop, calls=%fused_computation | loop fusion | flops 2359296 | bytes 1048577 | tf_op jit(solution)/shard_map/jit(_where)/select_n | solution.py:355
  14.1 0.7 slice_bitcast_fusion
  14.8 3.8 %collective-permute-start.12 = (bf16[512,128]{1,0:T(8,128)(2,1)S(1)}, bf16[512,128]{1,0:T(8,128)(2,1)S(1)}, u32[]{:S(2)}, u32[]{:S(2)}) collective-permute-start(bf16[512,128]{1,0:T(8,128)(2,1)S(1)} %get-tuple-element.76.refs_0_), channel_id=1, source_target_pairs={{0,24},{4,28},{8,0},{12,4},{16,8},{20,12},{24,16},{28,20},{1,25},{... | collective-permute-start | bytes 393224 | tf_op jit(solution)/shard_map/ppermute | solution.py:394
  18.6 0.0 collective-permute-start.11
  18.6 2.2 %shard_map.101 = (bf16[2,8,128,128]{3,2,1,0:T(8,128)(2,1)}, bf16[2,8,128,128]{3,2,1,0:T(8,128)(2,1)}) custom-call(s32[1]{0:T(128)} %bitcast.1.side_ref, s32[1]{0:T(128)} %bitcast.2.tp_ref, bf16[8,128,256]{2,1,0:T(8,128)(2,1)} %refs_0_.5, bf16[8,128,256]{2,1,0:T(8,128)(2,1)} %refs_1_.3), custom_call_target="tpu_custom_call" | custom-call | tf_op jit(solution)/shard_map/pallas_call | solution.py:69
  20.8 1.6 %collective-permute-start.9 = (bf16[2,8,128,128]{3,2,1,0:T(8,128)(2,1)}, bf16[2,8,128,128]{3,2,1,0:T(8,128)(2,1)S(1)}, u32[]{:S(2)}, u32[]{:S(2)}) collective-permute-start(bf16[2,8,128,128]{3,2,1,0:T(8,128)(2,1)} %get-tuple-element.56), channel_id=1, source_target_pairs={{0,4},{4,0},{8,12},{12,8},{16,20},{20,16},{24,28},{28,24},{1,5},{5... | collective-permute-start | bytes 1572872 | tf_op jit(solution)/shard_map/ppermute | solution.py:382
  22.4 1.0 collective-permute-start.10
  23.4 0.5 collective-permute-start.8
  23.9 3.5 %shard_map.96 = (bf16[256,1024]{1,0:T(8,128)(2,1)}, bf16[256,1024]{1,0:T(8,128)(2,1)}, bf16[256,1024]{1,0:T(8,128)(2,1)}, bf16[256,1024]{1,0:T(8,128)(2,1)}, bf1...) custom-call(s32[1]{0:T(128)} %bitcast.1.side_ref, s32[1]{0:T(128)} %bitcast.2.tp_ref, bf16[256,8192]{1,0:T(8,128)(2,1)} %refs_0_.4), custom_call_target="tpu_custom_call" | custom-call | tf_op jit(solution)/shard_map/pallas_call | solution.py:69
  27.5 6.2 %collective-permute-done.8.other_ref = s32[8]{0:T(128)S(1)} collective-permute-done((s32[8]{0:T(128)S(1)}, s32[8]{0:T(128)S(1)}, u32[]{:S(2)}, u32[]{:S(2)}) %collective-permute-start.8) | collective-permute-done | bytes 64 | tf_op jit(solution)/shard_map/ppermute | solution.py:383
  33.7 1.5 %collective-permute-start.4 = (bf16[256,1024]{1,0:T(8,128)(2,1)}, bf16[256,1024]{1,0:T(8,128)(2,1)S(1)}, u32[]{:S(2)}, u32[]{:S(2)}) collective-permute-start(bf16[256,1024]{1,0:T(8,128)(2,1)} %get-tuple-element.43), channel_id=1, source_target_pairs={{0,2},{1,3},{2,0},{3,1},{4,6},{5,7},{6,4},{7,5},{8,10},{9,11},{10,... | collective-permute-start | bytes 1572872 | tf_op jit(solution)/shard_map/ppermute | solution.py:377
  35.2 0.0 collective-permute-done.12.refs_3_
  35.2 0.0 collective-permute-start.5
  35.2 0.0 collective-permute-done.11.refs_2_
  35.2 0.6 copy-done.3
  35.8 0.6 collective-permute-start.3
  36.5 0.9 pad_maximum_fusion.kv_ref
  37.4 0.0 collective-permute-done.10.refs_1_
  37.4 0.0 copy-start.5
  37.4 0.6 copy-done.5
  38.1 3.3 %collective-permute-start.1 = (bf16[512,256]{1,0:T(8,128)(2,1)S(1)}, bf16[512,256]{1,0:T(8,128)(2,1)}, u32[]{:S(2)}, u32[]{:S(2)}) collective-permute-start(bf16[512,256]{1,0:T(8,128)(2,1)S(1)} %pad_maximum_fusion.kv_ref), channel_id=1, source_target_pairs={{0,8},{4,12},{8,16},{12,20},{16,24},{20,28},{1,9},{5,13},{9,17},{1... | collective-permute-start | bytes 786440 | tf_op jit(solution)/shard_map/ppermute | solution.py:410
  41.4 5.0 %collective-permute-done.1.kv_ref = bf16[512,256]{1,0:T(8,128)(2,1)} collective-permute-done((bf16[512,256]{1,0:T(8,128)(2,1)S(1)}, bf16[512,256]{1,0:T(8,128)(2,1)}, u32[]{:S(2)}, u32[]{:S(2)}) %collective-permute-start.1) | collective-permute-done | bytes 262176 | tf_op jit(solution)/shard_map/ppermute | solution.py:410
  46.4 4.5 %collective-permute-start.2 = (bf16[512,256]{1,0:T(8,128)(2,1)}, bf16[512,256]{1,0:T(8,128)(2,1)S(1)}, u32[]{:S(2)}, u32[]{:S(2)}) collective-permute-start(bf16[512,256]{1,0:T(8,128)(2,1)} %collective-permute-done.1.kv_ref), channel_id=1, source_target_pairs={{0,8},{4,12},{8,16},{12,20},{16,24},{20,28},{1,9},{5,13},{9,17},{1... | collective-permute-start | bytes 786440 | tf_op jit(solution)/shard_map/ppermute | solution.py:410
  50.9 0.0 collective-permute-done.9.kv_other
  50.9 0.1 collective-permute-start.23
  51.0 0.1 pad_add_fusion.refs_0_
  51.1 0.9 copy-done.4
  52.0 0.9 copy-done.6
  52.9 6.5 %shard_map.102 = (bf16[576,128]{1,0:T(8,128)(2,1)S(1)}, bf16[576,128]{1,0:T(8,128)(2,1)S(1)}, bf16[576,128]{1,0:T(8,128)(2,1)S(1)}, bf16[576,128]{1,0:T(8,128)(2,1)S(1)}) custom-call(s32[1]{0:T(128)} %bitcast.pair_ref, s32[8]{0:T(128)S(1)} %copy-done.7, s32[8]{0:T(128)S(1)} %collective-permute-done.8.other_ref, bf16[2,8,128,128]{3,2,1,0:T(8,128)(2,1)S(1)} %copy-done, ...), custom_call_target="tpu_custom_call" | custom-call | tf_op jit(solution)/shard_map/pallas_call | solution.py:130
  59.5 2.5 %collective-permute-start.16 = (bf16[576,128]{1,0:T(8,128)(2,1)S(1)}, bf16[576,128]{1,0:T(8,128)(2,1)S(1)}, u32[]{:S(2)}, u32[]{:S(2)}) collective-permute-start(bf16[576,128]{1,0:T(8,128)(2,1)S(1)} %get-tuple-element.63), channel_id=1, source_target_pairs={{0,8},{4,12},{8,16},{12,20},{16,24},{20,28},{24,0},{28,4},{1,9},{5... | collective-permute-start | bytes 442376 | tf_op jit(solution)/shard_map/ppermute | solution.py:399
  62.0 0.0 collective-permute-done.5.refs_7_
  62.0 2.6 %collective-permute-start.15 = (s32[16]{0:T(128)S(1)}, s32[16]{0:T(128)S(1)}, u32[]{:S(2)}, u32[]{:S(2)}) collective-permute-start(s32[16]{0:T(128)S(1)} %pad_add_fusion.refs_0_), channel_id=1, source_target_pairs={{0,24},{4,28},{8,0},{12,4},{16,8},{20,12},{24,16},{28,20},{1,25},{... | collective-permute-start | bytes 200 | tf_op jit(solution)/shard_map/ppermute | solution.py:400
  64.6 4.4 %collective-permute-done.15.refs_3_ = s32[16]{0:T(128)S(1)} collective-permute-done((s32[16]{0:T(128)S(1)}, s32[16]{0:T(128)S(1)}, u32[]{:S(2)}, u32[]{:S(2)}) %collective-permute-start.15) | collective-permute-done | bytes 96 | tf_op jit(solution)/shard_map/ppermute | solution.py:400
  69.0 4.5 %collective-permute-start.14 = (s32[16]{0:T(128)S(1)}, s32[16]{0:T(128)S(1)}, u32[]{:S(2)}, u32[]{:S(2)}) collective-permute-start(s32[16]{0:T(128)S(1)} %pad_add_fusion.refs_0_), channel_id=1, source_target_pairs={{0,16},{4,20},{8,24},{12,28},{16,0},{20,4},{24,8},{28,12},{1,17},{... | collective-permute-start | bytes 200 | tf_op jit(solution)/shard_map/ppermute | solution.py:400
  73.5 1.5 %collective-permute-done.14.refs_2_ = s32[16]{0:T(128)S(1)} collective-permute-done((s32[16]{0:T(128)S(1)}, s32[16]{0:T(128)S(1)}, u32[]{:S(2)}, u32[]{:S(2)}) %collective-permute-start.14) | collective-permute-done | bytes 96 | tf_op jit(solution)/shard_map/ppermute | solution.py:400
  75.0 3.9 %collective-permute-start.13 = (s32[16]{0:T(128)S(1)}, s32[16]{0:T(128)S(1)}, u32[]{:S(2)}, u32[]{:S(2)}) collective-permute-start(s32[16]{0:T(128)S(1)} %pad_add_fusion.refs_0_), channel_id=1, source_target_pairs={{0,8},{4,12},{8,16},{12,20},{16,24},{20,28},{24,0},{28,4},{1,9},{5... | collective-permute-start | bytes 200 | tf_op jit(solution)/shard_map/ppermute | solution.py:400
  78.9 1.5 %collective-permute-done.13.refs_1_ = s32[16]{0:T(128)S(1)} collective-permute-done((s32[16]{0:T(128)S(1)}, s32[16]{0:T(128)S(1)}, u32[]{:S(2)}, u32[]{:S(2)}) %collective-permute-start.13) | collective-permute-done | bytes 96 | tf_op jit(solution)/shard_map/ppermute | solution.py:400
  80.3 1.5 %collective-permute-start.18 = (bf16[576,128]{1,0:T(8,128)(2,1)S(1)}, bf16[576,128]{1,0:T(8,128)(2,1)S(1)}, u32[]{:S(2)}, u32[]{:S(2)}) collective-permute-start(bf16[576,128]{1,0:T(8,128)(2,1)S(1)} %get-tuple-element.65), channel_id=1, source_target_pairs={{0,24},{4,28},{8,0},{12,4},{16,8},{20,12},{24,16},{28,20},{1,25},{... | collective-permute-start | bytes 442376 | tf_op jit(solution)/shard_map/ppermute | solution.py:399
  81.8 1.5 %collective-permute-start.24 = (bf16[256,1024]{1,0:T(8,128)(2,1)}, bf16[256,1024]{1,0:T(8,128)(2,1)S(1)}, u32[]{:S(2)}, u32[]{:S(2)}) collective-permute-start(bf16[256,1024]{1,0:T(8,128)(2,1)} %get-tuple-element.74), channel_id=1, source_target_pairs={{0,2},{1,3},{2,0},{3,1},{4,6},{5,7},{6,4},{7,5},{8,10},{9,11},{10,... | collective-permute-start | bytes 1572872 | tf_op jit(solution)/shard_map/ppermute | solution.py:387
  83.3 2.5 %collective-permute-start.6 = (bf16[512,256]{1,0:T(8,128)(2,1)S(1)}, bf16[512,256]{1,0:T(8,128)(2,1)S(1)}, u32[]{:S(2)}, u32[]{:S(2)}) collective-permute-start(bf16[512,256]{1,0:T(8,128)(2,1)S(1)} %collective-permute-done.2.kv_ref), channel_id=1, source_target_pairs={{0,8},{4,12},{8,16},{12,20},{16,24},{20,28},{1,9},{5,13},{9,17},{1... | collective-permute-start | bytes 786440 | tf_op jit(solution)/shard_map/ppermute | solution.py:410
  85.8 0.1 collective-permute-start.25
  85.9 2.5 %shard_map.103.table_ref = s32[18]{0:T(128)S(1)} custom-call(s32[1]{0:T(128)} %bitcast.pair_ref, s32[16]{0:T(128)S(1)} %pad_add_fusion.refs_0_, s32[16]{0:T(128)S(1)} %collective-permute-done.13.refs_1_, s32[16]{0:T(128)S(1)} %collective-permute-done.14.refs_2_, s32[16]{0:T(128)S(1)} %collective-permute-done.15.refs_3_), custom_call_target="tpu_custom_call" | custom-call | tf_op jit(solution)/shard_map/pallas_call | solution.py:172
  88.4 1.0 shard_map.104
  89.4 1.6 %collective-permute-start.19 = (bf16[256,128]{1,0:T(8,128)(2,1)S(1)}, bf16[256,128]{1,0:T(8,128)(2,1)S(1)}, u32[]{:S(2)}, u32[]{:S(2)}) collective-permute-start(bf16[256,128]{1,0:T(8,128)(2,1)S(1)} %get-tuple-element.67), channel_id=1, source_target_pairs={{0,4},{4,0},{8,12},{12,8},{16,20},{20,16},{24,28},{28,24},{1,5},{5... | collective-permute-start | bytes 196616 | tf_op jit(solution)/shard_map/ppermute | solution.py:418
  91.0 0.7 shard_map.97
  91.8 1.2 %shard_map.98 = (f32[512,128]{1,0:T(8,128)S(1)}, f32[512,128]{1,0:T(8,128)S(1)}, f32[512,128]{1,0:T(8,128)S(1)}) custom-call(s32[1]{0:T(128)} %bitcast.pair_ref, bf16[512,128]{1,0:T(8,128)(2,1)S(1)} %get-tuple-element.79.q_ref, bf16[512,256]{1,0:T(8,128)(2,1)} %collective-permute-done.1.kv_ref, f32[512,128]{1,0:T(8,128)S(1)} %get-tuple-element.46.refs_0_, ...), custom_call_target="tpu_custom_call" | custom-call | tf_op jit(solution)/shard_map/pallas_call | solution.py:303
  93.0 1.1 collective-permute-done.19
  94.2 0.7 collective-permute-start.22
  94.8 0.3 shard_map.99
  95.1 0.9 collective-permute-start.21
  96.0 0.2 shard_map.100
  96.2 0.5 collective-permute-start.20
  96.8 0.1 collective-permute-done.24.refs_10_
  96.9 1.5 %collective-permute-start.7 = (bf16[256,128]{1,0:T(8,128)(2,1)S(1)}, bf16[256,128]{1,0:T(8,128)(2,1)S(1)}, u32[]{:S(2)}, u32[]{:S(2)}) collective-permute-start(bf16[256,128]{1,0:T(8,128)(2,1)S(1)} %get-tuple-element.81), channel_id=1, source_target_pairs={{0,4},{4,0},{8,12},{12,8},{16,20},{20,16},{24,28},{28,24},{1,5},{5... | collective-permute-start | bytes 196616 | tf_op jit(solution)/shard_map/ppermute | solution.py:414
  98.4 8.1 %collective-permute-done.25.refs_11_ = bf16[256,1024]{1,0:T(8,128)(2,1)S(1)} collective-permute-done((bf16[256,1024]{1,0:T(8,128)(2,1)}, bf16[256,1024]{1,0:T(8,128)(2,1)S(1)}, u32[]{:S(2)}, u32[]{:S(2)}) %collective-permute-start.25) | collective-permute-done | bytes 524320 | tf_op jit(solution)/shard_map/ppermute | solution.py:387
  106.5 1.3 %collective-permute-done.22.refs_3_ = bf16[256,256]{1,0:T(8,128)(2,1)S(1)} collective-permute-done((bf16[256,256]{1,0:T(8,128)(2,1)S(1)}, bf16[256,256]{1,0:T(8,128)(2,1)S(1)}, u32[]{:S(2)}, u32[]{:S(2)}) %collective-permute-start.22) | collective-permute-done | bytes 131104 | tf_op jit(solution)/shard_map/ppermute | solution.py:421
  107.8 2.4 %collective-permute-done.21.refs_2_ = bf16[256,256]{1,0:T(8,128)(2,1)S(1)} collective-permute-done((bf16[256,256]{1,0:T(8,128)(2,1)S(1)}, bf16[256,256]{1,0:T(8,128)(2,1)S(1)}, u32[]{:S(2)}, u32[]{:S(2)}) %collective-permute-start.21) | collective-permute-done | bytes 131104 | tf_op jit(solution)/shard_map/ppermute | solution.py:421
  110.2 0.0 collective-permute-done.20.refs_1_
  110.2 3.6 %shard_map.105 = bf16[256,2048]{1,0:T(8,128)(2,1)} custom-call(bf16[256,256]{1,0:T(8,128)(2,1)S(1)} %maximum_select_fusion.2.refs_0_, bf16[256,256]{1,0:T(8,128)(2,1)S(1)} %collective-permute-done.20.refs_1_, bf16[256,256]{1,0:T(8,128)(2,1)S(1)} %collective-permute-done.21.refs_2_, bf16[256,256]{1,0:T(8,128)(2,1)S(1)} %collective-permute-done.22.refs_3_, ...), custom_call_target="tpu_custom_call" | custom-call | tf_op jit(solution)/shard_map/pallas_call | solution.py:331
  113.8 0.0 collective-permute-done.7
  113.8 0.7 maximum_select_fusion.1
  (22 shorter events, 0.1 us)
Async XLA Ops:
  0.6 22.8 %copy-start.7 = (s32[8]{0:T(128)S(1)}, s32[8]{0:T(128)}, u32[]{:S(2)}) copy-start(s32[8]{0:T(128)} %own_ref.1) | copy-start | bytes 100
  3.3 9.5 %collective-permute-start = (bf16[4,256,128]{2,1,0:T(8,128)(2,1)}, bf16[4,256,128]{2,1,0:T(8,128)(2,1)S(1)}, u32[]{:S(2)}, u32[]{:S(2)}) collective-permute-start(bf16[4,256,128]{2,1,0:T(8,128)(2,1)} %get-tuple-element.40), channel_id=1, source_target_pairs={{0,4},{4,0},{8,12},{12,8},{16,20},{20,16},{24,28},{28,24},{1,5},{5... | collective-permute-start | bytes 786440 | tf_op jit(solution)/shard_map/ppermute | solution.py:374
  14.8 20.4 %collective-permute-start.12 = (bf16[512,128]{1,0:T(8,128)(2,1)S(1)}, bf16[512,128]{1,0:T(8,128)(2,1)S(1)}, u32[]{:S(2)}, u32[]{:S(2)}) collective-permute-start(bf16[512,128]{1,0:T(8,128)(2,1)S(1)} %get-tuple-element.76.refs_0_), channel_id=1, source_target_pairs={{0,24},{4,28},{8,0},{12,4},{16,8},{20,12},{24,16},{28,20},{1,25},{... | collective-permute-start | bytes 393224 | tf_op jit(solution)/shard_map/ppermute | solution.py:394
  18.6 16.6 %collective-permute-start.11 = (bf16[512,128]{1,0:T(8,128)(2,1)S(1)}, bf16[512,128]{1,0:T(8,128)(2,1)S(1)}, u32[]{:S(2)}, u32[]{:S(2)}) collective-permute-start(bf16[512,128]{1,0:T(8,128)(2,1)S(1)} %get-tuple-element.76.refs_0_), channel_id=1, source_target_pairs={{0,16},{4,20},{8,24},{12,28},{16,0},{20,4},{24,8},{28,12},{1,17},{... | collective-permute-start | bytes 393224 | tf_op jit(solution)/shard_map/ppermute | solution.py:394
  20.8 30.3 %copy-start = (bf16[2,8,128,128]{3,2,1,0:T(8,128)(2,1)S(1)}, bf16[2,8,128,128]{3,2,1,0:T(8,128)(2,1)}, u32[]{:S(2)}) copy-start(bf16[2,8,128,128]{3,2,1,0:T(8,128)(2,1)} %get-tuple-element.55.kv_own) | copy-start | bytes 1572868
  20.8 30.1 %collective-permute-start.9 = (bf16[2,8,128,128]{3,2,1,0:T(8,128)(2,1)}, bf16[2,8,128,128]{3,2,1,0:T(8,128)(2,1)S(1)}, u32[]{:S(2)}, u32[]{:S(2)}) collective-permute-start(bf16[2,8,128,128]{3,2,1,0:T(8,128)(2,1)} %get-tuple-element.56), channel_id=1, source_target_pairs={{0,4},{4,0},{8,12},{12,8},{16,20},{20,16},{24,28},{28,24},{1,5},{5... | collective-permute-start | bytes 1572872 | tf_op jit(solution)/shard_map/ppermute | solution.py:382
  22.4 15.0 %collective-permute-start.10 = (bf16[512,128]{1,0:T(8,128)(2,1)S(1)}, bf16[512,128]{1,0:T(8,128)(2,1)S(1)}, u32[]{:S(2)}, u32[]{:S(2)}) collective-permute-start(bf16[512,128]{1,0:T(8,128)(2,1)S(1)} %get-tuple-element.76.refs_0_), channel_id=1, source_target_pairs={{0,8},{4,12},{8,16},{12,20},{16,24},{20,28},{24,0},{28,4},{1,9},{5... | collective-permute-start | bytes 393224 | tf_op jit(solution)/shard_map/ppermute | solution.py:394
  23.4 10.3 %collective-permute-start.8 = (s32[8]{0:T(128)S(1)}, s32[8]{0:T(128)S(1)}, u32[]{:S(2)}, u32[]{:S(2)}) collective-permute-start(s32[8]{0:T(128)S(1)} %copy-done.7), channel_id=1, source_target_pairs={{0,4},{4,0},{8,12},{12,8},{16,20},{20,16},{24,28},{28,24},{1,5},{5... | collective-permute-start | bytes 104 | tf_op jit(solution)/shard_map/ppermute | solution.py:383
  27.5 82.7 %copy-start.1 = (bf16[256,1024]{1,0:T(8,128)(2,1)S(1)}, bf16[256,1024]{1,0:T(8,128)(2,1)}, u32[]{:S(2)}) copy-start(bf16[256,1024]{1,0:T(8,128)(2,1)} %get-tuple-element.68.refs_4_) | copy-start | bytes 1572868
  27.5 82.7 %copy-start.2 = (bf16[256,1024]{1,0:T(8,128)(2,1)S(1)}, bf16[256,1024]{1,0:T(8,128)(2,1)}, u32[]{:S(2)}) copy-start(bf16[256,1024]{1,0:T(8,128)(2,1)} %get-tuple-element.72.refs_8_) | copy-start | bytes 1572868
  33.7 25.8 %collective-permute-start.4 = (bf16[256,1024]{1,0:T(8,128)(2,1)}, bf16[256,1024]{1,0:T(8,128)(2,1)S(1)}, u32[]{:S(2)}, u32[]{:S(2)}) collective-permute-start(bf16[256,1024]{1,0:T(8,128)(2,1)} %get-tuple-element.43), channel_id=1, source_target_pairs={{0,2},{1,3},{2,0},{3,1},{4,6},{5,7},{6,4},{7,5},{8,10},{9,11},{10,... | collective-permute-start | bytes 1572872 | tf_op jit(solution)/shard_map/ppermute | solution.py:377
  35.2 26.8 %collective-permute-start.5 = (bf16[256,1024]{1,0:T(8,128)(2,1)}, bf16[256,1024]{1,0:T(8,128)(2,1)}, u32[]{:S(2)}, u32[]{:S(2)}) collective-permute-start(bf16[256,1024]{1,0:T(8,128)(2,1)} %get-tuple-element.44), channel_id=1, source_target_pairs={{0,3},{1,2},{2,1},{3,0},{4,7},{5,6},{6,5},{7,4},{8,11},{9,10},{10,... | collective-permute-start | bytes 1572872 | tf_op jit(solution)/shard_map/ppermute | solution.py:377
  35.2 0.6 copy-start.3
  35.8 26.2 %collective-permute-start.3 = (bf16[256,1024]{1,0:T(8,128)(2,1)}, bf16[256,1024]{1,0:T(8,128)(2,1)}, u32[]{:S(2)}, u32[]{:S(2)}) collective-permute-start(bf16[256,1024]{1,0:T(8,128)(2,1)} %get-tuple-element.42), channel_id=1, source_target_pairs={{0,1},{1,0},{2,3},{3,2},{4,5},{5,4},{6,7},{7,6},{8,9},{9,8},{10,11... | collective-permute-start | bytes 1572872 | tf_op jit(solution)/shard_map/ppermute | solution.py:387
  37.4 0.7 copy-start.5
  38.1 8.3 %collective-permute-start.1 = (bf16[512,256]{1,0:T(8,128)(2,1)S(1)}, bf16[512,256]{1,0:T(8,128)(2,1)}, u32[]{:S(2)}, u32[]{:S(2)}) collective-permute-start(bf16[512,256]{1,0:T(8,128)(2,1)S(1)} %pad_maximum_fusion.kv_ref), channel_id=1, source_target_pairs={{0,8},{4,12},{8,16},{12,20},{16,24},{20,28},{1,9},{5,13},{9,17},{1... | collective-permute-start | bytes 786440 | tf_op jit(solution)/shard_map/ppermute | solution.py:410
  46.4 35.4 %collective-permute-start.2 = (bf16[512,256]{1,0:T(8,128)(2,1)}, bf16[512,256]{1,0:T(8,128)(2,1)S(1)}, u32[]{:S(2)}, u32[]{:S(2)}) collective-permute-start(bf16[512,256]{1,0:T(8,128)(2,1)} %collective-permute-done.1.kv_ref), channel_id=1, source_target_pairs={{0,8},{4,12},{8,16},{12,20},{16,24},{20,28},{1,9},{5,13},{9,17},{1... | collective-permute-start | bytes 786440 | tf_op jit(solution)/shard_map/ppermute | solution.py:410
  50.9 45.3 %collective-permute-start.23 = (bf16[256,1024]{1,0:T(8,128)(2,1)}, bf16[256,1024]{1,0:T(8,128)(2,1)}, u32[]{:S(2)}, u32[]{:S(2)}) collective-permute-start(bf16[256,1024]{1,0:T(8,128)(2,1)} %get-tuple-element.73), channel_id=1, source_target_pairs={{0,1},{1,0},{2,3},{3,2},{4,5},{5,4},{6,7},{7,6},{8,9},{9,8},{10,11... | collective-permute-start | bytes 1572872 | tf_op jit(solution)/shard_map/ppermute | solution.py:387
  51.1 0.9 copy-start.4
  52.0 0.9 copy-start.6
  59.5 23.9 %collective-permute-start.16 = (bf16[576,128]{1,0:T(8,128)(2,1)S(1)}, bf16[576,128]{1,0:T(8,128)(2,1)S(1)}, u32[]{:S(2)}, u32[]{:S(2)}) collective-permute-start(bf16[576,128]{1,0:T(8,128)(2,1)S(1)} %get-tuple-element.63), channel_id=1, source_target_pairs={{0,8},{4,12},{8,16},{12,20},{16,24},{20,28},{24,0},{28,4},{1,9},{5... | collective-permute-start | bytes 442376 | tf_op jit(solution)/shard_map/ppermute | solution.py:399
  62.0 23.8 %collective-permute-start.17 = (bf16[576,128]{1,0:T(8,128)(2,1)S(1)}, bf16[576,128]{1,0:T(8,128)(2,1)S(1)}, u32[]{:S(2)}, u32[]{:S(2)}) collective-permute-start(bf16[576,128]{1,0:T(8,128)(2,1)S(1)} %get-tuple-element.64), channel_id=1, source_target_pairs={{0,16},{4,20},{8,24},{12,28},{16,0},{20,4},{24,8},{28,12},{1,17},{... | collective-permute-start | bytes 442376 | tf_op jit(solution)/shard_map/ppermute | solution.py:399
  62.0 7.0 %collective-permute-start.15 = (s32[16]{0:T(128)S(1)}, s32[16]{0:T(128)S(1)}, u32[]{:S(2)}, u32[]{:S(2)}) collective-permute-start(s32[16]{0:T(128)S(1)} %pad_add_fusion.refs_0_), channel_id=1, source_target_pairs={{0,24},{4,28},{8,0},{12,4},{16,8},{20,12},{24,16},{28,20},{1,25},{... | collective-permute-start | bytes 200 | tf_op jit(solution)/shard_map/ppermute | solution.py:400
  69.0 6.0 %collective-permute-start.14 = (s32[16]{0:T(128)S(1)}, s32[16]{0:T(128)S(1)}, u32[]{:S(2)}, u32[]{:S(2)}) collective-permute-start(s32[16]{0:T(128)S(1)} %pad_add_fusion.refs_0_), channel_id=1, source_target_pairs={{0,16},{4,20},{8,24},{12,28},{16,0},{20,4},{24,8},{28,12},{1,17},{... | collective-permute-start | bytes 200 | tf_op jit(solution)/shard_map/ppermute | solution.py:400
  75.0 5.3 %collective-permute-start.13 = (s32[16]{0:T(128)S(1)}, s32[16]{0:T(128)S(1)}, u32[]{:S(2)}, u32[]{:S(2)}) collective-permute-start(s32[16]{0:T(128)S(1)} %pad_add_fusion.refs_0_), channel_id=1, source_target_pairs={{0,8},{4,12},{8,16},{12,20},{16,24},{20,28},{24,0},{28,4},{1,9},{5... | collective-permute-start | bytes 200 | tf_op jit(solution)/shard_map/ppermute | solution.py:400
  80.3 8.1 %collective-permute-start.18 = (bf16[576,128]{1,0:T(8,128)(2,1)S(1)}, bf16[576,128]{1,0:T(8,128)(2,1)S(1)}, u32[]{:S(2)}, u32[]{:S(2)}) collective-permute-start(bf16[576,128]{1,0:T(8,128)(2,1)S(1)} %get-tuple-element.65), channel_id=1, source_target_pairs={{0,24},{4,28},{8,0},{12,4},{16,8},{20,12},{24,16},{28,20},{1,25},{... | collective-permute-start | bytes 442376 | tf_op jit(solution)/shard_map/ppermute | solution.py:399
  81.8 15.1 %collective-permute-start.24 = (bf16[256,1024]{1,0:T(8,128)(2,1)}, bf16[256,1024]{1,0:T(8,128)(2,1)S(1)}, u32[]{:S(2)}, u32[]{:S(2)}) collective-permute-start(bf16[256,1024]{1,0:T(8,128)(2,1)} %get-tuple-element.74), channel_id=1, source_target_pairs={{0,2},{1,3},{2,0},{3,1},{4,6},{5,7},{6,4},{7,5},{8,10},{9,11},{10,... | collective-permute-start | bytes 1572872 | tf_op jit(solution)/shard_map/ppermute | solution.py:387
  83.3 11.8 %collective-permute-start.6 = (bf16[512,256]{1,0:T(8,128)(2,1)S(1)}, bf16[512,256]{1,0:T(8,128)(2,1)S(1)}, u32[]{:S(2)}, u32[]{:S(2)}) collective-permute-start(bf16[512,256]{1,0:T(8,128)(2,1)S(1)} %collective-permute-done.2.kv_ref), channel_id=1, source_target_pairs={{0,8},{4,12},{8,16},{12,20},{16,24},{20,28},{1,9},{5,13},{9,17},{1... | collective-permute-start | bytes 786440 | tf_op jit(solution)/shard_map/ppermute | solution.py:410
  85.8 20.7 %collective-permute-start.25 = (bf16[256,1024]{1,0:T(8,128)(2,1)}, bf16[256,1024]{1,0:T(8,128)(2,1)S(1)}, u32[]{:S(2)}, u32[]{:S(2)}) collective-permute-start(bf16[256,1024]{1,0:T(8,128)(2,1)} %get-tuple-element.75), channel_id=1, source_target_pairs={{0,3},{1,2},{2,1},{3,0},{4,7},{5,6},{6,5},{7,4},{8,11},{9,10},{10,... | collective-permute-start | bytes 1572872 | tf_op jit(solution)/shard_map/ppermute | solution.py:387
  89.4 4.7 %collective-permute-start.19 = (bf16[256,128]{1,0:T(8,128)(2,1)S(1)}, bf16[256,128]{1,0:T(8,128)(2,1)S(1)}, u32[]{:S(2)}, u32[]{:S(2)}) collective-permute-start(bf16[256,128]{1,0:T(8,128)(2,1)S(1)} %get-tuple-element.67), channel_id=1, source_target_pairs={{0,4},{4,0},{8,12},{12,8},{16,20},{20,16},{24,28},{28,24},{1,5},{5... | collective-permute-start | bytes 196616 | tf_op jit(solution)/shard_map/ppermute | solution.py:418
  94.2 13.6 %collective-permute-start.22 = (bf16[256,256]{1,0:T(8,128)(2,1)S(1)}, bf16[256,256]{1,0:T(8,128)(2,1)S(1)}, u32[]{:S(2)}, u32[]{:S(2)}) collective-permute-start(bf16[256,256]{1,0:T(8,128)(2,1)S(1)} %maximum_select_fusion.2.refs_0_), channel_id=1, source_target_pairs={{0,3},{1,2},{2,1},{3,0},{4,7},{5,6},{6,5},{7,4},{8,11},{9,10},{10,... | collective-permute-start | bytes 393224 | tf_op jit(solution)/shard_map/ppermute | solution.py:421
  95.1 15.1 %collective-permute-start.21 = (bf16[256,256]{1,0:T(8,128)(2,1)S(1)}, bf16[256,256]{1,0:T(8,128)(2,1)S(1)}, u32[]{:S(2)}, u32[]{:S(2)}) collective-permute-start(bf16[256,256]{1,0:T(8,128)(2,1)S(1)} %maximum_select_fusion.2.refs_0_), channel_id=1, source_target_pairs={{0,2},{1,3},{2,0},{3,1},{4,6},{5,7},{6,4},{7,5},{8,10},{9,11},{10,... | collective-permute-start | bytes 393224 | tf_op jit(solution)/shard_map/ppermute | solution.py:421
  96.2 13.9 %collective-permute-start.20 = (bf16[256,256]{1,0:T(8,128)(2,1)S(1)}, bf16[256,256]{1,0:T(8,128)(2,1)S(1)}, u32[]{:S(2)}, u32[]{:S(2)}) collective-permute-start(bf16[256,256]{1,0:T(8,128)(2,1)S(1)} %maximum_select_fusion.2.refs_0_), channel_id=1, source_target_pairs={{0,1},{1,0},{2,3},{3,2},{4,5},{5,4},{6,7},{7,6},{8,9},{9,8},{10,11... | collective-permute-start | bytes 393224 | tf_op jit(solution)/shard_map/ppermute | solution.py:421
  96.9 16.9 %collective-permute-start.7 = (bf16[256,128]{1,0:T(8,128)(2,1)S(1)}, bf16[256,128]{1,0:T(8,128)(2,1)S(1)}, u32[]{:S(2)}, u32[]{:S(2)}) collective-permute-start(bf16[256,128]{1,0:T(8,128)(2,1)S(1)} %get-tuple-element.81), channel_id=1, source_target_pairs={{0,4},{4,0},{8,12},{12,8},{16,20},{20,16},{24,28},{28,24},{1,5},{5... | collective-permute-start | bytes 196616 | tf_op jit(solution)/shard_map/ppermute | solution.py:414

commit v5 on v1

v5 whole, which is shorter than its diff:
```python
import functools
import math

import jax
import jax.numpy as jnp
from jax import lax
from jax.experimental import pallas as pl
from jax.experimental.pallas import tpu as pltpu
from jax.sharding import PartitionSpec as P

HD = 128
BLOCK = 64
LEAD = 16
WINDOW = BLOCK + LEAD
ENTRY = WINDOW + LEAD
NEGATIVE = -1e30
SCALE = HD ** -0.5 * math.log2(math.e)
VMEM = pl.BlockSpec(memory_space=pltpu.VMEM)
SMEM = pl.BlockSpec(memory_space=pltpu.SMEM)
ANY = pl.BlockSpec(memory_space=pl.ANY)
PARAMS = pltpu.CompilerParams(vmem_limit_bytes=16 * 1024 * 1024)


def dot(a, b):
    return jnp.dot(a, b, preferred_element_type=jnp.float32)


def dot_t(a, b):
    return lax.dot_general(a, b, (((1,), (1,)), ((), ())), preferred_element_type=jnp.float32)


def fetch(pieces, sems):
    copies = [
        pltpu.make_async_copy(source, target, sems.at[at])
        for at, (source, target) in enumerate(pieces)
    ]
    for copy in copies:
        copy.start()
    for copy in copies:
        copy.wait()


def cut_kernel(plan, side_ref, tp_ref, *refs):
    sems, refs = refs[-1], refs[:-1]
    sources, outs = refs[: len(refs) - len(plan)], refs[len(refs) - len(plan) :]
    pieces = []
    for out, parts in zip(outs, plan):
        for at, (index, step, total, offset, width, depth) in enumerate(parts):
            source = sources[index]
            key = tp_ref[0] if total else side_ref[0]
            lane = pl.multiple_of((key ^ step) * (total or HD) + offset, HD)
            row = pl.multiple_of(side_ref[0] * depth, LEAD) if depth < source.shape[0] else 0
            piece = source.at[pl.ds(row, depth), pl.ds(lane, width)]
            pieces.append((piece, out.at[at] if len(parts) > 1 else out))
    fetch(pieces, sems)


def cut(side, tp, sources, plan):
    shapes = []
    for parts in plan:
        stack = (len(parts),) if len(parts) > 1 else ()
        shape = stack + (parts[0][5], parts[0][4])
        shapes.append(jax.ShapeDtypeStruct(shape, sources[parts[0][0]].dtype))
    return pl.pallas_call(
        functools.partial(cut_kernel, plan),
        out_shape=tuple(shapes),
        in_specs=[SMEM] * 2 + [ANY] * len(sources),
        out_specs=(VMEM,) * len(plan),
        scratch_shapes=[pltpu.SemaphoreType.DMA((sum(len(parts) for parts in plan),))],
    )(side, tp, *sources)


def place_of(slots_ref, ctx, holder, count):
    place = jnp.int32(0)
    for n in range(count):
        slot = slots_ref[holder * count + n]
        place = jnp.where(slot // count == ctx, slot - ctx * count, place)
    return place


def ask_kernel(ctx_ref, slots_ref, queries_ref, spill_ref, out_ref, all_ref):
    rows = queries_ref.shape[0]
    all_ref[:rows, :] = queries_ref[...]
    all_ref[rows:, :] = spill_ref[...]
    holders = out_ref.shape[0]
    count = 2 * rows // BLOCK

    def send(holder, carry):
        block = place_of(slots_ref, ctx_ref[0], holder, count) // 2
        start = pl.multiple_of(block * BLOCK + BLOCK - LEAD, LEAD)
        out_ref[holder] = all_ref[pl.ds(start, WINDOW), :]
        return carry

    lax.fori_loop(0, holders, send, 0, unroll=min(holders, 8))


def ask(ctx, slots, queries, spill):
    rows, width = queries.shape
    holders = slots.shape[0] * BLOCK // (2 * rows)
    return pl.pallas_call(
        ask_kernel,
        out_shape=jax.ShapeDtypeStruct((holders, WINDOW, width), queries.dtype),
        in_specs=[SMEM, SMEM, VMEM, VMEM],
        out_specs=VMEM,
        scratch_shapes=[pltpu.VMEM((rows + BLOCK, width), queries.dtype)],
        compiler_params=PARAMS,
    )(ctx, slots, queries, spill)


def hold_kernel(slot_ref, asked_ref, keys_ref, values_ref, out_ref):
    count = slot_ref.shape[0]
    width = asked_ref.shape[2]
    row = lax.broadcasted_iota(jnp.int32, (LEAD, WINDOW), 0)

    def answer(owner, carry):
        held = jnp.int32(0)
        for n in range(count):
            held = jnp.where(slot_ref[n] // count == owner, n, held)
        for head in range(width // HD):
            feats = slice(head * HD, (head + 1) * HD)
            s = dot_t(keys_ref[held, :, feats], asked_ref[owner, :, feats])
            peak = jnp.max(s, axis=0, keepdims=True).astype(jnp.bfloat16).astype(jnp.float32)
            p = jnp.exp2((s - peak) * SCALE)
            total = jnp.sum(p, axis=0, keepdims=True)
            mixed = lax.dot_general(
                p.astype(jnp.bfloat16),
                values_ref[held, :, feats],
                (((0,), (0,)), ((), ())),
                preferred_element_type=jnp.float32,
            )
            high = total.astype(jnp.bfloat16).astype(jnp.float32)
            stats = jnp.where(row == 0, peak, jnp.where(row == 1, high, total - high))
            out_ref[owner, :WINDOW, feats] = mixed.astype(jnp.bfloat16)
            out_ref[owner, WINDOW:, head * HD : head * HD + WINDOW] = stats.astype(jnp.bfloat16)
        return carry

    owners = out_ref.shape[0]
    lax.fori_loop(0, owners, answer, 0, unroll=min(owners, 8))


def hold(slots, asked, keys, values):
    owners, _, width = asked.shape
    return pl.pallas_call(
        hold_kernel,
        out_shape=jax.ShapeDtypeStruct((owners, ENTRY, width), asked.dtype),
        in_specs=[SMEM] + [VMEM] * 3,
        out_specs=VMEM,
        compiler_params=PARAMS,
    )(slots, asked, keys, values)


def combine_kernel(ctx_ref, slots_ref, parts_ref, out_ref, next_ref, factor_ref, source_ref):
    rows, width = out_ref.shape
    blocks = rows // BLOCK
    holders = parts_ref.shape[0]
    for holder in range(holders):
        for n in range(2 * blocks):
            slot = slots_ref[holder * 2 * blocks + n]

            @pl.when(slot // (2 * blocks) == ctx_ref[0])
            def _():
                source_ref[slot - ctx_ref[0] * 2 * blocks] = holder

    heads = width // HD
    for block in range(blocks):
        held = [source_ref[2 * block], source_ref[2 * block + 1]]
        for head in range(heads):
            feats = slice(head * HD, (head + 1) * HD)
            one, two = (parts_ref[h, WINDOW:, feats].astype(jnp.float32) for h in held)
            peak = jnp.maximum(one[0:1], two[0:1])
            weights = [jnp.exp2((part[0:1] - peak) * SCALE) for part in (one, two)]
            sums = [part[1:2] + part[2:3] for part in (one, two)]
            total = weights[0] * sums[0] + weights[1] * sums[1]
            for at in range(2):
                place = (block * heads + head) * 2 + at
                factor_ref[place : place + 1, :] = weights[at] / total
    factors = factor_ref[...].T
    row = lax.broadcasted_iota(jnp.int32, (LEAD, HD), 0)
    for head in range(heads):
        feats = slice(head * HD, (head + 1) * HD)
        before = jnp.zeros((WINDOW, HD), jnp.bfloat16)
        for block in range(blocks):
            place = (block * heads + head) * 2
            first, second = source_ref[2 * block], source_ref[2 * block + 1]
            now = parts_ref[first, :WINDOW, feats].astype(jnp.float32)
            now = now * factors[:WINDOW, place : place + 1]
            then = parts_ref[second, :WINDOW, feats].astype(jnp.float32)
            now = now + then * factors[:WINDOW, place + 1 : place + 2]
            now = now.astype(jnp.bfloat16)
            top = block * BLOCK
            out_ref[top : top + BLOCK - LEAD, feats] = before[LEAD:BLOCK]
            out_ref[top + BLOCK - LEAD : top + BLOCK, feats] = jnp.where(
                row == LEAD - 1, now[:LEAD], before[BLOCK:]
            )
            before = now
        next_ref[:, feats] = before[LEAD:]


def combine(ctx, slots, parts, rows):
    width = parts.shape[2]
    return pl.pallas_call(
        combine_kernel,
        out_shape=(
            jax.ShapeDtypeStruct((rows, width), parts.dtype),
            jax.ShapeDtypeStruct((BLOCK, width), parts.dtype),
        ),
        in_specs=[SMEM, SMEM, VMEM],
        out_specs=(VMEM, VMEM),
        scratch_shapes=[
            pltpu.VMEM((HD, HD), jnp.float32),
            pltpu.SMEM((2 * rows // BLOCK,), jnp.int32),
        ],
        compiler_params=PARAMS,
    )(ctx, slots, parts)


def self_kernel(first, last, step, pair_ref, q_ref, kv_ref, *refs):
    if not first:
        peak_in, total_in, accum_in = refs[:3]
        refs = refs[3:]
    rows = q_ref.shape[0]
    tile = rows // 2
    for part in range(2):
        at = pl.ds(part * tile, tile)

        def emit(peak, total, accum):
            if last:
                refs[0][at, :] = (accum / total).astype(jnp.bfloat16)
            else:
                refs[0][at, :] = jnp.broadcast_to(peak, (tile, HD))
                refs[1][at, :] = jnp.broadcast_to(total, (tile, HD))
                refs[2][at, :] = accum

        def work():
            q = q_ref[at, :]
            count = (part + 1) * tile if first else rows
            s = dot_t(q, kv_ref[:count, :HD])
            if first:
                row = lax.broadcasted_iota(jnp.int32, (tile, count), 0) + part * tile
                col = lax.broadcasted_iota(jnp.int32, (tile, count), 1)
                s = jnp.where(col <= row, s, NEGATIVE)
            peak = jnp.max(s, axis=1, keepdims=True)
            if not first:
                old = peak_in[at, :1]
                peak = jnp.maximum(peak, old)
                factor = jnp.exp2((old - peak) * SCALE)
            p = jnp.exp2((s - peak) * SCALE)
            total = jnp.sum(p, axis=1, keepdims=True)
            accum = dot(p.astype(jnp.bfloat16), kv_ref[:count, HD:])
            if not first:
                total += total_in[at, :1] * factor
                accum += accum_in[at, :] * factor
            emit(peak, total, accum)

        if first:
            work()
        else:
            pl.when(pair_ref[0] >= step)(work)

            @pl.when(pair_ref[0] < step)
            def _():
                emit(peak_in[at, :1], total_in[at, :1], accum_in[at, :])


def self_step(pair, q, kv, state, step, last):
    rows = q.shape[0]
    first = state is None
    held = jax.ShapeDtypeStruct((rows, HD), jnp.float32)
    out_shape = jax.ShapeDtypeStruct((rows, HD), jnp.bfloat16) if last else (held,) * 3
    return pl.pallas_call(
        functools.partial(self_kernel, first, last, step),
        out_shape=out_shape,
        in_specs=[SMEM] + [VMEM] * (2 if first else 5),
        out_specs=VMEM if last else (VMEM,) * 3,
        compiler_params=PARAMS,
    )(pair, q, kv, *(() if first else state))


def project_kernel(groups, side_ref, *refs):
    crossed_ref = refs[-1]
    terms, near, far = refs[:groups], refs[groups : groups + 2], refs[groups + 2 : -1]
    direct = far[: groups - 2]
    shared = far[groups - 2 : 2 * groups - 4]
    fetched = far[2 * groups - 4 :]
    width = crossed_ref.shape[1]
    depth = terms[0].shape[1]
    half = width // 2
    share = depth // 2
    mine = pl.ds(pl.multiple_of(side_ref[0] * share, HD), share)
    other = pl.ds(pl.multiple_of((1 - side_ref[0]) * share, HD), share)
    tile = min(512, half)
    for column in range(0, width, tile):
        at = slice(column, column + tile)
        total = dot(terms[0][...], near[0][:, at]) + dot(terms[1][...], near[1][:, at])
        for index in range(groups - 2):
            term = terms[index + 2]
            if column < half:
                total += dot(term[:, mine], shared[index][:, at])
                total += dot(term[:, other], fetched[index][:, at])
            else:
                total += dot(term[...], direct[index][:, column - half : column - half + tile])
        crossed_ref[:, at] = total.astype(crossed_ref.dtype)


def project(side, terms, near, direct, shared, fetched):
    rows, width = terms[0].shape[0], near[0].shape[1]
    operands = (*terms, *near, *direct, *shared, *fetched)
    return pl.pallas_call(
        functools.partial(project_kernel, len(terms)),
        out_shape=jax.ShapeDtypeStruct((rows, width), jnp.bfloat16),
        in_specs=[SMEM] + [VMEM] * len(operands),
        out_specs=VMEM,
        compiler_params=PARAMS,
    )(side, *operands)


def shards(queries, keys, values, cross_queries, nbr_keys, nbr_values, nbr_slot, w_cross):
    ctx = lax.axis_index("ctx")
    count = lax.axis_size("ctx")
    tp = lax.axis_index("tp").reshape(1)
    groups = lax.axis_size("tp")
    side = (ctx & 1).reshape(1)
    pair = (ctx >> 1).reshape(1)
    left = ctx & 1 == 0
    pairs = count // 2
    rows = queries.shape[0]
    depth = w_cross.shape[0]
    width = w_cross.shape[1] // groups
    swap = [(i, i ^ 1) for i in range(count)]
    across = [[(i, i ^ step) for i in range(groups)] for step in range(groups)]

    def both(mine, other, axis):
        return jnp.where(
            left,
            jnp.concatenate([mine, other], axis),
            jnp.concatenate([other, mine], axis),
        )

    def exchange(value):
        return lax.all_to_all(value, "ctx", split_axis=0, concat_axis=0, tiled=True)

    spill = lax.ppermute(cross_queries[:BLOCK], "ctx", [(i + 1, i) for i in range(count - 1)])
    slots = exchange(jnp.broadcast_to(nbr_slot, (count,) + nbr_slot.shape)).reshape(-1)
    half = width // 2
    far = range(2, groups)
    away, mine, *blocks = cut(
        side, tp, (queries, keys, values, w_cross),
        [[(at, 1 - own, 0, 0, HD, rows) for at in range(3)] for own in range(2)]
        + [[(3, step, width, 0, half, depth // 2)] for step in far],
    )
    other = lax.ppermute(away, "ctx", swap)
    shared = [lax.ppermute(block, "tp", across[step]) for step, block in zip(far, blocks)]
    own, beside, *blocks = cut(
        side, tp, (w_cross,),
        [[(0, step, width, 0, width, depth)] for step in range(2)]
        + [[(0, step, width, half, half, depth)] for step in far],
    )
    near = [own, lax.ppermute(beside, "tp", across[1])]
    direct = [lax.ppermute(block, "tp", across[step]) for step, block in zip(far, blocks)]

    asked = exchange(ask(ctx.reshape(1), slots, cross_queries, spill))
    asked, shared = lax.optimization_barrier((asked, shared))
    fetched = [lax.ppermute(block, "ctx", swap) for block in shared]
    parts = exchange(hold(nbr_slot, asked, nbr_keys, nbr_values))
    parts, fetched = lax.optimization_barrier((parts, fetched))

    joint = both(mine, other, 1)
    q = joint[0]
    kv = jnp.concatenate([joint[1], joint[2]], axis=1)
    forward = [(i, i + 2) for i in range(count - 2)]
    state = None
    for step in range(pairs):
        if step == pairs - 1:
            kv, direct = lax.optimization_barrier((kv, direct))
        following = lax.ppermute(kv, "ctx", forward) if step < pairs - 1 else None
        state = self_step(pair, q, kv, state, step, step == pairs - 1)
        kv = following
    ours = jnp.where(left, state[:rows], state[rows:])
    theirs = lax.ppermute(jnp.where(left, state[rows:], state[:rows]), "ctx", swap)
    attended = both(ours, theirs, 1)

    answers, onward = combine(ctx.reshape(1), slots, parts, rows)
    back = lax.ppermute(onward, "ctx", [(i, i + 1) for i in range(count - 1)])
    early = jnp.arange(BLOCK)[:, None] < BLOCK - 1
    cca = jnp.concatenate([jnp.where(early, back, answers[:BLOCK]), answers[BLOCK:]], axis=0)
    terms = [cca] + [lax.ppermute(cca, "tp", across[step]) for step in range(1, groups)]
    crossed = project(side, terms, near, direct, shared, fetched)
    return (attended, crossed)


def solution(mesh):
    in_specs = (
        P("ctx", "tp"),
        P("ctx", "tp"),
        P("ctx", "tp"),
        P("ctx", "tp"),
        P("ctx", None, "tp"),
        P("ctx", None, "tp"),
        P("ctx"),
        P("tp", None),
    )
    out_specs = (P("ctx", "tp"), P("ctx", "tp"))
    return jax.shard_map(shards, mesh=mesh, in_specs=in_specs, out_specs=out_specs, check_vma=False)
```

time: 137 us -> 97.1 us (0.71); the launches traced: 134 us -> 95.7 us
  Pallas kernels: 44.6 us -> 22 us
  local copies, waits for them, and re-layouts: 12.6 us -> 1.25 us
  waiting for transfers between devices: 32.6 us -> 24 us
  starting transfers between devices: 39.6 us -> 44.9 us
    pallas_call x3 -> x6, Pallas kernels: 41.2 us -> 17.7 us  [the longest x2 5.78 us: cut(): pl.pallas_call(functools.partial(cut_kernel, plan), out_shape=tuple(shape...]
    ppermute x10 -> x14, waiting for transfers between devices: 24.2 us -> 13.5 us  [the longest x2 7.17 us: shards(): fetched = [lax.ppermute(block, 'ctx', swap) for block in shared]]
    unnamed x8 -> x10, local copies, waits for them, and re-layouts: 4.74 us -> 0.03 us
    dynamic_slice x1 -> x0, local copies, waits for them, and re-layouts: 3.64 us -> none  [shards(): lax.dynamic_slice_in_dim(w_cross, (tp ^ step) * width, width, axis=1)]
    all_to_all x2 -> x3, starting transfers between devices: 10.8 us -> 14.3 us  [exchange(): return lax.all_to_all(value, 'ctx', split_axis=0, concat_axis=0, tiled=True)]
    ppermute x10 -> x14, starting transfers between devices: 12.9 us -> 16.3 us  [the longest x1 3.65 us: shards(): back = lax.ppermute(onward, 'ctx', [(i, i + 1) for i in range(count - 1)])]
    slice x4 -> x2, local copies, waits for them, and re-layouts: 2.96 us -> 0.01 us  [the longest x1 0.01 us: shards(): answers[BLOCK:]]
    ppermute x3, waiting for transfers between devices: 3.16 us -> 5.59 us  [shards(): following = lax.ppermute(kv, 'ctx', forward) if step < pairs - 1 else None]
  transfers between devices with their start and end apart: 15 -> 20, of which waited for: 9 -> 8; matrix products, arithmetic and copies ran while one was open for 8% -> 4% of each run, Pallas kernels for 5% -> 17%
where the time goes in v5:
time: 97.1 us; the launch traced here: 95.7 us
  starting transfers between devices  44.9 us (46%)
  waiting for transfers between devices  24 us (25%)
  Pallas kernels  22 us (23%)
  other arithmetic  2.64 us (3%)
  local copies, waits for them, and re-layouts  1.25 us (1%)
    ppermute x3, starting transfers between devices, shards(): following = lax.ppermute(kv, 'ctx', forward) if step < pairs - 1 else None  14.3 us
    all_to_all x3, starting transfers between devices, exchange(): return lax.all_to_all(value, 'ctx', split_axis=0, concat_axis=0, tiled=True)  14.3 us
    ppermute x2, waiting for transfers between devices, shards(): fetched = [lax.ppermute(block, 'ctx', swap) for block in shared]  7.17 us
    pallas_call x2, Pallas kernels, cut(): pl.pallas_call(functools.partial(cut_kernel, plan), out_shape=tuple(shape...  5.78 us
    ppermute x3, waiting for transfers between devices, shards(): following = lax.ppermute(kv, 'ctx', forward) if step < pairs - 1 else None  5.59 us
    pallas_call x1, Pallas kernels, hold(): pl.pallas_call(hold_kernel, out_shape=jax.ShapeDtypeStruct((owners, ENTRY...  5.07 us
    ppermute x3, waiting for transfers between devices, shards(): lax.ppermute(cca, 'tp', across[step])  4.96 us
    all_to_all x3, waiting for transfers between devices, exchange(): return lax.all_to_all(value, 'ctx', split_axis=0, concat_axis=0, tiled=True)  4.9 us
  transfers between devices with their start and end apart: 20, of which 8 were waited for; matrix products, arithmetic and copies ran while one was open for 4% of the time, Pallas kernels for 17%

profile of v5, /device:TPU:0, one launch (start us, length us, event | category | flops | bytes accessed | tf_op | source)
XLA Modules:
  0.0 95.7 jit_solution(2357696321436853877)
XLA Ops:
  0.6 0.0 copy-start.3
  0.6 0.0 copy-start.4
  0.7 2.3 %shard_map.95 = (bf16[3,256,128]{2,1,0:T(8,128)(2,1)}, bf16[3,256,128]{2,1,0:T(8,128)(2,1)}, bf16[128,1024]{1,0:T(8,128)(2,1)}, bf16[128,1024]{1,0:T(8,128)(2,1)}) custom-call(s32[1]{0:T(128)} %bitcast.1.side_ref, s32[1]{0:T(128)} %bitcast.2.tp_ref, bf16[256,256]{1,0:T(8,128)(2,1)} %refs_0_.2, bf16[256,256]{1,0:T(8,128)(2,1)} %refs_1_.1, ...), custom_call_target="tpu_custom_call" | custom-call | tf_op jit(solution)/shard_map/pallas_call | solution.py:64
  2.9 0.0 copy-start.1
  2.9 0.0 copy-start.2
  2.9 3.0 %collective-permute-start = (bf16[3,256,128]{2,1,0:T(8,128)(2,1)}, bf16[3,256,128]{2,1,0:T(8,128)(2,1)S(1)}, u32[]{:S(2)}, u32[]{:S(2)}) collective-permute-start(bf16[3,256,128]{2,1,0:T(8,128)(2,1)} %get-tuple-element.31), channel_id=1, source_target_pairs={{0,4},{4,0},{8,12},{12,8},{16,20},{20,16},{24,28},{28,24},{1,5},{5... | collective-permute-start | bytes 589832 | tf_op jit(solution)/shard_map/ppermute | solution.py:351
  6.0 0.0 copy-done.3
  6.0 1.3 %collective-permute-start.7 = (bf16[64,256]{1,0:T(8,128)(2,1)S(1)}, bf16[64,256]{1,0:T(8,128)(2,1)S(1)}, u32[]{:S(2)}, u32[]{:S(2)}) collective-permute-start(bf16[64,256]{1,0:T(8,128)(2,1)S(1)} %slice.31), channel_id=1, source_target_pairs={{4,0},{8,4},{12,8},{16,12},{20,16},{24,20},{28,24},{5,1},{9,5},{13... | collective-permute-start | bytes 98312 | tf_op jit(solution)/shard_map/ppermute | solution.py:342
  7.3 0.6 broadcast_in_dim.13
  7.9 7.0 %all-to-all-start = ((s32[8,1,8]{2,1,0:T(1,128)}), s32[8,1,8]{2,1,0:T(1,128)S(1)}, u32[]{:S(2)}, u32[]{:S(2)}) async-start(s32[8,1,8]{2,1,0:T(1,128)} %broadcast_in_dim.13), calls=%async_computation | async-start | bytes 8192 | tf_op jit(solution)/shard_map/all_to_all | solution.py:340
  14.8 1.5 %collective-permute-start.8 = (bf16[128,1024]{1,0:T(8,128)(2,1)}, bf16[128,1024]{1,0:T(8,128)(2,1)}, u32[]{:S(2)}, u32[]{:S(2)}) collective-permute-start(bf16[128,1024]{1,0:T(8,128)(2,1)} %get-tuple-element.44), channel_id=1, source_target_pairs={{0,2},{1,3},{2,0},{3,1},{4,6},{5,7},{6,4},{7,5},{8,10},{9,11},{10,... | collective-permute-start | bytes 786440 | tf_op jit(solution)/shard_map/ppermute | solution.py:352
  16.3 0.0 collective-permute-start.9
  16.3 4.9 %all-to-all-done = s32[8,1,8]{2,1,0:T(1,128)S(1)} async-done(((s32[8,1,8]{2,1,0:T(1,128)}), s32[8,1,8]{2,1,0:T(1,128)S(1)}, u32[]{:S(2)}, u32[]{:S(2)}) %all-to-all-start) | async-done | bytes 288 | tf_op jit(solution)/shard_map/all_to_all | solution.py:340
  21.2 0.5 broadcast.11
  21.7 0.7 reduce.3
  22.4 0.1 reshape.34.slots_ref
  22.5 0.0 collective-permute-done.7.spill_ref
  22.5 1.7 %shard_map.101 = bf16[8,80,256]{2,1,0:T(8,128)(2,1)} custom-call(s32[1]{0:T(128)} %bitcast.6.ctx_ref, s32[64]{0:T(128)S(1)} %reshape.34.slots_ref, bf16[256,256]{1,0:T(8,128)(2,1)S(1)} %copy-done.3, bf16[64,256]{1,0:T(8,128)(2,1)S(1)} %collective-permute-done.7.spill_ref), custom_call_target="tpu_custom_call" | custom-call | tf_op jit(solution)/shard_map/pallas_call | solution.py:100
  24.1 3.4 %all-to-all-start.1 = ((bf16[8,80,256]{2,1,0:T(8,128)(2,1)}), bf16[8,80,256]{2,1,0:T(8,128)(2,1)S(1)}, u32[]{:S(2)}, u32[]{:S(2)}) async-start(bf16[8,80,256]{2,1,0:T(8,128)(2,1)} %shard_map.101), calls=%async_computation.1 | async-start | bytes 655360 | tf_op jit(solution)/shard_map/all_to_all | solution.py:340
  27.6 0.0 collective-permute-done
  27.6 1.1 %maximum_select_fusion = bf16[3,512,128]{2,1,0:T(8,128)(2,1)S(1)} fusion(bf16[3,256,128]{2,1,0:T(8,128)(2,1)S(1)} %collective-permute-done, bf16[3,256,128]{2,1,0:T(8,128)(2,1)} %get-tuple-element.30, pred[]{:T(512)S(6)} %eq.3), kind=kLoop, calls=%fused_computation | loop fusion | flops 1769472 | bytes 786433 | tf_op jit(solution)/shard_map/jit(_where)/select_n | solution.py:333
  28.8 4.5 %collective-permute-start.1 = (bf16[512,256]{1,0:T(8,128)(2,1)S(1)}, bf16[512,256]{1,0:T(8,128)(2,1)}, u32[]{:S(2)}, u32[]{:S(2)}) collective-permute-start(bf16[512,256]{1,0:T(8,128)(2,1)S(1)} %pad_maximum_fusion.kv_ref), channel_id=1, source_target_pairs={{0,8},{4,12},{8,16},{12,20},{16,24},{20,28},{1,9},{5,13},{9,17},{1... | collective-permute-start | bytes 786440 | tf_op jit(solution)/shard_map/ppermute | solution.py:375
  33.3 3.5 %shard_map.96 = (bf16[256,2048]{1,0:T(8,128)(2,1)}, bf16[256,2048]{1,0:T(8,128)(2,1)}, bf16[256,1024]{1,0:T(8,128)(2,1)}, bf16[256,1024]{1,0:T(8,128)(2,1)}) custom-call(s32[1]{0:T(128)} %bitcast.1.side_ref, s32[1]{0:T(128)} %bitcast.2.tp_ref, bf16[256,8192]{1,0:T(8,128)(2,1)} %refs_0_.3), custom_call_target="tpu_custom_call" | custom-call | tf_op jit(solution)/shard_map/pallas_call | solution.py:64
  36.9 0.0 copy-start
  36.9 1.6 %collective-permute-start.4 = (bf16[256,1024]{1,0:T(8,128)(2,1)}, bf16[256,1024]{1,0:T(8,128)(2,1)S(1)}, u32[]{:S(2)}, u32[]{:S(2)}) collective-permute-start(bf16[256,1024]{1,0:T(8,128)(2,1)} %get-tuple-element.32), channel_id=1, source_target_pairs={{0,2},{1,3},{2,0},{3,1},{4,6},{5,7},{6,4},{7,5},{8,10},{9,11},{10,... | collective-permute-start | bytes 1572872 | tf_op jit(solution)/shard_map/ppermute | solution.py:359
  38.4 0.0 collective-permute-done.8.refs_8_
  38.4 0.0 collective-permute-done.9.refs_9_
  38.4 0.0 all-to-all-done.1.asked_ref
  38.5 5.1 %shard_map.102 = bf16[8,96,256]{2,1,0:T(8,128)(2,1)} custom-call(s32[8]{0:T(128)S(1)} %copy-done.4, bf16[8,80,256]{2,1,0:T(8,128)(2,1)S(1)} %all-to-all-done.1.asked_ref, bf16[8,128,256]{2,1,0:T(8,128)(2,1)S(1)} %copy-done.1, bf16[8,128,256]{2,1,0:T(8,128)(2,1)S(1)} %copy-done.2), custom_call_target="tpu_custom_call" | custom-call | tf_op jit(solution)/shard_map/pallas_call | solution.py:143
  43.5 3.9 %all-to-all-start.2 = ((bf16[8,96,256]{2,1,0:T(8,128)(2,1)}), bf16[8,96,256]{2,1,0:T(8,128)(2,1)S(1)}, u32[]{:S(2)}, u32[]{:S(2)}) async-start(bf16[8,96,256]{2,1,0:T(8,128)(2,1)} %shard_map.102), calls=%async_computation.2 | async-start | bytes 786432 | tf_op jit(solution)/shard_map/all_to_all | solution.py:340
  47.4 0.0 collective-permute-start.5
  47.4 0.0 collective-permute-done.1.kv_ref
  47.4 4.6 %collective-permute-start.2 = (bf16[512,256]{1,0:T(8,128)(2,1)}, bf16[512,256]{1,0:T(8,128)(2,1)}, u32[]{:S(2)}, u32[]{:S(2)}) collective-permute-start(bf16[512,256]{1,0:T(8,128)(2,1)} %collective-permute-done.1.kv_ref), channel_id=1, source_target_pairs={{0,8},{4,12},{8,16},{12,20},{16,24},{20,28},{1,9},{5,13},{9,17},{1... | collective-permute-start | bytes 786440 | tf_op jit(solution)/shard_map/ppermute | solution.py:375
  52.1 0.4 collective-permute-start.16
  52.4 5.6 %collective-permute-done.2.kv_ref = bf16[512,256]{1,0:T(8,128)(2,1)} collective-permute-done((bf16[512,256]{1,0:T(8,128)(2,1)}, bf16[512,256]{1,0:T(8,128)(2,1)}, u32[]{:S(2)}, u32[]{:S(2)}) %collective-permute-start.2) | collective-permute-done | bytes 262176 | tf_op jit(solution)/shard_map/ppermute | solution.py:375
  58.0 5.2 %collective-permute-start.3 = (bf16[512,256]{1,0:T(8,128)(2,1)}, bf16[512,256]{1,0:T(8,128)(2,1)}, u32[]{:S(2)}, u32[]{:S(2)}) collective-permute-start(bf16[512,256]{1,0:T(8,128)(2,1)} %collective-permute-done.2.kv_ref), channel_id=1, source_target_pairs={{0,8},{4,12},{8,16},{12,20},{16,24},{20,28},{1,9},{5,13},{9,17},{1... | collective-permute-start | bytes 786440 | tf_op jit(solution)/shard_map/ppermute | solution.py:375
  63.2 1.8 %collective-permute-start.10 = (bf16[128,1024]{1,0:T(8,128)(2,1)}, bf16[128,1024]{1,0:T(8,128)(2,1)}, u32[]{:S(2)}, u32[]{:S(2)}) collective-permute-start(bf16[128,1024]{1,0:T(8,128)(2,1)} %collective-permute-done.8.refs_8_), channel_id=1, source_target_pairs={{0,4},{4,0},{8,12},{12,8},{16,20},{20,16},{24,28},{28,24},{1,5},{5... | collective-permute-start | bytes 786440 | tf_op jit(solution)/shard_map/ppermute | solution.py:363
  65.0 0.0 collective-permute-done.4.refs_6_
  65.0 0.2 collective-permute-start.11
  65.2 0.7 shard_map.97
  66.0 1.2 %shard_map.98 = (f32[512,128]{1,0:T(8,128)S(1)}, f32[512,128]{1,0:T(8,128)S(1)}, f32[512,128]{1,0:T(8,128)S(1)}) custom-call(s32[1]{0:T(128)} %bitcast.pair_ref, bf16[512,128]{1,0:T(8,128)(2,1)S(1)} %get-tuple-element.60.q_ref, bf16[512,256]{1,0:T(8,128)(2,1)} %collective-permute-done.1.kv_ref, f32[512,128]{1,0:T(8,128)S(1)} %get-tuple-element.35.refs_0_, ...), custom_call_target="tpu_custom_call" | custom-call | tf_op jit(solution)/shard_map/pallas_call | solution.py:270
  67.2 1.2 %shard_map.99 = (f32[512,128]{1,0:T(8,128)S(1)}, f32[512,128]{1,0:T(8,128)S(1)}, f32[512,128]{1,0:T(8,128)S(1)}) custom-call(s32[1]{0:T(128)} %bitcast.pair_ref, bf16[512,128]{1,0:T(8,128)(2,1)S(1)} %get-tuple-element.60.q_ref, bf16[512,256]{1,0:T(8,128)(2,1)} %collective-permute-done.2.kv_ref, f32[512,128]{1,0:T(8,128)S(1)} %get-tuple-element.38.refs_0_, ...), custom_call_target="tpu_custom_call" | custom-call | tf_op jit(solution)/shard_map/pallas_call | solution.py:270
  68.4 0.0 collective-permute-done.5.refs_7_
  68.4 0.0 collective-permute-done.3.kv_ref
  68.5 1.2 %shard_map.100 = bf16[512,128]{1,0:T(8,128)(2,1)S(1)} custom-call(s32[1]{0:T(128)} %bitcast.pair_ref, bf16[512,128]{1,0:T(8,128)(2,1)S(1)} %get-tuple-element.60.q_ref, bf16[512,256]{1,0:T(8,128)(2,1)} %collective-permute-done.3.kv_ref, f32[512,128]{1,0:T(8,128)S(1)} %get-tuple-element.41.refs_0_, f32[512,128]{1,0:T(8,128)S(1)} %get-tuple-element.42.refs_1_, ...), custom_call_target="tpu_custom_call" | custom-call | tf_op jit(solution)/shard_map/pallas_call | solution.py:270
  69.6 3.1 %collective-permute-done.10.refs_10_ = bf16[128,1024]{1,0:T(8,128)(2,1)} collective-permute-done((bf16[128,1024]{1,0:T(8,128)(2,1)}, bf16[128,1024]{1,0:T(8,128)(2,1)}, u32[]{:S(2)}, u32[]{:S(2)}) %collective-permute-start.10) | collective-permute-done | bytes 262176 | tf_op jit(solution)/shard_map/ppermute | solution.py:363
  72.8 4.0 %collective-permute-done.11.refs_11_ = bf16[128,1024]{1,0:T(8,128)(2,1)} collective-permute-done((bf16[128,1024]{1,0:T(8,128)(2,1)}, bf16[128,1024]{1,0:T(8,128)(2,1)}, u32[]{:S(2)}, u32[]{:S(2)}) %collective-permute-start.11) | collective-permute-done | bytes 262176 | tf_op jit(solution)/shard_map/ppermute | solution.py:363
  76.8 0.0 all-to-all-done.2.parts_ref
  76.8 1.3 %shard_map.103 = (bf16[256,256]{1,0:T(8,128)(2,1)S(1)}, bf16[64,256]{1,0:T(8,128)(2,1)S(1)}) custom-call(s32[1]{0:T(128)} %bitcast.6.ctx_ref, s32[64]{0:T(128)S(1)} %reshape.34.slots_ref, bf16[8,96,256]{2,1,0:T(8,128)(2,1)S(1)} %all-to-all-done.2.parts_ref), custom_call_target="tpu_custom_call" | custom-call | tf_op jit(solution)/shard_map/pallas_call | solution.py:201
  78.2 3.6 %collective-permute-start.12 = (bf16[64,256]{1,0:T(8,128)(2,1)S(1)}, bf16[64,256]{1,0:T(8,128)(2,1)S(1)}, u32[]{:S(2)}, u32[]{:S(2)}) collective-permute-start(bf16[64,256]{1,0:T(8,128)(2,1)S(1)} %get-tuple-element.50), channel_id=1, source_target_pairs={{0,4},{4,8},{8,12},{12,16},{16,20},{20,24},{24,28},{1,5},{5,9},{9,... | collective-permute-start | bytes 98312 | tf_op jit(solution)/shard_map/ppermute | solution.py:383
  81.8 1.0 collective-permute-start.6
  82.8 0.6 collective-permute-done.12
  83.4 0.1 slice_select_fusion
  83.5 0.1 collective-permute-start.13
  83.6 1.0 %collective-permute-start.14 = (bf16[256,256]{1,0:T(8,128)(2,1)S(1)}, bf16[256,256]{1,0:T(8,128)(2,1)S(1)}, u32[]{:S(2)}, u32[]{:S(2)}) collective-permute-start(bf16[256,256]{1,0:T(8,128)(2,1)S(1)} %pad_maximum_fusion.1.refs_0_), channel_id=1, source_target_pairs={{0,2},{1,3},{2,0},{3,1},{4,6},{5,7},{6,4},{7,5},{8,10},{9,11},{10,... | collective-permute-start | bytes 393224 | tf_op jit(solution)/shard_map/ppermute | solution.py:386
  84.5 0.9 collective-permute-start.15
  85.4 0.7 collective-permute-done.6
  86.2 0.7 maximum_select_fusion.1
  86.9 0.0 collective-permute-done.16.refs_5_
  86.9 0.0 collective-permute-done.13.refs_1_
  86.9 3.1 %collective-permute-done.14.refs_2_ = bf16[256,256]{1,0:T(8,128)(2,1)S(1)} collective-permute-done((bf16[256,256]{1,0:T(8,128)(2,1)S(1)}, bf16[256,256]{1,0:T(8,128)(2,1)S(1)}, u32[]{:S(2)}, u32[]{:S(2)}) %collective-permute-start.14) | collective-permute-done | bytes 131104 | tf_op jit(solution)/shard_map/ppermute | solution.py:386
  89.9 1.9 %collective-permute-done.15.refs_3_ = bf16[256,256]{1,0:T(8,128)(2,1)S(1)} collective-permute-done((bf16[256,256]{1,0:T(8,128)(2,1)S(1)}, bf16[256,256]{1,0:T(8,128)(2,1)S(1)}, u32[]{:S(2)}, u32[]{:S(2)}) %collective-permute-start.15) | collective-permute-done | bytes 131104 | tf_op jit(solution)/shard_map/ppermute | solution.py:386
  91.8 0.0 copy-done
  91.8 3.9 %shard_map.104 = bf16[256,2048]{1,0:T(8,128)(2,1)} custom-call(s32[1]{0:T(128)} %bitcast.1.side_ref, bf16[256,256]{1,0:T(8,128)(2,1)S(1)} %pad_maximum_fusion.1.refs_0_, bf16[256,256]{1,0:T(8,128)(2,1)S(1)} %collective-permute-done.13.refs_1_, bf16[256,256]{1,0:T(8,128)(2,1)S(1)} %collective-permute-done.14.refs_2_, ...), custom_call_target="tpu_custom_call" | custom-call | tf_op jit(solution)/shard_map/pallas_call | solution.py:308
  (10 shorter events, 0.1 us)
Async XLA Ops:
  0.6 5.3 %copy-start.3 = (bf16[256,256]{1,0:T(8,128)(2,1)S(1)}, bf16[256,256]{1,0:T(8,128)(2,1)}, u32[]{:S(2)}) copy-start(bf16[256,256]{1,0:T(8,128)(2,1)} %queries_ref.1) | copy-start | bytes 393220
  0.6 6.6 %copy-start.4 = (s32[8]{0:T(128)S(1)}, s32[8]{0:T(128)}, u32[]{:S(2)}) copy-start(s32[8]{0:T(128)} %slot_ref.1) | copy-start | bytes 100
  2.9 35.5 %copy-start.1 = (bf16[8,128,256]{2,1,0:T(8,128)(2,1)S(1)}, bf16[8,128,256]{2,1,0:T(8,128)(2,1)}, u32[]{:S(2)}) copy-start(bf16[8,128,256]{2,1,0:T(8,128)(2,1)} %keys_ref.1) | copy-start | bytes 1572868
  2.9 35.5 %copy-start.2 = (bf16[8,128,256]{2,1,0:T(8,128)(2,1)S(1)}, bf16[8,128,256]{2,1,0:T(8,128)(2,1)}, u32[]{:S(2)}) copy-start(bf16[8,128,256]{2,1,0:T(8,128)(2,1)} %values_ref.1) | copy-start | bytes 1572868
  2.9 24.6 %collective-permute-start = (bf16[3,256,128]{2,1,0:T(8,128)(2,1)}, bf16[3,256,128]{2,1,0:T(8,128)(2,1)S(1)}, u32[]{:S(2)}, u32[]{:S(2)}) collective-permute-start(bf16[3,256,128]{2,1,0:T(8,128)(2,1)} %get-tuple-element.31), channel_id=1, source_target_pairs={{0,4},{4,0},{8,12},{12,8},{16,20},{20,16},{24,28},{28,24},{1,5},{5... | collective-permute-start | bytes 589832 | tf_op jit(solution)/shard_map/ppermute | solution.py:351
  6.0 16.5 %collective-permute-start.7 = (bf16[64,256]{1,0:T(8,128)(2,1)S(1)}, bf16[64,256]{1,0:T(8,128)(2,1)S(1)}, u32[]{:S(2)}, u32[]{:S(2)}) collective-permute-start(bf16[64,256]{1,0:T(8,128)(2,1)S(1)} %slice.31), channel_id=1, source_target_pairs={{4,0},{8,4},{12,8},{16,12},{20,16},{24,20},{28,24},{5,1},{9,5},{13... | collective-permute-start | bytes 98312 | tf_op jit(solution)/shard_map/ppermute | solution.py:342
  7.9 13.3 %all-to-all-start = ((s32[8,1,8]{2,1,0:T(1,128)}), s32[8,1,8]{2,1,0:T(1,128)S(1)}, u32[]{:S(2)}, u32[]{:S(2)}) async-start(s32[8,1,8]{2,1,0:T(1,128)} %broadcast_in_dim.13), calls=%async_computation | async-start | bytes 8192 | tf_op jit(solution)/shard_map/all_to_all | solution.py:340
  14.8 23.6 %collective-permute-start.8 = (bf16[128,1024]{1,0:T(8,128)(2,1)}, bf16[128,1024]{1,0:T(8,128)(2,1)}, u32[]{:S(2)}, u32[]{:S(2)}) collective-permute-start(bf16[128,1024]{1,0:T(8,128)(2,1)} %get-tuple-element.44), channel_id=1, source_target_pairs={{0,2},{1,3},{2,0},{3,1},{4,6},{5,7},{6,4},{7,5},{8,10},{9,11},{10,... | collective-permute-start | bytes 786440 | tf_op jit(solution)/shard_map/ppermute | solution.py:352
  16.3 22.1 %collective-permute-start.9 = (bf16[128,1024]{1,0:T(8,128)(2,1)}, bf16[128,1024]{1,0:T(8,128)(2,1)}, u32[]{:S(2)}, u32[]{:S(2)}) collective-permute-start(bf16[128,1024]{1,0:T(8,128)(2,1)} %get-tuple-element.45), channel_id=1, source_target_pairs={{0,3},{1,2},{2,1},{3,0},{4,7},{5,6},{6,5},{7,4},{8,11},{9,10},{10,... | collective-permute-start | bytes 786440 | tf_op jit(solution)/shard_map/ppermute | solution.py:352
  24.1 14.3 %all-to-all-start.1 = ((bf16[8,80,256]{2,1,0:T(8,128)(2,1)}), bf16[8,80,256]{2,1,0:T(8,128)(2,1)S(1)}, u32[]{:S(2)}, u32[]{:S(2)}) async-start(bf16[8,80,256]{2,1,0:T(8,128)(2,1)} %shard_map.101), calls=%async_computation.1 | async-start | bytes 655360 | tf_op jit(solution)/shard_map/all_to_all | solution.py:340
  28.8 18.6 %collective-permute-start.1 = (bf16[512,256]{1,0:T(8,128)(2,1)S(1)}, bf16[512,256]{1,0:T(8,128)(2,1)}, u32[]{:S(2)}, u32[]{:S(2)}) collective-permute-start(bf16[512,256]{1,0:T(8,128)(2,1)S(1)} %pad_maximum_fusion.kv_ref), channel_id=1, source_target_pairs={{0,8},{4,12},{8,16},{12,20},{16,24},{20,28},{1,9},{5,13},{9,17},{1... | collective-permute-start | bytes 786440 | tf_op jit(solution)/shard_map/ppermute | solution.py:375
  36.9 55.0 %copy-start = (bf16[256,2048]{1,0:T(8,128)(2,1)S(1)}, bf16[256,2048]{1,0:T(8,128)(2,1)}, u32[]{:S(2)}) copy-start(bf16[256,2048]{1,0:T(8,128)(2,1)} %get-tuple-element.52.refs_4_) | copy-start | bytes 3145732
  36.9 28.1 %collective-permute-start.4 = (bf16[256,1024]{1,0:T(8,128)(2,1)}, bf16[256,1024]{1,0:T(8,128)(2,1)S(1)}, u32[]{:S(2)}, u32[]{:S(2)}) collective-permute-start(bf16[256,1024]{1,0:T(8,128)(2,1)} %get-tuple-element.32), channel_id=1, source_target_pairs={{0,2},{1,3},{2,0},{3,1},{4,6},{5,7},{6,4},{7,5},{8,10},{9,11},{10,... | collective-permute-start | bytes 1572872 | tf_op jit(solution)/shard_map/ppermute | solution.py:359
  43.5 33.3 %all-to-all-start.2 = ((bf16[8,96,256]{2,1,0:T(8,128)(2,1)}), bf16[8,96,256]{2,1,0:T(8,128)(2,1)S(1)}, u32[]{:S(2)}, u32[]{:S(2)}) async-start(bf16[8,96,256]{2,1,0:T(8,128)(2,1)} %shard_map.102), calls=%async_computation.2 | async-start | bytes 786432 | tf_op jit(solution)/shard_map/all_to_all | solution.py:340
  47.4 21.0 %collective-permute-start.5 = (bf16[256,1024]{1,0:T(8,128)(2,1)}, bf16[256,1024]{1,0:T(8,128)(2,1)}, u32[]{:S(2)}, u32[]{:S(2)}) collective-permute-start(bf16[256,1024]{1,0:T(8,128)(2,1)} %get-tuple-element.33), channel_id=1, source_target_pairs={{0,3},{1,2},{2,1},{3,0},{4,7},{5,6},{6,5},{7,4},{8,11},{9,10},{10,... | collective-permute-start | bytes 1572872 | tf_op jit(solution)/shard_map/ppermute | solution.py:359
  47.4 10.6 %collective-permute-start.2 = (bf16[512,256]{1,0:T(8,128)(2,1)}, bf16[512,256]{1,0:T(8,128)(2,1)}, u32[]{:S(2)}, u32[]{:S(2)}) collective-permute-start(bf16[512,256]{1,0:T(8,128)(2,1)} %collective-permute-done.1.kv_ref), channel_id=1, source_target_pairs={{0,8},{4,12},{8,16},{12,20},{16,24},{20,28},{1,9},{5,13},{9,17},{1... | collective-permute-start | bytes 786440 | tf_op jit(solution)/shard_map/ppermute | solution.py:375
  52.1 34.8 %collective-permute-start.16 = (bf16[256,2048]{1,0:T(8,128)(2,1)}, bf16[256,2048]{1,0:T(8,128)(2,1)S(1)}, u32[]{:S(2)}, u32[]{:S(2)}) collective-permute-start(bf16[256,2048]{1,0:T(8,128)(2,1)} %get-tuple-element.53), channel_id=1, source_target_pairs={{0,1},{1,0},{2,3},{3,2},{4,5},{5,4},{6,7},{7,6},{8,9},{9,8},{10,11... | collective-permute-start | bytes 3145736 | tf_op jit(solution)/shard_map/ppermute | solution.py:358
  58.0 10.4 %collective-permute-start.3 = (bf16[512,256]{1,0:T(8,128)(2,1)}, bf16[512,256]{1,0:T(8,128)(2,1)}, u32[]{:S(2)}, u32[]{:S(2)}) collective-permute-start(bf16[512,256]{1,0:T(8,128)(2,1)} %collective-permute-done.2.kv_ref), channel_id=1, source_target_pairs={{0,8},{4,12},{8,16},{12,20},{16,24},{20,28},{1,9},{5,13},{9,17},{1... | collective-permute-start | bytes 786440 | tf_op jit(solution)/shard_map/ppermute | solution.py:375
  63.2 9.6 %collective-permute-start.10 = (bf16[128,1024]{1,0:T(8,128)(2,1)}, bf16[128,1024]{1,0:T(8,128)(2,1)}, u32[]{:S(2)}, u32[]{:S(2)}) collective-permute-start(bf16[128,1024]{1,0:T(8,128)(2,1)} %collective-permute-done.8.refs_8_), channel_id=1, source_target_pairs={{0,4},{4,0},{8,12},{12,8},{16,20},{20,16},{24,28},{28,24},{1,5},{5... | collective-permute-start | bytes 786440 | tf_op jit(solution)/shard_map/ppermute | solution.py:363
  65.0 11.8 %collective-permute-start.11 = (bf16[128,1024]{1,0:T(8,128)(2,1)}, bf16[128,1024]{1,0:T(8,128)(2,1)}, u32[]{:S(2)}, u32[]{:S(2)}) collective-permute-start(bf16[128,1024]{1,0:T(8,128)(2,1)} %collective-permute-done.9.refs_9_), channel_id=1, source_target_pairs={{0,4},{4,0},{8,12},{12,8},{16,20},{20,16},{24,28},{28,24},{1,5},{5... | collective-permute-start | bytes 786440 | tf_op jit(solution)/shard_map/ppermute | solution.py:363
  78.2 5.2 %collective-permute-start.12 = (bf16[64,256]{1,0:T(8,128)(2,1)S(1)}, bf16[64,256]{1,0:T(8,128)(2,1)S(1)}, u32[]{:S(2)}, u32[]{:S(2)}) collective-permute-start(bf16[64,256]{1,0:T(8,128)(2,1)S(1)} %get-tuple-element.50), channel_id=1, source_target_pairs={{0,4},{4,8},{8,12},{12,16},{16,20},{20,24},{24,28},{1,5},{5,9},{9,... | collective-permute-start | bytes 98312 | tf_op jit(solution)/shard_map/ppermute | solution.py:383
  81.8 4.3 %collective-permute-start.6 = (bf16[256,128]{1,0:T(8,128)(2,1)S(1)}, bf16[256,128]{1,0:T(8,128)(2,1)S(1)}, u32[]{:S(2)}, u32[]{:S(2)}) collective-permute-start(bf16[256,128]{1,0:T(8,128)(2,1)S(1)} %get-tuple-element.62), channel_id=1, source_target_pairs={{0,4},{4,0},{8,12},{12,8},{16,20},{20,16},{24,28},{28,24},{1,5},{5... | collective-permute-start | bytes 196616 | tf_op jit(solution)/shard_map/ppermute | solution.py:379
  83.5 3.4 %collective-permute-start.13 = (bf16[256,256]{1,0:T(8,128)(2,1)S(1)}, bf16[256,256]{1,0:T(8,128)(2,1)S(1)}, u32[]{:S(2)}, u32[]{:S(2)}) collective-permute-start(bf16[256,256]{1,0:T(8,128)(2,1)S(1)} %pad_maximum_fusion.1.refs_0_), channel_id=1, source_target_pairs={{0,1},{1,0},{2,3},{3,2},{4,5},{5,4},{6,7},{7,6},{8,9},{9,8},{10,11... | collective-permute-start | bytes 393224 | tf_op jit(solution)/shard_map/ppermute | solution.py:386
  83.6 6.4 %collective-permute-start.14 = (bf16[256,256]{1,0:T(8,128)(2,1)S(1)}, bf16[256,256]{1,0:T(8,128)(2,1)S(1)}, u32[]{:S(2)}, u32[]{:S(2)}) collective-permute-start(bf16[256,256]{1,0:T(8,128)(2,1)S(1)} %pad_maximum_fusion.1.refs_0_), channel_id=1, source_target_pairs={{0,2},{1,3},{2,0},{3,1},{4,6},{5,7},{6,4},{7,5},{8,10},{9,11},{10,... | collective-permute-start | bytes 393224 | tf_op jit(solution)/shard_map/ppermute | solution.py:386
  84.5 7.3 %collective-permute-start.15 = (bf16[256,256]{1,0:T(8,128)(2,1)S(1)}, bf16[256,256]{1,0:T(8,128)(2,1)S(1)}, u32[]{:S(2)}, u32[]{:S(2)}) collective-permute-start(bf16[256,256]{1,0:T(8,128)(2,1)S(1)} %pad_maximum_fusion.1.refs_0_), channel_id=1, source_target_pairs={{0,3},{1,2},{2,1},{3,0},{4,7},{5,6},{6,5},{7,4},{8,11},{9,10},{10,... | collective-permute-start | bytes 393224 | tf_op jit(solution)/shard_map/ppermute | solution.py:386

commit v6 on v4

v6 whole, which is shorter than its diff:
```python
import functools
import math

import jax
import jax.numpy as jnp
from jax import lax
from jax.experimental import pallas as pl
from jax.experimental.pallas import tpu as pltpu
from jax.sharding import PartitionSpec as P

HD = 128
BLOCK = 64
LEAD = 16
NEIGHBOUR = 128
WINDOW = BLOCK + LEAD
ENTRY = WINDOW + LEAD
ENTRIES = 6
NEGATIVE = -1e30
SCALE = HD ** -0.5 * math.log2(math.e)
VMEM = pl.BlockSpec(memory_space=pltpu.VMEM)
SMEM = pl.BlockSpec(memory_space=pltpu.SMEM)
ANY = pl.BlockSpec(memory_space=pl.ANY)
PARAMS = pltpu.CompilerParams(vmem_limit_bytes=16 * 1024 * 1024)


def takes(microseconds):
    return pl.CostEstimate(
        flops=microseconds * 1000000000, bytes_accessed=0, transcendentals=0
    )


def dot(a, b):
    return jnp.dot(a, b, preferred_element_type=jnp.float32)


def dot_t(a, b):
    return lax.dot_general(a, b, (((1,), (1,)), ((), ())), preferred_element_type=jnp.float32)


def fetch(pieces, sems):
    copies = [
        pltpu.make_async_copy(source, target, sems.at[at])
        for at, (source, target) in enumerate(pieces)
    ]
    for copy in copies:
        copy.start()
    for copy in copies:
        copy.wait()


def cut_kernel(plan, side_ref, tp_ref, *refs):
    mark_ref, sems, refs = refs[-2], refs[-1], refs[:-2]
    sources, outs = refs, refs[len(refs) - len(plan) :]
    mark_ref[...] = jnp.zeros(mark_ref.shape, jnp.float32)
    pieces = []
    for out, parts in zip(outs, plan):
        for at, (index, step, total, offset, width, depth) in enumerate(parts):
            source = sources[index]
            key = tp_ref[0] if total else side_ref[0]
            lane = pl.multiple_of((key ^ step) * (total or HD) + offset, HD)
            row = pl.multiple_of(side_ref[0] * depth, LEAD) if depth < source.shape[0] else 0
            piece = source.at[pl.ds(row, depth), pl.ds(lane, width)]
            pieces.append((piece, out.at[:, pl.ds(at * width, width)]))
    fetch(pieces, sems)


def cut(side, tp, sources, plan, before=()):
    shapes = []
    for parts in plan:
        shape = (parts[0][5], len(parts) * parts[0][4])
        shapes.append(jax.ShapeDtypeStruct(shape, sources[parts[0][0]].dtype))
    shapes.append(jax.ShapeDtypeStruct((8, HD), jnp.float32))
    return pl.pallas_call(
        functools.partial(cut_kernel, plan),
        out_shape=tuple(shapes),
        in_specs=[SMEM] * 2 + [ANY] * (len(sources) + len(before)),
        out_specs=(VMEM,) * len(shapes),
        scratch_shapes=[pltpu.SemaphoreType.DMA((sum(len(parts) for parts in plan),))],
        cost_estimate=takes(2),
    )(side, tp, *sources, *before)


def spread_kernel(side_ref, mine_ref, other_ref, *refs):
    out_ref = refs[-1]
    rows = mine_ref.shape[0]
    first = jnp.where(side_ref[0] == 0, mine_ref[...], other_ref[...])
    second = jnp.where(side_ref[0] == 0, other_ref[...], mine_ref[...])
    for copy in range(out_ref.shape[0]):
        out_ref[copy, :rows, :] = first
        out_ref[copy, rows:, :] = second


def spread(side, mine, other, copies, before):
    rows, width = mine.shape
    return pl.pallas_call(
        spread_kernel,
        out_shape=jax.ShapeDtypeStruct((copies, 2 * rows, width), mine.dtype),
        in_specs=[SMEM, VMEM, VMEM] + [ANY] * len(before),
        out_specs=VMEM,
        compiler_params=PARAMS,
        cost_estimate=takes(1),
    )(side, mine, other, *before)


def hold_kernel(own_ref, other_ref, kv_own, kv_other, queries_ref, *refs):
    out_ref, all_ref, answer_ref = refs[-3:]
    pairs, rows, _ = queries_ref.shape
    blocks = rows // BLOCK
    for step in range(pairs):
        all_ref[step * rows : (step + 1) * rows, :] = queries_ref[step]
    all_ref[pairs * rows :, :] = jnp.zeros((BLOCK, HD), all_ref.dtype)
    empty = jnp.full((LEAD, HD), -1, jnp.bfloat16)
    for step in range(pairs):
        for entry in range(ENTRIES):
            out_ref[step, entry * ENTRY + WINDOW : (entry + 1) * ENTRY, :] = empty

    count = own_ref.shape[0]
    slots = [own_ref[n] for n in range(count)] + [other_ref[n] for n in range(count)]
    lane = lax.broadcasted_iota(jnp.int32, (HD, HD), 1)
    for first in range(0, len(slots), HD // 8):
        batch = slots[first : first + HD // 8]
        stats = jnp.zeros((HD, HD), jnp.float32)
        for j, slot in enumerate(batch):
            item = first + j
            kv = kv_own if item < count else kv_other
            held = slice((item % count) * NEIGHBOUR, (item % count + 1) * NEIGHBOUR)
            block = slot // 2
            start = pl.multiple_of(block * BLOCK + BLOCK - LEAD, LEAD)
            s = dot_t(all_ref[pl.ds(start, WINDOW), :], kv[held, :HD])
            peak = jnp.max(s, axis=1, keepdims=True).astype(jnp.bfloat16).astype(jnp.float32)
            p = jnp.exp2((s - peak) * SCALE)
            total = jnp.sum(p, axis=1, keepdims=True)
            mixed = dot(p.astype(jnp.bfloat16), kv[held, HD:])
            answer_ref[item] = mixed.astype(jnp.bfloat16)
            high = total.astype(jnp.bfloat16).astype(jnp.float32)
            place = lax.rem(slot, 2 * blocks).astype(jnp.float32)
            columns = (peak, high, total - high, jnp.full((WINDOW, 1), place))
            for at, column in enumerate(columns):
                column = jnp.concatenate([column, jnp.zeros((HD - WINDOW, 1), jnp.float32)])
                stats = jnp.where(lane == 8 * j + at, column, stats)
        turned = stats.T
        row = lax.broadcasted_iota(jnp.int32, (LEAD, HD), 0)
        for j, slot in enumerate(batch):
            item = first + j
            half = item // count
            block = slot // 2
            step = block // blocks
            entry = 2 * half + lax.rem(slot // count, 2)
            tile = jnp.concatenate([turned[8 * j : 8 * j + 8], jnp.zeros((8, HD), jnp.float32)])
            place = lax.rem(slot, 2 * blocks).astype(jnp.float32)
            tile = jnp.where(row == 3, place, tile)
            at = pl.multiple_of(entry * ENTRY, LEAD)
            out_ref[step, pl.ds(at, WINDOW), :] = answer_ref[item]
            out_ref[step, pl.ds(at + WINDOW, LEAD), :] = tile.astype(jnp.bfloat16)

            @pl.when(lax.rem(block, blocks) == blocks - 1)
            def _():
                after = lax.rem(step + 1, pairs)
                spill = (4 + half) * ENTRY
                moved = jnp.where(row == 3, place + 2, tile)
                out_ref[after, spill : spill + WINDOW, :] = answer_ref[item]
                out_ref[after, spill + WINDOW : spill + ENTRY, :] = moved.astype(jnp.bfloat16)


def hold(slots, other_slots, kv, other_kv, queries, before):
    pairs, rows, _ = queries.shape
    dtype = queries.dtype
    return pl.pallas_call(
        hold_kernel,
        out_shape=jax.ShapeDtypeStruct((pairs, ENTRIES * ENTRY, HD), dtype),
        in_specs=[SMEM] * 2 + [VMEM] * 3 + [ANY] * len(before),
        out_specs=VMEM,
        scratch_shapes=[
            pltpu.VMEM((pairs * rows + BLOCK, HD), dtype),
            pltpu.VMEM((2 * slots.shape[0], WINDOW, HD), dtype),
        ],
        compiler_params=PARAMS,
        cost_estimate=takes(3),
    )(slots, other_slots, kv, other_kv, queries, *before)


def combine_kernel(pair_ref, side_ref, parts_ref, *refs):
    keep_ref, give_ref, factor_ref, cca_ref, table_ref = refs[-5:]
    rows = cca_ref.shape[0]
    blocks = rows // BLOCK
    places = 2 * blocks + 2
    for place in range(places):
        table_ref[place] = 0
    for entry in range(parts_ref.shape[0] // ENTRY):
        top = entry * ENTRY + WINDOW
        held = parts_ref[top : top + LEAD, :].astype(jnp.float32)
        place = jnp.max(held[3:4]).astype(jnp.int32)
        table_ref[jnp.where(place < 0, places, place)] = entry

    def at(place):
        return pl.multiple_of(table_ref[place] * ENTRY, LEAD)

    def stats(place):
        held = parts_ref[pl.ds(at(place) + WINDOW, LEAD), :].astype(jnp.float32)
        return held[0:1], held[1:2] + held[2:3]

    for block in range(blocks + 1):
        peak1, total1 = stats(2 * block)
        peak2, total2 = stats(2 * block + 1)
        peak = jnp.maximum(peak1, peak2)
        weight1 = jnp.exp2((peak1 - peak) * SCALE)
        weight2 = jnp.exp2((peak2 - peak) * SCALE)
        total = weight1 * total1 + weight2 * total2
        factor_ref[2 * block : 2 * block + 1, :] = weight1 / total
        factor_ref[2 * block + 1 : 2 * block + 2, :] = weight2 / total
    factors = factor_ref[...].T

    def answer(block):
        result = None
        for place in (2 * block, 2 * block + 1):
            held = parts_ref[pl.ds(at(place), WINDOW), :].astype(jnp.float32)
            held = held * factors[:WINDOW, place : place + 1]
            result = held if result is None else result + held
        return result.astype(jnp.bfloat16)

    row = lax.broadcasted_iota(jnp.int32, (LEAD, HD), 0)
    before = answer(blocks)
    before = jnp.where(pair_ref[0] == 0, jnp.zeros_like(before), before)
    for block in range(blocks):
        now = answer(block)
        top = block * BLOCK
        cca_ref[top : top + BLOCK - LEAD, :] = before[LEAD:BLOCK]
        cca_ref[top + BLOCK - LEAD : top + BLOCK, :] = jnp.where(
            row == LEAD - 1, now[:LEAD], before[BLOCK:]
        )
        before = now
    half = rows // 2
    side = side_ref[0]
    keep_ref[...] = cca_ref[pl.ds(pl.multiple_of(side * half, half), half), :]
    give_ref[...] = cca_ref[pl.ds(pl.multiple_of((1 - side) * half, half), half), :]


def combine(pair, side, parts, rows):
    half = jax.ShapeDtypeStruct((rows // 2, HD), parts.dtype)
    return pl.pallas_call(
        combine_kernel,
        out_shape=(half, half),
        in_specs=[SMEM] * 2 + [VMEM],
        out_specs=(VMEM, VMEM),
        scratch_shapes=[
            pltpu.VMEM((HD, HD), jnp.float32),
            pltpu.VMEM((rows, HD), parts.dtype),
            pltpu.SMEM((2 * rows // BLOCK + 3,), jnp.int32),
        ],
        compiler_params=PARAMS,
        cost_estimate=takes(1),
    )(pair, side, parts.reshape(-1, HD))


def self_kernel(first, last, step, chunks, pair_ref, side_ref, mine_ref, other_ref, *refs):
    kvs, refs = refs[:chunks], refs[chunks:]
    if not first:
        peak_in, total_in, accum_in = refs[:3]
        refs = refs[3:]
    tile = mine_ref.shape[0]
    rows = 2 * tile
    peak_ref, total_ref, accum_ref = refs[-3:]
    refs = refs[-5:-3] if last else refs[-7:-3]
    if not last:
        refs[3][...] = jnp.zeros(refs[3].shape, jnp.float32)
    for part, q_ref in enumerate((mine_ref, other_ref)):
        at = pl.ds(part * tile, tile)
        if not first:
            peak_ref[at, :] = peak_in[at, :]
            total_ref[at, :] = total_in[at, :]
            accum_ref[at, :] = accum_in[at, :]
        for index, kv_ref in enumerate(kvs):
            fresh = first and index == 0

            def work():
                s = dot_t(q_ref[:, :HD], kv_ref[:, :HD])
                if fresh:
                    row = lax.broadcasted_iota(jnp.int32, (tile, rows), 0)
                    col = lax.broadcasted_iota(jnp.int32, (tile, rows), 1)
                    row = row + (side_ref[0] ^ part) * tile
                    turn = side_ref[0] * tile
                    col = jnp.where(col < tile, col + turn, col - turn)
                    s = jnp.where(col <= row, s, NEGATIVE)
                peak = jnp.max(s, axis=1, keepdims=True)
                if not fresh:
                    old = peak_ref[at, :1]
                    peak = jnp.maximum(peak, old)
                    factor = jnp.exp2((old - peak) * SCALE)
                p = jnp.exp2((s - peak) * SCALE)
                total = jnp.sum(p, axis=1, keepdims=True)
                accum = dot(p.astype(jnp.bfloat16), kv_ref[:, HD:])
                if not fresh:
                    total += total_ref[at, :1] * factor
                    accum += accum_ref[at, :] * factor
                peak_ref[at, :] = jnp.broadcast_to(peak, (tile, HD))
                total_ref[at, :] = jnp.broadcast_to(total, (tile, HD))
                accum_ref[at, :] = accum

            if fresh:
                work()
            else:
                pl.when(pair_ref[0] >= step + index)(work)
        if last:
            refs[part][...] = (accum_ref[at, :] / total_ref[at, :]).astype(jnp.bfloat16)
        else:
            refs[0][at, :] = peak_ref[at, :]
            refs[1][at, :] = total_ref[at, :]
            refs[2][at, :] = accum_ref[at, :]


def self_steps(pair, side, mine, other, kvs, state, step, last, before):
    tile = mine.shape[0]
    rows = 2 * tile
    first = state is None
    held = jax.ShapeDtypeStruct((rows, HD), jnp.float32)
    if last:
        out_shape = (jax.ShapeDtypeStruct((tile, HD), jnp.bfloat16),) * 2
    else:
        out_shape = (held,) * 3 + (jax.ShapeDtypeStruct((8, HD), jnp.float32),)
    return pl.pallas_call(
        functools.partial(self_kernel, first, last, step, len(kvs)),
        out_shape=out_shape,
        in_specs=[SMEM] * 2 + [VMEM] * (2 + len(kvs) + (0 if first else 3)) + [ANY] * len(before),
        out_specs=(VMEM,) * len(out_shape),
        scratch_shapes=[pltpu.VMEM((rows, HD), jnp.float32)] * 3,
        compiler_params=PARAMS,
        cost_estimate=takes(3),
    )(pair, side, mine, other, *kvs, *(() if first else state), *before)


def project_kernel(groups, *refs):
    crossed_ref, out_ref, sems = refs[-3:]
    terms, near, far = refs[:groups], refs[groups : groups + 2], refs[groups + 2 : -3]
    width = crossed_ref.shape[1]
    half = width // 2
    tile = min(512, half)
    term = jnp.concatenate([held[...] for held in terms], axis=1)
    outs = []
    for column in range(0, width, tile):
        at = slice(column, column + tile)
        blocks = far[: groups - 2] if column < half else far[groups - 2 :]
        start = column % half
        weight = [block[:, at] for block in near]
        weight += [block[:, start : start + tile] for block in blocks]
        total = dot(term, jnp.concatenate(weight, axis=0))
        out_ref[:, at] = total.astype(out_ref.dtype)
        out = pltpu.make_async_copy(
            out_ref.at[:, at], crossed_ref.at[:, at], sems.at[len(outs)]
        )
        out.start()
        outs.append(out)
    for out in outs:
        out.wait()


def project(terms, own, beside, firsts, seconds):
    rows, width = terms[0].shape[0], beside.shape[1]
    operands = (*terms, own, beside, *firsts, *seconds)
    return pl.pallas_call(
        functools.partial(project_kernel, len(terms)),
        out_shape=jax.ShapeDtypeStruct((rows, width), jnp.bfloat16),
        in_specs=[VMEM] * len(operands),
        out_specs=ANY,
        scratch_shapes=[
            pltpu.VMEM((rows, width), jnp.bfloat16),
            pltpu.SemaphoreType.DMA((width // min(512, width // 2),)),
        ],
        compiler_params=PARAMS,
        cost_estimate=takes(3),
    )(*operands)


def shards(queries, keys, values, cross_queries, nbr_keys, nbr_values, nbr_slot, w_cross):
    ctx = lax.axis_index("ctx")
    count = lax.axis_size("ctx")
    tp = lax.axis_index("tp").reshape(1)
    groups = lax.axis_size("tp")
    side = (ctx & 1).reshape(1)
    pair = (ctx >> 1).reshape(1)
    left = ctx & 1 == 0
    pairs = count // 2
    rows = queries.shape[0]
    depth = w_cross.shape[0]
    width = w_cross.shape[1] // groups
    swap = [(i, i ^ 1) for i in range(count)]
    across = [[(i, i ^ step) for i in range(groups)] for step in range(groups)]

    def both(mine, other, axis):
        return jnp.where(
            left,
            jnp.concatenate([mine, other], axis),
            jnp.concatenate([other, mine], axis),
        )

    half = width // 2
    far = range(2, groups)
    asking, asked_mine, _ = cut(
        side, tp, (cross_queries,), [[(0, 1 - own, 0, 0, HD, rows)] for own in range(2)]
    )
    asked_other = lax.ppermute(asking, "ctx", swap)
    held, length = nbr_keys.shape[:2]
    nbrs = (nbr_keys.reshape(held * length, -1), nbr_values.reshape(held * length, -1))
    away, mine, nbr_away, nbr_mine, *blocks, cut_mark = cut(
        side, tp, (queries, keys, values, *nbrs, w_cross),
        [[(at, 1 - own, 0, 0, HD, rows) for at in range(3)] for own in range(2)]
        + [[(at, 1 - own, 0, 0, HD, held * length) for at in (3, 4)] for own in range(2)]
        + [[(5, step, width, 0, half, depth)] for step in far],
    )
    other = lax.ppermute(away, "ctx", swap)
    nbr_other = lax.ppermute(nbr_away, "ctx", swap)
    slot_other = lax.ppermute(nbr_slot, "ctx", swap)
    firsts = [lax.ppermute(block, "tp", across[step]) for step, block in zip(far, blocks)]
    own, beside, *blocks, late_mark = cut(
        side, tp, (w_cross,),
        [[(0, step, width, 0, width, depth)] for step in range(2)]
        + [[(0, step, width, half, half, depth)] for step in far],
        (other,),
    )
    beside = lax.ppermute(beside, "tp", across[1])
    seconds = [lax.ppermute(block, "tp", across[step]) for step, block in zip(far, blocks)]

    sides = [list(range(start, count, 2)) for start in range(2)]

    def exchange(value):
        return lax.all_to_all(
            value, "ctx", split_axis=0, concat_axis=0, axis_index_groups=sides, tiled=True
        )

    asked = exchange(spread(side, asked_mine, asked_other, pairs, (cut_mark,)))

    forward = [(i, i + 2) for i in range(count - 2)]
    kv = jnp.concatenate([mine[:, HD:], other[:, HD:]], axis=0)
    kvs = [kv]
    while len(kvs) < pairs:
        kvs.append(lax.ppermute(kvs[-1], "ctx", forward))
    middle = (pairs + 1) // 2
    *state, mark = self_steps(pair, side, mine, other, kvs[:middle], None, 0, False, (late_mark,))
    before = (*firsts, mark)
    answers = hold(nbr_slot, slot_other, nbr_mine, nbr_other, asked, before)
    parts = exchange(answers)
    ours, theirs = self_steps(pair, side, mine, other, kvs[middle:], state, middle, True, ())
    attended = both(ours, lax.ppermute(theirs, "ctx", swap), 1)

    keep, give = combine(pair, side, parts, 2 * rows)
    cca = both(keep, lax.ppermute(give, "ctx", swap), 1)
    terms = [cca] + [lax.ppermute(cca, "tp", across[step]) for step in range(1, groups)]
    crossed = project(terms, own, beside, firsts, seconds)
    return (attended, crossed)


def solution(mesh):
    in_specs = (
        P("ctx", "tp"),
        P("ctx", "tp"),
        P("ctx", "tp"),
        P("ctx", "tp"),
        P("ctx", None, "tp"),
        P("ctx", None, "tp"),
        P("ctx"),
        P("tp", None),
    )
    out_specs = (P("ctx", "tp"), P("ctx", "tp"))
    return jax.shard_map(shards, mesh=mesh, in_specs=in_specs, out_specs=out_specs, check_vma=False)
```

time: 115 us -> 111 us (0.965)
  starting transfers between devices: 44.2 us -> 33.7 us
  waiting for transfers between devices: 38.1 us -> 46 us
  local copies, waits for them, and re-layouts: 3.8 us -> 7.63 us
  Pallas kernels: 24.5 us -> 20.9 us
  other arithmetic: 2.93 us -> 0.75 us
    ppermute x18 -> x9, starting transfers between devices: 35.2 us -> 19.5 us  [the longest x3 15.4 us: shards(): kvs.append(lax.ppermute(kvs[-1], 'ctx', forward))]
    ppermute x4, waiting for transfers between devices: 8.2 us -> 23.3 us  [shards(): lax.ppermute(block, 'tp', across[step])]
    all_to_all x0 -> x2, starting transfers between devices: none -> 9.11 us  [exchange(): lax.all_to_all(value, 'ctx', split_axis=0, concat_axis=0, axis_index_grou...]
    ppermute x18 -> x9, waiting for transfers between devices: 16.1 us -> 22.6 us  [the longest x3 17.8 us: shards(): kvs.append(lax.ppermute(kvs[-1], 'ctx', forward))]
    ppermute x1, waiting for transfers between devices: 6.52 us -> 0.01 us  [shards(): other = lax.ppermute(away, 'ctx', swap)]
    ppermute x1, waiting for transfers between devices: 6.17 us -> 0.01 us  [shards(): slot_other = lax.ppermute(nbr_slot, 'ctx', swap)]
    unnamed x16 -> x32, local copies, waits for them, and re-layouts: 3.11 us -> 7.61 us
    pallas_call x7 -> x5, Pallas kernels: 15.1 us -> 11.9 us  [the longest x1 5.76 us: hold(): pl.pallas_call(hold_kernel, out_shape=jax.ShapeDtypeStruct((pairs, ENTRIE...]
  transfers between devices with their start and end apart: 26 -> 19, of which waited for: 11 -> 9; matrix products, arithmetic and copies ran while one was open for 1% -> 1% of each run, Pallas kernels for 19% -> 9%
where the time goes in v6:
time: 111 us; the launch traced here: 110 us
  waiting for transfers between devices  46 us (41%)
  starting transfers between devices  33.7 us (30%)
  Pallas kernels  20.9 us (19%)
  local copies, waits for them, and re-layouts  7.63 us (7%)
    ppermute x4, waiting for transfers between devices, shards(): lax.ppermute(block, 'tp', across[step])  23.3 us
    ppermute x3, waiting for transfers between devices, shards(): kvs.append(lax.ppermute(kvs[-1], 'ctx', forward))  17.8 us
    ppermute x3, starting transfers between devices, shards(): kvs.append(lax.ppermute(kvs[-1], 'ctx', forward))  15.4 us
    all_to_all x2, starting transfers between devices, exchange(): lax.all_to_all(value, 'ctx', split_axis=0, concat_axis=0, axis_index_grou...  9.11 us
    pallas_call x3, Pallas kernels, cut(): pl.pallas_call(functools.partial(cut_kernel, plan), out_shape=tuple(shape...  8.33 us
    unnamed x32, local copies, waits for them, and re-layouts  7.61 us
    pallas_call x1, Pallas kernels, hold(): pl.pallas_call(hold_kernel, out_shape=jax.ShapeDtypeStruct((pairs, ENTRIE...  5.76 us
    ppermute x3, waiting for transfers between devices, shards(): lax.ppermute(cca, 'tp', across[step])  4.86 us
  transfers between devices with their start and end apart: 19, of which 9 were waited for; matrix products, arithmetic and copies ran while one was open for 1% of the time, Pallas kernels for 9%

profile of v6, /device:TPU:0, one launch (start us, length us, event | category | flops | bytes accessed | tf_op | source)
XLA Modules:
  0.0 109.8 jit_solution(10495595211060208554)
XLA Ops:
  0.6 1.5 %shard_map.99 = (bf16[256,128]{1,0:T(8,128)(2,1)}, bf16[256,128]{1,0:T(8,128)(2,1)}, f32[8,128]{1,0:T(8,128)}) custom-call(s32[1]{0:T(128)} %bitcast.1.side_ref, s32[1]{0:T(128)} %bitcast.2.tp_ref, bf16[256,256]{1,0:T(8,128)(2,1)} %refs_0_.5), custom_call_target="tpu_custom_call" | custom-call | flops 2000000000 | tf_op jit(solution)/shard_map/pallas_call | solution.py:73
  2.2 0.0 copy-start.7
  2.2 3.0 %collective-permute-start.7 = (bf16[256,128]{1,0:T(8,128)(2,1)}, bf16[256,128]{1,0:T(8,128)(2,1)S(1)}, u32[]{:S(2)}, u32[]{:S(2)}) collective-permute-start(bf16[256,128]{1,0:T(8,128)(2,1)} %get-tuple-element.35), channel_id=1, source_target_pairs={{0,4},{4,0},{8,12},{12,8},{16,20},{20,16},{24,28},{28,24},{1,5},{5... | collective-permute-start | bytes 196616 | tf_op jit(solution)/shard_map/ppermute | solution.py:400
  5.2 3.3 %shard_map.95 = (bf16[256,384]{1,0:T(8,128)(2,1)}, bf16[256,384]{1,0:T(8,128)(2,1)}, bf16[1024,256]{1,0:T(8,128)(2,1)}, bf16[1024,256]{1,0:T(8,128)(2,1)}, bf16[...) custom-call(s32[1]{0:T(128)} %bitcast.1.side_ref, s32[1]{0:T(128)} %bitcast.2.tp_ref, ...), custom_call_target="tpu_custom_call" | custom-call | flops 2000000000 | tf_op jit(solution)/shard_map/pallas_call | solution.py:73
  8.5 0.0 copy-start
  8.5 0.0 copy-start.4
  8.5 0.1 collective-permute-start
  8.6 0.0 collective-permute-done.7.other_ref
  8.6 0.0 copy-done.7
  8.6 0.0 copy-start.14
  8.6 0.7 copy-done.14
  9.3 0.9 shard_map.100
  10.2 5.3 %all-to-all-start = ((bf16[4,512,128]{2,1,0:T(8,128)(2,1)}), bf16[4,512,128]{2,1,0:T(8,128)(2,1)S(1)}, u32[]{:S(2)}, u32[]{:S(2)}) async-start(bf16[4,512,128]{2,1,0:T(8,128)(2,1)} %shard_map.100), calls=%async_computation | async-start | bytes 1048576 | tf_op jit(solution)/shard_map/all_to_all | solution.py:425
  15.5 0.0 copy-done
  15.5 0.0 collective-permute-done.refs_1_.other_ref
  15.6 3.9 %collective-permute-start.1 = (bf16[512,256]{1,0:T(8,128)(2,1)S(1)}, bf16[512,256]{1,0:T(8,128)(2,1)S(1)}, u32[]{:S(2)}, u32[]{:S(2)}) collective-permute-start(bf16[512,256]{1,0:T(8,128)(2,1)S(1)} %pad_maximum_fusion.refs_0_), channel_id=1, source_target_pairs={{0,8},{4,12},{8,16},{12,20},{16,24},{20,28},{1,9},{5,13},{9,17},{1... | collective-permute-start | bytes 786440 | tf_op jit(solution)/shard_map/ppermute | solution.py:435
  19.5 1.6 %collective-permute-start.6 = (bf16[1024,256]{1,0:T(8,128)(2,1)}, bf16[1024,256]{1,0:T(8,128)(2,1)S(1)}, u32[]{:S(2)}, u32[]{:S(2)}) collective-permute-start(bf16[1024,256]{1,0:T(8,128)(2,1)} %get-tuple-element.33), channel_id=1, source_target_pairs={{0,4},{4,0},{8,12},{12,8},{16,20},{20,16},{24,28},{28,24},{1,5},{5... | collective-permute-start | bytes 1572872 | tf_op jit(solution)/shard_map/ppermute | solution.py:410
  21.1 1.5 %collective-permute-start.8 = (bf16[256,1024]{1,0:T(8,128)(2,1)}, bf16[256,1024]{1,0:T(8,128)(2,1)S(1)}, u32[]{:S(2)}, u32[]{:S(2)}) collective-permute-start(bf16[256,1024]{1,0:T(8,128)(2,1)} %get-tuple-element.37), channel_id=1, source_target_pairs={{0,2},{1,3},{2,0},{3,1},{4,6},{5,7},{6,4},{7,5},{8,10},{9,11},{10,... | collective-permute-start | bytes 1572872 | tf_op jit(solution)/shard_map/ppermute | solution.py:412
  22.6 0.0 collective-permute-start.9
  22.6 0.5 collective-permute-start.5
  23.1 3.5 %shard_map.96 = (bf16[256,2048]{1,0:T(8,128)(2,1)}, bf16[256,2048]{1,0:T(8,128)(2,1)}, bf16[256,1024]{1,0:T(8,128)(2,1)}, bf16[256,1024]{1,0:T(8,128)(2,1)}, f32[8,128]{1,0:T(8,128)}) custom-call(s32[1]{0:T(128)} %bitcast.1.side_ref, s32[1]{0:T(128)} %bitcast.2.tp_ref, bf16[256,8192]{1,0:T(8,128)(2,1)} %refs_0_.4, bf16[256,384]{1,0:T(8,128)(2,1)} %copy-done.1), custom_call_target="tpu_custom_call" | custom-call | flops 2000000000 | tf_op jit(solution)/shard_map/pallas_call | solution.py:73
  26.7 2.5 %collective-permute-done.1.refs_1_ = bf16[512,256]{1,0:T(8,128)(2,1)S(1)} collective-permute-done((bf16[512,256]{1,0:T(8,128)(2,1)S(1)}, bf16[512,256]{1,0:T(8,128)(2,1)S(1)}, u32[]{:S(2)}, u32[]{:S(2)}) %collective-permute-start.1) | collective-permute-done | bytes 262176 | tf_op jit(solution)/shard_map/ppermute | solution.py:435
  29.2 0.9 copy-done.2
  30.1 0.7 copy-done.15
  30.8 1.0 shard_map.97
  31.8 0.7 copy-done.10
  32.4 0.7 copy-done.12
  33.2 0.0 collective-permute-done.5.other_ref
  33.2 0.0 collective-permute-done.6.kv_other
  33.2 3.0 %collective-permute-done.8.refs_0_.refs_6_ = bf16[256,1024]{1,0:T(8,128)(2,1)S(1)} collective-permute-done((bf16[256,1024]{1,0:T(8,128)(2,1)}, bf16[256,1024]{1,0:T(8,128)(2,1)S(1)}, u32[]{:S(2)}, u32[]{:S(2)}) %collective-permute-start.8) | collective-permute-done | bytes 524320 | tf_op jit(solution)/shard_map/ppermute | solution.py:412
  36.2 7.5 %collective-permute-done.9.refs_1_.refs_7_ = bf16[256,1024]{1,0:T(8,128)(2,1)S(1)} collective-permute-done((bf16[256,1024]{1,0:T(8,128)(2,1)}, bf16[256,1024]{1,0:T(8,128)(2,1)S(1)}, u32[]{:S(2)}, u32[]{:S(2)}) %collective-permute-start.9) | collective-permute-done | bytes 524320 | tf_op jit(solution)/shard_map/ppermute | solution.py:412
  43.7 0.0 all-to-all-done.queries_ref
  43.7 1.0 copy-done.5
  44.7 5.8 %shard_map.101 = bf16[4,576,128]{2,1,0:T(8,128)(2,1)} custom-call(s32[8]{0:T(128)S(1)} %copy-done.4, s32[8]{0:T(128)S(1)} %collective-permute-done.5.other_ref, bf16[1024,256]{1,0:T(8,128)(2,1)S(1)} %copy-done.5, bf16[1024,256]{1,0:T(8,128)(2,1)S(1)} %collective-permute-done.6.kv_other, bf16[4,512,128]{2,1,0:T(8,128)(2,1)S(1)} %all-to-all-done.queries_ref, ...), custom_call_target="tpu_custom_call" | custom-call | flops 3000000000 | tf_op jit(solution)/shard_map/pallas_call | solution.py:168
  50.5 0.0 copy-done.8
  50.5 3.8 %all-to-all-start.1 = ((bf16[4,576,128]{2,1,0:T(8,128)(2,1)}), bf16[4,576,128]{2,1,0:T(8,128)(2,1)S(1)}, u32[]{:S(2)}, u32[]{:S(2)}) async-start(bf16[4,576,128]{2,1,0:T(8,128)(2,1)} %shard_map.101), calls=%async_computation.1 | async-start | bytes 1179648 | tf_op jit(solution)/shard_map/all_to_all | solution.py:425
  54.2 4.6 %collective-permute-start.2 = (bf16[512,256]{1,0:T(8,128)(2,1)S(1)}, bf16[512,256]{1,0:T(8,128)(2,1)}, u32[]{:S(2)}, u32[]{:S(2)}) collective-permute-start(bf16[512,256]{1,0:T(8,128)(2,1)S(1)} %collective-permute-done.1.refs_1_), channel_id=1, source_target_pairs={{0,8},{4,12},{8,16},{12,20},{16,24},{20,28},{1,9},{5,13},{9,17},{1... | collective-permute-start | bytes 786440 | tf_op jit(solution)/shard_map/ppermute | solution.py:435
  58.9 0.0 collective-permute-start.14
  58.9 11.7 %collective-permute-done.2.refs_0_ = bf16[512,256]{1,0:T(8,128)(2,1)} collective-permute-done((bf16[512,256]{1,0:T(8,128)(2,1)S(1)}, bf16[512,256]{1,0:T(8,128)(2,1)}, u32[]{:S(2)}, u32[]{:S(2)}) %collective-permute-start.2) | collective-permute-done | bytes 262176 | tf_op jit(solution)/shard_map/ppermute | solution.py:435
  70.5 6.8 %collective-permute-start.3 = (bf16[512,256]{1,0:T(8,128)(2,1)}, bf16[512,256]{1,0:T(8,128)(2,1)S(1)}, u32[]{:S(2)}, u32[]{:S(2)}) collective-permute-start(bf16[512,256]{1,0:T(8,128)(2,1)} %collective-permute-done.2.refs_0_), channel_id=1, source_target_pairs={{0,8},{4,12},{8,16},{12,20},{16,24},{20,28},{1,9},{5,13},{9,17},{1... | collective-permute-start | bytes 786440 | tf_op jit(solution)/shard_map/ppermute | solution.py:435
  77.3 0.6 collective-permute-start.15
  77.9 0.3 collective-permute-start.16
  78.2 0.0 all-to-all-done.1
  78.2 0.7 shard_map.102
  78.9 0.6 collective-permute-start.10
  79.5 3.6 %collective-permute-done.3.refs_1_ = bf16[512,256]{1,0:T(8,128)(2,1)S(1)} collective-permute-done((bf16[512,256]{1,0:T(8,128)(2,1)}, bf16[512,256]{1,0:T(8,128)(2,1)S(1)}, u32[]{:S(2)}, u32[]{:S(2)}) %collective-permute-start.3) | collective-permute-done | bytes 262176 | tf_op jit(solution)/shard_map/ppermute | solution.py:435
  83.1 0.9 copy-done.9
  84.0 0.9 copy-done.11
  85.0 0.9 copy-done.13
  86.0 1.1 %shard_map.98 = (bf16[256,128]{1,0:T(8,128)(2,1)S(1)}, bf16[256,128]{1,0:T(8,128)(2,1)S(1)}) custom-call(s32[1]{0:T(128)} %bitcast.pair_ref, s32[1]{0:T(128)} %bitcast.1.side_ref, bf16[256,384]{1,0:T(8,128)(2,1)S(1)} %copy-done, bf16[256,384]{1,0:T(8,128)(2,1)S(1)} %copy-done.3, bf16[512,256]{1,0:T(8,128)(2,1)} %collective-permute-done.2.refs_0_, ...), custom_call_target="tpu_custom_call" | custom-call | flops 3000000000 | tf_op jit(solution)/shard_map/pallas_call | solution.py:320
  87.1 0.6 collective-permute-start.4
  87.7 0.0 collective-permute-done.10
  87.7 0.1 collective-permute-start.11
  87.8 4.8 %collective-permute-done.15.refs_8_ = bf16[256,1024]{1,0:T(8,128)(2,1)} collective-permute-done((bf16[256,1024]{1,0:T(8,128)(2,1)}, bf16[256,1024]{1,0:T(8,128)(2,1)}, u32[]{:S(2)}, u32[]{:S(2)}) %collective-permute-start.15) | collective-permute-done | bytes 524320 | tf_op jit(solution)/shard_map/ppermute | solution.py:420
  92.6 0.4 collective-permute-start.12
  93.0 0.0 collective-permute-done.4
  93.0 0.0 collective-permute-start.13
  93.0 0.7 maximum_select_fusion
  93.7 8.1 %collective-permute-done.16.refs_9_ = bf16[256,1024]{1,0:T(8,128)(2,1)} collective-permute-done((bf16[256,1024]{1,0:T(8,128)(2,1)}, bf16[256,1024]{1,0:T(8,128)(2,1)}, u32[]{:S(2)}, u32[]{:S(2)}) %collective-permute-start.16) | collective-permute-done | bytes 524320 | tf_op jit(solution)/shard_map/ppermute | solution.py:420
  101.8 0.0 collective-permute-done.14.refs_5_
  101.8 0.0 collective-permute-done.11.refs_1_
  101.8 4.6 %collective-permute-done.12.refs_2_ = bf16[256,256]{1,0:T(8,128)(2,1)S(1)} collective-permute-done((bf16[256,256]{1,0:T(8,128)(2,1)S(1)}, bf16[256,256]{1,0:T(8,128)(2,1)S(1)}, u32[]{:S(2)}, u32[]{:S(2)}) %collective-permute-start.12) | collective-permute-done | bytes 131104 | tf_op jit(solution)/shard_map/ppermute | solution.py:446
  106.4 0.3 collective-permute-done.13.refs_3_
  106.6 3.2 %shard_map.103 = bf16[256,2048]{1,0:T(8,128)(2,1)} custom-call(bf16[256,256]{1,0:T(8,128)(2,1)S(1)} %maximum_select_fusion.1.refs_0_, bf16[256,256]{1,0:T(8,128)(2,1)S(1)} %collective-permute-done.11.refs_1_, bf16[256,256]{1,0:T(8,128)(2,1)S(1)} %collective-permute-done.12.refs_2_, bf16[256,256]{1,0:T(8,128)(2,1)S(1)} %collective-permute-done.13.refs_3_, ...), custom_call_target="tpu_custom_call" | custom-call | flops 3000000000 | tf_op jit(solution)/shard_map/pallas_call | solution.py:359
  (20 shorter events, 0.1 us)
Async XLA Ops:
  2.2 6.4 %copy-start.7 = (bf16[256,128]{1,0:T(8,128)(2,1)S(1)}, bf16[256,128]{1,0:T(8,128)(2,1)}, u32[]{:S(2)}) copy-start(bf16[256,128]{1,0:T(8,128)(2,1)} %get-tuple-element.34.mine_ref) | copy-start | bytes 196612
  2.2 6.4 %collective-permute-start.7 = (bf16[256,128]{1,0:T(8,128)(2,1)}, bf16[256,128]{1,0:T(8,128)(2,1)S(1)}, u32[]{:S(2)}, u32[]{:S(2)}) collective-permute-start(bf16[256,128]{1,0:T(8,128)(2,1)} %get-tuple-element.35), channel_id=1, source_target_pairs={{0,4},{4,0},{8,12},{12,8},{16,20},{20,16},{24,28},{28,24},{1,5},{5... | collective-permute-start | bytes 196616 | tf_op jit(solution)/shard_map/ppermute | solution.py:400
  8.5 7.0 %copy-start = (bf16[256,384]{1,0:T(8,128)(2,1)S(1)}, bf16[256,384]{1,0:T(8,128)(2,1)}, u32[]{:S(2)}) copy-start(bf16[256,384]{1,0:T(8,128)(2,1)} %get-tuple-element.24.mine_ref) | copy-start | bytes 589828
  8.5 14.1 %copy-start.4 = (s32[8]{0:T(128)S(1)}, s32[8]{0:T(128)}, u32[]{:S(2)}) copy-start(s32[8]{0:T(128)} %own_ref.1) | copy-start | bytes 100
  8.5 7.0 %collective-permute-start = (bf16[256,384]{1,0:T(8,128)(2,1)}, bf16[256,384]{1,0:T(8,128)(2,1)S(1)}, u32[]{:S(2)}, u32[]{:S(2)}) collective-permute-start(bf16[256,384]{1,0:T(8,128)(2,1)} %get-tuple-element.25), channel_id=1, source_target_pairs={{0,4},{4,0},{8,12},{12,8},{16,20},{20,16},{24,28},{28,24},{1,5},{5... | collective-permute-start | bytes 589832 | tf_op jit(solution)/shard_map/ppermute | solution.py:409
  8.6 0.7 copy-start.14
  10.2 33.5 %all-to-all-start = ((bf16[4,512,128]{2,1,0:T(8,128)(2,1)}), bf16[4,512,128]{2,1,0:T(8,128)(2,1)S(1)}, u32[]{:S(2)}, u32[]{:S(2)}) async-start(bf16[4,512,128]{2,1,0:T(8,128)(2,1)} %shard_map.100), calls=%async_computation | async-start | bytes 1048576 | tf_op jit(solution)/shard_map/all_to_all | solution.py:425
  15.5 7.6 %copy-start.1 = (bf16[256,384]{1,0:T(8,128)(2,1)}, bf16[256,384]{1,0:T(8,128)(2,1)S(1)}, u32[]{:S(2)}) copy-start(bf16[256,384]{1,0:T(8,128)(2,1)S(1)} %collective-permute-done.refs_1_.other_ref) | copy-start | bytes 589828
  15.6 13.6 %collective-permute-start.1 = (bf16[512,256]{1,0:T(8,128)(2,1)S(1)}, bf16[512,256]{1,0:T(8,128)(2,1)S(1)}, u32[]{:S(2)}, u32[]{:S(2)}) collective-permute-start(bf16[512,256]{1,0:T(8,128)(2,1)S(1)} %pad_maximum_fusion.refs_0_), channel_id=1, source_target_pairs={{0,8},{4,12},{8,16},{12,20},{16,24},{20,28},{1,9},{5,13},{9,17},{1... | collective-permute-start | bytes 786440 | tf_op jit(solution)/shard_map/ppermute | solution.py:435
  19.5 13.6 %collective-permute-start.6 = (bf16[1024,256]{1,0:T(8,128)(2,1)}, bf16[1024,256]{1,0:T(8,128)(2,1)S(1)}, u32[]{:S(2)}, u32[]{:S(2)}) collective-permute-start(bf16[1024,256]{1,0:T(8,128)(2,1)} %get-tuple-element.33), channel_id=1, source_target_pairs={{0,4},{4,0},{8,12},{12,8},{16,20},{20,16},{24,28},{28,24},{1,5},{5... | collective-permute-start | bytes 1572872 | tf_op jit(solution)/shard_map/ppermute | solution.py:410
  21.1 15.1 %collective-permute-start.8 = (bf16[256,1024]{1,0:T(8,128)(2,1)}, bf16[256,1024]{1,0:T(8,128)(2,1)S(1)}, u32[]{:S(2)}, u32[]{:S(2)}) collective-permute-start(bf16[256,1024]{1,0:T(8,128)(2,1)} %get-tuple-element.37), channel_id=1, source_target_pairs={{0,2},{1,3},{2,0},{3,1},{4,6},{5,7},{6,4},{7,5},{8,10},{9,11},{10,... | collective-permute-start | bytes 1572872 | tf_op jit(solution)/shard_map/ppermute | solution.py:412
  22.6 21.1 %collective-permute-start.9 = (bf16[256,1024]{1,0:T(8,128)(2,1)}, bf16[256,1024]{1,0:T(8,128)(2,1)S(1)}, u32[]{:S(2)}, u32[]{:S(2)}) collective-permute-start(bf16[256,1024]{1,0:T(8,128)(2,1)} %get-tuple-element.38), channel_id=1, source_target_pairs={{0,3},{1,2},{2,1},{3,0},{4,7},{5,6},{6,5},{7,4},{8,11},{9,10},{10,... | collective-permute-start | bytes 1572872 | tf_op jit(solution)/shard_map/ppermute | solution.py:412
  22.6 10.5 %collective-permute-start.5 = (s32[8]{0:T(128)S(1)}, s32[8]{0:T(128)S(1)}, u32[]{:S(2)}, u32[]{:S(2)}) collective-permute-start(s32[8]{0:T(128)S(1)} %copy-done.4), channel_id=1, source_target_pairs={{0,4},{4,0},{8,12},{12,8},{16,20},{20,16},{24,28},{28,24},{1,5},{5... | collective-permute-start | bytes 104 | tf_op jit(solution)/shard_map/ppermute | solution.py:411
  29.2 0.9 copy-start.2
  30.1 0.7 copy-start.15
  31.7 0.7 copy-start.10
  32.4 0.7 copy-start.12
  33.2 17.3 %copy-start.8 = (f32[512,128]{1,0:T(8,128)}, f32[512,128]{1,0:T(8,128)S(1)}, u32[]{:S(2)}) copy-start(f32[512,128]{1,0:T(8,128)S(1)} %get-tuple-element.27.refs_2_) | copy-start | bytes 786436
  43.7 1.0 copy-start.5
  50.5 32.6 %copy-start.3 = (bf16[256,384]{1,0:T(8,128)(2,1)S(1)}, bf16[256,384]{1,0:T(8,128)(2,1)}, u32[]{:S(2)}) copy-start(bf16[256,384]{1,0:T(8,128)(2,1)} %copy-done.1) | copy-start | bytes 589828
  50.5 27.7 %all-to-all-start.1 = ((bf16[4,576,128]{2,1,0:T(8,128)(2,1)}), bf16[4,576,128]{2,1,0:T(8,128)(2,1)S(1)}, u32[]{:S(2)}, u32[]{:S(2)}) async-start(bf16[4,576,128]{2,1,0:T(8,128)(2,1)} %shard_map.101), calls=%async_computation.1 | async-start | bytes 1179648 | tf_op jit(solution)/shard_map/all_to_all | solution.py:425
  54.2 16.3 %collective-permute-start.2 = (bf16[512,256]{1,0:T(8,128)(2,1)S(1)}, bf16[512,256]{1,0:T(8,128)(2,1)}, u32[]{:S(2)}, u32[]{:S(2)}) collective-permute-start(bf16[512,256]{1,0:T(8,128)(2,1)S(1)} %collective-permute-done.1.refs_1_), channel_id=1, source_target_pairs={{0,8},{4,12},{8,16},{12,20},{16,24},{20,28},{1,9},{5,13},{9,17},{1... | collective-permute-start | bytes 786440 | tf_op jit(solution)/shard_map/ppermute | solution.py:435
  58.9 42.9 %collective-permute-start.14 = (bf16[256,2048]{1,0:T(8,128)(2,1)}, bf16[256,2048]{1,0:T(8,128)(2,1)S(1)}, u32[]{:S(2)}, u32[]{:S(2)}) collective-permute-start(bf16[256,2048]{1,0:T(8,128)(2,1)} %get-tuple-element.43), channel_id=1, source_target_pairs={{0,1},{1,0},{2,3},{3,2},{4,5},{5,4},{6,7},{7,6},{8,9},{9,8},{10,11... | collective-permute-start | bytes 3145736 | tf_op jit(solution)/shard_map/ppermute | solution.py:419
  70.5 12.6 %collective-permute-start.3 = (bf16[512,256]{1,0:T(8,128)(2,1)}, bf16[512,256]{1,0:T(8,128)(2,1)S(1)}, u32[]{:S(2)}, u32[]{:S(2)}) collective-permute-start(bf16[512,256]{1,0:T(8,128)(2,1)} %collective-permute-done.2.refs_0_), channel_id=1, source_target_pairs={{0,8},{4,12},{8,16},{12,20},{16,24},{20,28},{1,9},{5,13},{9,17},{1... | collective-permute-start | bytes 786440 | tf_op jit(solution)/shard_map/ppermute | solution.py:435
  77.3 15.2 %collective-permute-start.15 = (bf16[256,1024]{1,0:T(8,128)(2,1)}, bf16[256,1024]{1,0:T(8,128)(2,1)}, u32[]{:S(2)}, u32[]{:S(2)}) collective-permute-start(bf16[256,1024]{1,0:T(8,128)(2,1)} %get-tuple-element.44), channel_id=1, source_target_pairs={{0,2},{1,3},{2,0},{3,1},{4,6},{5,7},{6,4},{7,5},{8,10},{9,11},{10,... | collective-permute-start | bytes 1572872 | tf_op jit(solution)/shard_map/ppermute | solution.py:420
  77.9 23.8 %collective-permute-start.16 = (bf16[256,1024]{1,0:T(8,128)(2,1)}, bf16[256,1024]{1,0:T(8,128)(2,1)}, u32[]{:S(2)}, u32[]{:S(2)}) collective-permute-start(bf16[256,1024]{1,0:T(8,128)(2,1)} %get-tuple-element.45), channel_id=1, source_target_pairs={{0,3},{1,2},{2,1},{3,0},{4,7},{5,6},{6,5},{7,4},{8,11},{9,10},{10,... | collective-permute-start | bytes 1572872 | tf_op jit(solution)/shard_map/ppermute | solution.py:420
  78.9 8.8 %collective-permute-start.10 = (bf16[256,128]{1,0:T(8,128)(2,1)S(1)}, bf16[256,128]{1,0:T(8,128)(2,1)S(1)}, u32[]{:S(2)}, u32[]{:S(2)}) collective-permute-start(bf16[256,128]{1,0:T(8,128)(2,1)S(1)} %get-tuple-element.41), channel_id=1, source_target_pairs={{0,4},{4,0},{8,12},{12,8},{16,20},{20,16},{24,28},{28,24},{1,5},{5... | collective-permute-start | bytes 196616 | tf_op jit(solution)/shard_map/ppermute | solution.py:445
  83.1 1.0 copy-start.9
  84.0 0.9 copy-start.11
  85.0 0.9 copy-start.13
  85.9 20.7 %copy-start.6 = (bf16[256,2048]{1,0:T(8,128)(2,1)S(1)}, bf16[256,2048]{1,0:T(8,128)(2,1)}, u32[]{:S(2)}) copy-start(bf16[256,2048]{1,0:T(8,128)(2,1)} %get-tuple-element.42.refs_4_) | copy-start | bytes 3145732
  87.1 5.9 %collective-permute-start.4 = (bf16[256,128]{1,0:T(8,128)(2,1)S(1)}, bf16[256,128]{1,0:T(8,128)(2,1)S(1)}, u32[]{:S(2)}, u32[]{:S(2)}) collective-permute-start(bf16[256,128]{1,0:T(8,128)(2,1)S(1)} %get-tuple-element.31), channel_id=1, source_target_pairs={{0,4},{4,0},{8,12},{12,8},{16,20},{20,16},{24,28},{28,24},{1,5},{5... | collective-permute-start | bytes 196616 | tf_op jit(solution)/shard_map/ppermute | solution.py:442
  87.7 14.1 %collective-permute-start.11 = (bf16[256,256]{1,0:T(8,128)(2,1)S(1)}, bf16[256,256]{1,0:T(8,128)(2,1)S(1)}, u32[]{:S(2)}, u32[]{:S(2)}) collective-permute-start(bf16[256,256]{1,0:T(8,128)(2,1)S(1)} %maximum_select_fusion.1.refs_0_), channel_id=1, source_target_pairs={{0,1},{1,0},{2,3},{3,2},{4,5},{5,4},{6,7},{7,6},{8,9},{9,8},{10,11... | collective-permute-start | bytes 393224 | tf_op jit(solution)/shard_map/ppermute | solution.py:446
  92.6 13.8 %collective-permute-start.12 = (bf16[256,256]{1,0:T(8,128)(2,1)S(1)}, bf16[256,256]{1,0:T(8,128)(2,1)S(1)}, u32[]{:S(2)}, u32[]{:S(2)}) collective-permute-start(bf16[256,256]{1,0:T(8,128)(2,1)S(1)} %maximum_select_fusion.1.refs_0_), channel_id=1, source_target_pairs={{0,2},{1,3},{2,0},{3,1},{4,6},{5,7},{6,4},{7,5},{8,10},{9,11},{10,... | collective-permute-start | bytes 393224 | tf_op jit(solution)/shard_map/ppermute | solution.py:446
  93.0 13.6 %collective-permute-start.13 = (bf16[256,256]{1,0:T(8,128)(2,1)S(1)}, bf16[256,256]{1,0:T(8,128)(2,1)S(1)}, u32[]{:S(2)}, u32[]{:S(2)}) collective-permute-start(bf16[256,256]{1,0:T(8,128)(2,1)S(1)} %maximum_select_fusion.1.refs_0_), channel_id=1, source_target_pairs={{0,3},{1,2},{2,1},{3,0},{4,7},{5,6},{6,5},{7,4},{8,11},{9,10},{10,... | collective-permute-start | bytes 393224 | tf_op jit(solution)/shard_map/ppermute | solution.py:446

commit v7 on v3

v7 whole, which is shorter than its diff:
```python
import functools
import math

import jax
import jax.numpy as jnp
from jax import lax
from jax.experimental import pallas as pl
from jax.experimental.pallas import tpu as pltpu
from jax.sharding import PartitionSpec as P

HD = 128
BLOCK = 64
LEAD = 16
NEGATIVE = -1e30
SCALE = HD ** -0.5 * math.log2(math.e)
VMEM = pl.BlockSpec(memory_space=pltpu.VMEM)
SMEM = pl.BlockSpec(memory_space=pltpu.SMEM)
ANY = pl.BlockSpec(memory_space=pl.ANY)
PARAMS = pltpu.CompilerParams(vmem_limit_bytes=16 * 1024 * 1024)


def takes(microseconds):
    return pl.CostEstimate(
        flops=microseconds * 1000000000, bytes_accessed=0, transcendentals=0
    )


def dot(a, b):
    return jnp.dot(a, b, preferred_element_type=jnp.float32)


def dot_t(a, b):
    return lax.dot_general(a, b, (((1,), (1,)), ((), ())), preferred_element_type=jnp.float32)


def fetch(pieces, sems):
    copies = [
        pltpu.make_async_copy(source, target, sems.at[at])
        for at, (source, target) in enumerate(pieces)
    ]
    for copy in copies:
        copy.start()
    for copy in copies:
        copy.wait()


def cut_kernel(plan, side_ref, tp_ref, *refs):
    mark_ref, sems, refs = refs[-2], refs[-1], refs[:-2]
    sources, outs = refs, refs[len(refs) - len(plan) :]
    mark_ref[...] = jnp.zeros(mark_ref.shape, jnp.float32)
    pieces = []
    for out, parts in zip(outs, plan):
        for at, (index, step, total, offset, width, depth) in enumerate(parts):
            source = sources[index]
            key = tp_ref[0] if total else side_ref[0]
            lane = pl.multiple_of((key ^ step) * (total or HD) + offset, HD)
            row = pl.multiple_of(side_ref[0] * depth, LEAD) if depth < source.shape[0] else 0
            piece = source.at[pl.ds(row, depth), pl.ds(lane, width)]
            pieces.append((piece, out.at[:, pl.ds(at * width, width)]))
    fetch(pieces, sems)


def cut(side, tp, sources, plan, before=()):
    shapes = []
    for parts in plan:
        shape = (parts[0][5], len(parts) * parts[0][4])
        shapes.append(jax.ShapeDtypeStruct(shape, sources[parts[0][0]].dtype))
    shapes.append(jax.ShapeDtypeStruct((8, HD), jnp.float32))
    return pl.pallas_call(
        functools.partial(cut_kernel, plan),
        out_shape=tuple(shapes),
        in_specs=[SMEM] * 2 + [ANY] * (len(sources) + len(before)),
        out_specs=(VMEM,) * len(shapes),
        scratch_shapes=[pltpu.SemaphoreType.DMA((sum(len(parts) for parts in plan),))],
        cost_estimate=takes(2),
    )(side, tp, *sources, *before)


def stack_kernel(one_ref, two_ref, kv_ref, mark_ref):
    rows = one_ref.shape[0]
    kv_ref[:rows, :] = one_ref[...]
    kv_ref[rows:, :] = two_ref[...]
    mark_ref[...] = jnp.zeros(mark_ref.shape, jnp.float32)


def stack(one, two):
    rows, width = one.shape
    return pl.pallas_call(
        stack_kernel,
        out_shape=(
            jax.ShapeDtypeStruct((2 * rows, width), one.dtype),
            jax.ShapeDtypeStruct((8, HD), jnp.float32),
        ),
        in_specs=[VMEM] * 2,
        out_specs=(VMEM, VMEM),
        compiler_params=PARAMS,
    )(one, two)


def fence_kernel(held_ref, mark_ref, out_ref, value_ref):
    value_ref[...] = mark_ref[...]


def fence(held, mark):
    return pl.pallas_call(
        fence_kernel,
        out_shape=jax.ShapeDtypeStruct(held.shape, held.dtype),
        in_specs=[ANY, VMEM],
        out_specs=ANY,
        scratch_shapes=[pltpu.VMEM(mark.shape, mark.dtype)],
        input_output_aliases={0: 0},
        cost_estimate=takes(5),
    )(held, mark)


def arrange_kernel(slot_ref, keys_ref, values_ref, out_ref, sems):
    count, length, width = keys_ref.shape
    pieces = []
    for n in range(count):
        owner = slot_ref[n] // count
        pieces.append((keys_ref.at[n], out_ref.at[owner, pl.ds(0, length)]))
        pieces.append((values_ref.at[n], out_ref.at[owner, pl.ds(length, length)]))
    for owner in range(out_ref.shape[0]):
        out_ref[owner, 2 * length :, :] = jnp.full((LEAD, width), -1, out_ref.dtype)
    for n in range(count):
        slot = slot_ref[n]
        owner = slot // count
        place = (slot - owner * count).astype(jnp.float32)
        out_ref[owner, 2 * length :, :] = jnp.full((LEAD, width), place).astype(out_ref.dtype)
    fetch(pieces, sems)


def arrange(slots, keys, values, owners):
    count, length, width = keys.shape
    return pl.pallas_call(
        arrange_kernel,
        out_shape=jax.ShapeDtypeStruct((owners, 2 * length + LEAD, width), keys.dtype),
        in_specs=[SMEM, ANY, ANY],
        out_specs=VMEM,
        scratch_shapes=[pltpu.SemaphoreType.DMA((2 * count,))],
        cost_estimate=takes(3),
    )(slots, keys, values)


def find_sources(incoming_ref, order_ref):
    rows = incoming_ref.shape[1]
    for source in range(incoming_ref.shape[0]):
        place = incoming_ref[source, rows - LEAD :, :HD].astype(jnp.float32)
        place = jnp.max(place).astype(jnp.int32)

        @pl.when(place >= 0)
        def _():
            order_ref[place] = source


def block_answer(order_ref, incoming_ref, block, feats, q):
    first = order_ref[2 * block]
    second = order_ref[2 * block + 1]
    length = (incoming_ref.shape[1] - LEAD) // 2
    s1 = dot_t(q, incoming_ref[first, :length, feats])
    s2 = dot_t(q, incoming_ref[second, :length, feats])
    peak = jnp.maximum(jnp.max(s1, axis=1, keepdims=True), jnp.max(s2, axis=1, keepdims=True))
    p1 = jnp.exp2((s1 - peak) * SCALE)
    p2 = jnp.exp2((s2 - peak) * SCALE)
    total = jnp.sum(p1, axis=1, keepdims=True) + jnp.sum(p2, axis=1, keepdims=True)
    mixed = dot(p1.astype(jnp.bfloat16), incoming_ref[first, length : 2 * length, feats])
    mixed += dot(p2.astype(jnp.bfloat16), incoming_ref[second, length : 2 * length, feats])
    return (mixed / total).astype(jnp.bfloat16)


def last_kernel(queries_ref, spill_ref, incoming_ref, tail_ref, next_ref, order_ref):
    find_sources(incoming_ref, order_ref)
    rows, width = queries_ref.shape
    last = rows // BLOCK - 1
    for head in range(width // HD):
        feats = pl.ds(head * HD, HD)
        q = jnp.concatenate([queries_ref[rows - LEAD :, feats], spill_ref[:BLOCK, feats]], axis=0)
        answer = block_answer(order_ref, incoming_ref, last, feats, q)
        tail_ref[:, feats] = answer[:LEAD]
        next_ref[:, feats] = answer[LEAD:]


def other_kernel(queries_ref, tail_ref, incoming_ref, out_ref, order_ref):
    find_sources(incoming_ref, order_ref)
    rows, width = queries_ref.shape
    blocks = rows // BLOCK
    row = lax.broadcasted_iota(jnp.int32, (LEAD, HD), 0)
    for head in range(width // HD):
        feats = pl.ds(head * HD, HD)
        before = jnp.zeros((LEAD, HD), jnp.bfloat16)
        out_ref[: BLOCK - LEAD, feats] = jnp.zeros((BLOCK - LEAD, HD), jnp.bfloat16)
        for block in range(blocks):
            start = (block + 1) * BLOCK - LEAD
            if block < blocks - 1:
                q = queries_ref[start : start + BLOCK + LEAD, feats]
                answer = block_answer(order_ref, incoming_ref, block, feats, q)
                head_rows = answer[:LEAD]
                out_ref[start + LEAD : start + BLOCK, feats] = answer[LEAD:BLOCK]
            else:
                head_rows = tail_ref[:, feats]
            out_ref[start : start + LEAD, feats] = jnp.where(row == LEAD - 1, head_rows, before)
            if block < blocks - 1:
                before = answer[BLOCK:]


def order_scratch(rows):
    return [pltpu.SMEM((2 * rows // BLOCK,), jnp.int32)]


def last_attend(queries, spill, incoming):
    rows, width = queries.shape
    return pl.pallas_call(
        last_kernel,
        out_shape=(
            jax.ShapeDtypeStruct((LEAD, width), queries.dtype),
            jax.ShapeDtypeStruct((BLOCK, width), queries.dtype),
        ),
        in_specs=[VMEM] * 3,
        out_specs=(VMEM, VMEM),
        scratch_shapes=order_scratch(rows),
        compiler_params=PARAMS,
        cost_estimate=takes(1),
    )(queries, spill, incoming)


def other_attend(queries, tail, incoming):
    return pl.pallas_call(
        other_kernel,
        out_shape=jax.ShapeDtypeStruct(queries.shape, queries.dtype),
        in_specs=[VMEM] * 3,
        out_specs=VMEM,
        scratch_shapes=order_scratch(queries.shape[0]),
        compiler_params=PARAMS,
        cost_estimate=takes(2),
    )(queries, tail, incoming)


def self_kernel(first, step, chunks, pair_ref, side_ref, *refs):
    queries, refs = refs[:2], refs[2:]
    held, refs = (refs[:2], refs[2:]) if first else (refs[:3], refs[3:])
    kvs, refs = refs[:chunks], refs[chunks:]
    peak_ref, total_ref, accum_ref = refs[-3:]
    outs = refs[-7:-3] if first else refs[-5:-3]
    tile = queries[0].shape[0]
    if first:
        outs[3][...] = jnp.zeros(outs[3].shape, jnp.float32)
    for part, q_ref in enumerate(queries):
        at = pl.ds(part * tile, tile)

        def attend(kv_ref, fresh):
            s = dot_t(q_ref[...], kv_ref[:, :HD])
            if fresh:
                row = lax.broadcasted_iota(jnp.int32, (tile, tile), 0)
                col = lax.broadcasted_iota(jnp.int32, (tile, tile), 1)
                s = jnp.where(col <= row, s, NEGATIVE)
            peak = jnp.max(s, axis=1, keepdims=True)
            if not fresh:
                old = peak_ref[at, :1]
                peak = jnp.maximum(peak, old)
                factor = jnp.exp2((old - peak) * SCALE)
            p = jnp.exp2((s - peak) * SCALE)
            total = jnp.sum(p, axis=1, keepdims=True)
            accum = dot(p.astype(jnp.bfloat16), kv_ref[:, HD:])
            if not fresh:
                total += total_ref[at, :1] * factor
                accum += accum_ref[at, :] * factor
            peak_ref[at, :] = jnp.broadcast_to(peak, (tile, HD))
            total_ref[at, :] = jnp.broadcast_to(total, (tile, HD))
            accum_ref[at, :] = accum

        if first:
            attend(held[part], True)
            pl.when((side_ref[0] ^ part) == 1)(
                functools.partial(attend, held[1 - part], False)
            )
        else:
            peak_ref[at, :] = held[0][at, :]
            total_ref[at, :] = held[1][at, :]
            accum_ref[at, :] = held[2][at, :]
        for index, kv_ref in enumerate(kvs):
            pl.when(pair_ref[0] >= step + index)(functools.partial(attend, kv_ref, False))
        if first:
            outs[0][at, :] = peak_ref[at, :]
            outs[1][at, :] = total_ref[at, :]
            outs[2][at, :] = accum_ref[at, :]
        else:
            outs[part][...] = (accum_ref[at, :] / total_ref[at, :]).astype(jnp.bfloat16)


def self_steps(pair, side, queries, held, kvs, step, first, before):
    tile = queries[0].shape[0]
    rows = 2 * tile
    if first:
        out_shape = (jax.ShapeDtypeStruct((rows, HD), jnp.float32),) * 3
        out_shape += (jax.ShapeDtypeStruct((8, HD), jnp.float32),)
    else:
        out_shape = (jax.ShapeDtypeStruct((tile, HD), jnp.bfloat16),) * 2
    operands = (*queries, *held, *kvs)
    return pl.pallas_call(
        functools.partial(self_kernel, first, step, len(kvs)),
        out_shape=out_shape,
        in_specs=[SMEM] * 2 + [VMEM] * len(operands) + [ANY] * len(before),
        out_specs=(VMEM,) * len(out_shape),
        scratch_shapes=[pltpu.VMEM((rows, HD), jnp.float32)] * 3,
        compiler_params=PARAMS,
        cost_estimate=takes(3),
    )(pair, side, *operands, *before)


def project_kernel(groups, *refs):
    crossed_ref, out_ref, sems = refs[-3:]
    terms, near, far = refs[:groups], refs[groups : groups + 2], refs[groups + 2 : -3]
    width = crossed_ref.shape[1]
    half = width // 2
    tile = min(512, half)
    term = jnp.concatenate([held[...] for held in terms], axis=1)
    outs = []
    for column in range(0, width, tile):
        at = slice(column, column + tile)
        blocks = far[: groups - 2] if column < half else far[groups - 2 :]
        start = column % half
        weight = [block[:, at] for block in near]
        weight += [block[:, start : start + tile] for block in blocks]
        total = dot(term, jnp.concatenate(weight, axis=0))
        out_ref[:, at] = total.astype(out_ref.dtype)
        out = pltpu.make_async_copy(
            out_ref.at[:, at], crossed_ref.at[:, at], sems.at[len(outs)]
        )
        out.start()
        outs.append(out)
    for out in outs:
        out.wait()


def project(terms, own, beside, firsts, seconds):
    rows, width = terms[0].shape[0], beside.shape[1]
    operands = (*terms, own, beside, *firsts, *seconds)
    return pl.pallas_call(
        functools.partial(project_kernel, len(terms)),
        out_shape=jax.ShapeDtypeStruct((rows, width), jnp.bfloat16),
        in_specs=[VMEM] * len(operands),
        out_specs=ANY,
        scratch_shapes=[
            pltpu.VMEM((rows, width), jnp.bfloat16),
            pltpu.SemaphoreType.DMA((width // min(512, width // 2),)),
        ],
        compiler_params=PARAMS,
        cost_estimate=takes(3),
    )(*operands)


def shards(queries, keys, values, cross_queries, nbr_keys, nbr_values, nbr_slot, w_cross):
    ctx = lax.axis_index("ctx")
    count = lax.axis_size("ctx")
    tp = lax.axis_index("tp").reshape(1)
    groups = lax.axis_size("tp")
    side = (ctx & 1).reshape(1)
    pair = (ctx >> 1).reshape(1)
    left = ctx & 1 == 0
    pairs = count // 2
    rows = queries.shape[0]
    depth = w_cross.shape[0]
    width = w_cross.shape[1] // groups
    swap = [(i, i ^ 1) for i in range(count)]
    across = [[(i, i ^ step) for i in range(groups)] for step in range(groups)]

    def both(mine, other, axis):
        return jnp.where(
            left,
            jnp.concatenate([mine, other], axis),
            jnp.concatenate([other, mine], axis),
        )

    half = width // 2
    far = range(2, groups)
    forward = [[(i, i + 2) for i in range(2 * turn, count - 2)] for turn in range(pairs)]
    diagonal = [(i, (i + 2) ^ 1) for i in range(count - 2)]
    mine, away, q_mine, q_away, *blocks, _ = cut(
        side, tp, (queries, keys, values, w_cross),
        [[(at, 1 - own, 0, 0, HD, rows) for at in (1, 2)] for own in (1, 0)]
        + [[(0, 1 - own, 0, 0, HD, rows)] for own in (1, 0)]
        + [[(3, step, width, 0, half, depth)] for step in far],
    )
    other = lax.ppermute(away, "ctx", swap)
    near = lax.ppermute(mine, "ctx", forward[0])
    apart = lax.ppermute(away, "ctx", diagonal)
    firsts = [lax.ppermute(block, "tp", across[step]) for step, block in zip(far, blocks)]
    q_other = lax.ppermute(q_away, "ctx", swap)
    spill = lax.ppermute(cross_queries[:BLOCK], "ctx", [(i + 1, i) for i in range(count - 1)])
    outgoing = arrange(nbr_slot, nbr_keys, nbr_values, count)
    kv, kv_mark = stack(near, apart)
    incoming = lax.all_to_all(
        fence(outgoing, kv_mark), "ctx", split_axis=0, concat_axis=0, tiled=True
    )
    own, beside, *blocks, late_mark = cut(
        side, tp, (w_cross,),
        [[(0, step, width, 0, width, depth)] for step in range(2)]
        + [[(0, step, width, half, half, depth)] for step in far],
        (kv_mark,),
    )
    beside = lax.ppermute(beside, "tp", across[1])
    seconds = [lax.ppermute(block, "tp", across[step]) for step, block in zip(far, blocks)]

    kvs = [kv]
    for step in range(2, pairs):
        kvs.append(lax.ppermute(kvs[-1], "ctx", forward[step - 1]))
    asking = (q_mine, q_other)
    *state, _ = self_steps(
        pair, side, asking, (mine, other), kvs[:1], 1, True, (late_mark, *firsts)
    )
    ours, theirs = self_steps(pair, side, asking, state, kvs[1:], 2, False, seconds)
    attended = both(ours, lax.ppermute(theirs, "ctx", swap), 1)

    tail, onward = last_attend(cross_queries, spill, incoming)
    back = lax.ppermute(onward, "ctx", [(i, i + 1) for i in range(count - 1)])
    answers = other_attend(cross_queries, tail, incoming)
    early = jnp.arange(BLOCK)[:, None] < BLOCK - 1
    cca = jnp.concatenate([jnp.where(early, back, answers[:BLOCK]), answers[BLOCK:]], axis=0)
    terms = [cca] + [lax.ppermute(cca, "tp", across[step]) for step in range(1, groups)]
    crossed = project(terms, own, beside, firsts, seconds)
    return (attended, crossed)


def solution(mesh):
    in_specs = (
        P("ctx", "tp"),
        P("ctx", "tp"),
        P("ctx", "tp"),
        P("ctx", "tp"),
        P("ctx", None, "tp"),
        P("ctx", None, "tp"),
        P("ctx"),
        P("tp", None),
    )
    out_specs = (P("ctx", "tp"), P("ctx", "tp"))
    return jax.shard_map(shards, mesh=mesh, in_specs=in_specs, out_specs=out_specs, check_vma=False)
```

time: 100 us -> 96.3 us (0.963)
  the two profiles are of different devices: /device:TPU:16 before, /device:TPU:25 now
where the time goes in v7:
time: 96.3 us; the launch traced here: 95.5 us
  starting transfers between devices  37.2 us (39%)
  waiting for transfers between devices  24.9 us (26%)
  Pallas kernels  21.5 us (22%)
  local copies, waits for them, and re-layouts  10.3 us (11%)
    ppermute x1, starting transfers between devices, shards(): lax.ppermute(cross_queries[:BLOCK], 'ctx', [(i + 1, i) for i in range(cou...  12.4 us
    unnamed x42, local copies, waits for them, and re-layouts  10.3 us
    ppermute x1, waiting for transfers between devices, shards(): q_other = lax.ppermute(q_away, 'ctx', swap)  8.68 us
    pallas_call x2, Pallas kernels, cut(): pl.pallas_call(functools.partial(cut_kernel, plan), out_shape=tuple(shape...  6.14 us
    pallas_call x2, Pallas kernels, self_steps(): pl.pallas_call(functools.partial(self_kernel, first, step, len(kvs)), out...  6.09 us
    ppermute x4, starting transfers between devices, shards(): lax.ppermute(block, 'tp', across[step])  6.04 us
    ppermute x3, waiting for transfers between devices, shards(): lax.ppermute(cca, 'tp', across[step])  4.99 us
    all_to_all x1, starting transfers between devices, shards(): lax.all_to_all(fence(outgoing, kv_mark), 'ctx', split_axis=0, concat_axis...  4.93 us
  transfers between devices with their start and end apart: 18, of which 7 were waited for; matrix products, arithmetic and copies ran while one was open for 1% of the time, Pallas kernels for 16%

profile of v7, /device:TPU:25, one launch (start us, length us, event | category | flops | bytes accessed | tf_op | source)
XLA Modules:
  0.0 95.5 jit_solution(13048245698073187387)
XLA Ops:
  0.6 2.6 %shard_map.95 = (bf16[256,256]{1,0:T(8,128)(2,1)}, bf16[256,256]{1,0:T(8,128)(2,1)}, bf16[256,128]{1,0:T(8,128)(2,1)}, bf16[256,128]{1,0:T(8,128)(2,1)}, bf16[25...) custom-call(s32[1]{0:T(128)} %bitcast.1.side_ref, s32[1]{0:T(128)} %bitcast.2.tp_ref, ...), custom_call_target="tpu_custom_call" | custom-call | flops 2000000000 | tf_op jit(solution)/shard_map/pallas_call | solution.py:69
  3.2 1.3 %collective-permute-start.2 = (bf16[256,256]{1,0:T(8,128)(2,1)}, bf16[256,256]{1,0:T(8,128)(2,1)S(1)}, u32[]{:S(2)}, u32[]{:S(2)}) collective-permute-start(bf16[256,256]{1,0:T(8,128)(2,1)} %get-tuple-element.24.refs_2_), channel_id=1, source_target_pairs={{0,8},{4,12},{8,16},{12,20},{16,24},{20,28},{1,9},{5,13},{9,17},{1... | collective-permute-start | bytes 393224 | tf_op jit(solution)/shard_map/ppermute | solution.py:385
  4.5 1.3 %collective-permute-start.3 = (bf16[256,256]{1,0:T(8,128)(2,1)}, bf16[256,256]{1,0:T(8,128)(2,1)S(1)}, u32[]{:S(2)}, u32[]{:S(2)}) collective-permute-start(bf16[256,256]{1,0:T(8,128)(2,1)} %get-tuple-element.25), channel_id=1, source_target_pairs={{0,12},{4,8},{8,20},{12,16},{16,28},{20,24},{1,13},{5,9},{9,21},{1... | collective-permute-start | bytes 393224 | tf_op jit(solution)/shard_map/ppermute | solution.py:386
  5.8 3.1 %shard_map.100.held_ref = bf16[8,272,256]{2,1,0:T(8,128)(2,1)} custom-call(s32[8]{0:T(128)} %slot_ref.1, bf16[8,128,256]{2,1,0:T(8,128)(2,1)} %keys_ref.1, bf16[8,128,256]{2,1,0:T(8,128)(2,1)} %values_ref.1), custom_call_target="tpu_custom_call" | custom-call | flops 3000000000 | tf_op jit(solution)/shard_map/pallas_call | solution.py:135
  8.9 0.8 collective-permute-done.2.one_ref
  9.7 4.0 %collective-permute-done.3.two_ref = bf16[256,256]{1,0:T(8,128)(2,1)S(1)} collective-permute-done((bf16[256,256]{1,0:T(8,128)(2,1)}, bf16[256,256]{1,0:T(8,128)(2,1)S(1)}, u32[]{:S(2)}, u32[]{:S(2)}) %collective-permute-start.3) | collective-permute-done | bytes 131104 | tf_op jit(solution)/shard_map/ppermute | solution.py:386
  13.7 0.0 copy-start.14
  13.7 0.6 copy-done.14
  14.3 0.7 shard_map.101
  15.0 4.9 %all-to-all-start = ((bf16[8,272,256]{2,1,0:T(8,128)(2,1)}), bf16[8,272,256]{2,1,0:T(8,128)(2,1)S(1)}, u32[]{:S(2)}, u32[]{:S(2)}) async-start(bf16[8,272,256]{2,1,0:T(8,128)(2,1)} %shard_map.101), calls=%async_computation | async-start | bytes 2228224 | tf_op jit(solution)/shard_map/all_to_all | solution.py:392
  19.9 1.2 %collective-permute-start.4 = (bf16[256,1024]{1,0:T(8,128)(2,1)}, bf16[256,1024]{1,0:T(8,128)(2,1)S(1)}, u32[]{:S(2)}, u32[]{:S(2)}) collective-permute-start(bf16[256,1024]{1,0:T(8,128)(2,1)} %get-tuple-element.29), channel_id=1, source_target_pairs={{0,2},{1,3},{2,0},{3,1},{4,6},{5,7},{6,4},{7,5},{8,10},{9,11},{10,... | collective-permute-start | bytes 1572872 | tf_op jit(solution)/shard_map/ppermute | solution.py:387
  21.1 2.3 %collective-permute-start.5 = (bf16[256,1024]{1,0:T(8,128)(2,1)}, bf16[256,1024]{1,0:T(8,128)(2,1)S(1)}, u32[]{:S(2)}, u32[]{:S(2)}) collective-permute-start(bf16[256,1024]{1,0:T(8,128)(2,1)} %get-tuple-element.30), channel_id=1, source_target_pairs={{0,3},{1,2},{2,1},{3,0},{4,7},{5,6},{6,5},{7,4},{8,11},{9,10},{10,... | collective-permute-start | bytes 1572872 | tf_op jit(solution)/shard_map/ppermute | solution.py:387
  23.5 0.0 copy-done.19
  23.5 1.2 %collective-permute-start.1 = (bf16[256,256]{1,0:T(8,128)(2,1)S(1)}, bf16[256,256]{1,0:T(8,128)(2,1)S(1)}, u32[]{:S(2)}, u32[]{:S(2)}) collective-permute-start(bf16[256,256]{1,0:T(8,128)(2,1)S(1)} %copy-done.19), channel_id=1, source_target_pairs={{0,4},{4,0},{8,12},{12,8},{16,20},{20,16},{24,28},{28,24},{1,5},{5... | collective-permute-start | bytes 393224 | tf_op jit(solution)/shard_map/ppermute | solution.py:384
  24.7 0.0 copy-done.20
  24.7 0.3 collective-permute-start
  25.0 1.4 %collective-permute-start.6 = (bf16[512,256]{1,0:T(8,128)(2,1)S(1)}, bf16[512,256]{1,0:T(8,128)(2,1)S(1)}, u32[]{:S(2)}, u32[]{:S(2)}) collective-permute-start(bf16[512,256]{1,0:T(8,128)(2,1)S(1)} %get-tuple-element.26.refs_4_), channel_id=1, source_target_pairs={{8,16},{12,20},{16,24},{20,28},{9,17},{13,21},{17,25},{21,29},{10,... | collective-permute-start | bytes 786440 | tf_op jit(solution)/shard_map/ppermute | solution.py:406
  26.4 3.6 %shard_map.97 = (bf16[256,2048]{1,0:T(8,128)(2,1)}, bf16[256,2048]{1,0:T(8,128)(2,1)}, bf16[256,1024]{1,0:T(8,128)(2,1)}, bf16[256,1024]{1,0:T(8,128)(2,1)}, f32[8,128]{1,0:T(8,128)}) custom-call(s32[1]{0:T(128)} %bitcast.1.side_ref, s32[1]{0:T(128)} %bitcast.2.tp_ref, bf16[256,8192]{1,0:T(8,128)(2,1)} %refs_0_.3, f32[8,128]{1,0:T(8,128)} %copy-done.14), custom_call_target="tpu_custom_call" | custom-call | flops 2000000000 | tf_op jit(solution)/shard_map/pallas_call | solution.py:69
  29.9 8.7 %collective-permute-done.refs_1_ = bf16[256,128]{1,0:T(8,128)(2,1)S(1)} collective-permute-done((bf16[256,128]{1,0:T(8,128)(2,1)S(1)}, bf16[256,128]{1,0:T(8,128)(2,1)S(1)}, u32[]{:S(2)}, u32[]{:S(2)}) %collective-permute-start) | collective-permute-done | bytes 65568 | tf_op jit(solution)/shard_map/ppermute | solution.py:388
  38.6 1.2 %collective-permute-start.8 = (bf16[256,1024]{1,0:T(8,128)(2,1)}, bf16[256,1024]{1,0:T(8,128)(2,1)}, u32[]{:S(2)}, u32[]{:S(2)}) collective-permute-start(bf16[256,1024]{1,0:T(8,128)(2,1)} %get-tuple-element.34), channel_id=1, source_target_pairs={{0,2},{1,3},{2,0},{3,1},{4,6},{5,7},{6,4},{7,5},{8,10},{9,11},{10,... | collective-permute-start | bytes 1572872 | tf_op jit(solution)/shard_map/ppermute | solution.py:402
  39.8 0.0 collective-permute-done.1.refs_3_
  39.8 0.6 copy-done.6
  40.5 1.3 %collective-permute-start.9 = (bf16[256,1024]{1,0:T(8,128)(2,1)}, bf16[256,1024]{1,0:T(8,128)(2,1)}, u32[]{:S(2)}, u32[]{:S(2)}) collective-permute-start(bf16[256,1024]{1,0:T(8,128)(2,1)} %get-tuple-element.35), channel_id=1, source_target_pairs={{0,3},{1,2},{2,1},{3,0},{4,7},{5,6},{6,5},{7,4},{8,11},{9,10},{10,... | collective-permute-start | bytes 1572872 | tf_op jit(solution)/shard_map/ppermute | solution.py:402
  41.8 0.0 copy-done
  41.8 0.0 collective-permute-done.6.refs_5_
  41.8 12.4 %collective-permute-start.11 = (bf16[64,256]{1,0:T(8,128)(2,1)S(1)}, bf16[64,256]{1,0:T(8,128)(2,1)S(1)}, u32[]{:S(2)}, u32[]{:S(2)}) collective-permute-start(bf16[64,256]{1,0:T(8,128)(2,1)S(1)} %slice.9), channel_id=1, source_target_pairs={{4,0},{8,4},{12,8},{16,12},{20,16},{24,20},{28,24},{5,1},{9,5},{13... | collective-permute-start | bytes 98312 | tf_op jit(solution)/shard_map/ppermute | solution.py:389
  54.3 0.0 collective-permute-done.4.refs_6_
  54.3 0.7 collective-permute-start.16
  55.0 0.0 collective-permute-done.5.refs_7_
  55.0 1.3 %collective-permute-start.7 = (bf16[512,256]{1,0:T(8,128)(2,1)}, bf16[512,256]{1,0:T(8,128)(2,1)S(1)}, u32[]{:S(2)}, u32[]{:S(2)}) collective-permute-start(bf16[512,256]{1,0:T(8,128)(2,1)} %copy-done.3), channel_id=1, source_target_pairs={{16,24},{20,28},{17,25},{21,29},{18,26},{22,30},{19,27},{23,31}} | collective-permute-start | bytes 786440 | tf_op jit(solution)/shard_map/ppermute | solution.py:406
  56.3 0.9 copy-done.2
  57.3 0.9 copy-done.7
  58.2 0.8 copy-done.16
  59.0 0.7 copy-done.18
  59.7 3.1 %shard_map.98 = (f32[512,128]{1,0:T(8,128)S(1)}, f32[512,128]{1,0:T(8,128)S(1)}, f32[512,128]{1,0:T(8,128)S(1)}, f32[8,128]{1,0:T(8,128)}) custom-call(s32[1]{0:T(128)} %bitcast.pair_ref, s32[1]{0:T(128)} %bitcast.1.side_ref, bf16[256,128]{1,0:T(8,128)(2,1)S(1)} %copy-done.16, bf16[256,128]{1,0:T(8,128)(2,1)S(1)} %collective-permute-done.refs_1_, ...), custom_call_target="tpu_custom_call" | custom-call | flops 3000000000 | tf_op jit(solution)/shard_map/pallas_call | solution.py:299
  62.8 0.0 collective-permute-done.8.refs_7_.refs_8_
  62.8 4.8 %collective-permute-done.9.refs_8_.refs_9_ = bf16[256,1024]{1,0:T(8,128)(2,1)} collective-permute-done((bf16[256,1024]{1,0:T(8,128)(2,1)}, bf16[256,1024]{1,0:T(8,128)(2,1)}, u32[]{:S(2)}, u32[]{:S(2)}) %collective-permute-start.9) | collective-permute-done | bytes 524320 | tf_op jit(solution)/shard_map/ppermute | solution.py:402
  67.6 0.0 collective-permute-done.7.refs_6_
  67.6 3.0 %shard_map.99 = (bf16[256,128]{1,0:T(8,128)(2,1)S(1)}, bf16[256,128]{1,0:T(8,128)(2,1)}) custom-call(s32[1]{0:T(128)} %bitcast.pair_ref, s32[1]{0:T(128)} %bitcast.1.side_ref, bf16[256,128]{1,0:T(8,128)(2,1)S(1)} %copy-done.17, bf16[256,128]{1,0:T(8,128)(2,1)S(1)} %collective-permute-done.refs_1_, f32[512,128]{1,0:T(8,128)S(1)} %get-tuple-element.31.refs_2_, ...), custom_call_target="tpu_custom_call" | custom-call | flops 3000000000 | tf_op jit(solution)/shard_map/pallas_call | solution.py:299
  70.6 1.2 %collective-permute-start.10 = (bf16[256,128]{1,0:T(8,128)(2,1)}, bf16[256,128]{1,0:T(8,128)(2,1)S(1)}, u32[]{:S(2)}, u32[]{:S(2)}) collective-permute-start(bf16[256,128]{1,0:T(8,128)(2,1)} %get-tuple-element.37), channel_id=1, source_target_pairs={{0,4},{4,0},{8,12},{12,8},{16,20},{20,16},{24,28},{28,24},{1,5},{5... | collective-permute-start | bytes 196616 | tf_op jit(solution)/shard_map/ppermute | solution.py:412
  71.8 0.0 collective-permute-done.11.spill_ref
  71.8 0.6 copy-done.12
  72.4 0.0 all-to-all-done.incoming_ref
  72.4 0.8 copy-done.13
  73.2 0.6 shard_map.102
  73.8 2.2 %collective-permute-start.12 = (bf16[64,256]{1,0:T(8,128)(2,1)S(1)}, bf16[64,256]{1,0:T(8,128)(2,1)S(1)}, u32[]{:S(2)}, u32[]{:S(2)}) collective-permute-start(bf16[64,256]{1,0:T(8,128)(2,1)S(1)} %get-tuple-element.38), channel_id=1, source_target_pairs={{0,4},{4,8},{8,12},{12,16},{16,20},{20,24},{24,28},{1,5},{5,9},{9,... | collective-permute-start | bytes 98312 | tf_op jit(solution)/shard_map/ppermute | solution.py:415
  76.0 1.6 %shard_map.103 = bf16[256,256]{1,0:T(8,128)(2,1)S(1)} custom-call(bf16[256,256]{1,0:T(8,128)(2,1)S(1)} %copy-done, bf16[16,256]{1,0:T(8,128)(2,1)S(1)} %get-tuple-element.39.tail_ref, bf16[8,272,256]{2,1,0:T(8,128)(2,1)S(1)} %all-to-all-done.incoming_ref), custom_call_target="tpu_custom_call" | custom-call | flops 2000000000 | tf_op jit(solution)/shard_map/pallas_call | solution.py:227
  77.6 1.7 %collective-permute-done.12 = bf16[64,256]{1,0:T(8,128)(2,1)S(1)} collective-permute-done((bf16[64,256]{1,0:T(8,128)(2,1)S(1)}, bf16[64,256]{1,0:T(8,128)(2,1)S(1)}, u32[]{:S(2)}, u32[]{:S(2)}) %collective-permute-start.12) | collective-permute-done | bytes 32800 | tf_op jit(solution)/shard_map/ppermute | solution.py:415
  79.3 0.1 slice_select_fusion
  79.4 1.2 %collective-permute-start.13 = (bf16[256,256]{1,0:T(8,128)(2,1)S(1)}, bf16[256,256]{1,0:T(8,128)(2,1)S(1)}, u32[]{:S(2)}, u32[]{:S(2)}) collective-permute-start(bf16[256,256]{1,0:T(8,128)(2,1)S(1)} %pad_maximum_fusion.refs_0_), channel_id=1, source_target_pairs={{0,1},{1,0},{2,3},{3,2},{4,5},{5,4},{6,7},{7,6},{8,9},{9,8},{10,11... | collective-permute-start | bytes 393224 | tf_op jit(solution)/shard_map/ppermute | solution.py:419
  80.6 0.3 collective-permute-start.14
  80.9 1.5 %collective-permute-start.15 = (bf16[256,256]{1,0:T(8,128)(2,1)S(1)}, bf16[256,256]{1,0:T(8,128)(2,1)S(1)}, u32[]{:S(2)}, u32[]{:S(2)}) collective-permute-start(bf16[256,256]{1,0:T(8,128)(2,1)S(1)} %pad_maximum_fusion.refs_0_), channel_id=1, source_target_pairs={{0,3},{1,2},{2,1},{3,0},{4,7},{5,6},{6,5},{7,4},{8,11},{9,10},{10,... | collective-permute-start | bytes 393224 | tf_op jit(solution)/shard_map/ppermute | solution.py:419
  82.3 0.0 collective-permute-done.10
  82.3 0.7 maximum_select_fusion
  83.0 0.0 collective-permute-done.16.refs_5_
  83.0 0.0 collective-permute-done.13.refs_1_
  83.0 2.7 %collective-permute-done.14.refs_2_ = bf16[256,256]{1,0:T(8,128)(2,1)S(1)} collective-permute-done((bf16[256,256]{1,0:T(8,128)(2,1)S(1)}, bf16[256,256]{1,0:T(8,128)(2,1)S(1)}, u32[]{:S(2)}, u32[]{:S(2)}) %collective-permute-start.14) | collective-permute-done | bytes 131104 | tf_op jit(solution)/shard_map/ppermute | solution.py:419
  85.7 0.6 copy-done.8
  86.3 2.3 %collective-permute-done.15.refs_3_ = bf16[256,256]{1,0:T(8,128)(2,1)S(1)} collective-permute-done((bf16[256,256]{1,0:T(8,128)(2,1)S(1)}, bf16[256,256]{1,0:T(8,128)(2,1)S(1)}, u32[]{:S(2)}, u32[]{:S(2)}) %collective-permute-start.15) | collective-permute-done | bytes 131104 | tf_op jit(solution)/shard_map/ppermute | solution.py:419
  88.7 0.7 copy-done.10
  89.3 0.9 copy-done.9
  90.2 0.9 copy-done.11
  91.1 1.2 %copy-done.15 = bf16[256,2048]{1,0:T(8,128)(2,1)S(1)} copy-done((bf16[256,2048]{1,0:T(8,128)(2,1)S(1)}, bf16[256,2048]{1,0:T(8,128)(2,1)}, u32[]{:S(2)}) %copy-start.15) | copy-done | bytes 1048600
  92.3 3.2 %shard_map.104 = bf16[256,2048]{1,0:T(8,128)(2,1)} custom-call(bf16[256,256]{1,0:T(8,128)(2,1)S(1)} %pad_maximum_fusion.refs_0_, bf16[256,256]{1,0:T(8,128)(2,1)S(1)} %collective-permute-done.13.refs_1_, bf16[256,256]{1,0:T(8,128)(2,1)S(1)} %copy-done.9, bf16[256,256]{1,0:T(8,128)(2,1)S(1)} %copy-done.11, bf16[256,2048]{1,0:T(8,128)(2,1)S(1)} %copy-done.15, ...), custom_call_target="tpu_custom_call" | custom-call | flops 3000000000 | tf_op jit(solution)/shard_map/pallas_call | solution.py:338
  (30 shorter events, 0.1 us)
Async XLA Ops:
  3.2 6.5 %collective-permute-start.2 = (bf16[256,256]{1,0:T(8,128)(2,1)}, bf16[256,256]{1,0:T(8,128)(2,1)S(1)}, u32[]{:S(2)}, u32[]{:S(2)}) collective-permute-start(bf16[256,256]{1,0:T(8,128)(2,1)} %get-tuple-element.24.refs_2_), channel_id=1, source_target_pairs={{0,8},{4,12},{8,16},{12,20},{16,24},{20,28},{1,9},{5,13},{9,17},{1... | collective-permute-start | bytes 393224 | tf_op jit(solution)/shard_map/ppermute | solution.py:385
  4.5 9.2 %collective-permute-start.3 = (bf16[256,256]{1,0:T(8,128)(2,1)}, bf16[256,256]{1,0:T(8,128)(2,1)S(1)}, u32[]{:S(2)}, u32[]{:S(2)}) collective-permute-start(bf16[256,256]{1,0:T(8,128)(2,1)} %get-tuple-element.25), channel_id=1, source_target_pairs={{0,12},{4,8},{8,20},{12,16},{16,28},{20,24},{1,13},{5,9},{9,21},{1... | collective-permute-start | bytes 393224 | tf_op jit(solution)/shard_map/ppermute | solution.py:386
  13.7 0.6 copy-start.14
  14.3 10.6 %copy-start.1 = (bf16[512,256]{1,0:T(8,128)(2,1)}, bf16[512,256]{1,0:T(8,128)(2,1)S(1)}, u32[]{:S(2)}) copy-start(bf16[512,256]{1,0:T(8,128)(2,1)S(1)} %get-tuple-element.26.refs_4_) | copy-start | bytes 786436
  15.0 8.5 %copy-start.19 = (bf16[256,256]{1,0:T(8,128)(2,1)S(1)}, bf16[256,256]{1,0:T(8,128)(2,1)}, u32[]{:S(2)}) copy-start(bf16[256,256]{1,0:T(8,128)(2,1)} %get-tuple-element.25) | copy-start | bytes 393220
  15.0 9.7 %copy-start.20 = (bf16[256,128]{1,0:T(8,128)(2,1)S(1)}, bf16[256,128]{1,0:T(8,128)(2,1)}, u32[]{:S(2)}) copy-start(bf16[256,128]{1,0:T(8,128)(2,1)} %get-tuple-element.23) | copy-start | bytes 196612
  15.0 57.4 %all-to-all-start = ((bf16[8,272,256]{2,1,0:T(8,128)(2,1)}), bf16[8,272,256]{2,1,0:T(8,128)(2,1)S(1)}, u32[]{:S(2)}, u32[]{:S(2)}) async-start(bf16[8,272,256]{2,1,0:T(8,128)(2,1)} %shard_map.101), calls=%async_computation | async-start | bytes 2228224 | tf_op jit(solution)/shard_map/all_to_all | solution.py:392
  19.9 34.3 %collective-permute-start.4 = (bf16[256,1024]{1,0:T(8,128)(2,1)}, bf16[256,1024]{1,0:T(8,128)(2,1)S(1)}, u32[]{:S(2)}, u32[]{:S(2)}) collective-permute-start(bf16[256,1024]{1,0:T(8,128)(2,1)} %get-tuple-element.29), channel_id=1, source_target_pairs={{0,2},{1,3},{2,0},{3,1},{4,6},{5,7},{6,4},{7,5},{8,10},{9,11},{10,... | collective-permute-start | bytes 1572872 | tf_op jit(solution)/shard_map/ppermute | solution.py:387
  21.1 33.9 %collective-permute-start.5 = (bf16[256,1024]{1,0:T(8,128)(2,1)}, bf16[256,1024]{1,0:T(8,128)(2,1)S(1)}, u32[]{:S(2)}, u32[]{:S(2)}) collective-permute-start(bf16[256,1024]{1,0:T(8,128)(2,1)} %get-tuple-element.30), channel_id=1, source_target_pairs={{0,3},{1,2},{2,1},{3,0},{4,7},{5,6},{6,5},{7,4},{8,11},{9,10},{10,... | collective-permute-start | bytes 1572872 | tf_op jit(solution)/shard_map/ppermute | solution.py:387
  23.5 16.4 %collective-permute-start.1 = (bf16[256,256]{1,0:T(8,128)(2,1)S(1)}, bf16[256,256]{1,0:T(8,128)(2,1)S(1)}, u32[]{:S(2)}, u32[]{:S(2)}) collective-permute-start(bf16[256,256]{1,0:T(8,128)(2,1)S(1)} %copy-done.19), channel_id=1, source_target_pairs={{0,4},{4,0},{8,12},{12,8},{16,20},{20,16},{24,28},{28,24},{1,5},{5... | collective-permute-start | bytes 393224 | tf_op jit(solution)/shard_map/ppermute | solution.py:384
  24.7 14.0 %collective-permute-start = (bf16[256,128]{1,0:T(8,128)(2,1)S(1)}, bf16[256,128]{1,0:T(8,128)(2,1)S(1)}, u32[]{:S(2)}, u32[]{:S(2)}) collective-permute-start(bf16[256,128]{1,0:T(8,128)(2,1)S(1)} %copy-done.20), channel_id=1, source_target_pairs={{0,4},{4,0},{8,12},{12,8},{16,20},{20,16},{24,28},{28,24},{1,5},{5... | collective-permute-start | bytes 196616 | tf_op jit(solution)/shard_map/ppermute | solution.py:388
  25.0 16.8 %copy-start = (bf16[256,256]{1,0:T(8,128)(2,1)S(1)}, bf16[256,256]{1,0:T(8,128)(2,1)}, u32[]{:S(2)}) copy-start(bf16[256,256]{1,0:T(8,128)(2,1)} %queries_ref.3) | copy-start | bytes 393220
  25.0 31.3 %copy-start.5 = (bf16[256,256]{1,0:T(8,128)(2,1)S(1)}, bf16[256,256]{1,0:T(8,128)(2,1)}, u32[]{:S(2)}) copy-start(bf16[256,256]{1,0:T(8,128)(2,1)} %get-tuple-element.24.refs_2_) | copy-start | bytes 393220
  25.0 16.8 %collective-permute-start.6 = (bf16[512,256]{1,0:T(8,128)(2,1)S(1)}, bf16[512,256]{1,0:T(8,128)(2,1)S(1)}, u32[]{:S(2)}, u32[]{:S(2)}) collective-permute-start(bf16[512,256]{1,0:T(8,128)(2,1)S(1)} %get-tuple-element.26.refs_4_), channel_id=1, source_target_pairs={{8,16},{12,20},{16,24},{20,28},{9,17},{13,21},{17,25},{21,29},{10,... | collective-permute-start | bytes 786440 | tf_op jit(solution)/shard_map/ppermute | solution.py:406
  38.6 24.2 %collective-permute-start.8 = (bf16[256,1024]{1,0:T(8,128)(2,1)}, bf16[256,1024]{1,0:T(8,128)(2,1)}, u32[]{:S(2)}, u32[]{:S(2)}) collective-permute-start(bf16[256,1024]{1,0:T(8,128)(2,1)} %get-tuple-element.34), channel_id=1, source_target_pairs={{0,2},{1,3},{2,0},{3,1},{4,6},{5,7},{6,4},{7,5},{8,10},{9,11},{10,... | collective-permute-start | bytes 1572872 | tf_op jit(solution)/shard_map/ppermute | solution.py:402
  39.8 0.6 copy-start.6
  40.5 27.1 %collective-permute-start.9 = (bf16[256,1024]{1,0:T(8,128)(2,1)}, bf16[256,1024]{1,0:T(8,128)(2,1)}, u32[]{:S(2)}, u32[]{:S(2)}) collective-permute-start(bf16[256,1024]{1,0:T(8,128)(2,1)} %get-tuple-element.35), channel_id=1, source_target_pairs={{0,3},{1,2},{2,1},{3,0},{4,7},{5,6},{6,5},{7,4},{8,11},{9,10},{10,... | collective-permute-start | bytes 1572872 | tf_op jit(solution)/shard_map/ppermute | solution.py:402
  41.8 12.5 %copy-start.3 = (bf16[512,256]{1,0:T(8,128)(2,1)}, bf16[512,256]{1,0:T(8,128)(2,1)S(1)}, u32[]{:S(2)}) copy-start(bf16[512,256]{1,0:T(8,128)(2,1)S(1)} %collective-permute-done.6.refs_5_) | copy-start | bytes 786436
  41.8 30.0 %collective-permute-start.11 = (bf16[64,256]{1,0:T(8,128)(2,1)S(1)}, bf16[64,256]{1,0:T(8,128)(2,1)S(1)}, u32[]{:S(2)}, u32[]{:S(2)}) collective-permute-start(bf16[64,256]{1,0:T(8,128)(2,1)S(1)} %slice.9), channel_id=1, source_target_pairs={{4,0},{8,4},{12,8},{16,12},{20,16},{24,20},{28,24},{5,1},{9,5},{13... | collective-permute-start | bytes 98312 | tf_op jit(solution)/shard_map/ppermute | solution.py:389
  54.3 28.7 %collective-permute-start.16 = (bf16[256,2048]{1,0:T(8,128)(2,1)}, bf16[256,2048]{1,0:T(8,128)(2,1)S(1)}, u32[]{:S(2)}, u32[]{:S(2)}) collective-permute-start(bf16[256,2048]{1,0:T(8,128)(2,1)} %get-tuple-element.41), channel_id=1, source_target_pairs={{0,1},{1,0},{2,3},{3,2},{4,5},{5,4},{6,7},{7,6},{8,9},{9,8},{10,11... | collective-permute-start | bytes 3145736 | tf_op jit(solution)/shard_map/ppermute | solution.py:401
  55.0 12.6 %collective-permute-start.7 = (bf16[512,256]{1,0:T(8,128)(2,1)}, bf16[512,256]{1,0:T(8,128)(2,1)S(1)}, u32[]{:S(2)}, u32[]{:S(2)}) collective-permute-start(bf16[512,256]{1,0:T(8,128)(2,1)} %copy-done.3), channel_id=1, source_target_pairs={{16,24},{20,28},{17,25},{21,29},{18,26},{22,30},{19,27},{23,31}} | collective-permute-start | bytes 786440 | tf_op jit(solution)/shard_map/ppermute | solution.py:406
  56.3 1.0 copy-start.2
  57.3 0.9 copy-start.7
  58.2 0.8 copy-start.16
  59.0 0.7 copy-start.18
  59.7 7.9 %copy-start.4 = (bf16[512,256]{1,0:T(8,128)(2,1)S(1)}, bf16[512,256]{1,0:T(8,128)(2,1)}, u32[]{:S(2)}) copy-start(bf16[512,256]{1,0:T(8,128)(2,1)} %copy-done.3) | copy-start | bytes 786436
  59.7 7.9 %copy-start.17 = (bf16[256,128]{1,0:T(8,128)(2,1)S(1)}, bf16[256,128]{1,0:T(8,128)(2,1)}, u32[]{:S(2)}) copy-start(bf16[256,128]{1,0:T(8,128)(2,1)} %get-tuple-element.22.refs_0_) | copy-start | bytes 196612
  70.6 11.7 %collective-permute-start.10 = (bf16[256,128]{1,0:T(8,128)(2,1)}, bf16[256,128]{1,0:T(8,128)(2,1)S(1)}, u32[]{:S(2)}, u32[]{:S(2)}) collective-permute-start(bf16[256,128]{1,0:T(8,128)(2,1)} %get-tuple-element.37), channel_id=1, source_target_pairs={{0,4},{4,0},{8,12},{12,8},{16,20},{20,16},{24,28},{28,24},{1,5},{5... | collective-permute-start | bytes 196616 | tf_op jit(solution)/shard_map/ppermute | solution.py:412
  71.8 0.6 copy-start.12
  72.4 0.8 copy-start.13
  73.8 5.6 %collective-permute-start.12 = (bf16[64,256]{1,0:T(8,128)(2,1)S(1)}, bf16[64,256]{1,0:T(8,128)(2,1)S(1)}, u32[]{:S(2)}, u32[]{:S(2)}) collective-permute-start(bf16[64,256]{1,0:T(8,128)(2,1)S(1)} %get-tuple-element.38), channel_id=1, source_target_pairs={{0,4},{4,8},{8,12},{12,16},{16,20},{20,24},{24,28},{1,5},{5,9},{9,... | collective-permute-start | bytes 98312 | tf_op jit(solution)/shard_map/ppermute | solution.py:415
  79.4 3.6 %collective-permute-start.13 = (bf16[256,256]{1,0:T(8,128)(2,1)S(1)}, bf16[256,256]{1,0:T(8,128)(2,1)S(1)}, u32[]{:S(2)}, u32[]{:S(2)}) collective-permute-start(bf16[256,256]{1,0:T(8,128)(2,1)S(1)} %pad_maximum_fusion.refs_0_), channel_id=1, source_target_pairs={{0,1},{1,0},{2,3},{3,2},{4,5},{5,4},{6,7},{7,6},{8,9},{9,8},{10,11... | collective-permute-start | bytes 393224 | tf_op jit(solution)/shard_map/ppermute | solution.py:419
  80.6 5.1 %collective-permute-start.14 = (bf16[256,256]{1,0:T(8,128)(2,1)S(1)}, bf16[256,256]{1,0:T(8,128)(2,1)S(1)}, u32[]{:S(2)}, u32[]{:S(2)}) collective-permute-start(bf16[256,256]{1,0:T(8,128)(2,1)S(1)} %pad_maximum_fusion.refs_0_), channel_id=1, source_target_pairs={{0,2},{1,3},{2,0},{3,1},{4,6},{5,7},{6,4},{7,5},{8,10},{9,11},{10,... | collective-permute-start | bytes 393224 | tf_op jit(solution)/shard_map/ppermute | solution.py:419
  80.9 7.8 %collective-permute-start.15 = (bf16[256,256]{1,0:T(8,128)(2,1)S(1)}, bf16[256,256]{1,0:T(8,128)(2,1)S(1)}, u32[]{:S(2)}, u32[]{:S(2)}) collective-permute-start(bf16[256,256]{1,0:T(8,128)(2,1)S(1)} %pad_maximum_fusion.refs_0_), channel_id=1, source_target_pairs={{0,3},{1,2},{2,1},{3,0},{4,7},{5,6},{6,5},{7,4},{8,11},{9,10},{10,... | collective-permute-start | bytes 393224 | tf_op jit(solution)/shard_map/ppermute | solution.py:419
  85.7 0.6 copy-start.8
  88.6 0.7 copy-start.10
  89.3 0.9 copy-start.9
  90.2 0.9 copy-start.11
  91.1 1.2 %copy-start.15 = (bf16[256,2048]{1,0:T(8,128)(2,1)S(1)}, bf16[256,2048]{1,0:T(8,128)(2,1)}, u32[]{:S(2)}) copy-start(bf16[256,2048]{1,0:T(8,128)(2,1)} %get-tuple-element.40.refs_4_) | copy-start | bytes 3145732

commit v8 on v7

--- a/solution.py
+++ b/solution.py
@@ -45,9 +45,8 @@
 
 
 def cut_kernel(plan, side_ref, tp_ref, *refs):
-    mark_ref, sems, refs = refs[-2], refs[-1], refs[:-2]
+    sems, refs = refs[-1], refs[:-1]
     sources, outs = refs, refs[len(refs) - len(plan) :]
-    mark_ref[...] = jnp.zeros(mark_ref.shape, jnp.float32)
     pieces = []
     for out, parts in zip(outs, plan):
         for at, (index, step, total, offset, width, depth) in enumerate(parts):
@@ -65,7 +64,6 @@
     for parts in plan:
         shape = (parts[0][5], len(parts) * parts[0][4])
         shapes.append(jax.ShapeDtypeStruct(shape, sources[parts[0][0]].dtype))
-    shapes.append(jax.ShapeDtypeStruct((8, HD), jnp.float32))
     return pl.pallas_call(
         functools.partial(cut_kernel, plan),
         out_shape=tuple(shapes),
@@ -76,68 +74,81 @@
     )(side, tp, *sources, *before)
 
 
-def stack_kernel(one_ref, two_ref, kv_ref, mark_ref):
+def stack_kernel(one_ref, two_ref, kv_ref):
     rows = one_ref.shape[0]
     kv_ref[:rows, :] = one_ref[...]
     kv_ref[rows:, :] = two_ref[...]
-    mark_ref[...] = jnp.zeros(mark_ref.shape, jnp.float32)
 
 
 def stack(one, two):
     rows, width = one.shape
     return pl.pallas_call(
         stack_kernel,
-        out_shape=(
-            jax.ShapeDtypeStruct((2 * rows, width), one.dtype),
-            jax.ShapeDtypeStruct((8, HD), jnp.float32),
-        ),
+        out_shape=jax.ShapeDtypeStruct((2 * rows, width), one.dtype),
         in_specs=[VMEM] * 2,
-        out_specs=(VMEM, VMEM),
+        out_specs=VMEM,
         compiler_params=PARAMS,
     )(one, two)
 
 
-def fence_kernel(held_ref, mark_ref, out_ref, value_ref):
-    value_ref[...] = mark_ref[...]
-
-
-def fence(held, mark):
-    return pl.pallas_call(
-        fence_kernel,
-        out_shape=jax.ShapeDtypeStruct(held.shape, held.dtype),
-        in_specs=[ANY, VMEM],
-        out_specs=ANY,
-        scratch_shapes=[pltpu.VMEM(mark.shape, mark.dtype)],
-        input_output_aliases={0: 0},
-        cost_estimate=takes(5),
-    )(held, mark)
-
-
-def arrange_kernel(slot_ref, keys_ref, values_ref, out_ref, sems):
+def arrange_kernel(slot_ref, keys_ref, values_ref, out_ref, held_ref, sems):
     count, length, width = keys_ref.shape
-    pieces = []
-    for n in range(count):
-        owner = slot_ref[n] // count
-        pieces.append((keys_ref.at[n], out_ref.at[owner, pl.ds(0, length)]))
-        pieces.append((values_ref.at[n], out_ref.at[owner, pl.ds(length, length)]))
+    owners = [slot_ref[n] // count for n in range(count)]
+    copies = []
+    for n, owner in enumerate(owners):
+        for half, source in enumerate((keys_ref, values_ref)):
+            target = held_ref.at[owner, pl.ds(half * length, length)]
+            copies.append(pltpu.make_async_copy(source.at[n], target, sems.at[2 * n + half]))
+    for copy in copies:
+        copy.start()
+    for owner in range(held_ref.shape[0]):
+        held_ref[owner, 2 * length :, :] = jnp.full((LEAD, width), -1, held_ref.dtype)
+    for n, owner in enumerate(owners):
+        place = (slot_ref[n] - owner * count).astype(jnp.float32)
+        held_ref[owner, 2 * length :, :] = jnp.full((LEAD, width), place).astype(held_ref.dtype)
+    outs = []
+    for n, owner in enumerate(owners):
+        copies[2 * n].wait()
+        copies[2 * n + 1].wait()
+        out = pltpu.make_async_copy(
+            held_ref.at[owner], out_ref.at[owner], sems.at[2 * count + n]
+        )
+        out.start()
+        outs.append(out)
+    for out in outs:
+        out.wait()
+
+
+def unheld_kernel(slot_ref, keys_ref, values_ref, out_ref, held_ref, sems):
+    arrange_kernel(slot_ref, keys_ref, values_ref, out_ref, held_ref, sems)
+    count, length = keys_ref.shape[:2]
     for owner in range(out_ref.shape[0]):
-        out_ref[owner, 2 * length :, :] = jnp.full((LEAD, width), -1, out_ref.dtype)
-    for n in range(count):
-        slot = slot_ref[n]
-        owner = slot // count
-        place = (slot - owner * count).astype(jnp.float32)
-        out_ref[owner, 2 * length :, :] = jnp.full((LEAD, width), place).astype(out_ref.dtype)
-    fetch(pieces, sems)
+        taken = slot_ref[0] // count == owner
+        for n in range(1, count):
+            taken = taken | (slot_ref[n] // count == owner)
+
+        @pl.when(jnp.logical_not(taken))
+        def _():
+            rows = pl.ds(2 * length, LEAD)
+            copy = pltpu.make_async_copy(
+                held_ref.at[owner, rows], out_ref.at[owner, rows], sems.at[0]
+            )
+            copy.start()
+            copy.wait()
 
 
 def arrange(slots, keys, values, owners):
     count, length, width = keys.shape
-    return pl.pallas_call(
-        arrange_kernel,
-        out_shape=jax.ShapeDtypeStruct((owners, 2 * length + LEAD, width), keys.dtype),
+    shape = (owners, 2 * length + LEAD, width)
+    return pl.pallas_call(
+        arrange_kernel if owners == count else unheld_kernel,
+        out_shape=jax.ShapeDtypeStruct(shape, keys.dtype),
         in_specs=[SMEM, ANY, ANY],
-        out_specs=VMEM,
-        scratch_shapes=[pltpu.SemaphoreType.DMA((2 * count,))],
+        out_specs=ANY,
+        scratch_shapes=[
+            pltpu.VMEM(shape, keys.dtype),
+            pltpu.SemaphoreType.DMA((3 * count,)),
+        ],
         cost_estimate=takes(3),
     )(slots, keys, values)
 
@@ -236,19 +247,18 @@
 
 
 def self_kernel(first, step, chunks, pair_ref, side_ref, *refs):
-    queries, refs = refs[:2], refs[2:]
-    held, refs = (refs[:2], refs[2:]) if first else (refs[:3], refs[3:])
+    tokens, refs = refs[:2], refs[2:]
+    state, refs = ((), refs) if first else (refs[:3], refs[3:])
     kvs, refs = refs[:chunks], refs[chunks:]
     peak_ref, total_ref, accum_ref = refs[-3:]
-    outs = refs[-7:-3] if first else refs[-5:-3]
-    tile = queries[0].shape[0]
-    if first:
-        outs[3][...] = jnp.zeros(outs[3].shape, jnp.float32)
-    for part, q_ref in enumerate(queries):
+    outs = refs[-6:-3] if first else refs[-5:-3]
+    tile = tokens[0].shape[0]
+    for part, q_ref in enumerate(tokens):
         at = pl.ds(part * tile, tile)
 
         def attend(kv_ref, fresh):
-            s = dot_t(q_ref[...], kv_ref[:, :HD])
+            width = kv_ref.shape[1]
+            s = dot_t(q_ref[:, :HD], kv_ref[:, width - 2 * HD : width - HD])
             if fresh:
                 row = lax.broadcasted_iota(jnp.int32, (tile, tile), 0)
                 col = lax.broadcasted_iota(jnp.int32, (tile, tile), 1)
@@ -260,7 +270,7 @@
                 factor = jnp.exp2((old - peak) * SCALE)
             p = jnp.exp2((s - peak) * SCALE)
             total = jnp.sum(p, axis=1, keepdims=True)
-            accum = dot(p.astype(jnp.bfloat16), kv_ref[:, HD:])
+            accum = dot(p.astype(jnp.bfloat16), kv_ref[:, width - HD :])
             if not fresh:
                 total += total_ref[at, :1] * factor
                 accum += accum_ref[at, :] * factor
@@ -269,14 +279,14 @@
             accum_ref[at, :] = accum
 
         if first:
-            attend(held[part], True)
+            attend(q_ref, True)
             pl.when((side_ref[0] ^ part) == 1)(
-                functools.partial(attend, held[1 - part], False)
+                functools.partial(attend, tokens[1 - part], False)
             )
         else:
-            peak_ref[at, :] = held[0][at, :]
-            total_ref[at, :] = held[1][at, :]
-            accum_ref[at, :] = held[2][at, :]
+            peak_ref[at, :] = state[0][at, :]
+            total_ref[at, :] = state[1][at, :]
+            accum_ref[at, :] = state[2][at, :]
         for index, kv_ref in enumerate(kvs):
             pl.when(pair_ref[0] >= step + index)(functools.partial(attend, kv_ref, False))
         if first:
@@ -287,15 +297,15 @@
             outs[part][...] = (accum_ref[at, :] / total_ref[at, :]).astype(jnp.bfloat16)
 
 
-def self_steps(pair, side, queries, held, kvs, step, first, before):
-    tile = queries[0].shape[0]
+def self_steps(pair, side, tokens, state, kvs, step, before):
+    tile = tokens[0].shape[0]
     rows = 2 * tile
+    first = not state
     if first:
         out_shape = (jax.ShapeDtypeStruct((rows, HD), jnp.float32),) * 3
-        out_shape += (jax.ShapeDtypeStruct((8, HD), jnp.float32),)
     else:
         out_shape = (jax.ShapeDtypeStruct((tile, HD), jnp.bfloat16),) * 2
-    operands = (*queries, *held, *kvs)
+    operands = (*tokens, *state, *kvs)
     return pl.pallas_call(
         functools.partial(self_kernel, first, step, len(kvs)),
         out_shape=out_shape,
@@ -307,21 +317,31 @@
     )(pair, side, *operands, *before)
 
 
-def project_kernel(groups, *refs):
+def project_kernel(groups, side_ref, *refs):
     crossed_ref, out_ref, sems = refs[-3:]
     terms, near, far = refs[:groups], refs[groups : groups + 2], refs[groups + 2 : -3]
+    direct, shared, fetched = (far[at * (groups - 2) : (at + 1) * (groups - 2)] for at in range(3))
     width = crossed_ref.shape[1]
     half = width // 2
     tile = min(512, half)
+    share = shared[0].shape[0]
+    mine = pl.ds(pl.multiple_of(side_ref[0] * share, HD), share)
+    other = pl.ds(pl.multiple_of((1 - side_ref[0]) * share, HD), share)
     term = jnp.concatenate([held[...] for held in terms], axis=1)
+    split = [held[...] for held in terms[:2]]
+    split += [held[:, part] for held in terms[2:] for part in (mine, other)]
+    split = jnp.concatenate(split, axis=1)
     outs = []
     for column in range(0, width, tile):
         at = slice(column, column + tile)
-        blocks = far[: groups - 2] if column < half else far[groups - 2 :]
-        start = column % half
         weight = [block[:, at] for block in near]
-        weight += [block[:, start : start + tile] for block in blocks]
-        total = dot(term, jnp.concatenate(weight, axis=0))
+        if column < half:
+            for pieces in zip(shared, fetched):
+                weight += [piece[:, at] for piece in pieces]
+        else:
+            start = column - half
+            weight += [block[:, start : start + tile] for block in direct]
+        total = dot(split if column < half else term, jnp.concatenate(weight, axis=0))
         out_ref[:, at] = total.astype(out_ref.dtype)
         out = pltpu.make_async_copy(
             out_ref.at[:, at], crossed_ref.at[:, at], sems.at[len(outs)]
@@ -332,13 +352,13 @@
         out.wait()
 
 
-def project(terms, own, beside, firsts, seconds):
+def project(side, terms, own, beside, direct, shared, fetched):
     rows, width = terms[0].shape[0], beside.shape[1]
-    operands = (*terms, own, beside, *firsts, *seconds)
+    operands = (*terms, own, beside, *direct, *shared, *fetched)
     return pl.pallas_call(
         functools.partial(project_kernel, len(terms)),
         out_shape=jax.ShapeDtypeStruct((rows, width), jnp.bfloat16),
-        in_specs=[VMEM] * len(operands),
+        in_specs=[SMEM] + [VMEM] * len(operands),
         out_specs=ANY,
         scratch_shapes=[
             pltpu.VMEM((rows, width), jnp.bfloat16),
@@ -346,7 +366,7 @@
         ],
         compiler_params=PARAMS,
         cost_estimate=takes(3),
-    )(*operands)
+    )(side, *operands)
 
 
 def shards(queries, keys, values, cross_queries, nbr_keys, nbr_values, nbr_slot, w_cross):
@@ -375,40 +395,36 @@
     far = range(2, groups)
     forward = [[(i, i + 2) for i in range(2 * turn, count - 2)] for turn in range(pairs)]
     diagonal = [(i, (i + 2) ^ 1) for i in range(count - 2)]
-    mine, away, q_mine, q_away, *blocks, _ = cut(
+    mine, away, kv_mine, kv_away, *blocks = cut(
         side, tp, (queries, keys, values, w_cross),
-        [[(at, 1 - own, 0, 0, HD, rows) for at in (1, 2)] for own in (1, 0)]
-        + [[(0, 1 - own, 0, 0, HD, rows)] for own in (1, 0)]
-        + [[(3, step, width, 0, half, depth)] for step in far],
+        [[(at, 1 - own, 0, 0, HD, rows) for at in (0, 1, 2)] for own in (1, 0)]
+        + [[(at, 1 - own, 0, 0, HD, rows) for at in (1, 2)] for own in (1, 0)]
+        + [[(3, step, width, 0, half, depth // 2)] for step in far],
     )
+    near = lax.ppermute(kv_mine, "ctx", forward[0])
+    apart = lax.ppermute(kv_away, "ctx", diagonal)
     other = lax.ppermute(away, "ctx", swap)
-    near = lax.ppermute(mine, "ctx", forward[0])
-    apart = lax.ppermute(away, "ctx", diagonal)
-    firsts = [lax.ppermute(block, "tp", across[step]) for step, block in zip(far, blocks)]
-    q_other = lax.ppermute(q_away, "ctx", swap)
+    shared = [lax.ppermute(block, "tp", across[step]) for step, block in zip(far, blocks)]
     spill = lax.ppermute(cross_queries[:BLOCK], "ctx", [(i + 1, i) for i in range(count - 1)])
     outgoing = arrange(nbr_slot, nbr_keys, nbr_values, count)
-    kv, kv_mark = stack(near, apart)
-    incoming = lax.all_to_all(
-        fence(outgoing, kv_mark), "ctx", split_axis=0, concat_axis=0, tiled=True
-    )
-    own, beside, *blocks, late_mark = cut(
+    incoming = lax.all_to_all(outgoing, "ctx", split_axis=0, concat_axis=0, tiled=True)
+    kv = stack(near, apart)
+    own, beside, *blocks = cut(
         side, tp, (w_cross,),
         [[(0, step, width, 0, width, depth)] for step in range(2)]
         + [[(0, step, width, half, half, depth)] for step in far],
-        (kv_mark,),
+        (kv,),
     )
     beside = lax.ppermute(beside, "tp", across[1])
-    seconds = [lax.ppermute(block, "tp", across[step]) for step, block in zip(far, blocks)]
+    direct = [lax.ppermute(block, "tp", across[step]) for step, block in zip(far, blocks)]
+    fetched = [lax.ppermute(block, "ctx", swap) for block in shared]
 
     kvs = [kv]
     for step in range(2, pairs):
         kvs.append(lax.ppermute(kvs[-1], "ctx", forward[step - 1]))
-    asking = (q_mine, q_other)
-    *state, _ = self_steps(
-        pair, side, asking, (mine, other), kvs[:1], 1, True, (late_mark, *firsts)
-    )
-    ours, theirs = self_steps(pair, side, asking, state, kvs[1:], 2, False, seconds)
+    tokens = (mine, other)
+    state = self_steps(pair, side, tokens, (), kvs[:1], 1, shared)
+    ours, theirs = self_steps(pair, side, tokens, state, kvs[1:], 2, direct)
     attended = both(ours, lax.ppermute(theirs, "ctx", swap), 1)
 
     tail, onward = last_attend(cross_queries, spill, incoming)
@@ -417,7 +433,7 @@
     early = jnp.arange(BLOCK)[:, None] < BLOCK - 1
     cca = jnp.concatenate([jnp.where(early, back, answers[:BLOCK]), answers[BLOCK:]], axis=0)
     terms = [cca] + [lax.ppermute(cca, "tp", across[step]) for step in range(1, groups)]
-    crossed = project(terms, own, beside, firsts, seconds)
+    crossed = project(side, terms, own, beside, direct, shared, fetched)
     return (attended, crossed)
 
 

time: 96.3 us -> 97.8 us (1.016)
  the two profiles are of different devices: /device:TPU:25 before, /device:TPU:9 now
where the time goes in v8:
time: 97.8 us; the launch traced here: 97.2 us
  waiting for transfers between devices  36.6 us (37%)
  starting transfers between devices  36 us (37%)
  Pallas kernels  18.5 us (19%)
  local copies, waits for them, and re-layouts  4.47 us (5%)
    ppermute x4, waiting for transfers between devices, shards(): lax.ppermute(block, 'tp', across[step])  13.9 us
    ppermute x1, waiting for transfers between devices, shards(): near = lax.ppermute(kv_mine, 'ctx', forward[0])  13.7 us
    ppermute x2, starting transfers between devices, shards(): kvs.append(lax.ppermute(kvs[-1], 'ctx', forward[step - 1]))  6.64 us
    ppermute x4, starting transfers between devices, shards(): lax.ppermute(block, 'tp', across[step])  6.18 us
    pallas_call x2, Pallas kernels, cut(): pl.pallas_call(functools.partial(cut_kernel, plan), out_shape=tuple(shape...  5.97 us
    all_to_all x1, starting transfers between devices, shards(): lax.all_to_all(outgoing, 'ctx', split_axis=0, concat_axis=0, tiled=True)  5.73 us
    ppermute x3, waiting for transfers between devices, shards(): lax.ppermute(cca, 'tp', across[step])  5.62 us
    unnamed x14, local copies, waits for them, and re-layouts  4.46 us
  transfers between devices with their start and end apart: 19, of which 7 were waited for; matrix products, arithmetic and copies ran while one was open for 1% of the time, Pallas kernels for 13%

profile of v8, /device:TPU:9, one launch (start us, length us, event | category | flops | bytes accessed | tf_op | source)
XLA Modules:
  0.0 97.2 jit_solution(783536017959559470)
XLA Ops:
  0.6 2.8 %shard_map.100 = bf16[8,272,256]{2,1,0:T(8,128)(2,1)} custom-call(s32[8]{0:T(128)} %slot_ref.1, bf16[8,128,256]{2,1,0:T(8,128)(2,1)} %keys_ref.1, bf16[8,128,256]{2,1,0:T(8,128)(2,1)} %values_ref.1), custom_call_target="tpu_custom_call" | custom-call | flops 3000000000 | tf_op jit(solution)/shard_map/pallas_call | solution.py:143
  3.5 5.7 %all-to-all-start = ((bf16[8,272,256]{2,1,0:T(8,128)(2,1)}), bf16[8,272,256]{2,1,0:T(8,128)(2,1)S(1)}, u32[]{:S(2)}, u32[]{:S(2)}) async-start(bf16[8,272,256]{2,1,0:T(8,128)(2,1)} %shard_map.100), calls=%async_computation | async-start | bytes 2228224 | tf_op jit(solution)/shard_map/all_to_all | solution.py:410
  9.2 2.5 %shard_map.95 = (bf16[256,384]{1,0:T(8,128)(2,1)}, bf16[256,384]{1,0:T(8,128)(2,1)}, bf16[256,256]{1,0:T(8,128)(2,1)}, bf16[256,256]{1,0:T(8,128)(2,1)}, bf16[12...) custom-call(s32[1]{0:T(128)} %bitcast.1.side_ref, s32[1]{0:T(128)} %bitcast.2.tp_ref, bf16[256,256]{1,0:T(8,128)(2,1)} %refs_0_.2, ...), custom_call_target="tpu_custom_call" | custom-call | flops 2000000000 | tf_op jit(solution)/shard_map/pallas_call | solution.py:67
  11.7 3.1 %collective-permute-start.1 = (bf16[256,256]{1,0:T(8,128)(2,1)}, bf16[256,256]{1,0:T(8,128)(2,1)S(1)}, u32[]{:S(2)}, u32[]{:S(2)}) collective-permute-start(bf16[256,256]{1,0:T(8,128)(2,1)} %get-tuple-element.21), channel_id=1, source_target_pairs={{0,8},{4,12},{8,16},{12,20},{16,24},{20,28},{1,9},{5,13},{9,17},{1... | collective-permute-start | bytes 393224 | tf_op jit(solution)/shard_map/ppermute | solution.py:404
  14.8 4.0 %collective-permute-start.2 = (bf16[256,256]{1,0:T(8,128)(2,1)}, bf16[256,256]{1,0:T(8,128)(2,1)S(1)}, u32[]{:S(2)}, u32[]{:S(2)}) collective-permute-start(bf16[256,256]{1,0:T(8,128)(2,1)} %get-tuple-element.22), channel_id=1, source_target_pairs={{0,12},{4,8},{8,20},{12,16},{16,28},{20,24},{1,13},{5,9},{9,21},{1... | collective-permute-start | bytes 393224 | tf_op jit(solution)/shard_map/ppermute | solution.py:405
  18.8 0.3 collective-permute-start
  19.1 1.2 %collective-permute-start.3 = (bf16[128,1024]{1,0:T(8,128)(2,1)}, bf16[128,1024]{1,0:T(8,128)(2,1)S(1)}, u32[]{:S(2)}, u32[]{:S(2)}) collective-permute-start(bf16[128,1024]{1,0:T(8,128)(2,1)} %get-tuple-element.23), channel_id=1, source_target_pairs={{0,2},{1,3},{2,0},{3,1},{4,6},{5,7},{6,4},{7,5},{8,10},{9,11},{10,... | collective-permute-start | bytes 786440 | tf_op jit(solution)/shard_map/ppermute | solution.py:407
  20.3 2.5 %collective-permute-start.4 = (bf16[128,1024]{1,0:T(8,128)(2,1)}, bf16[128,1024]{1,0:T(8,128)(2,1)}, u32[]{:S(2)}, u32[]{:S(2)}) collective-permute-start(bf16[128,1024]{1,0:T(8,128)(2,1)} %get-tuple-element.24), channel_id=1, source_target_pairs={{0,3},{1,2},{2,1},{3,0},{4,7},{5,6},{6,5},{7,4},{8,11},{9,10},{10,... | collective-permute-start | bytes 786440 | tf_op jit(solution)/shard_map/ppermute | solution.py:407
  22.8 13.7 %collective-permute-done.1.one_ref = bf16[256,256]{1,0:T(8,128)(2,1)S(1)} collective-permute-done((bf16[256,256]{1,0:T(8,128)(2,1)}, bf16[256,256]{1,0:T(8,128)(2,1)S(1)}, u32[]{:S(2)}, u32[]{:S(2)}) %collective-permute-start.1) | collective-permute-done | bytes 131104 | tf_op jit(solution)/shard_map/ppermute | solution.py:404
  36.5 2.8 %collective-permute-done.2.two_ref = bf16[256,256]{1,0:T(8,128)(2,1)S(1)} collective-permute-done((bf16[256,256]{1,0:T(8,128)(2,1)}, bf16[256,256]{1,0:T(8,128)(2,1)S(1)}, u32[]{:S(2)}, u32[]{:S(2)}) %collective-permute-start.2) | collective-permute-done | bytes 131104 | tf_op jit(solution)/shard_map/ppermute | solution.py:405
  39.3 0.0 copy-start
  39.3 0.0 copy-start.2
  39.3 6.0 %collective-permute-start.5 = (bf16[512,256]{1,0:T(8,128)(2,1)S(1)}, bf16[512,256]{1,0:T(8,128)(2,1)}, u32[]{:S(2)}, u32[]{:S(2)}) collective-permute-start(bf16[512,256]{1,0:T(8,128)(2,1)S(1)} %shard_map.96.refs_2_.refs_1_), channel_id=1, source_target_pairs={{8,16},{12,20},{16,24},{20,28},{9,17},{13,21},{17,25},{21,29},{10,... | collective-permute-start | bytes 786440 | tf_op jit(solution)/shard_map/ppermute | solution.py:424
  45.3 0.0 copy-done
  45.3 3.5 %shard_map.98 = (bf16[256,2048]{1,0:T(8,128)(2,1)}, bf16[256,2048]{1,0:T(8,128)(2,1)}, bf16[256,1024]{1,0:T(8,128)(2,1)}, bf16[256,1024]{1,0:T(8,128)(2,1)}) custom-call(s32[1]{0:T(128)} %bitcast.1.side_ref, s32[1]{0:T(128)} %bitcast.2.tp_ref, bf16[256,8192]{1,0:T(8,128)(2,1)} %refs_0_.3, bf16[512,256]{1,0:T(8,128)(2,1)} %copy-done), custom_call_target="tpu_custom_call" | custom-call | flops 2000000000 | tf_op jit(solution)/shard_map/pallas_call | solution.py:67
  48.8 1.3 %collective-permute-start.7 = (bf16[256,1024]{1,0:T(8,128)(2,1)}, bf16[256,1024]{1,0:T(8,128)(2,1)S(1)}, u32[]{:S(2)}, u32[]{:S(2)}) collective-permute-start(bf16[256,1024]{1,0:T(8,128)(2,1)} %get-tuple-element.28), channel_id=1, source_target_pairs={{0,2},{1,3},{2,0},{3,1},{4,6},{5,7},{6,4},{7,5},{8,10},{9,11},{10,... | collective-permute-start | bytes 1572872 | tf_op jit(solution)/shard_map/ppermute | solution.py:419
  50.1 0.0 collective-permute-done.refs_1_
  50.1 1.2 %collective-permute-start.8 = (bf16[256,1024]{1,0:T(8,128)(2,1)}, bf16[256,1024]{1,0:T(8,128)(2,1)}, u32[]{:S(2)}, u32[]{:S(2)}) collective-permute-start(bf16[256,1024]{1,0:T(8,128)(2,1)} %get-tuple-element.29), channel_id=1, source_target_pairs={{0,3},{1,2},{2,1},{3,0},{4,7},{5,6},{6,5},{7,4},{8,11},{9,10},{10,... | collective-permute-start | bytes 1572872 | tf_op jit(solution)/shard_map/ppermute | solution.py:419
  51.3 0.0 copy-done.2
  51.3 0.0 collective-permute-done.3.refs_3_.refs_8_
  51.3 1.9 %collective-permute-start.10 = (bf16[64,256]{1,0:T(8,128)(2,1)S(1)}, bf16[64,256]{1,0:T(8,128)(2,1)S(1)}, u32[]{:S(2)}, u32[]{:S(2)}) collective-permute-start(bf16[64,256]{1,0:T(8,128)(2,1)S(1)} %slice.9), channel_id=1, source_target_pairs={{4,0},{8,4},{12,8},{16,12},{20,16},{24,20},{28,24},{5,1},{9,5},{13... | collective-permute-start | bytes 98312 | tf_op jit(solution)/shard_map/ppermute | solution.py:408
  53.3 0.0 collective-permute-done.4.refs_4_.refs_9_
  53.3 0.1 collective-permute-start.15
  53.3 0.0 collective-permute-done.5.refs_5_
  53.4 0.7 collective-permute-start.6
  54.0 0.0 copy-start.1
  54.0 0.9 copy-done.1
  55.0 0.0 copy-start.6
  55.0 0.9 copy-done.6
  55.9 2.5 %shard_map.97 = (f32[512,128]{1,0:T(8,128)S(1)}, f32[512,128]{1,0:T(8,128)S(1)}, f32[512,128]{1,0:T(8,128)S(1)}) custom-call(s32[1]{0:T(128)} %bitcast.pair_ref, s32[1]{0:T(128)} %bitcast.1.side_ref, bf16[256,384]{1,0:T(8,128)(2,1)S(1)} %copy-done.6, bf16[256,384]{1,0:T(8,128)(2,1)S(1)} %collective-permute-done.refs_1_, bf16[512,256]{1,0:T(8,128)(2,1)S(1)} %copy-done.1, ...), custom_call_target="tpu_custom_call" | custom-call | flops 3000000000 | tf_op jit(solution)/shard_map/pallas_call | solution.py:309
  58.5 0.0 collective-permute-done.6.refs_6_
  58.5 1.6 %collective-permute-start.16 = (bf16[128,1024]{1,0:T(8,128)(2,1)S(1)}, bf16[128,1024]{1,0:T(8,128)(2,1)}, u32[]{:S(2)}, u32[]{:S(2)}) collective-permute-start(bf16[128,1024]{1,0:T(8,128)(2,1)S(1)} %collective-permute-done.3.refs_3_.refs_8_), channel_id=1, source_target_pairs={{0,4},{4,0},{8,12},{12,8},{16,20},{20,16},{24,28},{28,24},{1,5},{5... | collective-permute-start | bytes 786440 | tf_op jit(solution)/shard_map/ppermute | solution.py:420
  60.1 1.7 %collective-permute-done.7.refs_7_.refs_6_ = bf16[256,1024]{1,0:T(8,128)(2,1)S(1)} collective-permute-done((bf16[256,1024]{1,0:T(8,128)(2,1)}, bf16[256,1024]{1,0:T(8,128)(2,1)S(1)}, u32[]{:S(2)}, u32[]{:S(2)}) %collective-permute-start.7) | collective-permute-done | bytes 524320 | tf_op jit(solution)/shard_map/ppermute | solution.py:419
  61.8 0.1 collective-permute-start.17
  61.9 12.2 %collective-permute-done.8.refs_8_.refs_7_ = bf16[256,1024]{1,0:T(8,128)(2,1)} collective-permute-done((bf16[256,1024]{1,0:T(8,128)(2,1)}, bf16[256,1024]{1,0:T(8,128)(2,1)}, u32[]{:S(2)}, u32[]{:S(2)}) %collective-permute-start.8) | collective-permute-done | bytes 524320 | tf_op jit(solution)/shard_map/ppermute | solution.py:419
  74.1 1.7 %shard_map.99 = (bf16[256,128]{1,0:T(8,128)(2,1)S(1)}, bf16[256,128]{1,0:T(8,128)(2,1)}) custom-call(s32[1]{0:T(128)} %bitcast.pair_ref, s32[1]{0:T(128)} %bitcast.1.side_ref, bf16[256,384]{1,0:T(8,128)(2,1)S(1)} %copy-done.6, bf16[256,384]{1,0:T(8,128)(2,1)S(1)} %collective-permute-done.refs_1_, f32[512,128]{1,0:T(8,128)S(1)} %get-tuple-element.25.refs_2_, ...), custom_call_target="tpu_custom_call" | custom-call | flops 3000000000 | tf_op jit(solution)/shard_map/pallas_call | solution.py:309
  75.8 0.1 collective-permute-start.9
  75.8 0.0 collective-permute-done.10.spill_ref
  75.9 0.0 copy-start.3
  75.9 0.6 copy-done.3
  76.5 0.0 all-to-all-done.incoming_ref
  76.5 0.0 copy-start.4
  76.5 0.8 copy-done.4
  77.2 0.6 shard_map.101
  77.8 3.3 %collective-permute-start.11 = (bf16[64,256]{1,0:T(8,128)(2,1)S(1)}, bf16[64,256]{1,0:T(8,128)(2,1)S(1)}, u32[]{:S(2)}, u32[]{:S(2)}) collective-permute-start(bf16[64,256]{1,0:T(8,128)(2,1)S(1)} %get-tuple-element.32), channel_id=1, source_target_pairs={{0,4},{4,8},{8,12},{12,16},{16,20},{20,24},{24,28},{1,5},{5,9},{9,... | collective-permute-start | bytes 98312 | tf_op jit(solution)/shard_map/ppermute | solution.py:431
  81.1 1.6 %shard_map.102 = bf16[256,256]{1,0:T(8,128)(2,1)S(1)} custom-call(bf16[256,256]{1,0:T(8,128)(2,1)S(1)} %copy-done.2, bf16[16,256]{1,0:T(8,128)(2,1)S(1)} %get-tuple-element.33.tail_ref, bf16[8,272,256]{2,1,0:T(8,128)(2,1)S(1)} %all-to-all-done.incoming_ref), custom_call_target="tpu_custom_call" | custom-call | flops 2000000000 | tf_op jit(solution)/shard_map/pallas_call | solution.py:238
  82.8 0.6 collective-permute-done.11
  83.4 0.1 slice_select_fusion
  83.5 1.2 %collective-permute-start.12 = (bf16[256,256]{1,0:T(8,128)(2,1)S(1)}, bf16[256,256]{1,0:T(8,128)(2,1)S(1)}, u32[]{:S(2)}, u32[]{:S(2)}) collective-permute-start(bf16[256,256]{1,0:T(8,128)(2,1)S(1)} %pad_maximum_fusion.refs_0_), channel_id=1, source_target_pairs={{0,1},{1,0},{2,3},{3,2},{4,5},{5,4},{6,7},{7,6},{8,9},{9,8},{10,11... | collective-permute-start | bytes 393224 | tf_op jit(solution)/shard_map/ppermute | solution.py:435
  84.7 0.0 collective-permute-done.16.refs_10_
  84.7 1.1 %collective-permute-start.13 = (bf16[256,256]{1,0:T(8,128)(2,1)S(1)}, bf16[256,256]{1,0:T(8,128)(2,1)S(1)}, u32[]{:S(2)}, u32[]{:S(2)}) collective-permute-start(bf16[256,256]{1,0:T(8,128)(2,1)S(1)} %pad_maximum_fusion.refs_0_), channel_id=1, source_target_pairs={{0,2},{1,3},{2,0},{3,1},{4,6},{5,7},{6,4},{7,5},{8,10},{9,11},{10,... | collective-permute-start | bytes 393224 | tf_op jit(solution)/shard_map/ppermute | solution.py:435
  85.8 0.0 collective-permute-done.9
  85.8 0.6 collective-permute-start.14
  86.4 0.7 maximum_select_fusion
  87.1 0.0 collective-permute-done.17.refs_11_
  87.1 0.0 collective-permute-done.15.refs_5_
  87.1 0.0 collective-permute-done.12.refs_1_
  87.1 2.6 %collective-permute-done.13.refs_2_ = bf16[256,256]{1,0:T(8,128)(2,1)S(1)} collective-permute-done((bf16[256,256]{1,0:T(8,128)(2,1)S(1)}, bf16[256,256]{1,0:T(8,128)(2,1)S(1)}, u32[]{:S(2)}, u32[]{:S(2)}) %collective-permute-start.13) | collective-permute-done | bytes 131104 | tf_op jit(solution)/shard_map/ppermute | solution.py:435
  89.7 3.0 %collective-permute-done.14.refs_3_ = bf16[256,256]{1,0:T(8,128)(2,1)S(1)} collective-permute-done((bf16[256,256]{1,0:T(8,128)(2,1)S(1)}, bf16[256,256]{1,0:T(8,128)(2,1)S(1)}, u32[]{:S(2)}, u32[]{:S(2)}) %collective-permute-start.14) | collective-permute-done | bytes 131104 | tf_op jit(solution)/shard_map/ppermute | solution.py:435
  92.7 0.0 copy-start.5
  92.7 1.2 %copy-done.5 = bf16[256,2048]{1,0:T(8,128)(2,1)S(1)} copy-done((bf16[256,2048]{1,0:T(8,128)(2,1)S(1)}, bf16[256,2048]{1,0:T(8,128)(2,1)}, u32[]{:S(2)}) %copy-start.5) | copy-done | bytes 1048600
  93.9 3.3 %shard_map.103 = bf16[256,2048]{1,0:T(8,128)(2,1)} custom-call(s32[1]{0:T(128)} %bitcast.1.side_ref, bf16[256,256]{1,0:T(8,128)(2,1)S(1)} %pad_maximum_fusion.refs_0_, bf16[256,256]{1,0:T(8,128)(2,1)S(1)} %collective-permute-done.12.refs_1_, bf16[256,256]{1,0:T(8,128)(2,1)S(1)} %collective-permute-done.13.refs_2_, ...), custom_call_target="tpu_custom_call" | custom-call | flops 3000000000 | tf_op jit(solution)/shard_map/pallas_call | solution.py:358
  (5 shorter events, 0.0 us)
Async XLA Ops:
  3.5 73.0 %all-to-all-start = ((bf16[8,272,256]{2,1,0:T(8,128)(2,1)}), bf16[8,272,256]{2,1,0:T(8,128)(2,1)S(1)}, u32[]{:S(2)}, u32[]{:S(2)}) async-start(bf16[8,272,256]{2,1,0:T(8,128)(2,1)} %shard_map.100), calls=%async_computation | async-start | bytes 2228224 | tf_op jit(solution)/shard_map/all_to_all | solution.py:410
  11.7 24.8 %collective-permute-start.1 = (bf16[256,256]{1,0:T(8,128)(2,1)}, bf16[256,256]{1,0:T(8,128)(2,1)S(1)}, u32[]{:S(2)}, u32[]{:S(2)}) collective-permute-start(bf16[256,256]{1,0:T(8,128)(2,1)} %get-tuple-element.21), channel_id=1, source_target_pairs={{0,8},{4,12},{8,16},{12,20},{16,24},{20,28},{1,9},{5,13},{9,17},{1... | collective-permute-start | bytes 393224 | tf_op jit(solution)/shard_map/ppermute | solution.py:404
  14.8 24.5 %collective-permute-start.2 = (bf16[256,256]{1,0:T(8,128)(2,1)}, bf16[256,256]{1,0:T(8,128)(2,1)S(1)}, u32[]{:S(2)}, u32[]{:S(2)}) collective-permute-start(bf16[256,256]{1,0:T(8,128)(2,1)} %get-tuple-element.22), channel_id=1, source_target_pairs={{0,12},{4,8},{8,20},{12,16},{16,28},{20,24},{1,13},{5,9},{9,21},{1... | collective-permute-start | bytes 393224 | tf_op jit(solution)/shard_map/ppermute | solution.py:405
  18.8 31.4 %collective-permute-start = (bf16[256,384]{1,0:T(8,128)(2,1)}, bf16[256,384]{1,0:T(8,128)(2,1)S(1)}, u32[]{:S(2)}, u32[]{:S(2)}) collective-permute-start(bf16[256,384]{1,0:T(8,128)(2,1)} %get-tuple-element.20), channel_id=1, source_target_pairs={{0,4},{4,0},{8,12},{12,8},{16,20},{20,16},{24,28},{28,24},{1,5},{5... | collective-permute-start | bytes 589832 | tf_op jit(solution)/shard_map/ppermute | solution.py:406
  19.1 32.2 %collective-permute-start.3 = (bf16[128,1024]{1,0:T(8,128)(2,1)}, bf16[128,1024]{1,0:T(8,128)(2,1)S(1)}, u32[]{:S(2)}, u32[]{:S(2)}) collective-permute-start(bf16[128,1024]{1,0:T(8,128)(2,1)} %get-tuple-element.23), channel_id=1, source_target_pairs={{0,2},{1,3},{2,0},{3,1},{4,6},{5,7},{6,4},{7,5},{8,10},{9,11},{10,... | collective-permute-start | bytes 786440 | tf_op jit(solution)/shard_map/ppermute | solution.py:407
  20.3 32.9 %collective-permute-start.4 = (bf16[128,1024]{1,0:T(8,128)(2,1)}, bf16[128,1024]{1,0:T(8,128)(2,1)}, u32[]{:S(2)}, u32[]{:S(2)}) collective-permute-start(bf16[128,1024]{1,0:T(8,128)(2,1)} %get-tuple-element.24), channel_id=1, source_target_pairs={{0,3},{1,2},{2,1},{3,0},{4,7},{5,6},{6,5},{7,4},{8,11},{9,10},{10,... | collective-permute-start | bytes 786440 | tf_op jit(solution)/shard_map/ppermute | solution.py:407
  39.3 6.0 %copy-start = (bf16[512,256]{1,0:T(8,128)(2,1)}, bf16[512,256]{1,0:T(8,128)(2,1)S(1)}, u32[]{:S(2)}) copy-start(bf16[512,256]{1,0:T(8,128)(2,1)S(1)} %shard_map.96.refs_2_.refs_1_) | copy-start | bytes 786436
  39.3 12.0 %copy-start.2 = (bf16[256,256]{1,0:T(8,128)(2,1)S(1)}, bf16[256,256]{1,0:T(8,128)(2,1)}, u32[]{:S(2)}) copy-start(bf16[256,256]{1,0:T(8,128)(2,1)} %queries_ref.3) | copy-start | bytes 393220
  39.3 14.0 %collective-permute-start.5 = (bf16[512,256]{1,0:T(8,128)(2,1)S(1)}, bf16[512,256]{1,0:T(8,128)(2,1)}, u32[]{:S(2)}, u32[]{:S(2)}) collective-permute-start(bf16[512,256]{1,0:T(8,128)(2,1)S(1)} %shard_map.96.refs_2_.refs_1_), channel_id=1, source_target_pairs={{8,16},{12,20},{16,24},{20,28},{9,17},{13,21},{17,25},{21,29},{10,... | collective-permute-start | bytes 786440 | tf_op jit(solution)/shard_map/ppermute | solution.py:424
  48.8 13.0 %collective-permute-start.7 = (bf16[256,1024]{1,0:T(8,128)(2,1)}, bf16[256,1024]{1,0:T(8,128)(2,1)S(1)}, u32[]{:S(2)}, u32[]{:S(2)}) collective-permute-start(bf16[256,1024]{1,0:T(8,128)(2,1)} %get-tuple-element.28), channel_id=1, source_target_pairs={{0,2},{1,3},{2,0},{3,1},{4,6},{5,7},{6,4},{7,5},{8,10},{9,11},{10,... | collective-permute-start | bytes 1572872 | tf_op jit(solution)/shard_map/ppermute | solution.py:419
  50.1 24.0 %collective-permute-start.8 = (bf16[256,1024]{1,0:T(8,128)(2,1)}, bf16[256,1024]{1,0:T(8,128)(2,1)}, u32[]{:S(2)}, u32[]{:S(2)}) collective-permute-start(bf16[256,1024]{1,0:T(8,128)(2,1)} %get-tuple-element.29), channel_id=1, source_target_pairs={{0,3},{1,2},{2,1},{3,0},{4,7},{5,6},{6,5},{7,4},{8,11},{9,10},{10,... | collective-permute-start | bytes 1572872 | tf_op jit(solution)/shard_map/ppermute | solution.py:419
  51.3 24.5 %collective-permute-start.10 = (bf16[64,256]{1,0:T(8,128)(2,1)S(1)}, bf16[64,256]{1,0:T(8,128)(2,1)S(1)}, u32[]{:S(2)}, u32[]{:S(2)}) collective-permute-start(bf16[64,256]{1,0:T(8,128)(2,1)S(1)} %slice.9), channel_id=1, source_target_pairs={{4,0},{8,4},{12,8},{16,12},{20,16},{24,20},{28,24},{5,1},{9,5},{13... | collective-permute-start | bytes 98312 | tf_op jit(solution)/shard_map/ppermute | solution.py:408
  53.3 33.8 %collective-permute-start.15 = (bf16[256,2048]{1,0:T(8,128)(2,1)}, bf16[256,2048]{1,0:T(8,128)(2,1)S(1)}, u32[]{:S(2)}, u32[]{:S(2)}) collective-permute-start(bf16[256,2048]{1,0:T(8,128)(2,1)} %get-tuple-element.35), channel_id=1, source_target_pairs={{0,1},{1,0},{2,3},{3,2},{4,5},{5,4},{6,7},{7,6},{8,9},{9,8},{10,11... | collective-permute-start | bytes 3145736 | tf_op jit(solution)/shard_map/ppermute | solution.py:418
  53.4 5.1 %collective-permute-start.6 = (bf16[512,256]{1,0:T(8,128)(2,1)}, bf16[512,256]{1,0:T(8,128)(2,1)S(1)}, u32[]{:S(2)}, u32[]{:S(2)}) collective-permute-start(bf16[512,256]{1,0:T(8,128)(2,1)} %collective-permute-done.5.refs_5_), channel_id=1, source_target_pairs={{16,24},{20,28},{17,25},{21,29},{18,26},{22,30},{19,27},{23,31}} | collective-permute-start | bytes 786440 | tf_op jit(solution)/shard_map/ppermute | solution.py:424
  54.0 1.0 copy-start.1
  55.0 0.9 copy-start.6
  58.5 26.2 %collective-permute-start.16 = (bf16[128,1024]{1,0:T(8,128)(2,1)S(1)}, bf16[128,1024]{1,0:T(8,128)(2,1)}, u32[]{:S(2)}, u32[]{:S(2)}) collective-permute-start(bf16[128,1024]{1,0:T(8,128)(2,1)S(1)} %collective-permute-done.3.refs_3_.refs_8_), channel_id=1, source_target_pairs={{0,4},{4,0},{8,12},{12,8},{16,20},{20,16},{24,28},{28,24},{1,5},{5... | collective-permute-start | bytes 786440 | tf_op jit(solution)/shard_map/ppermute | solution.py:420
  61.8 25.3 %collective-permute-start.17 = (bf16[128,1024]{1,0:T(8,128)(2,1)}, bf16[128,1024]{1,0:T(8,128)(2,1)}, u32[]{:S(2)}, u32[]{:S(2)}) collective-permute-start(bf16[128,1024]{1,0:T(8,128)(2,1)} %collective-permute-done.4.refs_4_.refs_9_), channel_id=1, source_target_pairs={{0,4},{4,0},{8,12},{12,8},{16,20},{20,16},{24,28},{28,24},{1,5},{5... | collective-permute-start | bytes 786440 | tf_op jit(solution)/shard_map/ppermute | solution.py:420
  75.8 10.0 %collective-permute-start.9 = (bf16[256,128]{1,0:T(8,128)(2,1)}, bf16[256,128]{1,0:T(8,128)(2,1)S(1)}, u32[]{:S(2)}, u32[]{:S(2)}) collective-permute-start(bf16[256,128]{1,0:T(8,128)(2,1)} %get-tuple-element.31), channel_id=1, source_target_pairs={{0,4},{4,0},{8,12},{12,8},{16,20},{20,16},{24,28},{28,24},{1,5},{5... | collective-permute-start | bytes 196616 | tf_op jit(solution)/shard_map/ppermute | solution.py:428
  75.9 0.6 copy-start.3
  76.5 0.8 copy-start.4
  77.8 5.6 %collective-permute-start.11 = (bf16[64,256]{1,0:T(8,128)(2,1)S(1)}, bf16[64,256]{1,0:T(8,128)(2,1)S(1)}, u32[]{:S(2)}, u32[]{:S(2)}) collective-permute-start(bf16[64,256]{1,0:T(8,128)(2,1)S(1)} %get-tuple-element.32), channel_id=1, source_target_pairs={{0,4},{4,8},{8,12},{12,16},{16,20},{20,24},{24,28},{1,5},{5,9},{9,... | collective-permute-start | bytes 98312 | tf_op jit(solution)/shard_map/ppermute | solution.py:431
  83.5 3.6 %collective-permute-start.12 = (bf16[256,256]{1,0:T(8,128)(2,1)S(1)}, bf16[256,256]{1,0:T(8,128)(2,1)S(1)}, u32[]{:S(2)}, u32[]{:S(2)}) collective-permute-start(bf16[256,256]{1,0:T(8,128)(2,1)S(1)} %pad_maximum_fusion.refs_0_), channel_id=1, source_target_pairs={{0,1},{1,0},{2,3},{3,2},{4,5},{5,4},{6,7},{7,6},{8,9},{9,8},{10,11... | collective-permute-start | bytes 393224 | tf_op jit(solution)/shard_map/ppermute | solution.py:435
  84.7 5.1 %collective-permute-start.13 = (bf16[256,256]{1,0:T(8,128)(2,1)S(1)}, bf16[256,256]{1,0:T(8,128)(2,1)S(1)}, u32[]{:S(2)}, u32[]{:S(2)}) collective-permute-start(bf16[256,256]{1,0:T(8,128)(2,1)S(1)} %pad_maximum_fusion.refs_0_), channel_id=1, source_target_pairs={{0,2},{1,3},{2,0},{3,1},{4,6},{5,7},{6,4},{7,5},{8,10},{9,11},{10,... | collective-permute-start | bytes 393224 | tf_op jit(solution)/shard_map/ppermute | solution.py:435
  85.8 6.9 %collective-permute-start.14 = (bf16[256,256]{1,0:T(8,128)(2,1)S(1)}, bf16[256,256]{1,0:T(8,128)(2,1)S(1)}, u32[]{:S(2)}, u32[]{:S(2)}) collective-permute-start(bf16[256,256]{1,0:T(8,128)(2,1)S(1)} %pad_maximum_fusion.refs_0_), channel_id=1, source_target_pairs={{0,3},{1,2},{2,1},{3,0},{4,7},{5,6},{6,5},{7,4},{8,11},{9,10},{10,... | collective-permute-start | bytes 393224 | tf_op jit(solution)/shard_map/ppermute | solution.py:435
  92.7 1.2 %copy-start.5 = (bf16[256,2048]{1,0:T(8,128)(2,1)S(1)}, bf16[256,2048]{1,0:T(8,128)(2,1)}, u32[]{:S(2)}) copy-start(bf16[256,2048]{1,0:T(8,128)(2,1)} %get-tuple-element.34.refs_4_) | copy-start | bytes 3145732

commit v9 on v8

--- a/solution.py
+++ b/solution.py
@@ -45,8 +45,9 @@
 
 
 def cut_kernel(plan, side_ref, tp_ref, *refs):
-    sems, refs = refs[-1], refs[:-1]
+    mark_ref, sems, refs = refs[-2], refs[-1], refs[:-2]
     sources, outs = refs, refs[len(refs) - len(plan) :]
+    mark_ref[0] = 0
     pieces = []
     for out, parts in zip(outs, plan):
         for at, (index, step, total, offset, width, depth) in enumerate(parts):
@@ -64,31 +65,53 @@
     for parts in plan:
         shape = (parts[0][5], len(parts) * parts[0][4])
         shapes.append(jax.ShapeDtypeStruct(shape, sources[parts[0][0]].dtype))
+    shapes.append(jax.ShapeDtypeStruct((1,), jnp.int32))
     return pl.pallas_call(
         functools.partial(cut_kernel, plan),
         out_shape=tuple(shapes),
         in_specs=[SMEM] * 2 + [ANY] * (len(sources) + len(before)),
-        out_specs=(VMEM,) * len(shapes),
+        out_specs=(VMEM,) * len(plan) + (SMEM,),
         scratch_shapes=[pltpu.SemaphoreType.DMA((sum(len(parts) for parts in plan),))],
         cost_estimate=takes(2),
     )(side, tp, *sources, *before)
 
 
-def stack_kernel(one_ref, two_ref, kv_ref):
+def stack_kernel(one_ref, two_ref, *refs):
+    kv_ref, mark_ref = refs[-2:]
     rows = one_ref.shape[0]
     kv_ref[:rows, :] = one_ref[...]
     kv_ref[rows:, :] = two_ref[...]
-
-
-def stack(one, two):
+    mark_ref[...] = jnp.zeros(mark_ref.shape, jnp.float32)
+
+
+def stack(one, two, mark, before):
     rows, width = one.shape
     return pl.pallas_call(
         stack_kernel,
-        out_shape=jax.ShapeDtypeStruct((2 * rows, width), one.dtype),
-        in_specs=[VMEM] * 2,
-        out_specs=VMEM,
-        compiler_params=PARAMS,
-    )(one, two)
+        out_shape=(
+            jax.ShapeDtypeStruct((2 * rows, width), one.dtype),
+            jax.ShapeDtypeStruct((8, HD), jnp.float32),
+        ),
+        in_specs=[VMEM] * 2 + [SMEM] + [ANY] * len(before),
+        out_specs=(VMEM, VMEM),
+        compiler_params=PARAMS,
+    )(one, two, mark, *before)
+
+
+def fence_kernel(held_ref, mark_ref, out_ref, value_ref):
+    value_ref[...] = mark_ref[...]
+
+
+def fence(held, mark):
+    return pl.pallas_call(
+        fence_kernel,
+        out_shape=jax.ShapeDtypeStruct(held.shape, held.dtype),
+        in_specs=[ANY, VMEM],
+        out_specs=ANY,
+        scratch_shapes=[pltpu.VMEM(mark.shape, mark.dtype)],
+        input_output_aliases={0: 0},
+        cost_estimate=takes(5),
+    )(held, mark)
 
 
 def arrange_kernel(slot_ref, keys_ref, values_ref, out_ref, held_ref, sems):
@@ -179,7 +202,8 @@
     return (mixed / total).astype(jnp.bfloat16)
 
 
-def last_kernel(queries_ref, spill_ref, incoming_ref, tail_ref, next_ref, order_ref):
+def last_kernel(queries_ref, spill_ref, incoming_ref, *refs):
+    tail_ref, next_ref, order_ref = refs[-3:]
     find_sources(incoming_ref, order_ref)
     rows, width = queries_ref.shape
     last = rows // BLOCK - 1
@@ -218,7 +242,7 @@
     return [pltpu.SMEM((2 * rows // BLOCK,), jnp.int32)]
 
 
-def last_attend(queries, spill, incoming):
+def last_attend(queries, spill, incoming, mark, before):
     rows, width = queries.shape
     return pl.pallas_call(
         last_kernel,
@@ -226,12 +250,12 @@
             jax.ShapeDtypeStruct((LEAD, width), queries.dtype),
             jax.ShapeDtypeStruct((BLOCK, width), queries.dtype),
         ),
-        in_specs=[VMEM] * 3,
+        in_specs=[VMEM] * 3 + [SMEM] + [ANY] * len(before),
         out_specs=(VMEM, VMEM),
         scratch_shapes=order_scratch(rows),
         compiler_params=PARAMS,
         cost_estimate=takes(1),
-    )(queries, spill, incoming)
+    )(queries, spill, incoming, mark, *before)
 
 
 def other_attend(queries, tail, incoming):
@@ -248,10 +272,12 @@
 
 def self_kernel(first, step, chunks, pair_ref, side_ref, *refs):
     tokens, refs = refs[:2], refs[2:]
-    state, refs = ((), refs) if first else (refs[:3], refs[3:])
+    state, refs = ((), refs) if first else (refs[:1], refs[1:])
     kvs, refs = refs[:chunks], refs[chunks:]
     peak_ref, total_ref, accum_ref = refs[-3:]
-    outs = refs[-6:-3] if first else refs[-5:-3]
+    outs = refs[-5:-3]
+    if first:
+        outs[1][0] = 0
     tile = tokens[0].shape[0]
     for part, q_ref in enumerate(tokens):
         at = pl.ds(part * tile, tile)
@@ -284,25 +310,28 @@
                 functools.partial(attend, tokens[1 - part], False)
             )
         else:
-            peak_ref[at, :] = state[0][at, :]
-            total_ref[at, :] = state[1][at, :]
-            accum_ref[at, :] = state[2][at, :]
+            accum_ref[at, :] = state[0][at, :HD]
+            peak_ref[at, :] = jnp.broadcast_to(state[0][at, HD : HD + 1], (tile, HD))
+            total_ref[at, :] = jnp.broadcast_to(state[0][at, 2 * HD - 1 :], (tile, HD))
         for index, kv_ref in enumerate(kvs):
             pl.when(pair_ref[0] >= step + index)(functools.partial(attend, kv_ref, False))
         if first:
-            outs[0][at, :] = peak_ref[at, :]
-            outs[1][at, :] = total_ref[at, :]
-            outs[2][at, :] = accum_ref[at, :]
+            lane = lax.broadcasted_iota(jnp.int32, (tile, HD), 1)
+            outs[0][at, :HD] = accum_ref[at, :]
+            outs[0][at, HD:] = jnp.where(lane == 0, peak_ref[at, :], total_ref[at, :])
         else:
             outs[part][...] = (accum_ref[at, :] / total_ref[at, :]).astype(jnp.bfloat16)
 
 
-def self_steps(pair, side, tokens, state, kvs, step, before):
+def self_steps(pair, side, tokens, state, kvs, step, before, cost):
     tile = tokens[0].shape[0]
     rows = 2 * tile
     first = not state
     if first:
-        out_shape = (jax.ShapeDtypeStruct((rows, HD), jnp.float32),) * 3
+        out_shape = (
+            jax.ShapeDtypeStruct((rows, 2 * HD), jnp.float32),
+            jax.ShapeDtypeStruct((1,), jnp.int32),
+        )
     else:
         out_shape = (jax.ShapeDtypeStruct((tile, HD), jnp.bfloat16),) * 2
     operands = (*tokens, *state, *kvs)
@@ -310,39 +339,50 @@
         functools.partial(self_kernel, first, step, len(kvs)),
         out_shape=out_shape,
         in_specs=[SMEM] * 2 + [VMEM] * len(operands) + [ANY] * len(before),
-        out_specs=(VMEM,) * len(out_shape),
+        out_specs=(VMEM, SMEM if first else VMEM),
         scratch_shapes=[pltpu.VMEM((rows, HD), jnp.float32)] * 3,
         compiler_params=PARAMS,
-        cost_estimate=takes(3),
+        cost_estimate=takes(cost),
     )(pair, side, *operands, *before)
 
 
-def project_kernel(groups, side_ref, *refs):
+def near_kernel(one_ref, two_ref, own_ref, beside_ref, partial_ref):
+    width = partial_ref.shape[1]
+    term = jnp.concatenate([one_ref[...], two_ref[...]], axis=1)
+    tile = min(512, width)
+    for column in range(0, width, tile):
+        at = slice(column, column + tile)
+        partial_ref[:, at] = dot(
+            term, jnp.concatenate([own_ref[:, at], beside_ref[:, at]], axis=0)
+        )
+
+
+def project_near(terms, own, beside):
+    return pl.pallas_call(
+        near_kernel,
+        out_shape=jax.ShapeDtypeStruct((terms[0].shape[0], own.shape[1]), jnp.float32),
+        in_specs=[VMEM] * 4,
+        out_specs=VMEM,
+        compiler_params=PARAMS,
+    )(*terms, own, beside)
+
+
+def far_kernel(count, side_ref, partial_ref, *refs):
     crossed_ref, out_ref, sems = refs[-3:]
-    terms, near, far = refs[:groups], refs[groups : groups + 2], refs[groups + 2 : -3]
-    direct, shared, fetched = (far[at * (groups - 2) : (at + 1) * (groups - 2)] for at in range(3))
+    terms, shared, fetched = (refs[at * count : (at + 1) * count] for at in range(3))
     width = crossed_ref.shape[1]
-    half = width // 2
-    tile = min(512, half)
+    tile = min(512, width)
     share = shared[0].shape[0]
     mine = pl.ds(pl.multiple_of(side_ref[0] * share, HD), share)
     other = pl.ds(pl.multiple_of((1 - side_ref[0]) * share, HD), share)
-    term = jnp.concatenate([held[...] for held in terms], axis=1)
-    split = [held[...] for held in terms[:2]]
-    split += [held[:, part] for held in terms[2:] for part in (mine, other)]
-    split = jnp.concatenate(split, axis=1)
+    term = [held[:, part] for held in terms for part in (mine, other)]
+    term = jnp.concatenate(term, axis=1)
     outs = []
     for column in range(0, width, tile):
         at = slice(column, column + tile)
-        weight = [block[:, at] for block in near]
-        if column < half:
-            for pieces in zip(shared, fetched):
-                weight += [piece[:, at] for piece in pieces]
-        else:
-            start = column - half
-            weight += [block[:, start : start + tile] for block in direct]
-        total = dot(split if column < half else term, jnp.concatenate(weight, axis=0))
-        out_ref[:, at] = total.astype(out_ref.dtype)
+        weight = [piece[:, at] for pieces in zip(shared, fetched) for piece in pieces]
+        total = dot(term, jnp.concatenate(weight, axis=0))
+        out_ref[:, at] = (partial_ref[:, at] + total).astype(out_ref.dtype)
         out = pltpu.make_async_copy(
             out_ref.at[:, at], crossed_ref.at[:, at], sems.at[len(outs)]
         )
@@ -352,21 +392,21 @@
         out.wait()
 
 
-def project(side, terms, own, beside, direct, shared, fetched):
-    rows, width = terms[0].shape[0], beside.shape[1]
-    operands = (*terms, own, beside, *direct, *shared, *fetched)
-    return pl.pallas_call(
-        functools.partial(project_kernel, len(terms)),
+def project_far(side, partial, terms, shared, fetched):
+    rows, width = partial.shape
+    operands = (*terms, *shared, *fetched)
+    return pl.pallas_call(
+        functools.partial(far_kernel, len(terms)),
         out_shape=jax.ShapeDtypeStruct((rows, width), jnp.bfloat16),
-        in_specs=[SMEM] + [VMEM] * len(operands),
+        in_specs=[SMEM] + [VMEM] * (1 + len(operands)),
         out_specs=ANY,
         scratch_shapes=[
             pltpu.VMEM((rows, width), jnp.bfloat16),
-            pltpu.SemaphoreType.DMA((width // min(512, width // 2),)),
+            pltpu.SemaphoreType.DMA((width // min(512, width),)),
         ],
         compiler_params=PARAMS,
-        cost_estimate=takes(3),
-    )(side, *operands)
+        cost_estimate=takes(2),
+    )(side, partial, *operands)
 
 
 def shards(queries, keys, values, cross_queries, nbr_keys, nbr_values, nbr_slot, w_cross):
@@ -391,49 +431,50 @@
             jnp.concatenate([other, mine], axis),
         )
 
-    half = width // 2
     far = range(2, groups)
     forward = [[(i, i + 2) for i in range(2 * turn, count - 2)] for turn in range(pairs)]
     diagonal = [(i, (i + 2) ^ 1) for i in range(count - 2)]
-    mine, away, kv_mine, kv_away, *blocks = cut(
+    mine, away, kv_mine, kv_away, *blocks, mark = cut(
         side, tp, (queries, keys, values, w_cross),
         [[(at, 1 - own, 0, 0, HD, rows) for at in (0, 1, 2)] for own in (1, 0)]
         + [[(at, 1 - own, 0, 0, HD, rows) for at in (1, 2)] for own in (1, 0)]
-        + [[(3, step, width, 0, half, depth // 2)] for step in far],
+        + [[(3, step, width, 0, width, depth // 2)] for step in far],
     )
     near = lax.ppermute(kv_mine, "ctx", forward[0])
     apart = lax.ppermute(kv_away, "ctx", diagonal)
     other = lax.ppermute(away, "ctx", swap)
     shared = [lax.ppermute(block, "tp", across[step]) for step, block in zip(far, blocks)]
+    fetched = [lax.ppermute(block, "ctx", swap) for block in shared]
     spill = lax.ppermute(cross_queries[:BLOCK], "ctx", [(i + 1, i) for i in range(count - 1)])
     outgoing = arrange(nbr_slot, nbr_keys, nbr_values, count)
-    incoming = lax.all_to_all(outgoing, "ctx", split_axis=0, concat_axis=0, tiled=True)
-    kv = stack(near, apart)
-    own, beside, *blocks = cut(
-        side, tp, (w_cross,),
-        [[(0, step, width, 0, width, depth)] for step in range(2)]
-        + [[(0, step, width, half, half, depth)] for step in far],
-        (kv,),
+    own, beside, mark = cut(
+        side, tp, (w_cross,), [[(0, step, width, 0, width, depth)] for step in range(2)], (kv_away,)
     )
     beside = lax.ppermute(beside, "tp", across[1])
-    direct = [lax.ppermute(block, "tp", across[step]) for step, block in zip(far, blocks)]
-    fetched = [lax.ppermute(block, "ctx", swap) for block in shared]
+    kv, kv_mark = stack(near, apart, mark, (other,))
+    incoming = lax.all_to_all(
+        fence(outgoing, kv_mark), "ctx", split_axis=0, concat_axis=0, tiled=True
+    )
 
     kvs = [kv]
     for step in range(2, pairs):
         kvs.append(lax.ppermute(kvs[-1], "ctx", forward[step - 1]))
     tokens = (mine, other)
-    state = self_steps(pair, side, tokens, (), kvs[:1], 1, shared)
-    ours, theirs = self_steps(pair, side, tokens, state, kvs[1:], 2, direct)
-    attended = both(ours, lax.ppermute(theirs, "ctx", swap), 1)
-
-    tail, onward = last_attend(cross_queries, spill, incoming)
+    middle = pairs // 2
+    *state, mark = self_steps(pair, side, tokens, (), kvs[:middle], 1, (), 12)
+
+    tail, onward = last_attend(cross_queries, spill, incoming, mark, (*shared, beside))
     back = lax.ppermute(onward, "ctx", [(i, i + 1) for i in range(count - 1)])
     answers = other_attend(cross_queries, tail, incoming)
     early = jnp.arange(BLOCK)[:, None] < BLOCK - 1
     cca = jnp.concatenate([jnp.where(early, back, answers[:BLOCK]), answers[BLOCK:]], axis=0)
     terms = [cca] + [lax.ppermute(cca, "tp", across[step]) for step in range(1, groups)]
-    crossed = project(side, terms, own, beside, direct, shared, fetched)
+    partial = project_near(terms[:2], own, beside)
+
+    before = (*terms[2:], *fetched)
+    ours, theirs = self_steps(pair, side, tokens, state, kvs[middle:], middle + 1, before, 2)
+    attended = both(ours, lax.ppermute(theirs, "ctx", swap), 1)
+    crossed = project_far(side, partial, terms[2:], shared, fetched)
     return (attended, crossed)
 
 

time: 97.8 us -> 106 us (1.084)
  the two profiles are of different devices: /device:TPU:9 before, /device:TPU:17 now
where the time goes in v9:
time: 106 us
  waiting for transfers between devices  39.9 us (38%)
  starting transfers between devices  35.1 us (33%)
  Pallas kernels  24 us (23%)
  local copies, waits for them, and re-layouts  4.91 us (5%)
    ppermute x2, waiting for transfers between devices, shards(): kvs.append(lax.ppermute(kvs[-1], 'ctx', forward[step - 1]))  18.7 us
    ppermute x1, waiting for transfers between devices, shards(): back = lax.ppermute(onward, 'ctx', [(i, i + 1) for i in range(count - 1)])  15.7 us
    pallas_call x2, Pallas kernels, self_steps(): pl.pallas_call(functools.partial(self_kernel, first, step, len(kvs)), out...  6.51 us
    pallas_call x2, Pallas kernels, cut(): pl.pallas_call(functools.partial(cut_kernel, plan), out_shape=tuple(shape...  5.7 us
    ppermute x3, waiting for transfers between devices, shards(): lax.ppermute(cca, 'tp', across[step])  5.43 us
    ppermute x2, starting transfers between devices, shards(): kvs.append(lax.ppermute(kvs[-1], 'ctx', forward[step - 1]))  5.06 us
    all_to_all x1, starting transfers between devices, shards(): lax.all_to_all(fence(outgoing, kv_mark), 'ctx', split_axis=0, concat_axis...  5.01 us
    unnamed x14, local copies, waits for them, and re-layouts  4.28 us
  transfers between devices with their start and end apart: 17, of which 4 were waited for; matrix products, arithmetic and copies ran while one was open for 1% of the time, Pallas kernels for 18%

profile of v9, /device:TPU:17, one launch (start us, length us, event | category | flops | bytes accessed | tf_op | source)
XLA Modules:
  0.0 105.5 jit_solution(5780139972631216753)
XLA Ops:
  0.6 2.8 %shard_map.95 = (bf16[256,384]{1,0:T(8,128)(2,1)}, bf16[256,384]{1,0:T(8,128)(2,1)}, bf16[256,256]{1,0:T(8,128)(2,1)}, bf16[256,256]{1,0:T(8,128)(2,1)}, bf16[12...) custom-call(s32[1]{0:T(128)} %bitcast.1.side_ref, s32[1]{0:T(128)} %bitcast.2.tp_ref, ...), custom_call_target="tpu_custom_call" | custom-call | flops 2000000000 | tf_op jit(solution)/shard_map/pallas_call | solution.py:69
  3.5 1.3 %collective-permute-start = (bf16[256,384]{1,0:T(8,128)(2,1)}, bf16[256,384]{1,0:T(8,128)(2,1)S(1)}, u32[]{:S(2)}, u32[]{:S(2)}) collective-permute-start(bf16[256,384]{1,0:T(8,128)(2,1)} %get-tuple-element.20), channel_id=1, source_target_pairs={{0,4},{4,0},{8,12},{12,8},{16,20},{20,16},{24,28},{28,24},{1,5},{5... | collective-permute-start | bytes 589832 | tf_op jit(solution)/shard_map/ppermute | solution.py:445
  4.8 3.1 %collective-permute-start.2 = (bf16[256,256]{1,0:T(8,128)(2,1)}, bf16[256,256]{1,0:T(8,128)(2,1)S(1)}, u32[]{:S(2)}, u32[]{:S(2)}) collective-permute-start(bf16[256,256]{1,0:T(8,128)(2,1)} %get-tuple-element.22.refs_1_), channel_id=1, source_target_pairs={{0,12},{4,8},{8,20},{12,16},{16,28},{20,24},{1,13},{5,9},{9,21},{1... | collective-permute-start | bytes 393224 | tf_op jit(solution)/shard_map/ppermute | solution.py:444
  7.9 1.9 %collective-permute-start.1 = (bf16[256,256]{1,0:T(8,128)(2,1)}, bf16[256,256]{1,0:T(8,128)(2,1)S(1)}, u32[]{:S(2)}, u32[]{:S(2)}) collective-permute-start(bf16[256,256]{1,0:T(8,128)(2,1)} %get-tuple-element.21), channel_id=1, source_target_pairs={{0,8},{4,12},{8,16},{12,20},{16,24},{20,28},{1,9},{5,13},{9,17},{1... | collective-permute-start | bytes 393224 | tf_op jit(solution)/shard_map/ppermute | solution.py:443
  9.8 2.8 %shard_map.99.held_ref = bf16[8,272,256]{2,1,0:T(8,128)(2,1)} custom-call(s32[8]{0:T(128)} %slot_ref.1, bf16[8,128,256]{2,1,0:T(8,128)(2,1)} %keys_ref.1, bf16[8,128,256]{2,1,0:T(8,128)(2,1)} %values_ref.1), custom_call_target="tpu_custom_call" | custom-call | flops 3000000000 | tf_op jit(solution)/shard_map/pallas_call | solution.py:166
  12.7 2.9 %shard_map.96 = (bf16[256,2048]{1,0:T(8,128)(2,1)}, bf16[256,2048]{1,0:T(8,128)(2,1)}, s32[1]{0:T(128)}) custom-call(s32[1]{0:T(128)} %bitcast.1.side_ref, s32[1]{0:T(128)} %bitcast.2.tp_ref, bf16[256,8192]{1,0:T(8,128)(2,1)} %refs_0_.3, bf16[256,256]{1,0:T(8,128)(2,1)} %get-tuple-element.22.refs_1_), custom_call_target="tpu_custom_call" | custom-call | flops 2000000000 | tf_op jit(solution)/shard_map/pallas_call | solution.py:69
  15.6 0.0 collective-permute-done.2.two_ref
  15.6 0.0 collective-permute-done.1.one_ref
  15.6 0.0 collective-permute-done.refs_1_
  15.6 1.3 %shard_map.97 = (bf16[512,256]{1,0:T(8,128)(2,1)}, f32[8,128]{1,0:T(8,128)S(1)}) custom-call(bf16[256,256]{1,0:T(8,128)(2,1)S(1)} %collective-permute-done.1.one_ref, bf16[256,256]{1,0:T(8,128)(2,1)S(1)} %collective-permute-done.2.two_ref, s32[1]{0:T(128)} %get-tuple-element.23.refs_0_, bf16[256,384]{1,0:T(8,128)(2,1)S(1)} %collective-permute-done.refs_1_), custom_call_target="tpu_custom_call" | custom-call | tf_op jit(solution)/shard_map/pallas_call | solution.py:89
  16.9 0.0 copy-start.2
  16.9 0.6 copy-done.2
  17.5 0.7 shard_map.100
  18.2 0.0 copy-start.1
  18.2 5.0 %all-to-all-start = ((bf16[8,272,256]{2,1,0:T(8,128)(2,1)}), bf16[8,272,256]{2,1,0:T(8,128)(2,1)S(1)}, u32[]{:S(2)}, u32[]{:S(2)}) async-start(bf16[8,272,256]{2,1,0:T(8,128)(2,1)} %shard_map.100), calls=%async_computation | async-start | bytes 2228224 | tf_op jit(solution)/shard_map/all_to_all | solution.py:455
  23.2 3.1 %collective-permute-start.3 = (bf16[512,256]{1,0:T(8,128)(2,1)}, bf16[512,256]{1,0:T(8,128)(2,1)}, u32[]{:S(2)}, u32[]{:S(2)}) collective-permute-start(bf16[512,256]{1,0:T(8,128)(2,1)} %get-tuple-element.24.refs_2_), channel_id=1, source_target_pairs={{8,16},{12,20},{16,24},{20,28},{9,17},{13,21},{17,25},{21,29},{10,... | collective-permute-start | bytes 786440 | tf_op jit(solution)/shard_map/ppermute | solution.py:461
  26.3 2.4 %collective-permute-start.8 = (bf16[256,2048]{1,0:T(8,128)(2,1)}, bf16[256,2048]{1,0:T(8,128)(2,1)S(1)}, u32[]{:S(2)}, u32[]{:S(2)}) collective-permute-start(bf16[256,2048]{1,0:T(8,128)(2,1)} %get-tuple-element.30), channel_id=1, source_target_pairs={{0,1},{1,0},{2,3},{3,2},{4,5},{5,4},{6,7},{7,6},{8,9},{9,8},{10,11... | collective-permute-start | bytes 3145736 | tf_op jit(solution)/shard_map/ppermute | solution.py:453
  28.7 1.2 %collective-permute-start.6 = (bf16[128,2048]{1,0:T(8,128)(2,1)}, bf16[128,2048]{1,0:T(8,128)(2,1)S(1)}, u32[]{:S(2)}, u32[]{:S(2)}) collective-permute-start(bf16[128,2048]{1,0:T(8,128)(2,1)} %get-tuple-element.28), channel_id=1, source_target_pairs={{0,2},{1,3},{2,0},{3,1},{4,6},{5,7},{6,4},{7,5},{8,10},{9,11},{10,... | collective-permute-start | bytes 1572872 | tf_op jit(solution)/shard_map/ppermute | solution.py:446
  30.0 0.5 collective-permute-start.7
  30.5 0.0 copy-done.1
  30.5 0.6 slice.9
  31.1 3.6 %collective-permute-start.5 = (bf16[64,256]{1,0:T(8,128)(2,1)}, bf16[64,256]{1,0:T(8,128)(2,1)}, u32[]{:S(2)}, u32[]{:S(2)}) collective-permute-start(bf16[64,256]{1,0:T(8,128)(2,1)} %slice.9), channel_id=1, source_target_pairs={{4,0},{8,4},{12,8},{16,12},{20,16},{24,20},{28,24},{5,1},{9,5},{13... | collective-permute-start | bytes 98312 | tf_op jit(solution)/shard_map/ppermute | solution.py:448
  34.7 18.7 %collective-permute-done.3.refs_3_ = bf16[512,256]{1,0:T(8,128)(2,1)} collective-permute-done((bf16[512,256]{1,0:T(8,128)(2,1)}, bf16[512,256]{1,0:T(8,128)(2,1)}, u32[]{:S(2)}, u32[]{:S(2)}) %collective-permute-start.3) | collective-permute-done | bytes 262176 | tf_op jit(solution)/shard_map/ppermute | solution.py:461
  53.4 2.0 %collective-permute-start.4 = (bf16[512,256]{1,0:T(8,128)(2,1)}, bf16[512,256]{1,0:T(8,128)(2,1)}, u32[]{:S(2)}, u32[]{:S(2)}) collective-permute-start(bf16[512,256]{1,0:T(8,128)(2,1)} %collective-permute-done.3.refs_3_), channel_id=1, source_target_pairs={{16,24},{20,28},{17,25},{21,29},{18,26},{22,30},{19,27},{23,31}} | collective-permute-start | bytes 786440 | tf_op jit(solution)/shard_map/ppermute | solution.py:461
  55.4 0.0 copy-start.3
  55.4 0.9 copy-done.3
  56.3 5.2 %shard_map.98 = (f32[512,256]{1,0:T(8,128)S(1)}, s32[1]{0:T(128)}) custom-call(s32[1]{0:T(128)} %bitcast.pair_ref, s32[1]{0:T(128)} %bitcast.1.side_ref, bf16[256,384]{1,0:T(8,128)(2,1)S(1)} %copy-done.3, bf16[256,384]{1,0:T(8,128)(2,1)S(1)} %collective-permute-done.refs_1_, bf16[512,256]{1,0:T(8,128)(2,1)} %get-tuple-element.24.refs_2_, ...), custom_call_target="tpu_custom_call" | custom-call | flops 12000000000 | tf_op jit(solution)/shard_map/pallas_call | solution.py:338
  61.5 0.0 copy-start.5
  61.5 0.8 copy-done.5
  62.3 0.0 collective-permute-done.6.refs_1_.refs_2_
  62.3 2.2 %collective-permute-start.12 = (bf16[128,2048]{1,0:T(8,128)(2,1)S(1)}, bf16[128,2048]{1,0:T(8,128)(2,1)}, u32[]{:S(2)}, u32[]{:S(2)}) collective-permute-start(bf16[128,2048]{1,0:T(8,128)(2,1)S(1)} %collective-permute-done.6.refs_1_.refs_2_), channel_id=1, source_target_pairs={{0,4},{4,0},{8,12},{12,8},{16,20},{20,16},{24,28},{28,24},{1,5},{5... | collective-permute-start | bytes 1572872 | tf_op jit(solution)/shard_map/ppermute | solution.py:447
  64.5 0.0 collective-permute-done.7.refs_2_.refs_3_
  64.5 0.1 collective-permute-start.13
  64.6 0.0 collective-permute-done.5.spill_ref
  64.6 0.0 collective-permute-done.8.refs_3_.beside_ref
  64.6 0.0 all-to-all-done.incoming_ref
  64.6 1.9 %shard_map.101 = (bf16[16,256]{1,0:T(8,128)(2,1)S(1)}, bf16[64,256]{1,0:T(8,128)(2,1)S(1)}) custom-call(bf16[256,256]{1,0:T(8,128)(2,1)S(1)} %copy-done.1, bf16[64,256]{1,0:T(8,128)(2,1)} %collective-permute-done.5.spill_ref, bf16[8,272,256]{2,1,0:T(8,128)(2,1)S(1)} %all-to-all-done.incoming_ref, s32[1]{0:T(128)} %get-tuple-element.27.refs_0_, ...), custom_call_target="tpu_custom_call" | custom-call | flops 1000000000 | tf_op jit(solution)/shard_map/pallas_call | solution.py:247
  66.6 3.3 %collective-permute-start.9 = (bf16[64,256]{1,0:T(8,128)(2,1)S(1)}, bf16[64,256]{1,0:T(8,128)(2,1)S(1)}, u32[]{:S(2)}, u32[]{:S(2)}) collective-permute-start(bf16[64,256]{1,0:T(8,128)(2,1)S(1)} %get-tuple-element.31), channel_id=1, source_target_pairs={{0,4},{4,8},{8,12},{12,16},{16,20},{20,24},{24,28},{1,5},{5,9},{9,... | collective-permute-start | bytes 98312 | tf_op jit(solution)/shard_map/ppermute | solution.py:467
  69.9 1.6 %shard_map.102 = bf16[256,256]{1,0:T(8,128)(2,1)S(1)} custom-call(bf16[256,256]{1,0:T(8,128)(2,1)S(1)} %copy-done.1, bf16[16,256]{1,0:T(8,128)(2,1)S(1)} %get-tuple-element.32.tail_ref, bf16[8,272,256]{2,1,0:T(8,128)(2,1)S(1)} %all-to-all-done.incoming_ref), custom_call_target="tpu_custom_call" | custom-call | flops 2000000000 | tf_op jit(solution)/shard_map/pallas_call | solution.py:262
  71.5 15.7 %collective-permute-done.9 = bf16[64,256]{1,0:T(8,128)(2,1)S(1)} collective-permute-done((bf16[64,256]{1,0:T(8,128)(2,1)S(1)}, bf16[64,256]{1,0:T(8,128)(2,1)S(1)}, u32[]{:S(2)}, u32[]{:S(2)}) %collective-permute-start.9) | collective-permute-done | bytes 32800 | tf_op jit(solution)/shard_map/ppermute | solution.py:467
  87.3 0.1 slice_select_fusion
  87.4 1.3 %collective-permute-start.10 = (bf16[256,256]{1,0:T(8,128)(2,1)S(1)}, bf16[256,256]{1,0:T(8,128)(2,1)S(1)}, u32[]{:S(2)}, u32[]{:S(2)}) collective-permute-start(bf16[256,256]{1,0:T(8,128)(2,1)S(1)} %pad_maximum_fusion.one_ref), channel_id=1, source_target_pairs={{0,2},{1,3},{2,0},{3,1},{4,6},{5,7},{6,4},{7,5},{8,10},{9,11},{10,... | collective-permute-start | bytes 393224 | tf_op jit(solution)/shard_map/ppermute | solution.py:471
  88.6 1.8 %collective-permute-start.11 = (bf16[256,256]{1,0:T(8,128)(2,1)S(1)}, bf16[256,256]{1,0:T(8,128)(2,1)S(1)}, u32[]{:S(2)}, u32[]{:S(2)}) collective-permute-start(bf16[256,256]{1,0:T(8,128)(2,1)S(1)} %pad_maximum_fusion.one_ref), channel_id=1, source_target_pairs={{0,3},{1,2},{2,1},{3,0},{4,7},{5,6},{6,5},{7,4},{8,11},{9,10},{10,... | collective-permute-start | bytes 393224 | tf_op jit(solution)/shard_map/ppermute | solution.py:471
  90.4 0.0 collective-permute-done.4.refs_3_
  90.4 0.0 collective-permute-start.15
  90.4 0.0 collective-permute-done.12.refs_6_.refs_4_
  90.4 0.0 collective-permute-done.13.refs_7_.refs_5_
  90.4 0.8 collective-permute-done.10.refs_4_.refs_0_
  91.3 4.6 %collective-permute-done.11.refs_5_.refs_1_ = bf16[256,256]{1,0:T(8,128)(2,1)S(1)} collective-permute-done((bf16[256,256]{1,0:T(8,128)(2,1)S(1)}, bf16[256,256]{1,0:T(8,128)(2,1)S(1)}, u32[]{:S(2)}, u32[]{:S(2)}) %collective-permute-start.11) | collective-permute-done | bytes 131104 | tf_op jit(solution)/shard_map/ppermute | solution.py:471
  95.9 0.0 copy-start.4
  95.9 0.9 copy-done.4
  96.8 0.0 copy-start.6
  96.8 1.0 copy-done.6
  97.9 0.0 copy-start
  97.9 1.3 %shard_map.103 = (bf16[256,128]{1,0:T(8,128)(2,1)S(1)}, bf16[256,128]{1,0:T(8,128)(2,1)S(1)}) custom-call(s32[1]{0:T(128)} %bitcast.pair_ref, s32[1]{0:T(128)} %bitcast.1.side_ref, bf16[256,384]{1,0:T(8,128)(2,1)S(1)} %copy-done.4, bf16[256,384]{1,0:T(8,128)(2,1)S(1)} %collective-permute-done.refs_1_, f32[512,256]{1,0:T(8,128)S(1)} %copy-done.6, ...), custom_call_target="tpu_custom_call" | custom-call | flops 2000000000 | tf_op jit(solution)/shard_map/pallas_call | solution.py:338
  99.2 2.3 %collective-permute-start.14 = (bf16[256,128]{1,0:T(8,128)(2,1)S(1)}, bf16[256,128]{1,0:T(8,128)(2,1)S(1)}, u32[]{:S(2)}, u32[]{:S(2)}) collective-permute-start(bf16[256,128]{1,0:T(8,128)(2,1)S(1)} %get-tuple-element.34), channel_id=1, source_target_pairs={{0,4},{4,0},{8,12},{12,8},{16,20},{20,16},{24,28},{28,24},{1,5},{5... | collective-permute-start | bytes 196616 | tf_op jit(solution)/shard_map/ppermute | solution.py:476
  101.4 0.0 collective-permute-done.15.two_ref
  101.5 0.0 copy-done
  101.5 0.7 shard_map.104.partial_ref
  102.2 2.7 %shard_map.105 = bf16[256,2048]{1,0:T(8,128)(2,1)} custom-call(s32[1]{0:T(128)} %bitcast.1.side_ref, f32[256,2048]{1,0:T(8,128)S(1)} %shard_map.104.partial_ref, bf16[256,256]{1,0:T(8,128)(2,1)S(1)} %collective-permute-done.10.refs_4_.refs_0_, bf16[256,256]{1,0:T(8,128)(2,1)S(1)} %collective-permute-done.11.refs_5_.refs_1_, ...), custom_call_target="tpu_custom_call" | custom-call | flops 2000000000 | tf_op jit(solution)/shard_map/pallas_call | solution.py:398
  104.8 0.0 collective-permute-done.14
  104.8 0.7 maximum_select_fusion
  (3 shorter events, 0.0 us)
Async XLA Ops:
  3.5 12.1 %collective-permute-start = (bf16[256,384]{1,0:T(8,128)(2,1)}, bf16[256,384]{1,0:T(8,128)(2,1)S(1)}, u32[]{:S(2)}, u32[]{:S(2)}) collective-permute-start(bf16[256,384]{1,0:T(8,128)(2,1)} %get-tuple-element.20), channel_id=1, source_target_pairs={{0,4},{4,0},{8,12},{12,8},{16,20},{20,16},{24,28},{28,24},{1,5},{5... | collective-permute-start | bytes 589832 | tf_op jit(solution)/shard_map/ppermute | solution.py:445
  4.8 10.8 %collective-permute-start.2 = (bf16[256,256]{1,0:T(8,128)(2,1)}, bf16[256,256]{1,0:T(8,128)(2,1)S(1)}, u32[]{:S(2)}, u32[]{:S(2)}) collective-permute-start(bf16[256,256]{1,0:T(8,128)(2,1)} %get-tuple-element.22.refs_1_), channel_id=1, source_target_pairs={{0,12},{4,8},{8,20},{12,16},{16,28},{20,24},{1,13},{5,9},{9,21},{1... | collective-permute-start | bytes 393224 | tf_op jit(solution)/shard_map/ppermute | solution.py:444
  7.9 7.7 %collective-permute-start.1 = (bf16[256,256]{1,0:T(8,128)(2,1)}, bf16[256,256]{1,0:T(8,128)(2,1)S(1)}, u32[]{:S(2)}, u32[]{:S(2)}) collective-permute-start(bf16[256,256]{1,0:T(8,128)(2,1)} %get-tuple-element.21), channel_id=1, source_target_pairs={{0,8},{4,12},{8,16},{12,20},{16,24},{20,28},{1,9},{5,13},{9,17},{1... | collective-permute-start | bytes 393224 | tf_op jit(solution)/shard_map/ppermute | solution.py:443
  16.9 0.6 copy-start.2
  18.2 12.2 %copy-start.1 = (bf16[256,256]{1,0:T(8,128)(2,1)S(1)}, bf16[256,256]{1,0:T(8,128)(2,1)}, u32[]{:S(2)}) copy-start(bf16[256,256]{1,0:T(8,128)(2,1)} %queries_ref.3) | copy-start | bytes 393220
  18.2 46.4 %all-to-all-start = ((bf16[8,272,256]{2,1,0:T(8,128)(2,1)}), bf16[8,272,256]{2,1,0:T(8,128)(2,1)S(1)}, u32[]{:S(2)}, u32[]{:S(2)}) async-start(bf16[8,272,256]{2,1,0:T(8,128)(2,1)} %shard_map.100), calls=%async_computation | async-start | bytes 2228224 | tf_op jit(solution)/shard_map/all_to_all | solution.py:455
  23.2 30.2 %collective-permute-start.3 = (bf16[512,256]{1,0:T(8,128)(2,1)}, bf16[512,256]{1,0:T(8,128)(2,1)}, u32[]{:S(2)}, u32[]{:S(2)}) collective-permute-start(bf16[512,256]{1,0:T(8,128)(2,1)} %get-tuple-element.24.refs_2_), channel_id=1, source_target_pairs={{8,16},{12,20},{16,24},{20,28},{9,17},{13,21},{17,25},{21,29},{10,... | collective-permute-start | bytes 786440 | tf_op jit(solution)/shard_map/ppermute | solution.py:461
  26.3 38.3 %collective-permute-start.8 = (bf16[256,2048]{1,0:T(8,128)(2,1)}, bf16[256,2048]{1,0:T(8,128)(2,1)S(1)}, u32[]{:S(2)}, u32[]{:S(2)}) collective-permute-start(bf16[256,2048]{1,0:T(8,128)(2,1)} %get-tuple-element.30), channel_id=1, source_target_pairs={{0,1},{1,0},{2,3},{3,2},{4,5},{5,4},{6,7},{7,6},{8,9},{9,8},{10,11... | collective-permute-start | bytes 3145736 | tf_op jit(solution)/shard_map/ppermute | solution.py:453
  28.7 33.6 %collective-permute-start.6 = (bf16[128,2048]{1,0:T(8,128)(2,1)}, bf16[128,2048]{1,0:T(8,128)(2,1)S(1)}, u32[]{:S(2)}, u32[]{:S(2)}) collective-permute-start(bf16[128,2048]{1,0:T(8,128)(2,1)} %get-tuple-element.28), channel_id=1, source_target_pairs={{0,2},{1,3},{2,0},{3,1},{4,6},{5,7},{6,4},{7,5},{8,10},{9,11},{10,... | collective-permute-start | bytes 1572872 | tf_op jit(solution)/shard_map/ppermute | solution.py:446
  30.0 34.6 %collective-permute-start.7 = (bf16[128,2048]{1,0:T(8,128)(2,1)}, bf16[128,2048]{1,0:T(8,128)(2,1)S(1)}, u32[]{:S(2)}, u32[]{:S(2)}) collective-permute-start(bf16[128,2048]{1,0:T(8,128)(2,1)} %get-tuple-element.29), channel_id=1, source_target_pairs={{0,3},{1,2},{2,1},{3,0},{4,7},{5,6},{6,5},{7,4},{8,11},{9,10},{10,... | collective-permute-start | bytes 1572872 | tf_op jit(solution)/shard_map/ppermute | solution.py:446
  31.1 33.5 %collective-permute-start.5 = (bf16[64,256]{1,0:T(8,128)(2,1)}, bf16[64,256]{1,0:T(8,128)(2,1)}, u32[]{:S(2)}, u32[]{:S(2)}) collective-permute-start(bf16[64,256]{1,0:T(8,128)(2,1)} %slice.9), channel_id=1, source_target_pairs={{4,0},{8,4},{12,8},{16,12},{20,16},{24,20},{28,24},{5,1},{9,5},{13... | collective-permute-start | bytes 98312 | tf_op jit(solution)/shard_map/ppermute | solution.py:448
  53.4 37.0 %collective-permute-start.4 = (bf16[512,256]{1,0:T(8,128)(2,1)}, bf16[512,256]{1,0:T(8,128)(2,1)}, u32[]{:S(2)}, u32[]{:S(2)}) collective-permute-start(bf16[512,256]{1,0:T(8,128)(2,1)} %collective-permute-done.3.refs_3_), channel_id=1, source_target_pairs={{16,24},{20,28},{17,25},{21,29},{18,26},{22,30},{19,27},{23,31}} | collective-permute-start | bytes 786440 | tf_op jit(solution)/shard_map/ppermute | solution.py:461
  55.4 0.9 copy-start.3
  61.5 0.8 copy-start.5
  62.3 28.1 %collective-permute-start.12 = (bf16[128,2048]{1,0:T(8,128)(2,1)S(1)}, bf16[128,2048]{1,0:T(8,128)(2,1)}, u32[]{:S(2)}, u32[]{:S(2)}) collective-permute-start(bf16[128,2048]{1,0:T(8,128)(2,1)S(1)} %collective-permute-done.6.refs_1_.refs_2_), channel_id=1, source_target_pairs={{0,4},{4,0},{8,12},{12,8},{16,20},{20,16},{24,28},{28,24},{1,5},{5... | collective-permute-start | bytes 1572872 | tf_op jit(solution)/shard_map/ppermute | solution.py:447
  64.5 25.9 %collective-permute-start.13 = (bf16[128,2048]{1,0:T(8,128)(2,1)S(1)}, bf16[128,2048]{1,0:T(8,128)(2,1)}, u32[]{:S(2)}, u32[]{:S(2)}) collective-permute-start(bf16[128,2048]{1,0:T(8,128)(2,1)S(1)} %collective-permute-done.7.refs_2_.refs_3_), channel_id=1, source_target_pairs={{0,4},{4,0},{8,12},{12,8},{16,20},{20,16},{24,28},{28,24},{1,5},{5... | collective-permute-start | bytes 1572872 | tf_op jit(solution)/shard_map/ppermute | solution.py:447
  66.6 20.7 %collective-permute-start.9 = (bf16[64,256]{1,0:T(8,128)(2,1)S(1)}, bf16[64,256]{1,0:T(8,128)(2,1)S(1)}, u32[]{:S(2)}, u32[]{:S(2)}) collective-permute-start(bf16[64,256]{1,0:T(8,128)(2,1)S(1)} %get-tuple-element.31), channel_id=1, source_target_pairs={{0,4},{4,8},{8,12},{12,16},{16,20},{20,24},{24,28},{1,5},{5,9},{9,... | collective-permute-start | bytes 98312 | tf_op jit(solution)/shard_map/ppermute | solution.py:467
  87.4 3.9 %collective-permute-start.10 = (bf16[256,256]{1,0:T(8,128)(2,1)S(1)}, bf16[256,256]{1,0:T(8,128)(2,1)S(1)}, u32[]{:S(2)}, u32[]{:S(2)}) collective-permute-start(bf16[256,256]{1,0:T(8,128)(2,1)S(1)} %pad_maximum_fusion.one_ref), channel_id=1, source_target_pairs={{0,2},{1,3},{2,0},{3,1},{4,6},{5,7},{6,4},{7,5},{8,10},{9,11},{10,... | collective-permute-start | bytes 393224 | tf_op jit(solution)/shard_map/ppermute | solution.py:471
  88.6 7.2 %collective-permute-start.11 = (bf16[256,256]{1,0:T(8,128)(2,1)S(1)}, bf16[256,256]{1,0:T(8,128)(2,1)S(1)}, u32[]{:S(2)}, u32[]{:S(2)}) collective-permute-start(bf16[256,256]{1,0:T(8,128)(2,1)S(1)} %pad_maximum_fusion.one_ref), channel_id=1, source_target_pairs={{0,3},{1,2},{2,1},{3,0},{4,7},{5,6},{6,5},{7,4},{8,11},{9,10},{10,... | collective-permute-start | bytes 393224 | tf_op jit(solution)/shard_map/ppermute | solution.py:471
  90.4 11.0 %collective-permute-start.15 = (bf16[256,256]{1,0:T(8,128)(2,1)S(1)}, bf16[256,256]{1,0:T(8,128)(2,1)S(1)}, u32[]{:S(2)}, u32[]{:S(2)}) collective-permute-start(bf16[256,256]{1,0:T(8,128)(2,1)S(1)} %pad_maximum_fusion.one_ref), channel_id=1, source_target_pairs={{0,1},{1,0},{2,3},{3,2},{4,5},{5,4},{6,7},{7,6},{8,9},{9,8},{10,11... | collective-permute-start | bytes 393224 | tf_op jit(solution)/shard_map/ppermute | solution.py:471
  95.9 0.9 copy-start.4
  96.8 1.0 copy-start.6
  97.9 3.6 %copy-start = (bf16[256,2048]{1,0:T(8,128)(2,1)S(1)}, bf16[256,2048]{1,0:T(8,128)(2,1)}, u32[]{:S(2)}) copy-start(bf16[256,2048]{1,0:T(8,128)(2,1)} %get-tuple-element.35.own_ref) | copy-start | bytes 3145732
  99.2 5.6 %collective-permute-start.14 = (bf16[256,128]{1,0:T(8,128)(2,1)S(1)}, bf16[256,128]{1,0:T(8,128)(2,1)S(1)}, u32[]{:S(2)}, u32[]{:S(2)}) collective-permute-start(bf16[256,128]{1,0:T(8,128)(2,1)S(1)} %get-tuple-element.34), channel_id=1, source_target_pairs={{0,4},{4,0},{8,12},{12,8},{16,20},{20,16},{24,28},{28,24},{1,5},{5... | collective-permute-start | bytes 196616 | tf_op jit(solution)/shard_map/ppermute | solution.py:476

commit v10 on v9

v10 whole, which is shorter than its diff:
```python
import functools
import math

import jax
import jax.numpy as jnp
from jax import lax
from jax.experimental import pallas as pl
from jax.experimental.pallas import tpu as pltpu
from jax.sharding import PartitionSpec as P

HD = 128
BLOCK = 64
LEAD = 16
NEGATIVE = -1e30
SCALE = HD ** -0.5 * math.log2(math.e)
VMEM = pl.BlockSpec(memory_space=pltpu.VMEM)
SMEM = pl.BlockSpec(memory_space=pltpu.SMEM)
ANY = pl.BlockSpec(memory_space=pl.ANY)
PARAMS = pltpu.CompilerParams(vmem_limit_bytes=16 * 1024 * 1024)


def takes(microseconds):
    return pl.CostEstimate(
        flops=microseconds * 1000000000, bytes_accessed=0, transcendentals=0
    )


def dot(a, b):
    return jnp.dot(a, b, preferred_element_type=jnp.float32)


def dot_t(a, b):
    return lax.dot_general(a, b, (((1,), (1,)), ((), ())), preferred_element_type=jnp.float32)


def fetch(pieces, sems):
    copies = [
        pltpu.make_async_copy(source, target, sems.at[at])
        for at, (source, target) in enumerate(pieces)
    ]
    for copy in copies:
        copy.start()
    for copy in copies:
        copy.wait()


def cut_kernel(plan, side_ref, tp_ref, *refs):
    sems, refs = refs[-1], refs[:-1]
    sources, outs = refs, refs[len(refs) - len(plan) :]
    pieces = []
    for out, parts in zip(outs, plan):
        for at, (index, step, total, offset, width, depth) in enumerate(parts):
            source = sources[index]
            key = tp_ref[0] if total else side_ref[0]
            lane = pl.multiple_of((key ^ step) * (total or HD) + offset, HD)
            row = pl.multiple_of(side_ref[0] * depth, LEAD) if depth < source.shape[0] else 0
            piece = source.at[pl.ds(row, depth), pl.ds(lane, width)]
            pieces.append((piece, out.at[:, pl.ds(at * width, width)]))
    fetch(pieces, sems)


def cut(side, tp, sources, plan, before=()):
    shapes = []
    for parts in plan:
        shape = (parts[0][5], len(parts) * parts[0][4])
        shapes.append(jax.ShapeDtypeStruct(shape, sources[parts[0][0]].dtype))
    return pl.pallas_call(
        functools.partial(cut_kernel, plan),
        out_shape=tuple(shapes),
        in_specs=[SMEM] * 2 + [ANY] * (len(sources) + len(before)),
        out_specs=(VMEM,) * len(plan),
        scratch_shapes=[pltpu.SemaphoreType.DMA((sum(len(parts) for parts in plan),))],
        cost_estimate=takes(2),
    )(side, tp, *sources, *before)


def arrange_kernel(slot_ref, keys_ref, values_ref, own_keys, own_values, out_ref, *refs):
    held_ref, own_ref, sems = refs
    count, length, width = keys_ref.shape
    indices = out_ref.shape[0]
    rows = own_keys.shape[0]
    front = 2 * length + LEAD
    owners = [slot_ref[n] // count for n in range(count)]
    at = 0
    copies = []
    for n, owner in enumerate(owners):
        for half, source in enumerate((keys_ref, values_ref)):
            target = held_ref.at[owner, pl.ds(half * length, length)]
            copies.append(pltpu.make_async_copy(source.at[n], target, sems.at[at]))
            at += 1
    for head in range(2):
        for half, source in enumerate((own_keys, own_values)):
            piece = source.at[:, pl.ds(head * HD, HD)]
            target = own_ref.at[head, :, pl.ds(half * HD, HD)]
            copies.append(pltpu.make_async_copy(piece, target, sems.at[at]))
            at += 1
    for copy in copies:
        copy.start()
    for index in range(indices):
        held_ref[index, 2 * length :, :] = jnp.full((LEAD, width), -1, held_ref.dtype)
    for n, owner in enumerate(owners):
        place = (slot_ref[n] - owner * count).astype(jnp.float32)
        held_ref[owner, 2 * length :, :] = jnp.full((LEAD, width), place).astype(held_ref.dtype)
    outs = []
    for head in range(2):
        copies[2 * count + 2 * head].wait()
        copies[2 * count + 2 * head + 1].wait()
        for index in range(head, indices, 2):
            target = out_ref.at[index, pl.ds(front, rows)]
            outs.append(pltpu.make_async_copy(own_ref.at[head], target, sems.at[at]))
            outs[-1].start()
            at += 1
    for copy in copies[: 2 * count]:
        copy.wait()
    for index in range(indices):
        source, target = held_ref.at[index], out_ref.at[index, pl.ds(0, front)]
        outs.append(pltpu.make_async_copy(source, target, sems.at[at]))
        outs[-1].start()
        at += 1
    for out in outs:
        out.wait()


def arrange(slots, keys, values, own_keys, own_values, indices):
    count, length, width = keys.shape
    rows = own_keys.shape[0]
    front = 2 * length + LEAD
    return pl.pallas_call(
        arrange_kernel,
        out_shape=jax.ShapeDtypeStruct((indices, front + rows, width), keys.dtype),
        in_specs=[SMEM] + [ANY] * 4,
        out_specs=ANY,
        scratch_shapes=[
            pltpu.VMEM((indices, front, width), keys.dtype),
            pltpu.VMEM((2, rows, 2 * HD), keys.dtype),
            pltpu.SemaphoreType.DMA((2 * count + 4 + 2 * indices,)),
        ],
        cost_estimate=takes(4),
    )(slots, keys, values, own_keys, own_values)


def find_sources(incoming_ref, order_ref, length):
    for source in range(incoming_ref.shape[0]):
        place = incoming_ref[source, 2 * length : 2 * length + LEAD, :HD].astype(jnp.float32)
        place = jnp.max(place).astype(jnp.int32)

        @pl.when(place >= 0)
        def _():
            order_ref[place] = source


def block_answer(order_ref, incoming_ref, length, block, feats, q):
    first = order_ref[2 * block]
    second = order_ref[2 * block + 1]
    s1 = dot_t(q, incoming_ref[first, :length, feats])
    s2 = dot_t(q, incoming_ref[second, :length, feats])
    peak = jnp.maximum(jnp.max(s1, axis=1, keepdims=True), jnp.max(s2, axis=1, keepdims=True))
    p1 = jnp.exp2((s1 - peak) * SCALE)
    p2 = jnp.exp2((s2 - peak) * SCALE)
    total = jnp.sum(p1, axis=1, keepdims=True) + jnp.sum(p2, axis=1, keepdims=True)
    mixed = dot(p1.astype(jnp.bfloat16), incoming_ref[first, length : 2 * length, feats])
    mixed += dot(p2.astype(jnp.bfloat16), incoming_ref[second, length : 2 * length, feats])
    return (mixed / total).astype(jnp.bfloat16)


def last_kernel(queries_ref, spill_ref, incoming_ref, *refs):
    tail_ref, next_ref, order_ref = refs[-3:]
    rows, width = queries_ref.shape
    length = (incoming_ref.shape[1] - LEAD - rows) // 2
    find_sources(incoming_ref, order_ref, length)
    last = rows // BLOCK - 1
    for head in range(width // HD):
        feats = pl.ds(head * HD, HD)
        q = jnp.concatenate([queries_ref[rows - LEAD :, feats], spill_ref[:BLOCK, feats]], axis=0)
        answer = block_answer(order_ref, incoming_ref, length, last, feats, q)
        tail_ref[:, feats] = answer[:LEAD]
        next_ref[:, feats] = answer[LEAD:]


def other_kernel(queries_ref, tail_ref, incoming_ref, out_ref, mark_ref, order_ref):
    mark_ref[0] = 0
    rows, width = queries_ref.shape
    length = (incoming_ref.shape[1] - LEAD - rows) // 2
    find_sources(incoming_ref, order_ref, length)
    blocks = rows // BLOCK
    row = lax.broadcasted_iota(jnp.int32, (LEAD, HD), 0)
    for head in range(width // HD):
        feats = pl.ds(head * HD, HD)
        before = jnp.zeros((LEAD, HD), jnp.bfloat16)
        out_ref[: BLOCK - LEAD, feats] = jnp.zeros((BLOCK - LEAD, HD), jnp.bfloat16)
        for block in range(blocks):
            start = (block + 1) * BLOCK - LEAD
            if block < blocks - 1:
                q = queries_ref[start : start + BLOCK + LEAD, feats]
                answer = block_answer(order_ref, incoming_ref, length, block, feats, q)
                head_rows = answer[:LEAD]
                out_ref[start + LEAD : start + BLOCK, feats] = answer[LEAD:BLOCK]
            else:
                head_rows = tail_ref[:, feats]
            out_ref[start : start + LEAD, feats] = jnp.where(row == LEAD - 1, head_rows, before)
            if block < blocks - 1:
                before = answer[BLOCK:]


def order_scratch(rows):
    return [pltpu.SMEM((2 * rows // BLOCK,), jnp.int32)]


def last_attend(queries, spill, incoming):
    rows, width = queries.shape
    return pl.pallas_call(
        last_kernel,
        out_shape=(
            jax.ShapeDtypeStruct((LEAD, width), queries.dtype),
            jax.ShapeDtypeStruct((BLOCK, width), queries.dtype),
        ),
        in_specs=[VMEM] * 3,
        out_specs=(VMEM, VMEM),
        scratch_shapes=order_scratch(rows),
        compiler_params=PARAMS,
        cost_estimate=takes(1),
    )(queries, spill, incoming)


def other_attend(queries, tail, incoming):
    return pl.pallas_call(
        other_kernel,
        out_shape=(
            jax.ShapeDtypeStruct(queries.shape, queries.dtype),
            jax.ShapeDtypeStruct((1,), jnp.int32),
        ),
        in_specs=[VMEM] * 3,
        out_specs=(VMEM, SMEM),
        scratch_shapes=order_scratch(queries.shape[0]),
        compiler_params=PARAMS,
        cost_estimate=takes(2),
    )(queries, tail, incoming)


def self_kernel(pair_ref, side_ref, mark_ref, mine_ref, other_ref, incoming_ref, *refs):
    ours_ref, theirs_ref, peak_ref, total_ref, accum_ref = refs[-5:]
    pair, side = pair_ref[0], side_ref[0]
    tile = mine_ref.shape[0]
    rows = 2 * tile
    front = incoming_ref.shape[1] - tile
    q = jnp.concatenate([mine_ref[...], other_ref[...]], axis=0)

    def attend(at, fresh):
        kv = incoming_ref[pl.ds(2 * at, 2), front:, :].reshape(rows, 2 * HD)
        s = dot_t(q, kv[:, :HD])
        if fresh:
            row = lax.broadcasted_iota(jnp.int32, (rows, rows), 0)
            col = lax.broadcasted_iota(jnp.int32, (rows, rows), 1)
            turn = side * tile
            row = jnp.where(row < tile, row + turn, row - turn)
            s = jnp.where(col <= row, s, NEGATIVE)
        peak = jnp.max(s, axis=1, keepdims=True)
        if not fresh:
            old = peak_ref[:, :1]
            peak = jnp.maximum(peak, old)
            factor = jnp.exp2((old - peak) * SCALE)
        p = jnp.exp2((s - peak) * SCALE)
        total = jnp.sum(p, axis=1, keepdims=True)
        accum = dot(p.astype(jnp.bfloat16), kv[:, HD:])
        if not fresh:
            total += total_ref[:, :1] * factor
            accum += accum_ref[...] * factor
        peak_ref[...] = jnp.broadcast_to(peak, (rows, HD))
        total_ref[...] = jnp.broadcast_to(total, (rows, HD))
        accum_ref[...] = accum

    attend(pair, True)

    def earlier(at, carry):
        attend(at, False)
        return carry

    lax.fori_loop(0, pair, earlier, 0)
    result = (accum_ref[...] / total_ref[...]).astype(jnp.bfloat16)
    ours_ref[...] = result[:tile]
    theirs_ref[...] = result[tile:]


def self_attend(pair, side, mark, mine, other, incoming):
    tile = mine.shape[0]
    return pl.pallas_call(
        self_kernel,
        out_shape=(jax.ShapeDtypeStruct((tile, HD), jnp.bfloat16),) * 2,
        in_specs=[SMEM] * 3 + [VMEM] * 3,
        out_specs=(VMEM, VMEM),
        scratch_shapes=[pltpu.VMEM((2 * tile, HD), jnp.float32)] * 3,
        compiler_params=PARAMS,
        cost_estimate=takes(4),
    )(pair, side, mark, mine, other, incoming)


def near_kernel(one_ref, two_ref, own_ref, beside_ref, partial_ref):
    width = partial_ref.shape[1]
    term = jnp.concatenate([one_ref[...], two_ref[...]], axis=1)
    tile = min(512, width)
    for column in range(0, width, tile):
        at = slice(column, column + tile)
        partial_ref[:, at] = dot(
            term, jnp.concatenate([own_ref[:, at], beside_ref[:, at]], axis=0)
        )


def project_near(terms, own, beside):
    return pl.pallas_call(
        near_kernel,
        out_shape=jax.ShapeDtypeStruct((terms[0].shape[0], own.shape[1]), jnp.float32),
        in_specs=[VMEM] * 4,
        out_specs=VMEM,
        compiler_params=PARAMS,
    )(*terms, own, beside)


def far_kernel(count, partial_ref, *refs):
    crossed_ref, out_ref, sems = refs[-3:]
    terms, direct = refs[:count], refs[count : 2 * count]
    width = crossed_ref.shape[1]
    tile = min(512, width)
    term = jnp.concatenate([held[...] for held in terms], axis=1)
    outs = []
    for column in range(0, width, tile):
        at = slice(column, column + tile)
        total = dot(term, jnp.concatenate([block[:, at] for block in direct], axis=0))
        out_ref[:, at] = (partial_ref[:, at] + total).astype(out_ref.dtype)
        out = pltpu.make_async_copy(
            out_ref.at[:, at], crossed_ref.at[:, at], sems.at[len(outs)]
        )
        out.start()
        outs.append(out)
    for out in outs:
        out.wait()


def project_far(partial, terms, direct):
    rows, width = partial.shape
    operands = (*terms, *direct)
    return pl.pallas_call(
        functools.partial(far_kernel, len(terms)),
        out_shape=jax.ShapeDtypeStruct((rows, width), jnp.bfloat16),
        in_specs=[VMEM] * (1 + len(operands)),
        out_specs=ANY,
        scratch_shapes=[
            pltpu.VMEM((rows, width), jnp.bfloat16),
            pltpu.SemaphoreType.DMA((width // min(512, width),)),
        ],
        compiler_params=PARAMS,
        cost_estimate=takes(2),
    )(partial, *operands)


def shards(queries, keys, values, cross_queries, nbr_keys, nbr_values, nbr_slot, w_cross):
    ctx = lax.axis_index("ctx")
    count = lax.axis_size("ctx")
    tp = lax.axis_index("tp").reshape(1)
    groups = lax.axis_size("tp")
    side = (ctx & 1).reshape(1)
    pair = (ctx >> 1).reshape(1)
    left = ctx & 1 == 0
    pairs = count // 2
    rows = queries.shape[0]
    depth = w_cross.shape[0]
    width = w_cross.shape[1] // groups
    swap = [(i, i ^ 1) for i in range(count)]
    across = [[(i, i ^ step) for i in range(groups)] for step in range(groups)]

    def both(mine, other, axis):
        return jnp.where(
            left,
            jnp.concatenate([mine, other], axis),
            jnp.concatenate([other, mine], axis),
        )

    def exchange(value):
        return lax.all_to_all(value, "ctx", split_axis=0, concat_axis=0, tiled=True)

    incoming = exchange(arrange(nbr_slot, nbr_keys, nbr_values, keys, values, count))
    q_mine, q_away, own, *blocks = cut(
        side, tp, (queries, w_cross),
        [[(0, turn, 0, 0, HD, rows)] for turn in range(2)]
        + [[(1, step, width, 0, width, depth)] for step in range(groups)],
    )
    q_other = lax.ppermute(q_away, "ctx", swap)
    beside, *direct = [
        lax.ppermute(block, "tp", across[step]) for step, block in enumerate(blocks, 1)
    ]
    spill = lax.ppermute(cross_queries[:BLOCK], "ctx", [(i + 1, i) for i in range(count - 1)])

    tail, onward = last_attend(cross_queries, spill, incoming)
    back = lax.ppermute(onward, "ctx", [(i, i + 1) for i in range(count - 1)])
    answers, mark = other_attend(cross_queries, tail, incoming)
    early = jnp.arange(BLOCK)[:, None] < BLOCK - 1
    cca = jnp.concatenate([jnp.where(early, back, answers[:BLOCK]), answers[BLOCK:]], axis=0)
    terms = [cca] + [lax.ppermute(cca, "tp", across[step]) for step in range(1, groups)]
    partial = project_near(terms[:2], own, beside)

    ours, theirs = self_attend(pair, side, mark, q_mine, q_other, incoming)
    attended = both(ours, lax.ppermute(theirs, "ctx", swap), 1)
    crossed = project_far(partial, terms[2:], direct)
    return (attended, crossed)


def solution(mesh):
    in_specs = (
        P("ctx", "tp"),
        P("ctx", "tp"),
        P("ctx", "tp"),
        P("ctx", "tp"),
        P("ctx", None, "tp"),
        P("ctx", None, "tp"),
        P("ctx"),
        P("tp", None),
    )
    out_specs = (P("ctx", "tp"), P("ctx", "tp"))
    return jax.shard_map(shards, mesh=mesh, in_specs=in_specs, out_specs=out_specs, check_vma=False)
```

time: 106 us -> 84.3 us (0.80)
  the two profiles are of different devices: /device:TPU:17 before, /device:TPU:25 now
where the time goes in v10:
time: 84.3 us; the launch traced here: 83.9 us
  waiting for transfers between devices  40.1 us (48%)
  Pallas kernels  22.3 us (26%)
  starting transfers between devices  19.9 us (24%)
    ppermute x1, waiting for transfers between devices, shards(): lax.ppermute(cross_queries[:BLOCK], 'ctx', [(i + 1, i) for i in range(cou...  23.6 us
    all_to_all x1, waiting for transfers between devices, exchange(): return lax.all_to_all(value, 'ctx', split_axis=0, concat_axis=0, tiled=True)  13.9 us
    pallas_call x1, Pallas kernels, self_attend(): pl.pallas_call(self_kernel, out_shape=(jax.ShapeDtypeStruct((tile, HD), j...  7.11 us
    all_to_all x1, starting transfers between devices, exchange(): return lax.all_to_all(value, 'ctx', split_axis=0, concat_axis=0, tiled=True)  5.64 us
    ppermute x3, starting transfers between devices, shards(): lax.ppermute(cca, 'tp', across[step])  5.08 us
    pallas_call x1, Pallas kernels, cut(): pl.pallas_call(functools.partial(cut_kernel, plan), out_shape=tuple(shape...  4.36 us
    pallas_call x1, Pallas kernels, arrange(): pl.pallas_call(arrange_kernel, out_shape=jax.ShapeDtypeStruct((indices, f...  3.64 us
    ppermute x3, starting transfers between devices, shards(): lax.ppermute(block, 'tp', across[step])  3.43 us
  transfers between devices with their start and end apart: 11, of which 4 were waited for; matrix products, arithmetic and copies ran while one was open for 1% of the time, Pallas kernels for 19%

profile of v10, /device:TPU:25, one launch (start us, length us, event | category | flops | bytes accessed | tf_op | source)
XLA Modules:
  0.0 83.9 jit_solution(17511022810606777785)
XLA Ops:
  0.6 3.6 %shard_map.95 = bf16[8,528,256]{2,1,0:T(8,128)(2,1)} custom-call(s32[8]{0:T(128)} %slot_ref.1, bf16[8,128,256]{2,1,0:T(8,128)(2,1)} %keys_ref.1, bf16[8,128,256]{2,1,0:T(8,128)(2,1)} %values_ref.1, bf16[256,256]{1,0:T(8,128)(2,1)} %own_keys.1, bf16[256,256]{1,0:T(8,128)(2,1)} %own_values.1), custom_call_target="tpu_custom_call" | custom-call | flops 4000000000 | tf_op jit(solution)/shard_map/pallas_call | solution.py:128
  4.3 0.0 copy-start.1
  4.3 5.6 %all-to-all-start = ((bf16[8,528,256]{2,1,0:T(8,128)(2,1)}), bf16[8,528,256]{2,1,0:T(8,128)(2,1)S(1)}, u32[]{:S(2)}, u32[]{:S(2)}) async-start(bf16[8,528,256]{2,1,0:T(8,128)(2,1)} %shard_map.95), calls=%async_computation | async-start | bytes 4325376 | tf_op jit(solution)/shard_map/all_to_all | solution.py:378
  9.9 0.0 copy-done.1
  9.9 3.1 %collective-permute-start = (bf16[64,256]{1,0:T(8,128)(2,1)S(1)}, bf16[64,256]{1,0:T(8,128)(2,1)S(1)}, u32[]{:S(2)}, u32[]{:S(2)}) collective-permute-start(bf16[64,256]{1,0:T(8,128)(2,1)S(1)} %slice.9), channel_id=1, source_target_pairs={{4,0},{8,4},{12,8},{16,12},{20,16},{24,20},{28,24},{5,1},{9,5},{13... | collective-permute-start | bytes 98312 | tf_op jit(solution)/shard_map/ppermute | solution.py:390
  13.0 4.4 %shard_map.98 = (bf16[256,128]{1,0:T(8,128)(2,1)}, bf16[256,128]{1,0:T(8,128)(2,1)}, bf16[256,2048]{1,0:T(8,128)(2,1)}, bf16[256,2048]{1,0:T(8,128)(2,1)}, bf16[...) custom-call(s32[1]{0:T(128)} %bitcast.1.side_ref, s32[1]{0:T(128)} %bitcast.2.tp_ref, bf16[256,256]{1,0:T(8,128)(2,1)} %refs_0_.1, ...), custom_call_target="tpu_custom_call" | custom-call | flops 2000000000 | tf_op jit(solution)/shard_map/pallas_call | solution.py:67
  17.4 0.3 collective-permute-start.1
  17.8 1.8 %collective-permute-start.5 = (bf16[256,2048]{1,0:T(8,128)(2,1)}, bf16[256,2048]{1,0:T(8,128)(2,1)}, u32[]{:S(2)}, u32[]{:S(2)}) collective-permute-start(bf16[256,2048]{1,0:T(8,128)(2,1)} %get-tuple-element.23), channel_id=1, source_target_pairs={{0,1},{1,0},{2,3},{3,2},{4,5},{5,4},{6,7},{7,6},{8,9},{9,8},{10,11... | collective-permute-start | bytes 3145736 | tf_op jit(solution)/shard_map/ppermute | solution.py:388
  19.6 1.2 %collective-permute-start.8 = (bf16[256,2048]{1,0:T(8,128)(2,1)}, bf16[256,2048]{1,0:T(8,128)(2,1)}, u32[]{:S(2)}, u32[]{:S(2)}) collective-permute-start(bf16[256,2048]{1,0:T(8,128)(2,1)} %get-tuple-element.24), channel_id=1, source_target_pairs={{0,2},{1,3},{2,0},{3,1},{4,6},{5,7},{6,4},{7,5},{8,10},{9,11},{10,... | collective-permute-start | bytes 3145736 | tf_op jit(solution)/shard_map/ppermute | solution.py:388
  20.8 0.4 collective-permute-start.9
  21.2 23.6 %collective-permute-done.spill_ref = bf16[64,256]{1,0:T(8,128)(2,1)S(1)} collective-permute-done((bf16[64,256]{1,0:T(8,128)(2,1)S(1)}, bf16[64,256]{1,0:T(8,128)(2,1)S(1)}, u32[]{:S(2)}, u32[]{:S(2)}) %collective-permute-start) | collective-permute-done | bytes 32800 | tf_op jit(solution)/shard_map/ppermute | solution.py:390
  44.8 13.9 %all-to-all-done.incoming_ref = bf16[8,528,256]{2,1,0:T(8,128)(2,1)S(1)} async-done(((bf16[8,528,256]{2,1,0:T(8,128)(2,1)}), bf16[8,528,256]{2,1,0:T(8,128)(2,1)S(1)}, u32[]{:S(2)}, u32[]{:S(2)}) %all-to-all-start) | async-done | bytes 2162720 | tf_op jit(solution)/shard_map/all_to_all | solution.py:378
  58.8 0.6 shard_map.96
  59.4 2.3 %collective-permute-start.3 = (bf16[64,256]{1,0:T(8,128)(2,1)S(1)}, bf16[64,256]{1,0:T(8,128)(2,1)S(1)}, u32[]{:S(2)}, u32[]{:S(2)}) collective-permute-start(bf16[64,256]{1,0:T(8,128)(2,1)S(1)} %get-tuple-element.20), channel_id=1, source_target_pairs={{0,4},{4,8},{8,12},{12,16},{16,20},{20,24},{24,28},{1,5},{5,9},{9,... | collective-permute-start | bytes 98312 | tf_op jit(solution)/shard_map/ppermute | solution.py:393
  61.7 0.0 copy-start.2
  61.7 1.7 %shard_map.97 = (bf16[256,256]{1,0:T(8,128)(2,1)S(1)}, s32[1]{0:T(128)}) custom-call(bf16[256,256]{1,0:T(8,128)(2,1)S(1)} %copy-done.1, bf16[16,256]{1,0:T(8,128)(2,1)S(1)} %get-tuple-element.14.tail_ref, bf16[8,528,256]{2,1,0:T(8,128)(2,1)S(1)} %all-to-all-done.incoming_ref), custom_call_target="tpu_custom_call" | custom-call | flops 2000000000 | tf_op jit(solution)/shard_map/pallas_call | solution.py:226
  63.3 0.0 collective-permute-done.1.other_ref
  63.4 0.0 copy-done.2
  63.4 0.0 copy-start
  63.4 7.1 %shard_map.99 = (bf16[256,128]{1,0:T(8,128)(2,1)S(1)}, bf16[256,128]{1,0:T(8,128)(2,1)S(1)}) custom-call(s32[1]{0:T(128)} %bitcast.pair_ref, s32[1]{0:T(128)} %bitcast.1.side_ref, s32[1]{0:T(128)} %get-tuple-element.15.mark_ref, bf16[256,128]{1,0:T(8,128)(2,1)S(1)} %copy-done.2, bf16[256,128]{1,0:T(8,128)(2,1)S(1)} %collective-permute-done.1.other_ref, ...), custom_call_target="tpu_custom_call" | custom-call | flops 4000000000 | tf_op jit(solution)/shard_map/pallas_call | solution.py:286
  70.5 0.1 collective-permute-start.2
  70.6 0.0 collective-permute-done.3
  70.6 0.1 slice_select_fusion
  70.7 0.8 collective-permute-start.4
  71.5 0.0 collective-permute-done.5.beside_ref
  71.5 1.2 %collective-permute-start.6 = (bf16[256,256]{1,0:T(8,128)(2,1)S(1)}, bf16[256,256]{1,0:T(8,128)(2,1)S(1)}, u32[]{:S(2)}, u32[]{:S(2)}) collective-permute-start(bf16[256,256]{1,0:T(8,128)(2,1)S(1)} %pad_maximum_fusion.one_ref), channel_id=1, source_target_pairs={{0,2},{1,3},{2,0},{3,1},{4,6},{5,7},{6,4},{7,5},{8,10},{9,11},{10,... | collective-permute-start | bytes 393224 | tf_op jit(solution)/shard_map/ppermute | solution.py:397
  72.8 0.9 %collective-permute-done.2 = bf16[256,128]{1,0:T(8,128)(2,1)S(1)} collective-permute-done((bf16[256,128]{1,0:T(8,128)(2,1)S(1)}, bf16[256,128]{1,0:T(8,128)(2,1)S(1)}, u32[]{:S(2)}, u32[]{:S(2)}) %collective-permute-start.2) | collective-permute-done | bytes 65568 | tf_op jit(solution)/shard_map/ppermute | solution.py:401
  73.7 3.0 %collective-permute-start.7 = (bf16[256,256]{1,0:T(8,128)(2,1)S(1)}, bf16[256,256]{1,0:T(8,128)(2,1)S(1)}, u32[]{:S(2)}, u32[]{:S(2)}) collective-permute-start(bf16[256,256]{1,0:T(8,128)(2,1)S(1)} %pad_maximum_fusion.one_ref), channel_id=1, source_target_pairs={{0,3},{1,2},{2,1},{3,0},{4,7},{5,6},{6,5},{7,4},{8,11},{9,10},{10,... | collective-permute-start | bytes 393224 | tf_op jit(solution)/shard_map/ppermute | solution.py:397
  76.7 0.7 maximum_select_fusion
  77.4 0.0 collective-permute-done.4.two_ref
  77.4 0.0 copy-done
  77.4 1.9 %shard_map.100.partial_ref = f32[256,2048]{1,0:T(8,128)S(1)} custom-call(bf16[256,256]{1,0:T(8,128)(2,1)S(1)} %pad_maximum_fusion.one_ref, bf16[256,256]{1,0:T(8,128)(2,1)S(1)} %collective-permute-done.4.two_ref, bf16[256,2048]{1,0:T(8,128)(2,1)S(1)} %copy-done, bf16[256,2048]{1,0:T(8,128)(2,1)} %collective-permute-done.5.beside_ref), custom_call_target="tpu_custom_call" | custom-call | tf_op jit(solution)/shard_map/pallas_call | solution.py:309
  79.3 0.0 collective-permute-done.8.refs_2_
  79.3 0.0 collective-permute-done.9.refs_3_
  79.3 0.0 collective-permute-done.6.refs_0_
  79.4 1.6 %collective-permute-done.7.refs_1_ = bf16[256,256]{1,0:T(8,128)(2,1)S(1)} collective-permute-done((bf16[256,256]{1,0:T(8,128)(2,1)S(1)}, bf16[256,256]{1,0:T(8,128)(2,1)S(1)}, u32[]{:S(2)}, u32[]{:S(2)}) %collective-permute-start.7) | collective-permute-done | bytes 131104 | tf_op jit(solution)/shard_map/ppermute | solution.py:397
  80.9 3.0 %shard_map.101 = bf16[256,2048]{1,0:T(8,128)(2,1)} custom-call(f32[256,2048]{1,0:T(8,128)S(1)} %shard_map.100.partial_ref, bf16[256,256]{1,0:T(8,128)(2,1)S(1)} %collective-permute-done.6.refs_0_, bf16[256,256]{1,0:T(8,128)(2,1)S(1)} %collective-permute-done.7.refs_1_, bf16[256,2048]{1,0:T(8,128)(2,1)} %collective-permute-done.8.refs_2_, ...), custom_call_target="tpu_custom_call" | custom-call | flops 2000000000 | tf_op jit(solution)/shard_map/pallas_call | solution.py:341
  (4 shorter events, 0.0 us)
Async XLA Ops:
  4.3 5.7 %copy-start.1 = (bf16[256,256]{1,0:T(8,128)(2,1)S(1)}, bf16[256,256]{1,0:T(8,128)(2,1)}, u32[]{:S(2)}) copy-start(bf16[256,256]{1,0:T(8,128)(2,1)} %queries_ref.3) | copy-start | bytes 393220
  4.3 54.5 %all-to-all-start = ((bf16[8,528,256]{2,1,0:T(8,128)(2,1)}), bf16[8,528,256]{2,1,0:T(8,128)(2,1)S(1)}, u32[]{:S(2)}, u32[]{:S(2)}) async-start(bf16[8,528,256]{2,1,0:T(8,128)(2,1)} %shard_map.95), calls=%async_computation | async-start | bytes 4325376 | tf_op jit(solution)/shard_map/all_to_all | solution.py:378
  9.9 34.9 %collective-permute-start = (bf16[64,256]{1,0:T(8,128)(2,1)S(1)}, bf16[64,256]{1,0:T(8,128)(2,1)S(1)}, u32[]{:S(2)}, u32[]{:S(2)}) collective-permute-start(bf16[64,256]{1,0:T(8,128)(2,1)S(1)} %slice.9), channel_id=1, source_target_pairs={{4,0},{8,4},{12,8},{16,12},{20,16},{24,20},{28,24},{5,1},{9,5},{13... | collective-permute-start | bytes 98312 | tf_op jit(solution)/shard_map/ppermute | solution.py:390
  17.4 45.9 %collective-permute-start.1 = (bf16[256,128]{1,0:T(8,128)(2,1)}, bf16[256,128]{1,0:T(8,128)(2,1)S(1)}, u32[]{:S(2)}, u32[]{:S(2)}) collective-permute-start(bf16[256,128]{1,0:T(8,128)(2,1)} %get-tuple-element.17), channel_id=1, source_target_pairs={{0,4},{4,0},{8,12},{12,8},{16,20},{20,16},{24,28},{28,24},{1,5},{5... | collective-permute-start | bytes 196616 | tf_op jit(solution)/shard_map/ppermute | solution.py:386
  17.8 53.8 %collective-permute-start.5 = (bf16[256,2048]{1,0:T(8,128)(2,1)}, bf16[256,2048]{1,0:T(8,128)(2,1)}, u32[]{:S(2)}, u32[]{:S(2)}) collective-permute-start(bf16[256,2048]{1,0:T(8,128)(2,1)} %get-tuple-element.23), channel_id=1, source_target_pairs={{0,1},{1,0},{2,3},{3,2},{4,5},{5,4},{6,7},{7,6},{8,9},{9,8},{10,11... | collective-permute-start | bytes 3145736 | tf_op jit(solution)/shard_map/ppermute | solution.py:388
  19.6 59.8 %collective-permute-start.8 = (bf16[256,2048]{1,0:T(8,128)(2,1)}, bf16[256,2048]{1,0:T(8,128)(2,1)}, u32[]{:S(2)}, u32[]{:S(2)}) collective-permute-start(bf16[256,2048]{1,0:T(8,128)(2,1)} %get-tuple-element.24), channel_id=1, source_target_pairs={{0,2},{1,3},{2,0},{3,1},{4,6},{5,7},{6,4},{7,5},{8,10},{9,11},{10,... | collective-permute-start | bytes 3145736 | tf_op jit(solution)/shard_map/ppermute | solution.py:388
  20.8 58.6 %collective-permute-start.9 = (bf16[256,2048]{1,0:T(8,128)(2,1)}, bf16[256,2048]{1,0:T(8,128)(2,1)}, u32[]{:S(2)}, u32[]{:S(2)}) collective-permute-start(bf16[256,2048]{1,0:T(8,128)(2,1)} %get-tuple-element.25), channel_id=1, source_target_pairs={{0,3},{1,2},{2,1},{3,0},{4,7},{5,6},{6,5},{7,4},{8,11},{9,10},{10,... | collective-permute-start | bytes 3145736 | tf_op jit(solution)/shard_map/ppermute | solution.py:388
  59.4 11.2 %collective-permute-start.3 = (bf16[64,256]{1,0:T(8,128)(2,1)S(1)}, bf16[64,256]{1,0:T(8,128)(2,1)S(1)}, u32[]{:S(2)}, u32[]{:S(2)}) collective-permute-start(bf16[64,256]{1,0:T(8,128)(2,1)S(1)} %get-tuple-element.20), channel_id=1, source_target_pairs={{0,4},{4,8},{8,12},{12,16},{16,20},{20,24},{24,28},{1,5},{5,9},{9,... | collective-permute-start | bytes 98312 | tf_op jit(solution)/shard_map/ppermute | solution.py:393
  61.7 1.7 %copy-start.2 = (bf16[256,128]{1,0:T(8,128)(2,1)S(1)}, bf16[256,128]{1,0:T(8,128)(2,1)}, u32[]{:S(2)}) copy-start(bf16[256,128]{1,0:T(8,128)(2,1)} %get-tuple-element.16.mine_ref) | copy-start | bytes 196612
  63.4 14.0 %copy-start = (bf16[256,2048]{1,0:T(8,128)(2,1)S(1)}, bf16[256,2048]{1,0:T(8,128)(2,1)}, u32[]{:S(2)}) copy-start(bf16[256,2048]{1,0:T(8,128)(2,1)} %get-tuple-element.22.own_ref) | copy-start | bytes 3145732
  70.5 3.2 %collective-permute-start.2 = (bf16[256,128]{1,0:T(8,128)(2,1)S(1)}, bf16[256,128]{1,0:T(8,128)(2,1)S(1)}, u32[]{:S(2)}, u32[]{:S(2)}) collective-permute-start(bf16[256,128]{1,0:T(8,128)(2,1)S(1)} %get-tuple-element.19), channel_id=1, source_target_pairs={{0,4},{4,0},{8,12},{12,8},{16,20},{20,16},{24,28},{28,24},{1,5},{5... | collective-permute-start | bytes 196616 | tf_op jit(solution)/shard_map/ppermute | solution.py:401
  70.7 6.7 %collective-permute-start.4 = (bf16[256,256]{1,0:T(8,128)(2,1)S(1)}, bf16[256,256]{1,0:T(8,128)(2,1)S(1)}, u32[]{:S(2)}, u32[]{:S(2)}) collective-permute-start(bf16[256,256]{1,0:T(8,128)(2,1)S(1)} %pad_maximum_fusion.one_ref), channel_id=1, source_target_pairs={{0,1},{1,0},{2,3},{3,2},{4,5},{5,4},{6,7},{7,6},{8,9},{9,8},{10,11... | collective-permute-start | bytes 393224 | tf_op jit(solution)/shard_map/ppermute | solution.py:397
  71.5 7.8 %collective-permute-start.6 = (bf16[256,256]{1,0:T(8,128)(2,1)S(1)}, bf16[256,256]{1,0:T(8,128)(2,1)S(1)}, u32[]{:S(2)}, u32[]{:S(2)}) collective-permute-start(bf16[256,256]{1,0:T(8,128)(2,1)S(1)} %pad_maximum_fusion.one_ref), channel_id=1, source_target_pairs={{0,2},{1,3},{2,0},{3,1},{4,6},{5,7},{6,4},{7,5},{8,10},{9,11},{10,... | collective-permute-start | bytes 393224 | tf_op jit(solution)/shard_map/ppermute | solution.py:397
  73.7 7.3 %collective-permute-start.7 = (bf16[256,256]{1,0:T(8,128)(2,1)S(1)}, bf16[256,256]{1,0:T(8,128)(2,1)S(1)}, u32[]{:S(2)}, u32[]{:S(2)}) collective-permute-start(bf16[256,256]{1,0:T(8,128)(2,1)S(1)} %pad_maximum_fusion.one_ref), channel_id=1, source_target_pairs={{0,3},{1,2},{2,1},{3,0},{4,7},{5,6},{6,5},{7,4},{8,11},{9,10},{10,... | collective-permute-start | bytes 393224 | tf_op jit(solution)/shard_map/ppermute | solution.py:397

commit v11 on v10

--- a/solution.py
+++ b/solution.py
@@ -177,8 +177,7 @@
         next_ref[:, feats] = answer[LEAD:]
 
 
-def other_kernel(queries_ref, tail_ref, incoming_ref, out_ref, mark_ref, order_ref):
-    mark_ref[0] = 0
+def other_kernel(queries_ref, tail_ref, incoming_ref, out_ref, order_ref):
     rows, width = queries_ref.shape
     length = (incoming_ref.shape[1] - LEAD - rows) // 2
     find_sources(incoming_ref, order_ref, length)
@@ -225,16 +224,29 @@
 def other_attend(queries, tail, incoming):
     return pl.pallas_call(
         other_kernel,
-        out_shape=(
-            jax.ShapeDtypeStruct(queries.shape, queries.dtype),
-            jax.ShapeDtypeStruct((1,), jnp.int32),
-        ),
+        out_shape=jax.ShapeDtypeStruct(queries.shape, queries.dtype),
         in_specs=[VMEM] * 3,
-        out_specs=(VMEM, SMEM),
+        out_specs=VMEM,
         scratch_shapes=order_scratch(queries.shape[0]),
         compiler_params=PARAMS,
         cost_estimate=takes(2),
     )(queries, tail, incoming)
+
+
+def merge_kernel(back_ref, answers_ref, out_ref):
+    row = lax.broadcasted_iota(jnp.int32, back_ref.shape, 0)
+    out_ref[:BLOCK, :] = jnp.where(row < BLOCK - 1, back_ref[...], answers_ref[:BLOCK, :])
+    out_ref[BLOCK:, :] = answers_ref[BLOCK:, :]
+
+
+def merge(back, answers):
+    return pl.pallas_call(
+        merge_kernel,
+        out_shape=jax.ShapeDtypeStruct(answers.shape, answers.dtype),
+        in_specs=[VMEM] * 2,
+        out_specs=VMEM,
+        compiler_params=PARAMS,
+    )(back, answers)
 
 
 def self_kernel(pair_ref, side_ref, mark_ref, mine_ref, other_ref, incoming_ref, *refs):
@@ -243,31 +255,34 @@
     tile = mine_ref.shape[0]
     rows = 2 * tile
     front = incoming_ref.shape[1] - tile
-    q = jnp.concatenate([mine_ref[...], other_ref[...]], axis=0)
+    chunk = min(128, tile)
 
     def attend(at, fresh):
         kv = incoming_ref[pl.ds(2 * at, 2), front:, :].reshape(rows, 2 * HD)
-        s = dot_t(q, kv[:, :HD])
-        if fresh:
-            row = lax.broadcasted_iota(jnp.int32, (rows, rows), 0)
-            col = lax.broadcasted_iota(jnp.int32, (rows, rows), 1)
-            turn = side * tile
-            row = jnp.where(row < tile, row + turn, row - turn)
-            s = jnp.where(col <= row, s, NEGATIVE)
-        peak = jnp.max(s, axis=1, keepdims=True)
-        if not fresh:
-            old = peak_ref[:, :1]
-            peak = jnp.maximum(peak, old)
-            factor = jnp.exp2((old - peak) * SCALE)
-        p = jnp.exp2((s - peak) * SCALE)
-        total = jnp.sum(p, axis=1, keepdims=True)
-        accum = dot(p.astype(jnp.bfloat16), kv[:, HD:])
-        if not fresh:
-            total += total_ref[:, :1] * factor
-            accum += accum_ref[...] * factor
-        peak_ref[...] = jnp.broadcast_to(peak, (rows, HD))
-        total_ref[...] = jnp.broadcast_to(total, (rows, HD))
-        accum_ref[...] = accum
+        for start in range(0, rows, chunk):
+            here = slice(start, start + chunk)
+            q_ref, offset = (mine_ref, start) if start < tile else (other_ref, start - tile)
+            s = dot_t(q_ref[offset : offset + chunk, :], kv[:, :HD])
+            if fresh:
+                row = lax.broadcasted_iota(jnp.int32, (chunk, rows), 0) + start
+                col = lax.broadcasted_iota(jnp.int32, (chunk, rows), 1)
+                turn = side * tile
+                row = row + turn if start < tile else row - turn
+                s = jnp.where(col <= row, s, NEGATIVE)
+            peak = jnp.max(s, axis=1, keepdims=True)
+            if not fresh:
+                old = peak_ref[here, :1]
+                peak = jnp.maximum(peak, old)
+                factor = jnp.exp2((old - peak) * SCALE)
+            p = jnp.exp2((s - peak) * SCALE)
+            total = jnp.sum(p, axis=1, keepdims=True)
+            accum = dot(p.astype(jnp.bfloat16), kv[:, HD:])
+            if not fresh:
+                total += total_ref[here, :1] * factor
+                accum += accum_ref[here, :] * factor
+            peak_ref[here, :] = jnp.broadcast_to(peak, (chunk, HD))
+            total_ref[here, :] = jnp.broadcast_to(total, (chunk, HD))
+            accum_ref[here, :] = accum
 
     attend(pair, True)
 
@@ -290,11 +305,12 @@
         out_specs=(VMEM, VMEM),
         scratch_shapes=[pltpu.VMEM((2 * tile, HD), jnp.float32)] * 3,
         compiler_params=PARAMS,
-        cost_estimate=takes(4),
+        cost_estimate=takes(6),
     )(pair, side, mark, mine, other, incoming)
 
 
-def near_kernel(one_ref, two_ref, own_ref, beside_ref, partial_ref):
+def near_kernel(one_ref, two_ref, own_ref, beside_ref, partial_ref, mark_ref):
+    mark_ref[0] = 0
     width = partial_ref.shape[1]
     term = jnp.concatenate([one_ref[...], two_ref[...]], axis=1)
     tile = min(512, width)
@@ -308,9 +324,12 @@
 def project_near(terms, own, beside):
     return pl.pallas_call(
         near_kernel,
-        out_shape=jax.ShapeDtypeStruct((terms[0].shape[0], own.shape[1]), jnp.float32),
+        out_shape=(
+            jax.ShapeDtypeStruct((terms[0].shape[0], own.shape[1]), jnp.float32),
+            jax.ShapeDtypeStruct((1,), jnp.int32),
+        ),
         in_specs=[VMEM] * 4,
-        out_specs=VMEM,
+        out_specs=(VMEM, SMEM),
         compiler_params=PARAMS,
     )(*terms, own, beside)
 
@@ -391,11 +410,9 @@
 
     tail, onward = last_attend(cross_queries, spill, incoming)
     back = lax.ppermute(onward, "ctx", [(i, i + 1) for i in range(count - 1)])
-    answers, mark = other_attend(cross_queries, tail, incoming)
-    early = jnp.arange(BLOCK)[:, None] < BLOCK - 1
-    cca = jnp.concatenate([jnp.where(early, back, answers[:BLOCK]), answers[BLOCK:]], axis=0)
+    cca = merge(back, other_attend(cross_queries, tail, incoming))
     terms = [cca] + [lax.ppermute(cca, "tp", across[step]) for step in range(1, groups)]
-    partial = project_near(terms[:2], own, beside)
+    partial, mark = project_near(terms[:2], own, beside)
 
     ours, theirs = self_attend(pair, side, mark, q_mine, q_other, incoming)
     attended = both(ours, lax.ppermute(theirs, "ctx", swap), 1)

time: 84.3 us -> 82.7 us (0.981)
    ppermute x1, waiting for transfers between devices: 0.01 us -> 1.61 us  [shards(): back = lax.ppermute(onward, 'ctx', [(i, i + 1) for i in range(count - 1)])]
    ppermute x3, waiting for transfers between devices: 1.59 us -> 0.01 us  [shards(): lax.ppermute(cca, 'tp', across[step])]
    ppermute x1, starting transfers between devices: 0.07 us -> 1.09 us  [shards(): attended = both(ours, lax.ppermute(theirs, 'ctx', swap), 1)]
    ppermute x3, starting transfers between devices: 5.08 us -> 4.14 us  [shards(): lax.ppermute(cca, 'tp', across[step])]
    ppermute x1, waiting for transfers between devices: 0.91 us -> 0.01 us  [shards(): attended = both(ours, lax.ppermute(theirs, 'ctx', swap), 1)]
    pallas_call x2 -> x3, Pallas kernels: 3.59 us -> 3.82 us  [the longest x1 2.16 us: project_near(): pl.pallas_call(near_kernel, out_shape=(jax.ShapeDtypeStruct((terms[0].sha...]
  transfers between devices with their start and end apart: 11 -> 11, of which waited for: 4 -> 3; matrix products, arithmetic and copies ran while one was open for 1% -> 0% of each run, Pallas kernels for 19% -> 22%
where the time goes in v11:
time: 82.7 us; the launch traced here: 82.3 us
  waiting for transfers between devices  40 us (48%)
  Pallas kernels  21.8 us (26%)
  starting transfers between devices  19.1 us (23%)
    ppermute x1, waiting for transfers between devices, shards(): lax.ppermute(cross_queries[:BLOCK], 'ctx', [(i + 1, i) for i in range(cou...  24.4 us
    all_to_all x1, waiting for transfers between devices, exchange(): return lax.all_to_all(value, 'ctx', split_axis=0, concat_axis=0, tiled=True)  13.9 us
    pallas_call x1, Pallas kernels, self_attend(): pl.pallas_call(self_kernel, out_shape=(jax.ShapeDtypeStruct((tile, HD), j...  6.35 us
    all_to_all x1, starting transfers between devices, exchange(): return lax.all_to_all(value, 'ctx', split_axis=0, concat_axis=0, tiled=True)  5.51 us
    pallas_call x1, Pallas kernels, cut(): pl.pallas_call(functools.partial(cut_kernel, plan), out_shape=tuple(shape...  4.39 us
    ppermute x3, starting transfers between devices, shards(): lax.ppermute(cca, 'tp', across[step])  4.14 us
    pallas_call x1, Pallas kernels, arrange(): pl.pallas_call(arrange_kernel, out_shape=jax.ShapeDtypeStruct((indices, f...  3.64 us
    ppermute x1, starting transfers between devices, shards(): lax.ppermute(cross_queries[:BLOCK], 'ctx', [(i + 1, i) for i in range(cou...  3.08 us
  transfers between devices with their start and end apart: 11, of which 3 were waited for; matrix products, arithmetic and copies ran while one was open for 0% of the time, Pallas kernels for 22%

profile of v11, /device:TPU:25, one launch (start us, length us, event | category | flops | bytes accessed | tf_op | source)
XLA Modules:
  0.0 82.3 jit_solution(5636515630339261268)
XLA Ops:
  0.6 3.6 %shard_map.95 = bf16[8,528,256]{2,1,0:T(8,128)(2,1)} custom-call(s32[8]{0:T(128)} %slot_ref.1, bf16[8,128,256]{2,1,0:T(8,128)(2,1)} %keys_ref.1, bf16[8,128,256]{2,1,0:T(8,128)(2,1)} %values_ref.1, bf16[256,256]{1,0:T(8,128)(2,1)} %own_keys.1, bf16[256,256]{1,0:T(8,128)(2,1)} %own_values.1), custom_call_target="tpu_custom_call" | custom-call | flops 4000000000 | tf_op jit(solution)/shard_map/pallas_call | solution.py:128
  4.3 5.5 %all-to-all-start = ((bf16[8,528,256]{2,1,0:T(8,128)(2,1)}), bf16[8,528,256]{2,1,0:T(8,128)(2,1)S(1)}, u32[]{:S(2)}, u32[]{:S(2)}) async-start(bf16[8,528,256]{2,1,0:T(8,128)(2,1)} %shard_map.95), calls=%async_computation | async-start | bytes 4325376 | tf_op jit(solution)/shard_map/all_to_all | solution.py:397
  9.8 0.0 copy-start.1
  9.8 4.4 %shard_map.99 = (bf16[256,128]{1,0:T(8,128)(2,1)}, bf16[256,128]{1,0:T(8,128)(2,1)}, bf16[256,2048]{1,0:T(8,128)(2,1)}, bf16[256,2048]{1,0:T(8,128)(2,1)}, bf16[...) custom-call(s32[1]{0:T(128)} %bitcast.1.side_ref, s32[1]{0:T(128)} %bitcast.2.tp_ref, bf16[256,256]{1,0:T(8,128)(2,1)} %refs_0_.1, ...), custom_call_target="tpu_custom_call" | custom-call | flops 2000000000 | tf_op jit(solution)/shard_map/pallas_call | solution.py:67
  14.2 1.3 %collective-permute-start.3 = (bf16[256,2048]{1,0:T(8,128)(2,1)}, bf16[256,2048]{1,0:T(8,128)(2,1)}, u32[]{:S(2)}, u32[]{:S(2)}) collective-permute-start(bf16[256,2048]{1,0:T(8,128)(2,1)} %get-tuple-element.17), channel_id=1, source_target_pairs={{0,1},{1,0},{2,3},{3,2},{4,5},{5,4},{6,7},{7,6},{8,9},{9,8},{10,11... | collective-permute-start | bytes 3145736 | tf_op jit(solution)/shard_map/ppermute | solution.py:407
  15.5 1.2 %collective-permute-start.8 = (bf16[256,2048]{1,0:T(8,128)(2,1)}, bf16[256,2048]{1,0:T(8,128)(2,1)}, u32[]{:S(2)}, u32[]{:S(2)}) collective-permute-start(bf16[256,2048]{1,0:T(8,128)(2,1)} %get-tuple-element.24), channel_id=1, source_target_pairs={{0,2},{1,3},{2,0},{3,1},{4,6},{5,7},{6,4},{7,5},{8,10},{9,11},{10,... | collective-permute-start | bytes 3145736 | tf_op jit(solution)/shard_map/ppermute | solution.py:407
  16.7 0.5 collective-permute-start.9
  17.2 0.0 copy-done.1
  17.2 3.1 %collective-permute-start = (bf16[64,256]{1,0:T(8,128)(2,1)S(1)}, bf16[64,256]{1,0:T(8,128)(2,1)S(1)}, u32[]{:S(2)}, u32[]{:S(2)}) collective-permute-start(bf16[64,256]{1,0:T(8,128)(2,1)S(1)} %slice.3), channel_id=1, source_target_pairs={{4,0},{8,4},{12,8},{16,12},{20,16},{24,20},{28,24},{5,1},{9,5},{13... | collective-permute-start | bytes 98312 | tf_op jit(solution)/shard_map/ppermute | solution.py:409
  20.3 24.4 %collective-permute-done.spill_ref = bf16[64,256]{1,0:T(8,128)(2,1)S(1)} collective-permute-done((bf16[64,256]{1,0:T(8,128)(2,1)S(1)}, bf16[64,256]{1,0:T(8,128)(2,1)S(1)}, u32[]{:S(2)}, u32[]{:S(2)}) %collective-permute-start) | collective-permute-done | bytes 32800 | tf_op jit(solution)/shard_map/ppermute | solution.py:409
  44.7 13.9 %all-to-all-done.incoming_ref = bf16[8,528,256]{2,1,0:T(8,128)(2,1)S(1)} async-done(((bf16[8,528,256]{2,1,0:T(8,128)(2,1)}), bf16[8,528,256]{2,1,0:T(8,128)(2,1)S(1)}, u32[]{:S(2)}, u32[]{:S(2)}) %all-to-all-start) | async-done | bytes 2162720 | tf_op jit(solution)/shard_map/all_to_all | solution.py:397
  58.6 0.6 shard_map.96
  59.2 2.3 %collective-permute-start.1 = (bf16[64,256]{1,0:T(8,128)(2,1)S(1)}, bf16[64,256]{1,0:T(8,128)(2,1)S(1)}, u32[]{:S(2)}, u32[]{:S(2)}) collective-permute-start(bf16[64,256]{1,0:T(8,128)(2,1)S(1)} %get-tuple-element.14), channel_id=1, source_target_pairs={{0,4},{4,8},{8,12},{12,16},{16,20},{20,24},{24,28},{1,5},{5,9},{9,... | collective-permute-start | bytes 98312 | tf_op jit(solution)/shard_map/ppermute | solution.py:412
  61.5 0.0 copy-start
  61.5 1.6 %shard_map.97.answers_ref = bf16[256,256]{1,0:T(8,128)(2,1)S(1)} custom-call(bf16[256,256]{1,0:T(8,128)(2,1)S(1)} %copy-done.1, bf16[16,256]{1,0:T(8,128)(2,1)S(1)} %get-tuple-element.15.tail_ref, bf16[8,528,256]{2,1,0:T(8,128)(2,1)S(1)} %all-to-all-done.incoming_ref), custom_call_target="tpu_custom_call" | custom-call | flops 2000000000 | tf_op jit(solution)/shard_map/pallas_call | solution.py:225
  63.2 1.6 %collective-permute-done.1.back_ref = bf16[64,256]{1,0:T(8,128)(2,1)S(1)} collective-permute-done((bf16[64,256]{1,0:T(8,128)(2,1)S(1)}, bf16[64,256]{1,0:T(8,128)(2,1)S(1)}, u32[]{:S(2)}, u32[]{:S(2)}) %collective-permute-start.1) | collective-permute-done | bytes 32800 | tf_op jit(solution)/shard_map/ppermute | solution.py:412
  64.8 1.7 %collective-permute-start.2 = (bf16[256,256]{1,0:T(8,128)(2,1)S(1)}, bf16[256,256]{1,0:T(8,128)(2,1)S(1)}, u32[]{:S(2)}, u32[]{:S(2)}) collective-permute-start(bf16[256,256]{1,0:T(8,128)(2,1)S(1)} %shard_map.98.one_ref), channel_id=1, source_target_pairs={{0,1},{1,0},{2,3},{3,2},{4,5},{5,4},{6,7},{7,6},{8,9},{9,8},{10,11... | collective-permute-start | bytes 393224 | tf_op jit(solution)/shard_map/ppermute | solution.py:414
  66.5 0.0 collective-permute-start.4
  66.5 0.0 copy-start.2
  66.5 0.0 collective-permute-done.3.beside_ref
  66.5 1.3 %collective-permute-start.6 = (bf16[256,256]{1,0:T(8,128)(2,1)S(1)}, bf16[256,256]{1,0:T(8,128)(2,1)S(1)}, u32[]{:S(2)}, u32[]{:S(2)}) collective-permute-start(bf16[256,256]{1,0:T(8,128)(2,1)S(1)} %shard_map.98.one_ref), channel_id=1, source_target_pairs={{0,2},{1,3},{2,0},{3,1},{4,6},{5,7},{6,4},{7,5},{8,10},{9,11},{10,... | collective-permute-start | bytes 393224 | tf_op jit(solution)/shard_map/ppermute | solution.py:414
  67.8 0.0 collective-permute-done.2.two_ref
  67.8 1.1 %collective-permute-start.7 = (bf16[256,256]{1,0:T(8,128)(2,1)S(1)}, bf16[256,256]{1,0:T(8,128)(2,1)S(1)}, u32[]{:S(2)}, u32[]{:S(2)}) collective-permute-start(bf16[256,256]{1,0:T(8,128)(2,1)S(1)} %shard_map.98.one_ref), channel_id=1, source_target_pairs={{0,3},{1,2},{2,1},{3,0},{4,7},{5,6},{6,5},{7,4},{8,11},{9,10},{10,... | collective-permute-start | bytes 393224 | tf_op jit(solution)/shard_map/ppermute | solution.py:414
  69.0 0.0 copy-done
  69.0 2.2 %shard_map.100 = (f32[256,2048]{1,0:T(8,128)S(1)}, s32[1]{0:T(128)}) custom-call(bf16[256,256]{1,0:T(8,128)(2,1)S(1)} %shard_map.98.one_ref, bf16[256,256]{1,0:T(8,128)(2,1)S(1)} %collective-permute-done.2.two_ref, bf16[256,2048]{1,0:T(8,128)(2,1)S(1)} %copy-done, bf16[256,2048]{1,0:T(8,128)(2,1)} %collective-permute-done.3.beside_ref), custom_call_target="tpu_custom_call" | custom-call | tf_op jit(solution)/shard_map/pallas_call | solution.py:325
  71.1 0.0 collective-permute-done.4.other_ref
  71.1 0.0 copy-done.2
  71.2 6.4 %shard_map.101 = (bf16[256,128]{1,0:T(8,128)(2,1)S(1)}, bf16[256,128]{1,0:T(8,128)(2,1)S(1)}) custom-call(s32[1]{0:T(128)} %bitcast.pair_ref, s32[1]{0:T(128)} %bitcast.1.side_ref, s32[1]{0:T(128)} %get-tuple-element.18.mark_ref, bf16[256,128]{1,0:T(8,128)(2,1)S(1)} %copy-done.2, bf16[256,128]{1,0:T(8,128)(2,1)S(1)} %collective-permute-done.4.other_ref, ...), custom_call_target="tpu_custom_call" | custom-call | flops 6000000000 | tf_op jit(solution)/shard_map/pallas_call | solution.py:301
  77.5 1.1 %collective-permute-start.5 = (bf16[256,128]{1,0:T(8,128)(2,1)S(1)}, bf16[256,128]{1,0:T(8,128)(2,1)S(1)}, u32[]{:S(2)}, u32[]{:S(2)}) collective-permute-start(bf16[256,128]{1,0:T(8,128)(2,1)S(1)} %get-tuple-element.22), channel_id=1, source_target_pairs={{0,4},{4,0},{8,12},{12,8},{16,20},{20,16},{24,28},{28,24},{1,5},{5... | collective-permute-start | bytes 196616 | tf_op jit(solution)/shard_map/ppermute | solution.py:418
  78.6 0.0 collective-permute-done.8.refs_2_
  78.6 0.0 collective-permute-done.9.refs_3_
  78.6 0.0 collective-permute-done.6.refs_0_
  78.6 0.0 collective-permute-done.7.refs_1_
  78.6 3.0 %shard_map.102 = bf16[256,2048]{1,0:T(8,128)(2,1)} custom-call(f32[256,2048]{1,0:T(8,128)S(1)} %get-tuple-element.23.partial_ref, bf16[256,256]{1,0:T(8,128)(2,1)S(1)} %collective-permute-done.6.refs_0_, bf16[256,256]{1,0:T(8,128)(2,1)S(1)} %collective-permute-done.7.refs_1_, bf16[256,2048]{1,0:T(8,128)(2,1)} %collective-permute-done.8.refs_2_, ...), custom_call_target="tpu_custom_call" | custom-call | flops 2000000000 | tf_op jit(solution)/shard_map/pallas_call | solution.py:360
  81.6 0.0 collective-permute-done.5
  81.6 0.7 maximum_select_fusion
  (2 shorter events, 0.0 us)
Async XLA Ops:
  4.3 54.3 %all-to-all-start = ((bf16[8,528,256]{2,1,0:T(8,128)(2,1)}), bf16[8,528,256]{2,1,0:T(8,128)(2,1)S(1)}, u32[]{:S(2)}, u32[]{:S(2)}) async-start(bf16[8,528,256]{2,1,0:T(8,128)(2,1)} %shard_map.95), calls=%async_computation | async-start | bytes 4325376 | tf_op jit(solution)/shard_map/all_to_all | solution.py:397
  9.8 7.4 %copy-start.1 = (bf16[256,256]{1,0:T(8,128)(2,1)S(1)}, bf16[256,256]{1,0:T(8,128)(2,1)}, u32[]{:S(2)}) copy-start(bf16[256,256]{1,0:T(8,128)(2,1)} %queries_ref.3) | copy-start | bytes 393220
  14.2 52.3 %collective-permute-start.3 = (bf16[256,2048]{1,0:T(8,128)(2,1)}, bf16[256,2048]{1,0:T(8,128)(2,1)}, u32[]{:S(2)}, u32[]{:S(2)}) collective-permute-start(bf16[256,2048]{1,0:T(8,128)(2,1)} %get-tuple-element.17), channel_id=1, source_target_pairs={{0,1},{1,0},{2,3},{3,2},{4,5},{5,4},{6,7},{7,6},{8,9},{9,8},{10,11... | collective-permute-start | bytes 3145736 | tf_op jit(solution)/shard_map/ppermute | solution.py:407
  15.5 63.1 %collective-permute-start.8 = (bf16[256,2048]{1,0:T(8,128)(2,1)}, bf16[256,2048]{1,0:T(8,128)(2,1)}, u32[]{:S(2)}, u32[]{:S(2)}) collective-permute-start(bf16[256,2048]{1,0:T(8,128)(2,1)} %get-tuple-element.24), channel_id=1, source_target_pairs={{0,2},{1,3},{2,0},{3,1},{4,6},{5,7},{6,4},{7,5},{8,10},{9,11},{10,... | collective-permute-start | bytes 3145736 | tf_op jit(solution)/shard_map/ppermute | solution.py:407
  16.7 61.9 %collective-permute-start.9 = (bf16[256,2048]{1,0:T(8,128)(2,1)}, bf16[256,2048]{1,0:T(8,128)(2,1)}, u32[]{:S(2)}, u32[]{:S(2)}) collective-permute-start(bf16[256,2048]{1,0:T(8,128)(2,1)} %get-tuple-element.25), channel_id=1, source_target_pairs={{0,3},{1,2},{2,1},{3,0},{4,7},{5,6},{6,5},{7,4},{8,11},{9,10},{10,... | collective-permute-start | bytes 3145736 | tf_op jit(solution)/shard_map/ppermute | solution.py:407
  17.2 27.5 %collective-permute-start = (bf16[64,256]{1,0:T(8,128)(2,1)S(1)}, bf16[64,256]{1,0:T(8,128)(2,1)S(1)}, u32[]{:S(2)}, u32[]{:S(2)}) collective-permute-start(bf16[64,256]{1,0:T(8,128)(2,1)S(1)} %slice.3), channel_id=1, source_target_pairs={{4,0},{8,4},{12,8},{16,12},{20,16},{24,20},{28,24},{5,1},{9,5},{13... | collective-permute-start | bytes 98312 | tf_op jit(solution)/shard_map/ppermute | solution.py:409
  59.2 5.6 %collective-permute-start.1 = (bf16[64,256]{1,0:T(8,128)(2,1)S(1)}, bf16[64,256]{1,0:T(8,128)(2,1)S(1)}, u32[]{:S(2)}, u32[]{:S(2)}) collective-permute-start(bf16[64,256]{1,0:T(8,128)(2,1)S(1)} %get-tuple-element.14), channel_id=1, source_target_pairs={{0,4},{4,8},{8,12},{12,16},{16,20},{20,24},{24,28},{1,5},{5,9},{9,... | collective-permute-start | bytes 98312 | tf_op jit(solution)/shard_map/ppermute | solution.py:412
  61.5 7.4 %copy-start = (bf16[256,2048]{1,0:T(8,128)(2,1)S(1)}, bf16[256,2048]{1,0:T(8,128)(2,1)}, u32[]{:S(2)}) copy-start(bf16[256,2048]{1,0:T(8,128)(2,1)} %get-tuple-element.16.own_ref) | copy-start | bytes 3145732
  64.8 3.0 %collective-permute-start.2 = (bf16[256,256]{1,0:T(8,128)(2,1)S(1)}, bf16[256,256]{1,0:T(8,128)(2,1)S(1)}, u32[]{:S(2)}, u32[]{:S(2)}) collective-permute-start(bf16[256,256]{1,0:T(8,128)(2,1)S(1)} %shard_map.98.one_ref), channel_id=1, source_target_pairs={{0,1},{1,0},{2,3},{3,2},{4,5},{5,4},{6,7},{7,6},{8,9},{9,8},{10,11... | collective-permute-start | bytes 393224 | tf_op jit(solution)/shard_map/ppermute | solution.py:414
  66.5 4.6 %collective-permute-start.4 = (bf16[256,128]{1,0:T(8,128)(2,1)}, bf16[256,128]{1,0:T(8,128)(2,1)S(1)}, u32[]{:S(2)}, u32[]{:S(2)}) collective-permute-start(bf16[256,128]{1,0:T(8,128)(2,1)} %get-tuple-element.20), channel_id=1, source_target_pairs={{0,4},{4,0},{8,12},{12,8},{16,20},{20,16},{24,28},{28,24},{1,5},{5... | collective-permute-start | bytes 196616 | tf_op jit(solution)/shard_map/ppermute | solution.py:405
  66.5 4.6 %copy-start.2 = (bf16[256,128]{1,0:T(8,128)(2,1)S(1)}, bf16[256,128]{1,0:T(8,128)(2,1)}, u32[]{:S(2)}) copy-start(bf16[256,128]{1,0:T(8,128)(2,1)} %get-tuple-element.19.mine_ref) | copy-start | bytes 196612
  66.5 12.1 %collective-permute-start.6 = (bf16[256,256]{1,0:T(8,128)(2,1)S(1)}, bf16[256,256]{1,0:T(8,128)(2,1)S(1)}, u32[]{:S(2)}, u32[]{:S(2)}) collective-permute-start(bf16[256,256]{1,0:T(8,128)(2,1)S(1)} %shard_map.98.one_ref), channel_id=1, source_target_pairs={{0,2},{1,3},{2,0},{3,1},{4,6},{5,7},{6,4},{7,5},{8,10},{9,11},{10,... | collective-permute-start | bytes 393224 | tf_op jit(solution)/shard_map/ppermute | solution.py:414
  67.8 10.8 %collective-permute-start.7 = (bf16[256,256]{1,0:T(8,128)(2,1)S(1)}, bf16[256,256]{1,0:T(8,128)(2,1)S(1)}, u32[]{:S(2)}, u32[]{:S(2)}) collective-permute-start(bf16[256,256]{1,0:T(8,128)(2,1)S(1)} %shard_map.98.one_ref), channel_id=1, source_target_pairs={{0,3},{1,2},{2,1},{3,0},{4,7},{5,6},{6,5},{7,4},{8,11},{9,10},{10,... | collective-permute-start | bytes 393224 | tf_op jit(solution)/shard_map/ppermute | solution.py:414
  77.5 4.1 %collective-permute-start.5 = (bf16[256,128]{1,0:T(8,128)(2,1)S(1)}, bf16[256,128]{1,0:T(8,128)(2,1)S(1)}, u32[]{:S(2)}, u32[]{:S(2)}) collective-permute-start(bf16[256,128]{1,0:T(8,128)(2,1)S(1)} %get-tuple-element.22), channel_id=1, source_target_pairs={{0,4},{4,0},{8,12},{12,8},{16,20},{20,16},{24,28},{28,24},{1,5},{5... | collective-permute-start | bytes 196616 | tf_op jit(solution)/shard_map/ppermute | solution.py:418

commit v12 on v11

--- a/solution.py
+++ b/solution.py
@@ -74,69 +74,123 @@
     )(side, tp, *sources, *before)
 
 
-def arrange_kernel(slot_ref, keys_ref, values_ref, own_keys, own_values, out_ref, *refs):
-    held_ref, own_ref, sems = refs
+def keys_kernel(keys_ref, values_ref, out_ref, held_ref, sems):
+    owners = out_ref.shape[0]
+    copies = []
+    for head in range(2):
+        for half, source in enumerate((keys_ref, values_ref)):
+            copies.append(
+                pltpu.make_async_copy(
+                    source.at[:, pl.ds(head * HD, HD)],
+                    held_ref.at[head, :, pl.ds(half * HD, HD)],
+                    sems.at[2 * head + half],
+                )
+            )
+    for copy in copies:
+        copy.start()
+    outs = []
+    for head in range(2):
+        copies[2 * head].wait()
+        copies[2 * head + 1].wait()
+        for owner in range(head, owners, 2):
+            outs.append(
+                pltpu.make_async_copy(held_ref.at[head], out_ref.at[owner], sems.at[4 + owner])
+            )
+            outs[-1].start()
+    for out in outs:
+        out.wait()
+
+
+def spread_keys(keys, values, owners):
+    rows = keys.shape[0]
+    return pl.pallas_call(
+        keys_kernel,
+        out_shape=jax.ShapeDtypeStruct((owners, rows, 2 * HD), keys.dtype),
+        in_specs=[ANY, ANY],
+        out_specs=ANY,
+        scratch_shapes=[
+            pltpu.VMEM((2, rows, 2 * HD), keys.dtype),
+            pltpu.SemaphoreType.DMA((4 + owners,)),
+        ],
+        cost_estimate=takes(2),
+    )(keys, values)
+
+
+def arrange_kernel(slot_ref, keys_ref, values_ref, out_ref, held_ref, sems):
     count, length, width = keys_ref.shape
-    indices = out_ref.shape[0]
-    rows = own_keys.shape[0]
-    front = 2 * length + LEAD
     owners = [slot_ref[n] // count for n in range(count)]
-    at = 0
     copies = []
     for n, owner in enumerate(owners):
         for half, source in enumerate((keys_ref, values_ref)):
             target = held_ref.at[owner, pl.ds(half * length, length)]
-            copies.append(pltpu.make_async_copy(source.at[n], target, sems.at[at]))
-            at += 1
-    for head in range(2):
-        for half, source in enumerate((own_keys, own_values)):
-            piece = source.at[:, pl.ds(head * HD, HD)]
-            target = own_ref.at[head, :, pl.ds(half * HD, HD)]
-            copies.append(pltpu.make_async_copy(piece, target, sems.at[at]))
-            at += 1
+            copies.append(pltpu.make_async_copy(source.at[n], target, sems.at[2 * n + half]))
     for copy in copies:
         copy.start()
-    for index in range(indices):
-        held_ref[index, 2 * length :, :] = jnp.full((LEAD, width), -1, held_ref.dtype)
+    for owner in range(held_ref.shape[0]):
+        held_ref[owner, 2 * length :, :] = jnp.full((LEAD, width), -1, held_ref.dtype)
     for n, owner in enumerate(owners):
         place = (slot_ref[n] - owner * count).astype(jnp.float32)
         held_ref[owner, 2 * length :, :] = jnp.full((LEAD, width), place).astype(held_ref.dtype)
     outs = []
-    for head in range(2):
-        copies[2 * count + 2 * head].wait()
-        copies[2 * count + 2 * head + 1].wait()
-        for index in range(head, indices, 2):
-            target = out_ref.at[index, pl.ds(front, rows)]
-            outs.append(pltpu.make_async_copy(own_ref.at[head], target, sems.at[at]))
-            outs[-1].start()
-            at += 1
-    for copy in copies[: 2 * count]:
-        copy.wait()
-    for index in range(indices):
-        source, target = held_ref.at[index], out_ref.at[index, pl.ds(0, front)]
-        outs.append(pltpu.make_async_copy(source, target, sems.at[at]))
-        outs[-1].start()
-        at += 1
+    for n, owner in enumerate(owners):
+        copies[2 * n].wait()
+        copies[2 * n + 1].wait()
+        out = pltpu.make_async_copy(
+            held_ref.at[owner], out_ref.at[owner], sems.at[2 * count + n]
+        )
+        out.start()
+        outs.append(out)
     for out in outs:
         out.wait()
 
 
-def arrange(slots, keys, values, own_keys, own_values, indices):
+def unheld_kernel(slot_ref, keys_ref, values_ref, out_ref, held_ref, sems):
+    arrange_kernel(slot_ref, keys_ref, values_ref, out_ref, held_ref, sems)
+    count, length = keys_ref.shape[:2]
+    for owner in range(out_ref.shape[0]):
+        taken = slot_ref[0] // count == owner
+        for n in range(1, count):
+            taken = taken | (slot_ref[n] // count == owner)
+
+        @pl.when(jnp.logical_not(taken))
+        def _():
+            rows = pl.ds(2 * length, LEAD)
+            copy = pltpu.make_async_copy(
+                held_ref.at[owner, rows], out_ref.at[owner, rows], sems.at[0]
+            )
+            copy.start()
+            copy.wait()
+
+
+def arrange(slots, keys, values, owners):
     count, length, width = keys.shape
-    rows = own_keys.shape[0]
-    front = 2 * length + LEAD
-    return pl.pallas_call(
-        arrange_kernel,
-        out_shape=jax.ShapeDtypeStruct((indices, front + rows, width), keys.dtype),
-        in_specs=[SMEM] + [ANY] * 4,
+    shape = (owners, 2 * length + LEAD, width)
+    return pl.pallas_call(
+        arrange_kernel if owners == count else unheld_kernel,
+        out_shape=jax.ShapeDtypeStruct(shape, keys.dtype),
+        in_specs=[SMEM, ANY, ANY],
         out_specs=ANY,
         scratch_shapes=[
-            pltpu.VMEM((indices, front, width), keys.dtype),
-            pltpu.VMEM((2, rows, 2 * HD), keys.dtype),
-            pltpu.SemaphoreType.DMA((2 * count + 4 + 2 * indices,)),
+            pltpu.VMEM(shape, keys.dtype),
+            pltpu.SemaphoreType.DMA((3 * count,)),
         ],
-        cost_estimate=takes(4),
-    )(slots, keys, values, own_keys, own_values)
+        cost_estimate=takes(3),
+    )(slots, keys, values)
+
+
+def fence_kernel(held_ref, *refs):
+    refs[-1][0] = 0
+
+
+def fence(held, before):
+    return pl.pallas_call(
+        fence_kernel,
+        out_shape=jax.ShapeDtypeStruct(held.shape, held.dtype),
+        in_specs=[ANY] * (1 + len(before)),
+        out_specs=ANY,
+        scratch_shapes=[pltpu.SMEM((1,), jnp.int32)],
+        input_output_aliases={0: 0},
+    )(held, *before)
 
 
 def find_sources(incoming_ref, order_ref, length):
@@ -166,7 +220,7 @@
 def last_kernel(queries_ref, spill_ref, incoming_ref, *refs):
     tail_ref, next_ref, order_ref = refs[-3:]
     rows, width = queries_ref.shape
-    length = (incoming_ref.shape[1] - LEAD - rows) // 2
+    length = (incoming_ref.shape[1] - LEAD) // 2
     find_sources(incoming_ref, order_ref, length)
     last = rows // BLOCK - 1
     for head in range(width // HD):
@@ -179,7 +233,7 @@
 
 def other_kernel(queries_ref, tail_ref, incoming_ref, out_ref, order_ref):
     rows, width = queries_ref.shape
-    length = (incoming_ref.shape[1] - LEAD - rows) // 2
+    length = (incoming_ref.shape[1] - LEAD) // 2
     find_sources(incoming_ref, order_ref, length)
     blocks = rows // BLOCK
     row = lax.broadcasted_iota(jnp.int32, (LEAD, HD), 0)
@@ -249,16 +303,15 @@
     )(back, answers)
 
 
-def self_kernel(pair_ref, side_ref, mark_ref, mine_ref, other_ref, incoming_ref, *refs):
+def self_kernel(pair_ref, side_ref, mine_ref, other_ref, kv_ref, *refs):
     ours_ref, theirs_ref, peak_ref, total_ref, accum_ref = refs[-5:]
     pair, side = pair_ref[0], side_ref[0]
     tile = mine_ref.shape[0]
     rows = 2 * tile
-    front = incoming_ref.shape[1] - tile
     chunk = min(128, tile)
 
     def attend(at, fresh):
-        kv = incoming_ref[pl.ds(2 * at, 2), front:, :].reshape(rows, 2 * HD)
+        kv = kv_ref[pl.ds(2 * at, 2)].reshape(rows, 2 * HD)
         for start in range(0, rows, chunk):
             here = slice(start, start + chunk)
             q_ref, offset = (mine_ref, start) if start < tile else (other_ref, start - tile)
@@ -296,21 +349,20 @@
     theirs_ref[...] = result[tile:]
 
 
-def self_attend(pair, side, mark, mine, other, incoming):
+def self_attend(pair, side, mine, other, kv):
     tile = mine.shape[0]
     return pl.pallas_call(
         self_kernel,
         out_shape=(jax.ShapeDtypeStruct((tile, HD), jnp.bfloat16),) * 2,
-        in_specs=[SMEM] * 3 + [VMEM] * 3,
+        in_specs=[SMEM] * 2 + [VMEM] * 3,
         out_specs=(VMEM, VMEM),
         scratch_shapes=[pltpu.VMEM((2 * tile, HD), jnp.float32)] * 3,
         compiler_params=PARAMS,
         cost_estimate=takes(6),
-    )(pair, side, mark, mine, other, incoming)
-
-
-def near_kernel(one_ref, two_ref, own_ref, beside_ref, partial_ref, mark_ref):
-    mark_ref[0] = 0
+    )(pair, side, mine, other, kv)
+
+
+def near_kernel(one_ref, two_ref, own_ref, beside_ref, partial_ref):
     width = partial_ref.shape[1]
     term = jnp.concatenate([one_ref[...], two_ref[...]], axis=1)
     tile = min(512, width)
@@ -324,39 +376,41 @@
 def project_near(terms, own, beside):
     return pl.pallas_call(
         near_kernel,
-        out_shape=(
-            jax.ShapeDtypeStruct((terms[0].shape[0], own.shape[1]), jnp.float32),
-            jax.ShapeDtypeStruct((1,), jnp.int32),
-        ),
+        out_shape=jax.ShapeDtypeStruct((terms[0].shape[0], own.shape[1]), jnp.float32),
         in_specs=[VMEM] * 4,
-        out_specs=(VMEM, SMEM),
+        out_specs=VMEM,
         compiler_params=PARAMS,
     )(*terms, own, beside)
 
 
 def far_kernel(count, partial_ref, *refs):
     crossed_ref, out_ref, sems = refs[-3:]
-    terms, direct = refs[:count], refs[count : 2 * count]
-    width = crossed_ref.shape[1]
-    tile = min(512, width)
+    terms, refs = refs[:count], refs[count:-3]
+    parts = [refs[at : at + count] for at in range(0, len(refs), count)]
     term = jnp.concatenate([held[...] for held in terms], axis=1)
     outs = []
-    for column in range(0, width, tile):
-        at = slice(column, column + tile)
-        total = dot(term, jnp.concatenate([block[:, at] for block in direct], axis=0))
-        out_ref[:, at] = (partial_ref[:, at] + total).astype(out_ref.dtype)
-        out = pltpu.make_async_copy(
-            out_ref.at[:, at], crossed_ref.at[:, at], sems.at[len(outs)]
-        )
-        out.start()
-        outs.append(out)
+    column = 0
+    for blocks in parts:
+        width = blocks[0].shape[1]
+        tile = min(512, width) if width % 512 == 0 else HD * math.gcd(width // HD, 4)
+        for start in range(0, width, tile):
+            weight = [block[:, start : start + tile] for block in blocks]
+            total = dot(term, jnp.concatenate(weight, axis=0))
+            at = slice(column, column + tile)
+            out_ref[:, at] = (partial_ref[:, at] + total).astype(out_ref.dtype)
+            out = pltpu.make_async_copy(
+                out_ref.at[:, at], crossed_ref.at[:, at], sems.at[len(outs)]
+            )
+            out.start()
+            outs.append(out)
+            column += tile
     for out in outs:
         out.wait()
 
 
-def project_far(partial, terms, direct):
+def project_far(partial, terms, parts):
     rows, width = partial.shape
-    operands = (*terms, *direct)
+    operands = (*terms, *(block for blocks in parts for block in blocks))
     return pl.pallas_call(
         functools.partial(far_kernel, len(terms)),
         out_shape=jax.ShapeDtypeStruct((rows, width), jnp.bfloat16),
@@ -364,7 +418,7 @@
         out_specs=ANY,
         scratch_shapes=[
             pltpu.VMEM((rows, width), jnp.bfloat16),
-            pltpu.SemaphoreType.DMA((width // min(512, width),)),
+            pltpu.SemaphoreType.DMA((width // HD,)),
         ],
         compiler_params=PARAMS,
         cost_estimate=takes(2),
@@ -396,27 +450,38 @@
     def exchange(value):
         return lax.all_to_all(value, "ctx", split_axis=0, concat_axis=0, tiled=True)
 
-    incoming = exchange(arrange(nbr_slot, nbr_keys, nbr_values, keys, values, count))
-    q_mine, q_away, own, *blocks = cut(
+    kv = exchange(spread_keys(keys, values, count))
+    first = max(HD, width * 3 // 8 // HD * HD)
+    far = range(2, groups)
+    q_mine, q_away, *blocks = cut(
         side, tp, (queries, w_cross),
         [[(0, turn, 0, 0, HD, rows)] for turn in range(2)]
-        + [[(1, step, width, 0, width, depth)] for step in range(groups)],
+        + [[(1, step, width, 0, first, depth)] for step in far],
     )
+    early = [lax.ppermute(block, "tp", across[step]) for step, block in zip(far, blocks)]
     q_other = lax.ppermute(q_away, "ctx", swap)
-    beside, *direct = [
-        lax.ppermute(block, "tp", across[step]) for step, block in enumerate(blocks, 1)
-    ]
+    own, beside, *blocks = cut(
+        side, tp, (w_cross,),
+        [[(0, step, width, 0, width, depth)] for step in range(2)]
+        + [[(0, step, width, first, width - first, depth)] for step in far],
+        (q_away,),
+    )
+    beside = lax.ppermute(beside, "tp", across[1])
+    late = [lax.ppermute(block, "tp", across[step]) for step, block in zip(far, blocks)]
     spill = lax.ppermute(cross_queries[:BLOCK], "ctx", [(i + 1, i) for i in range(count - 1)])
+    outgoing = arrange(nbr_slot, nbr_keys, nbr_values, count)
+    incoming = exchange(fence(outgoing, (q_other, own, *early)))
+
+    ours, theirs = self_attend(pair, side, q_mine, q_other, kv)
+    attended = both(ours, lax.ppermute(theirs, "ctx", swap), 1)
 
     tail, onward = last_attend(cross_queries, spill, incoming)
     back = lax.ppermute(onward, "ctx", [(i, i + 1) for i in range(count - 1)])
     cca = merge(back, other_attend(cross_queries, tail, incoming))
     terms = [cca] + [lax.ppermute(cca, "tp", across[step]) for step in range(1, groups)]
-    partial, mark = project_near(terms[:2], own, beside)
-
-    ours, theirs = self_attend(pair, side, mark, q_mine, q_other, incoming)
-    attended = both(ours, lax.ppermute(theirs, "ctx", swap), 1)
-    crossed = project_far(partial, terms[2:], direct)
+    partial = project_near(terms[:2], own, beside)
+
+    crossed = project_far(partial, terms[2:], (early, late))
     return (attended, crossed)
 
 

time: 82.7 us -> 84.8 us (1.025)
  the two profiles are of different devices: /device:TPU:25 before, /device:TPU:0 now
where the time goes in v12:
time: 84.8 us; the launch traced here: 84.2 us
  waiting for transfers between devices  35.8 us (42%)
  starting transfers between devices  25.3 us (30%)
  Pallas kernels  18.4 us (22%)
  local copies, waits for them, and re-layouts  2.25 us (3%)
  other arithmetic  1.6 us (2%)
    all_to_all x2, waiting for transfers between devices, exchange(): return lax.all_to_all(value, 'ctx', split_axis=0, concat_axis=0, tiled=True)  21.7 us
    all_to_all x2, starting transfers between devices, exchange(): return lax.all_to_all(value, 'ctx', split_axis=0, concat_axis=0, tiled=True)  10.9 us
    ppermute x4, waiting for transfers between devices, shards(): lax.ppermute(block, 'tp', across[step])  9.71 us
    pallas_call x2, Pallas kernels, cut(): pl.pallas_call(functools.partial(cut_kernel, plan), out_shape=tuple(shape...  5.86 us
    ppermute x3, waiting for transfers between devices, shards(): lax.ppermute(cca, 'tp', across[step])  4.03 us
    ppermute x4, starting transfers between devices, shards(): lax.ppermute(block, 'tp', across[step])  3.4 us
    ppermute x1, starting transfers between devices, shards(): back = lax.ppermute(onward, 'ctx', [(i, i + 1) for i in range(count - 1)])  2.97 us
    pallas_call x1, Pallas kernels, project_far(): pl.pallas_call(functools.partial(far_kernel, len(terms)), out_shape=jax.S...  2.88 us
  transfers between devices with their start and end apart: 14, of which 7 were waited for; matrix products, arithmetic and copies ran while one was open for 3% of the time, Pallas kernels for 16%

profile of v12, /device:TPU:0, one launch (start us, length us, event | category | flops | bytes accessed | tf_op | source)
XLA Modules:
  0.0 84.2 jit_solution(8390073133582002301)
XLA Ops:
  0.6 1.9 %shard_map.96 = bf16[8,256,256]{2,1,0:T(8,128)(2,1)} custom-call(bf16[256,256]{1,0:T(8,128)(2,1)} %keys_ref.2, bf16[256,256]{1,0:T(8,128)(2,1)} %values_ref.2), custom_call_target="tpu_custom_call" | custom-call | flops 2000000000 | tf_op jit(solution)/shard_map/pallas_call | solution.py:106
  2.6 7.3 %all-to-all-start = ((bf16[8,256,256]{2,1,0:T(8,128)(2,1)}), bf16[8,256,256]{2,1,0:T(8,128)(2,1)S(1)}, u32[]{:S(2)}, u32[]{:S(2)}) async-start(bf16[8,256,256]{2,1,0:T(8,128)(2,1)} %shard_map.96), calls=%async_computation | async-start | bytes 2097152 | tf_op jit(solution)/shard_map/all_to_all | solution.py:451
  9.9 2.1 %shard_map.95 = (bf16[256,128]{1,0:T(8,128)(2,1)}, bf16[256,128]{1,0:T(8,128)(2,1)}, bf16[256,768]{1,0:T(8,128)(2,1)}, bf16[256,768]{1,0:T(8,128)(2,1)}) custom-call(s32[1]{0:T(128)} %bitcast.1.side_ref, s32[1]{0:T(128)} %bitcast.2.tp_ref, bf16[256,256]{1,0:T(8,128)(2,1)} %refs_0_.2, bf16[256,8192]{1,0:T(8,128)(2,1)} %refs_0_.3), custom_call_target="tpu_custom_call" | custom-call | flops 2000000000 | tf_op jit(solution)/shard_map/pallas_call | solution.py:67
  12.0 2.1 %collective-permute-start = (bf16[256,128]{1,0:T(8,128)(2,1)}, bf16[256,128]{1,0:T(8,128)(2,1)S(1)}, u32[]{:S(2)}, u32[]{:S(2)}) collective-permute-start(bf16[256,128]{1,0:T(8,128)(2,1)} %get-tuple-element.15.refs_1_), channel_id=1, source_target_pairs={{0,4},{4,0},{8,12},{12,8},{16,20},{20,16},{24,28},{28,24},{1,5},{5... | collective-permute-start | bytes 196616 | tf_op jit(solution)/shard_map/ppermute | solution.py:462
  14.1 1.5 %collective-permute-start.3 = (bf16[256,768]{1,0:T(8,128)(2,1)}, bf16[256,768]{1,0:T(8,128)(2,1)S(1)}, u32[]{:S(2)}, u32[]{:S(2)}) collective-permute-start(bf16[256,768]{1,0:T(8,128)(2,1)} %get-tuple-element.19), channel_id=1, source_target_pairs={{0,2},{1,3},{2,0},{3,1},{4,6},{5,7},{6,4},{7,5},{8,10},{9,11},{10,... | collective-permute-start | bytes 1179656 | tf_op jit(solution)/shard_map/ppermute | solution.py:461
  15.6 0.0 collective-permute-start.4
  15.6 2.8 %shard_map.98.held_ref = bf16[8,272,256]{2,1,0:T(8,128)(2,1)} custom-call(s32[8]{0:T(128)} %slot_ref.1, bf16[8,128,256]{2,1,0:T(8,128)(2,1)} %keys_ref.3, bf16[8,128,256]{2,1,0:T(8,128)(2,1)} %values_ref.3), custom_call_target="tpu_custom_call" | custom-call | flops 3000000000 | tf_op jit(solution)/shard_map/pallas_call | solution.py:168
  18.4 3.7 %shard_map.99 = (bf16[256,2048]{1,0:T(8,128)(2,1)}, bf16[256,2048]{1,0:T(8,128)(2,1)}, bf16[256,1280]{1,0:T(8,128)(2,1)}, bf16[256,1280]{1,0:T(8,128)(2,1)}) custom-call(s32[1]{0:T(128)} %bitcast.1.side_ref, s32[1]{0:T(128)} %bitcast.2.tp_ref, bf16[256,8192]{1,0:T(8,128)(2,1)} %refs_0_.3, bf16[256,128]{1,0:T(8,128)(2,1)} %get-tuple-element.15.refs_1_), custom_call_target="tpu_custom_call" | custom-call | flops 2000000000 | tf_op jit(solution)/shard_map/pallas_call | solution.py:67
  22.1 0.0 collective-permute-done.other_ref.refs_0_
  22.1 0.0 copy-start.5
  22.2 4.2 %collective-permute-done.3.refs_2_ = bf16[256,768]{1,0:T(8,128)(2,1)S(1)} collective-permute-done((bf16[256,768]{1,0:T(8,128)(2,1)}, bf16[256,768]{1,0:T(8,128)(2,1)S(1)}, u32[]{:S(2)}, u32[]{:S(2)}) %collective-permute-start.3) | collective-permute-done | bytes 393248 | tf_op jit(solution)/shard_map/ppermute | solution.py:461
  26.4 0.0 copy-start.1
  26.4 5.5 %collective-permute-done.4.refs_3_ = bf16[256,768]{1,0:T(8,128)(2,1)S(1)} collective-permute-done((bf16[256,768]{1,0:T(8,128)(2,1)}, bf16[256,768]{1,0:T(8,128)(2,1)S(1)}, u32[]{:S(2)}, u32[]{:S(2)}) %collective-permute-start.4) | collective-permute-done | bytes 393248 | tf_op jit(solution)/shard_map/ppermute | solution.py:461
  31.9 0.0 copy-start.3
  31.9 0.0 copy-done.5
  31.9 0.0 copy-done.1
  31.9 0.8 copy-done.3
  32.6 0.0 copy-start.7
  32.6 0.0 copy-start.6
  32.6 3.0 %all-to-all-done.kv_ref = bf16[8,256,256]{2,1,0:T(8,128)(2,1)S(1)} async-done(((bf16[8,256,256]{2,1,0:T(8,128)(2,1)}), bf16[8,256,256]{2,1,0:T(8,128)(2,1)S(1)}, u32[]{:S(2)}, u32[]{:S(2)}) %all-to-all-start) | async-done | bytes 1048608 | tf_op jit(solution)/shard_map/all_to_all | solution.py:451
  35.6 3.6 %all-to-all-start.1 = ((bf16[8,272,256]{2,1,0:T(8,128)(2,1)}), bf16[8,272,256]{2,1,0:T(8,128)(2,1)S(1)}, u32[]{:S(2)}, u32[]{:S(2)}) async-start(bf16[8,272,256]{2,1,0:T(8,128)(2,1)} %shard_map.100), calls=%async_computation.1 | async-start | bytes 2228224 | tf_op jit(solution)/shard_map/all_to_all | solution.py:451
  39.2 0.1 collective-permute-start.7
  39.3 0.0 copy-done.7
  39.3 0.6 slice.3
  39.9 1.3 %collective-permute-start.2 = (bf16[64,256]{1,0:T(8,128)(2,1)}, bf16[64,256]{1,0:T(8,128)(2,1)}, u32[]{:S(2)}, u32[]{:S(2)}) collective-permute-start(bf16[64,256]{1,0:T(8,128)(2,1)} %slice.3), channel_id=1, source_target_pairs={{4,0},{8,4},{12,8},{16,12},{20,16},{24,20},{28,24},{5,1},{9,5},{13... | collective-permute-start | bytes 98312 | tf_op jit(solution)/shard_map/ppermute | solution.py:471
  41.2 1.6 %collective-permute-start.10 = (bf16[256,1280]{1,0:T(8,128)(2,1)}, bf16[256,1280]{1,0:T(8,128)(2,1)}, u32[]{:S(2)}, u32[]{:S(2)}) collective-permute-start(bf16[256,1280]{1,0:T(8,128)(2,1)} %get-tuple-element.24), channel_id=1, source_target_pairs={{0,2},{1,3},{2,0},{3,1},{4,6},{5,7},{6,4},{7,5},{8,10},{9,11},{10,... | collective-permute-start | bytes 1966088 | tf_op jit(solution)/shard_map/ppermute | solution.py:470
  42.8 0.3 collective-permute-start.11
  43.1 0.0 copy-done.6
  43.1 0.0 copy-start.8
  43.1 0.8 copy-done.8
  43.9 1.2 %shard_map.97 = (bf16[256,128]{1,0:T(8,128)(2,1)S(1)}, bf16[256,128]{1,0:T(8,128)(2,1)S(1)}) custom-call(s32[1]{0:T(128)} %bitcast.pair_ref, s32[1]{0:T(128)} %bitcast.1.side_ref, bf16[256,128]{1,0:T(8,128)(2,1)S(1)} %copy-done.8, bf16[256,128]{1,0:T(8,128)(2,1)S(1)} %copy-done.6, bf16[8,256,256]{2,1,0:T(8,128)(2,1)S(1)} %all-to-all-done.kv_ref), custom_call_target="tpu_custom_call" | custom-call | flops 6000000000 | tf_op jit(solution)/shard_map/pallas_call | solution.py:354
  45.2 2.7 %collective-permute-start.1 = (bf16[256,128]{1,0:T(8,128)(2,1)S(1)}, bf16[256,128]{1,0:T(8,128)(2,1)}, u32[]{:S(2)}, u32[]{:S(2)}) collective-permute-start(bf16[256,128]{1,0:T(8,128)(2,1)S(1)} %get-tuple-element.17), channel_id=1, source_target_pairs={{0,4},{4,0},{8,12},{12,8},{16,20},{20,16},{24,28},{28,24},{1,5},{5... | collective-permute-start | bytes 196616 | tf_op jit(solution)/shard_map/ppermute | solution.py:476
  47.8 0.4 collective-permute-done.2.spill_ref
  48.3 18.7 %all-to-all-done.1.incoming_ref = bf16[8,272,256]{2,1,0:T(8,128)(2,1)S(1)} async-done(((bf16[8,272,256]{2,1,0:T(8,128)(2,1)}), bf16[8,272,256]{2,1,0:T(8,128)(2,1)S(1)}, u32[]{:S(2)}, u32[]{:S(2)}) %all-to-all-start.1) | async-done | bytes 1114144 | tf_op jit(solution)/shard_map/all_to_all | solution.py:451
  66.9 1.4 %shard_map.101 = (bf16[16,256]{1,0:T(8,128)(2,1)S(1)}, bf16[64,256]{1,0:T(8,128)(2,1)S(1)}) custom-call(bf16[256,256]{1,0:T(8,128)(2,1)S(1)} %copy-done.7, bf16[64,256]{1,0:T(8,128)(2,1)} %collective-permute-done.2.spill_ref, bf16[8,272,256]{2,1,0:T(8,128)(2,1)S(1)} %all-to-all-done.1.incoming_ref), custom_call_target="tpu_custom_call" | custom-call | flops 1000000000 | tf_op jit(solution)/shard_map/pallas_call | solution.py:264
  68.3 3.0 %collective-permute-start.5 = (bf16[64,256]{1,0:T(8,128)(2,1)S(1)}, bf16[64,256]{1,0:T(8,128)(2,1)S(1)}, u32[]{:S(2)}, u32[]{:S(2)}) collective-permute-start(bf16[64,256]{1,0:T(8,128)(2,1)S(1)} %get-tuple-element.21), channel_id=1, source_target_pairs={{0,4},{4,8},{8,12},{12,16},{16,20},{20,24},{24,28},{1,5},{5,9},{9,... | collective-permute-start | bytes 98312 | tf_op jit(solution)/shard_map/ppermute | solution.py:479
  71.3 0.0 copy-start
  71.3 1.6 %shard_map.102.answers_ref = bf16[256,256]{1,0:T(8,128)(2,1)S(1)} custom-call(bf16[256,256]{1,0:T(8,128)(2,1)S(1)} %copy-done.7, bf16[16,256]{1,0:T(8,128)(2,1)S(1)} %get-tuple-element.22.tail_ref, bf16[8,272,256]{2,1,0:T(8,128)(2,1)S(1)} %all-to-all-done.1.incoming_ref), custom_call_target="tpu_custom_call" | custom-call | flops 2000000000 | tf_op jit(solution)/shard_map/pallas_call | solution.py:279
  72.9 0.0 collective-permute-done.5.back_ref
  73.0 0.1 collective-permute-start.6
  73.0 0.0 collective-permute-done.7.beside_ref
  73.1 1.6 %collective-permute-start.8 = (bf16[256,256]{1,0:T(8,128)(2,1)S(1)}, bf16[256,256]{1,0:T(8,128)(2,1)S(1)}, u32[]{:S(2)}, u32[]{:S(2)}) collective-permute-start(bf16[256,256]{1,0:T(8,128)(2,1)S(1)} %shard_map.103.one_ref), channel_id=1, source_target_pairs={{0,2},{1,3},{2,0},{3,1},{4,6},{5,7},{6,4},{7,5},{8,10},{9,11},{10,... | collective-permute-start | bytes 393224 | tf_op jit(solution)/shard_map/ppermute | solution.py:481
  74.6 0.0 collective-permute-done.1
  74.6 0.3 collective-permute-start.9
  74.9 1.6 %maximum_select_fusion = bf16[256,256]{1,0:T(8,128)(2,1)} fusion(bf16[256,128]{1,0:T(8,128)(2,1)} %collective-permute-done.1, bf16[256,128]{1,0:T(8,128)(2,1)S(1)} %get-tuple-element.16, pred[]{:T(512)S(6)} %eq.3), kind=kLoop, calls=%fused_computation | loop fusion | flops 589824 | bytes 262145 | tf_op jit(solution)/shard_map/jit(_where)/select_n | solution.py:444
  76.5 0.0 copy-start.2
  76.5 0.0 copy-start.4
  76.5 0.0 collective-permute-done.6.two_ref
  76.5 0.0 copy-done
  76.5 0.7 shard_map.104.partial_ref
  77.3 0.0 collective-permute-done.10.refs_4_
  77.3 0.0 collective-permute-done.11.refs_5_
  77.3 2.2 %collective-permute-done.8.refs_0_ = bf16[256,256]{1,0:T(8,128)(2,1)S(1)} collective-permute-done((bf16[256,256]{1,0:T(8,128)(2,1)S(1)}, bf16[256,256]{1,0:T(8,128)(2,1)S(1)}, u32[]{:S(2)}, u32[]{:S(2)}) %collective-permute-start.8) | collective-permute-done | bytes 131104 | tf_op jit(solution)/shard_map/ppermute | solution.py:481
  79.4 1.9 %collective-permute-done.9.refs_1_ = bf16[256,256]{1,0:T(8,128)(2,1)S(1)} collective-permute-done((bf16[256,256]{1,0:T(8,128)(2,1)S(1)}, bf16[256,256]{1,0:T(8,128)(2,1)S(1)}, u32[]{:S(2)}, u32[]{:S(2)}) %collective-permute-start.9) | collective-permute-done | bytes 131104 | tf_op jit(solution)/shard_map/ppermute | solution.py:481
  81.3 0.0 copy-done.2
  81.3 0.0 copy-done.4
  81.3 2.9 %shard_map.105 = bf16[256,2048]{1,0:T(8,128)(2,1)} custom-call(f32[256,2048]{1,0:T(8,128)S(1)} %shard_map.104.partial_ref, bf16[256,256]{1,0:T(8,128)(2,1)S(1)} %collective-permute-done.8.refs_0_, bf16[256,256]{1,0:T(8,128)(2,1)S(1)} %collective-permute-done.9.refs_1_, bf16[256,768]{1,0:T(8,128)(2,1)S(1)} %copy-done.2, bf16[256,768]{1,0:T(8,128)(2,1)S(1)} %copy-done.4, ...), custom_call_target="tpu_custom_call" | custom-call | flops 2000000000 | tf_op jit(solution)/shard_map/pallas_call | solution.py:414
  (2 shorter events, 0.0 us)
Async XLA Ops:
  2.6 33.1 %all-to-all-start = ((bf16[8,256,256]{2,1,0:T(8,128)(2,1)}), bf16[8,256,256]{2,1,0:T(8,128)(2,1)S(1)}, u32[]{:S(2)}, u32[]{:S(2)}) async-start(bf16[8,256,256]{2,1,0:T(8,128)(2,1)} %shard_map.96), calls=%async_computation | async-start | bytes 2097152 | tf_op jit(solution)/shard_map/all_to_all | solution.py:451
  12.0 10.1 %collective-permute-start = (bf16[256,128]{1,0:T(8,128)(2,1)}, bf16[256,128]{1,0:T(8,128)(2,1)S(1)}, u32[]{:S(2)}, u32[]{:S(2)}) collective-permute-start(bf16[256,128]{1,0:T(8,128)(2,1)} %get-tuple-element.15.refs_1_), channel_id=1, source_target_pairs={{0,4},{4,0},{8,12},{12,8},{16,20},{20,16},{24,28},{28,24},{1,5},{5... | collective-permute-start | bytes 196616 | tf_op jit(solution)/shard_map/ppermute | solution.py:462
  14.1 12.3 %collective-permute-start.3 = (bf16[256,768]{1,0:T(8,128)(2,1)}, bf16[256,768]{1,0:T(8,128)(2,1)S(1)}, u32[]{:S(2)}, u32[]{:S(2)}) collective-permute-start(bf16[256,768]{1,0:T(8,128)(2,1)} %get-tuple-element.19), channel_id=1, source_target_pairs={{0,2},{1,3},{2,0},{3,1},{4,6},{5,7},{6,4},{7,5},{8,10},{9,11},{10,... | collective-permute-start | bytes 1179656 | tf_op jit(solution)/shard_map/ppermute | solution.py:461
  15.6 16.3 %collective-permute-start.4 = (bf16[256,768]{1,0:T(8,128)(2,1)}, bf16[256,768]{1,0:T(8,128)(2,1)S(1)}, u32[]{:S(2)}, u32[]{:S(2)}) collective-permute-start(bf16[256,768]{1,0:T(8,128)(2,1)} %get-tuple-element.20), channel_id=1, source_target_pairs={{0,3},{1,2},{2,1},{3,0},{4,7},{5,6},{6,5},{7,4},{8,11},{9,10},{10,... | collective-permute-start | bytes 1179656 | tf_op jit(solution)/shard_map/ppermute | solution.py:461
  22.1 9.7 %copy-start.5 = (bf16[256,128]{1,0:T(8,128)(2,1)}, bf16[256,128]{1,0:T(8,128)(2,1)S(1)}, u32[]{:S(2)}) copy-start(bf16[256,128]{1,0:T(8,128)(2,1)S(1)} %collective-permute-done.other_ref.refs_0_) | copy-start | bytes 196612
  26.4 5.5 %copy-start.1 = (bf16[256,768]{1,0:T(8,128)(2,1)}, bf16[256,768]{1,0:T(8,128)(2,1)S(1)}, u32[]{:S(2)}) copy-start(bf16[256,768]{1,0:T(8,128)(2,1)S(1)} %collective-permute-done.3.refs_2_) | copy-start | bytes 1179652
  31.9 0.8 copy-start.3
  32.6 6.7 %copy-start.7 = (bf16[256,256]{1,0:T(8,128)(2,1)S(1)}, bf16[256,256]{1,0:T(8,128)(2,1)}, u32[]{:S(2)}) copy-start(bf16[256,256]{1,0:T(8,128)(2,1)} %queries_ref.3) | copy-start | bytes 393220
  32.6 10.5 %copy-start.6 = (bf16[256,128]{1,0:T(8,128)(2,1)S(1)}, bf16[256,128]{1,0:T(8,128)(2,1)}, u32[]{:S(2)}) copy-start(bf16[256,128]{1,0:T(8,128)(2,1)} %copy-done.5) | copy-start | bytes 196612
  35.6 31.3 %all-to-all-start.1 = ((bf16[8,272,256]{2,1,0:T(8,128)(2,1)}), bf16[8,272,256]{2,1,0:T(8,128)(2,1)S(1)}, u32[]{:S(2)}, u32[]{:S(2)}) async-start(bf16[8,272,256]{2,1,0:T(8,128)(2,1)} %shard_map.100), calls=%async_computation.1 | async-start | bytes 2228224 | tf_op jit(solution)/shard_map/all_to_all | solution.py:451
  39.2 33.8 %collective-permute-start.7 = (bf16[256,2048]{1,0:T(8,128)(2,1)}, bf16[256,2048]{1,0:T(8,128)(2,1)S(1)}, u32[]{:S(2)}, u32[]{:S(2)}) collective-permute-start(bf16[256,2048]{1,0:T(8,128)(2,1)} %get-tuple-element.23), channel_id=1, source_target_pairs={{0,1},{1,0},{2,3},{3,2},{4,5},{5,4},{6,7},{7,6},{8,9},{9,8},{10,11... | collective-permute-start | bytes 3145736 | tf_op jit(solution)/shard_map/ppermute | solution.py:469
  39.9 8.3 %collective-permute-start.2 = (bf16[64,256]{1,0:T(8,128)(2,1)}, bf16[64,256]{1,0:T(8,128)(2,1)}, u32[]{:S(2)}, u32[]{:S(2)}) collective-permute-start(bf16[64,256]{1,0:T(8,128)(2,1)} %slice.3), channel_id=1, source_target_pairs={{4,0},{8,4},{12,8},{16,12},{20,16},{24,20},{28,24},{5,1},{9,5},{13... | collective-permute-start | bytes 98312 | tf_op jit(solution)/shard_map/ppermute | solution.py:471
  41.2 36.1 %collective-permute-start.10 = (bf16[256,1280]{1,0:T(8,128)(2,1)}, bf16[256,1280]{1,0:T(8,128)(2,1)}, u32[]{:S(2)}, u32[]{:S(2)}) collective-permute-start(bf16[256,1280]{1,0:T(8,128)(2,1)} %get-tuple-element.24), channel_id=1, source_target_pairs={{0,2},{1,3},{2,0},{3,1},{4,6},{5,7},{6,4},{7,5},{8,10},{9,11},{10,... | collective-permute-start | bytes 1966088 | tf_op jit(solution)/shard_map/ppermute | solution.py:470
  42.8 34.5 %collective-permute-start.11 = (bf16[256,1280]{1,0:T(8,128)(2,1)}, bf16[256,1280]{1,0:T(8,128)(2,1)}, u32[]{:S(2)}, u32[]{:S(2)}) collective-permute-start(bf16[256,1280]{1,0:T(8,128)(2,1)} %get-tuple-element.25), channel_id=1, source_target_pairs={{0,3},{1,2},{2,1},{3,0},{4,7},{5,6},{6,5},{7,4},{8,11},{9,10},{10,... | collective-permute-start | bytes 1966088 | tf_op jit(solution)/shard_map/ppermute | solution.py:470
  43.1 0.8 copy-start.8
  45.2 29.4 %collective-permute-start.1 = (bf16[256,128]{1,0:T(8,128)(2,1)S(1)}, bf16[256,128]{1,0:T(8,128)(2,1)}, u32[]{:S(2)}, u32[]{:S(2)}) collective-permute-start(bf16[256,128]{1,0:T(8,128)(2,1)S(1)} %get-tuple-element.17), channel_id=1, source_target_pairs={{0,4},{4,0},{8,12},{12,8},{16,20},{20,16},{24,28},{28,24},{1,5},{5... | collective-permute-start | bytes 196616 | tf_op jit(solution)/shard_map/ppermute | solution.py:476
  68.3 4.6 %collective-permute-start.5 = (bf16[64,256]{1,0:T(8,128)(2,1)S(1)}, bf16[64,256]{1,0:T(8,128)(2,1)S(1)}, u32[]{:S(2)}, u32[]{:S(2)}) collective-permute-start(bf16[64,256]{1,0:T(8,128)(2,1)S(1)} %get-tuple-element.21), channel_id=1, source_target_pairs={{0,4},{4,8},{8,12},{12,16},{16,20},{20,24},{24,28},{1,5},{5,9},{9,... | collective-permute-start | bytes 98312 | tf_op jit(solution)/shard_map/ppermute | solution.py:479
  71.3 5.3 %copy-start = (bf16[256,2048]{1,0:T(8,128)(2,1)S(1)}, bf16[256,2048]{1,0:T(8,128)(2,1)}, u32[]{:S(2)}) copy-start(bf16[256,2048]{1,0:T(8,128)(2,1)} %get-tuple-element.18.refs_1_.own_ref) | copy-start | bytes 3145732
  73.0 3.6 %collective-permute-start.6 = (bf16[256,256]{1,0:T(8,128)(2,1)S(1)}, bf16[256,256]{1,0:T(8,128)(2,1)S(1)}, u32[]{:S(2)}, u32[]{:S(2)}) collective-permute-start(bf16[256,256]{1,0:T(8,128)(2,1)S(1)} %shard_map.103.one_ref), channel_id=1, source_target_pairs={{0,1},{1,0},{2,3},{3,2},{4,5},{5,4},{6,7},{7,6},{8,9},{9,8},{10,11... | collective-permute-start | bytes 393224 | tf_op jit(solution)/shard_map/ppermute | solution.py:481
  73.1 6.4 %collective-permute-start.8 = (bf16[256,256]{1,0:T(8,128)(2,1)S(1)}, bf16[256,256]{1,0:T(8,128)(2,1)S(1)}, u32[]{:S(2)}, u32[]{:S(2)}) collective-permute-start(bf16[256,256]{1,0:T(8,128)(2,1)S(1)} %shard_map.103.one_ref), channel_id=1, source_target_pairs={{0,2},{1,3},{2,0},{3,1},{4,6},{5,7},{6,4},{7,5},{8,10},{9,11},{10,... | collective-permute-start | bytes 393224 | tf_op jit(solution)/shard_map/ppermute | solution.py:481
  74.6 6.7 %collective-permute-start.9 = (bf16[256,256]{1,0:T(8,128)(2,1)S(1)}, bf16[256,256]{1,0:T(8,128)(2,1)S(1)}, u32[]{:S(2)}, u32[]{:S(2)}) collective-permute-start(bf16[256,256]{1,0:T(8,128)(2,1)S(1)} %shard_map.103.one_ref), channel_id=1, source_target_pairs={{0,3},{1,2},{2,1},{3,0},{4,7},{5,6},{6,5},{7,4},{8,11},{9,10},{10,... | collective-permute-start | bytes 393224 | tf_op jit(solution)/shard_map/ppermute | solution.py:481
  76.5 4.8 %copy-start.2 = (bf16[256,768]{1,0:T(8,128)(2,1)S(1)}, bf16[256,768]{1,0:T(8,128)(2,1)}, u32[]{:S(2)}) copy-start(bf16[256,768]{1,0:T(8,128)(2,1)} %copy-done.1) | copy-start | bytes 1179652
  76.5 4.8 %copy-start.4 = (bf16[256,768]{1,0:T(8,128)(2,1)S(1)}, bf16[256,768]{1,0:T(8,128)(2,1)}, u32[]{:S(2)}) copy-start(bf16[256,768]{1,0:T(8,128)(2,1)} %copy-done.3) | copy-start | bytes 1179652

commit v13 on v12

--- a/solution.py
+++ b/solution.py
@@ -178,19 +178,19 @@
     )(slots, keys, values)
 
 
-def fence_kernel(held_ref, *refs):
-    refs[-1][0] = 0
-
-
-def fence(held, before):
+def fence_kernel(mark_ref, held_ref, *refs):
+    refs[-1][0] = mark_ref[0]
+
+
+def fence(held, mark, before):
     return pl.pallas_call(
         fence_kernel,
         out_shape=jax.ShapeDtypeStruct(held.shape, held.dtype),
-        in_specs=[ANY] * (1 + len(before)),
+        in_specs=[SMEM] + [ANY] * (1 + len(before)),
         out_specs=ANY,
         scratch_shapes=[pltpu.SMEM((1,), jnp.int32)],
-        input_output_aliases={0: 0},
-    )(held, *before)
+        input_output_aliases={1: 0},
+    )(mark, held, *before)
 
 
 def find_sources(incoming_ref, order_ref, length):
@@ -218,7 +218,8 @@
 
 
 def last_kernel(queries_ref, spill_ref, incoming_ref, *refs):
-    tail_ref, next_ref, order_ref = refs[-3:]
+    tail_ref, next_ref, mark_ref, order_ref = refs
+    mark_ref[0] = 0
     rows, width = queries_ref.shape
     length = (incoming_ref.shape[1] - LEAD) // 2
     find_sources(incoming_ref, order_ref, length)
@@ -266,9 +267,10 @@
         out_shape=(
             jax.ShapeDtypeStruct((LEAD, width), queries.dtype),
             jax.ShapeDtypeStruct((BLOCK, width), queries.dtype),
+            jax.ShapeDtypeStruct((1,), jnp.int32),
         ),
         in_specs=[VMEM] * 3,
-        out_specs=(VMEM, VMEM),
+        out_specs=(VMEM, VMEM, SMEM),
         scratch_shapes=order_scratch(rows),
         compiler_params=PARAMS,
         cost_estimate=takes(1),
@@ -362,7 +364,8 @@
     )(pair, side, mine, other, kv)
 
 
-def near_kernel(one_ref, two_ref, own_ref, beside_ref, partial_ref):
+def near_kernel(one_ref, two_ref, own_ref, beside_ref, *refs):
+    partial_ref = refs[-1]
     width = partial_ref.shape[1]
     term = jnp.concatenate([one_ref[...], two_ref[...]], axis=1)
     tile = min(512, width)
@@ -373,14 +376,14 @@
         )
 
 
-def project_near(terms, own, beside):
+def project_near(terms, own, beside, before):
     return pl.pallas_call(
         near_kernel,
         out_shape=jax.ShapeDtypeStruct((terms[0].shape[0], own.shape[1]), jnp.float32),
-        in_specs=[VMEM] * 4,
+        in_specs=[VMEM] * 4 + [ANY] * len(before),
         out_specs=VMEM,
         compiler_params=PARAMS,
-    )(*terms, own, beside)
+    )(*terms, own, beside, *before)
 
 
 def far_kernel(count, partial_ref, *refs):
@@ -450,8 +453,8 @@
     def exchange(value):
         return lax.all_to_all(value, "ctx", split_axis=0, concat_axis=0, tiled=True)
 
-    kv = exchange(spread_keys(keys, values, count))
-    first = max(HD, width * 3 // 8 // HD * HD)
+    incoming = exchange(arrange(nbr_slot, nbr_keys, nbr_values, count))
+    first = width // 2
     far = range(2, groups)
     q_mine, q_away, *blocks = cut(
         side, tp, (queries, w_cross),
@@ -469,19 +472,17 @@
     beside = lax.ppermute(beside, "tp", across[1])
     late = [lax.ppermute(block, "tp", across[step]) for step, block in zip(far, blocks)]
     spill = lax.ppermute(cross_queries[:BLOCK], "ctx", [(i + 1, i) for i in range(count - 1)])
-    outgoing = arrange(nbr_slot, nbr_keys, nbr_values, count)
-    incoming = exchange(fence(outgoing, (q_other, own, *early)))
+
+    tail, onward, mark = last_attend(cross_queries, spill, incoming)
+    back = lax.ppermute(onward, "ctx", [(i, i + 1) for i in range(count - 1)])
+    kv = exchange(fence(spread_keys(keys, values, count), mark, (own, *early)))
+    cca = merge(back, other_attend(cross_queries, tail, incoming))
+    terms = [cca] + [lax.ppermute(cca, "tp", across[step]) for step in range(1, groups)]
+    partial = project_near(terms[:2], own, beside, late)
+    crossed = project_far(partial, terms[2:], (early, late))
 
     ours, theirs = self_attend(pair, side, q_mine, q_other, kv)
     attended = both(ours, lax.ppermute(theirs, "ctx", swap), 1)
-
-    tail, onward = last_attend(cross_queries, spill, incoming)
-    back = lax.ppermute(onward, "ctx", [(i, i + 1) for i in range(count - 1)])
-    cca = merge(back, other_attend(cross_queries, tail, incoming))
-    terms = [cca] + [lax.ppermute(cca, "tp", across[step]) for step in range(1, groups)]
-    partial = project_near(terms[:2], own, beside)
-
-    crossed = project_far(partial, terms[2:], (early, late))
     return (attended, crossed)
 
 

time: 84.8 us -> 87.3 us (1.029)
  the two profiles are of different devices: /device:TPU:0 before, /device:TPU:24 now
where the time goes in v13:
time: 87.3 us; the launch traced here: 86.8 us
  waiting for transfers between devices  29.5 us (34%)
  starting transfers between devices  27.6 us (32%)
  Pallas kernels  24.2 us (28%)
  local copies, waits for them, and re-layouts  3.86 us (4%)
    all_to_all x2, starting transfers between devices, exchange(): return lax.all_to_all(value, 'ctx', split_axis=0, concat_axis=0, tiled=True)  12.5 us
    ppermute x1, waiting for transfers between devices, shards(): back = lax.ppermute(onward, 'ctx', [(i, i + 1) for i in range(count - 1)])  10 us
    ppermute x4, waiting for transfers between devices, shards(): lax.ppermute(block, 'tp', across[step])  7.57 us
    pallas_call x1, Pallas kernels, self_attend(): pl.pallas_call(self_kernel, out_shape=(jax.ShapeDtypeStruct((tile, HD), j...  7.03 us
    all_to_all x2, waiting for transfers between devices, exchange(): return lax.all_to_all(value, 'ctx', split_axis=0, concat_axis=0, tiled=True)  6.11 us
    pallas_call x2, Pallas kernels, cut(): pl.pallas_call(functools.partial(cut_kernel, plan), out_shape=tuple(shape...  5.84 us
    ppermute x1, waiting for transfers between devices, shards(): lax.ppermute(cross_queries[:BLOCK], 'ctx', [(i + 1, i) for i in range(cou...  5.79 us
    unnamed x18, local copies, waits for them, and re-layouts  3.86 us
  transfers between devices with their start and end apart: 14, of which 5 were waited for; matrix products, arithmetic and copies ran while one was open for 0% of the time, Pallas kernels for 24%

profile of v13, /device:TPU:24, one launch (start us, length us, event | category | flops | bytes accessed | tf_op | source)
XLA Modules:
  0.0 86.8 jit_solution(515132107544893914)
XLA Ops:
  0.6 2.8 %shard_map.96 = bf16[8,272,256]{2,1,0:T(8,128)(2,1)} custom-call(s32[8]{0:T(128)} %slot_ref.1, bf16[8,128,256]{2,1,0:T(8,128)(2,1)} %keys_ref.2, bf16[8,128,256]{2,1,0:T(8,128)(2,1)} %values_ref.2), custom_call_target="tpu_custom_call" | custom-call | flops 3000000000 | tf_op jit(solution)/shard_map/pallas_call | solution.py:168
  3.5 6.0 %all-to-all-start = ((bf16[8,272,256]{2,1,0:T(8,128)(2,1)}), bf16[8,272,256]{2,1,0:T(8,128)(2,1)S(1)}, u32[]{:S(2)}, u32[]{:S(2)}) async-start(bf16[8,272,256]{2,1,0:T(8,128)(2,1)} %shard_map.96), calls=%async_computation | async-start | bytes 2228224 | tf_op jit(solution)/shard_map/all_to_all | solution.py:454
  9.5 0.0 copy-start.7
  9.5 2.3 %shard_map.95 = (bf16[256,128]{1,0:T(8,128)(2,1)}, bf16[256,128]{1,0:T(8,128)(2,1)}, bf16[256,1024]{1,0:T(8,128)(2,1)}, bf16[256,1024]{1,0:T(8,128)(2,1)}) custom-call(s32[1]{0:T(128)} %bitcast.1.side_ref, s32[1]{0:T(128)} %bitcast.2.tp_ref, bf16[256,256]{1,0:T(8,128)(2,1)} %refs_0_.2, bf16[256,8192]{1,0:T(8,128)(2,1)} %refs_0_.3), custom_call_target="tpu_custom_call" | custom-call | flops 2000000000 | tf_op jit(solution)/shard_map/pallas_call | solution.py:67
  11.9 1.6 %collective-permute-start.2 = (bf16[256,1024]{1,0:T(8,128)(2,1)}, bf16[256,1024]{1,0:T(8,128)(2,1)S(1)}, u32[]{:S(2)}, u32[]{:S(2)}) collective-permute-start(bf16[256,1024]{1,0:T(8,128)(2,1)} %get-tuple-element.19), channel_id=1, source_target_pairs={{0,2},{1,3},{2,0},{3,1},{4,6},{5,7},{6,4},{7,5},{8,10},{9,11},{10,... | collective-permute-start | bytes 1572872 | tf_op jit(solution)/shard_map/ppermute | solution.py:464
  13.5 0.0 collective-permute-start.3
  13.5 0.0 copy-done.7
  13.5 3.4 %collective-permute-start.1 = (bf16[64,256]{1,0:T(8,128)(2,1)S(1)}, bf16[64,256]{1,0:T(8,128)(2,1)S(1)}, u32[]{:S(2)}, u32[]{:S(2)}) collective-permute-start(bf16[64,256]{1,0:T(8,128)(2,1)S(1)} %slice.3), channel_id=1, source_target_pairs={{4,0},{8,4},{12,8},{16,12},{20,16},{24,20},{28,24},{5,1},{9,5},{13... | collective-permute-start | bytes 98312 | tf_op jit(solution)/shard_map/ppermute | solution.py:474
  16.8 3.5 %shard_map.99 = (bf16[256,2048]{1,0:T(8,128)(2,1)}, bf16[256,2048]{1,0:T(8,128)(2,1)}, bf16[256,1024]{1,0:T(8,128)(2,1)}, bf16[256,1024]{1,0:T(8,128)(2,1)}) custom-call(s32[1]{0:T(128)} %bitcast.1.side_ref, s32[1]{0:T(128)} %bitcast.2.tp_ref, bf16[256,8192]{1,0:T(8,128)(2,1)} %refs_0_.3, bf16[256,128]{1,0:T(8,128)(2,1)} %get-tuple-element.16.refs_1_), custom_call_target="tpu_custom_call" | custom-call | flops 2000000000 | tf_op jit(solution)/shard_map/pallas_call | solution.py:67
  20.3 1.9 %shard_map.98.held_ref = bf16[8,256,256]{2,1,0:T(8,128)(2,1)} custom-call(bf16[256,256]{1,0:T(8,128)(2,1)} %keys_ref.3, bf16[256,256]{1,0:T(8,128)(2,1)} %values_ref.3), custom_call_target="tpu_custom_call" | custom-call | flops 2000000000 | tf_op jit(solution)/shard_map/pallas_call | solution.py:106
  22.3 5.8 %collective-permute-done.1.spill_ref = bf16[64,256]{1,0:T(8,128)(2,1)S(1)} collective-permute-done((bf16[64,256]{1,0:T(8,128)(2,1)S(1)}, bf16[64,256]{1,0:T(8,128)(2,1)S(1)}, u32[]{:S(2)}, u32[]{:S(2)}) %collective-permute-start.1) | collective-permute-done | bytes 32800 | tf_op jit(solution)/shard_map/ppermute | solution.py:474
  28.1 6.1 %all-to-all-done.incoming_ref = bf16[8,272,256]{2,1,0:T(8,128)(2,1)S(1)} async-done(((bf16[8,272,256]{2,1,0:T(8,128)(2,1)}), bf16[8,272,256]{2,1,0:T(8,128)(2,1)S(1)}, u32[]{:S(2)}, u32[]{:S(2)}) %all-to-all-start) | async-done | bytes 1114144 | tf_op jit(solution)/shard_map/all_to_all | solution.py:454
  34.2 0.7 shard_map.97
  34.9 0.0 collective-permute-done.2.refs_1_.refs_2_
  34.9 0.0 copy-start.3
  34.9 0.7 collective-permute-done.3.refs_2_.refs_3_
  35.6 0.0 copy-start.5
  35.6 0.1 copy-done.3
  35.7 0.7 copy-done.5
  36.4 0.6 shard_map.100
  37.1 6.5 %all-to-all-start.1 = ((bf16[8,256,256]{2,1,0:T(8,128)(2,1)}), bf16[8,256,256]{2,1,0:T(8,128)(2,1)}, u32[]{:S(2)}, u32[]{:S(2)}) async-start(bf16[8,256,256]{2,1,0:T(8,128)(2,1)} %shard_map.100), calls=%async_computation.1 | async-start | bytes 2097152 | tf_op jit(solution)/shard_map/all_to_all | solution.py:454
  43.5 0.0 collective-permute-start.7
  43.5 1.5 %collective-permute-start.8 = (bf16[256,1024]{1,0:T(8,128)(2,1)}, bf16[256,1024]{1,0:T(8,128)(2,1)}, u32[]{:S(2)}, u32[]{:S(2)}) collective-permute-start(bf16[256,1024]{1,0:T(8,128)(2,1)} %get-tuple-element.26), channel_id=1, source_target_pairs={{0,2},{1,3},{2,0},{3,1},{4,6},{5,7},{6,4},{7,5},{8,10},{9,11},{10,... | collective-permute-start | bytes 1572872 | tf_op jit(solution)/shard_map/ppermute | solution.py:473
  45.0 0.4 collective-permute-start.9
  45.4 3.4 %collective-permute-start.5 = (bf16[64,256]{1,0:T(8,128)(2,1)S(1)}, bf16[64,256]{1,0:T(8,128)(2,1)S(1)}, u32[]{:S(2)}, u32[]{:S(2)}) collective-permute-start(bf16[64,256]{1,0:T(8,128)(2,1)S(1)} %get-tuple-element.23), channel_id=1, source_target_pairs={{0,4},{4,8},{8,12},{12,16},{16,20},{20,24},{24,28},{1,5},{5,9},{9,... | collective-permute-start | bytes 98312 | tf_op jit(solution)/shard_map/ppermute | solution.py:477
  48.8 0.0 copy-start
  48.8 1.6 %shard_map.102.answers_ref = bf16[256,256]{1,0:T(8,128)(2,1)S(1)} custom-call(bf16[256,256]{1,0:T(8,128)(2,1)S(1)} %copy-done.7, bf16[16,256]{1,0:T(8,128)(2,1)S(1)} %get-tuple-element.24.tail_ref, bf16[8,272,256]{2,1,0:T(8,128)(2,1)S(1)} %all-to-all-done.incoming_ref), custom_call_target="tpu_custom_call" | custom-call | flops 2000000000 | tf_op jit(solution)/shard_map/pallas_call | solution.py:281
  50.4 10.0 %collective-permute-done.5.back_ref = bf16[64,256]{1,0:T(8,128)(2,1)S(1)} collective-permute-done((bf16[64,256]{1,0:T(8,128)(2,1)S(1)}, bf16[64,256]{1,0:T(8,128)(2,1)S(1)}, u32[]{:S(2)}, u32[]{:S(2)}) %collective-permute-start.5) | collective-permute-done | bytes 32800 | tf_op jit(solution)/shard_map/ppermute | solution.py:477
  60.5 0.1 collective-permute-start.6
  60.6 0.1 collective-permute-start
  60.7 0.0 collective-permute-done.8.refs_0_.refs_4_
  60.7 1.6 %collective-permute-start.10 = (bf16[256,256]{1,0:T(8,128)(2,1)S(1)}, bf16[256,256]{1,0:T(8,128)(2,1)}, u32[]{:S(2)}, u32[]{:S(2)}) collective-permute-start(bf16[256,256]{1,0:T(8,128)(2,1)S(1)} %shard_map.103.one_ref), channel_id=1, source_target_pairs={{0,2},{1,3},{2,0},{3,1},{4,6},{5,7},{6,4},{7,5},{8,10},{9,11},{10,... | collective-permute-start | bytes 393224 | tf_op jit(solution)/shard_map/ppermute | solution.py:480
  62.2 6.8 %collective-permute-done.9.refs_1_.refs_5_ = bf16[256,1024]{1,0:T(8,128)(2,1)} collective-permute-done((bf16[256,1024]{1,0:T(8,128)(2,1)}, bf16[256,1024]{1,0:T(8,128)(2,1)}, u32[]{:S(2)}, u32[]{:S(2)}) %collective-permute-start.9) | collective-permute-done | bytes 524320 | tf_op jit(solution)/shard_map/ppermute | solution.py:473
  69.0 1.7 %collective-permute-start.11 = (bf16[256,256]{1,0:T(8,128)(2,1)S(1)}, bf16[256,256]{1,0:T(8,128)(2,1)}, u32[]{:S(2)}, u32[]{:S(2)}) collective-permute-start(bf16[256,256]{1,0:T(8,128)(2,1)S(1)} %shard_map.103.one_ref), channel_id=1, source_target_pairs={{0,3},{1,2},{2,1},{3,0},{4,7},{5,6},{6,5},{7,4},{8,11},{9,10},{10,... | collective-permute-start | bytes 393224 | tf_op jit(solution)/shard_map/ppermute | solution.py:480
  70.7 0.0 collective-permute-done.7.beside_ref
  70.7 0.0 copy-start.1
  70.7 1.0 %copy-done.1 = bf16[256,2048]{1,0:T(8,128)(2,1)} copy-done((bf16[256,2048]{1,0:T(8,128)(2,1)}, bf16[256,2048]{1,0:T(8,128)(2,1)S(1)}, u32[]{:S(2)}) %copy-start.1) | copy-done | bytes 1048600
  71.7 0.0 collective-permute-done.6.two_ref
  71.7 0.0 copy-done
  71.7 0.0 copy-start.2
  71.7 1.2 %copy-done.2 = bf16[256,2048]{1,0:T(8,128)(2,1)S(1)} copy-done((bf16[256,2048]{1,0:T(8,128)(2,1)S(1)}, bf16[256,2048]{1,0:T(8,128)(2,1)}, u32[]{:S(2)}) %copy-start.2) | copy-done | bytes 1048600
  73.0 0.7 shard_map.104.partial_ref
  73.7 0.0 collective-permute-done.other_ref
  73.7 0.0 all-to-all-done.1.kv_ref
  73.7 0.0 copy-start.8
  73.7 0.8 copy-done.8
  74.5 0.0 copy-start.4
  74.5 0.0 copy-start.6
  74.5 7.0 %shard_map.101 = (bf16[256,128]{1,0:T(8,128)(2,1)S(1)}, bf16[256,128]{1,0:T(8,128)(2,1)S(1)}) custom-call(s32[1]{0:T(128)} %bitcast.pair_ref, s32[1]{0:T(128)} %bitcast.1.side_ref, bf16[256,128]{1,0:T(8,128)(2,1)S(1)} %copy-done.8, bf16[256,128]{1,0:T(8,128)(2,1)S(1)} %collective-permute-done.other_ref, bf16[8,256,256]{2,1,0:T(8,128)(2,1)} %all-to-all-done.1.kv_ref), custom_call_target="tpu_custom_call" | custom-call | flops 6000000000 | tf_op jit(solution)/shard_map/pallas_call | solution.py:356
  81.6 1.6 %collective-permute-start.4 = (bf16[256,128]{1,0:T(8,128)(2,1)S(1)}, bf16[256,128]{1,0:T(8,128)(2,1)S(1)}, u32[]{:S(2)}, u32[]{:S(2)}) collective-permute-start(bf16[256,128]{1,0:T(8,128)(2,1)S(1)} %get-tuple-element.22), channel_id=1, source_target_pairs={{0,4},{4,0},{8,12},{12,8},{16,20},{20,16},{24,28},{28,24},{1,5},{5... | collective-permute-start | bytes 196616 | tf_op jit(solution)/shard_map/ppermute | solution.py:485
  83.1 0.0 collective-permute-done.10.refs_0_
  83.1 0.0 collective-permute-done.11.refs_1_
  83.1 0.0 copy-done.4
  83.1 0.0 copy-done.6
  83.1 2.9 %shard_map.105 = bf16[256,2048]{1,0:T(8,128)(2,1)} custom-call(f32[256,2048]{1,0:T(8,128)S(1)} %shard_map.104.partial_ref, bf16[256,256]{1,0:T(8,128)(2,1)} %collective-permute-done.10.refs_0_, bf16[256,256]{1,0:T(8,128)(2,1)} %collective-permute-done.11.refs_1_, bf16[256,1024]{1,0:T(8,128)(2,1)S(1)} %copy-done.4, bf16[256,1024]{1,0:T(8,128)(2,1)S(1)} %copy-done.6, ...), custom_call_target="tpu_custom_call" | custom-call | flops 2000000000 | tf_op jit(solution)/shard_map/pallas_call | solution.py:417
  86.1 0.0 collective-permute-done.4
  86.1 0.7 maximum_select_fusion
  (2 shorter events, 0.0 us)
Async XLA Ops:
  3.5 30.7 %all-to-all-start = ((bf16[8,272,256]{2,1,0:T(8,128)(2,1)}), bf16[8,272,256]{2,1,0:T(8,128)(2,1)S(1)}, u32[]{:S(2)}, u32[]{:S(2)}) async-start(bf16[8,272,256]{2,1,0:T(8,128)(2,1)} %shard_map.96), calls=%async_computation | async-start | bytes 2228224 | tf_op jit(solution)/shard_map/all_to_all | solution.py:454
  9.5 3.9 %copy-start.7 = (bf16[256,256]{1,0:T(8,128)(2,1)S(1)}, bf16[256,256]{1,0:T(8,128)(2,1)}, u32[]{:S(2)}) copy-start(bf16[256,256]{1,0:T(8,128)(2,1)} %queries_ref.3) | copy-start | bytes 393220
  11.9 23.0 %collective-permute-start.2 = (bf16[256,1024]{1,0:T(8,128)(2,1)}, bf16[256,1024]{1,0:T(8,128)(2,1)S(1)}, u32[]{:S(2)}, u32[]{:S(2)}) collective-permute-start(bf16[256,1024]{1,0:T(8,128)(2,1)} %get-tuple-element.19), channel_id=1, source_target_pairs={{0,2},{1,3},{2,0},{3,1},{4,6},{5,7},{6,4},{7,5},{8,10},{9,11},{10,... | collective-permute-start | bytes 1572872 | tf_op jit(solution)/shard_map/ppermute | solution.py:464
  13.5 22.2 %collective-permute-start.3 = (bf16[256,1024]{1,0:T(8,128)(2,1)}, bf16[256,1024]{1,0:T(8,128)(2,1)S(1)}, u32[]{:S(2)}, u32[]{:S(2)}) collective-permute-start(bf16[256,1024]{1,0:T(8,128)(2,1)} %get-tuple-element.20), channel_id=1, source_target_pairs={{0,3},{1,2},{2,1},{3,0},{4,7},{5,6},{6,5},{7,4},{8,11},{9,10},{10,... | collective-permute-start | bytes 1572872 | tf_op jit(solution)/shard_map/ppermute | solution.py:464
  13.5 14.6 %collective-permute-start.1 = (bf16[64,256]{1,0:T(8,128)(2,1)S(1)}, bf16[64,256]{1,0:T(8,128)(2,1)S(1)}, u32[]{:S(2)}, u32[]{:S(2)}) collective-permute-start(bf16[64,256]{1,0:T(8,128)(2,1)S(1)} %slice.3), channel_id=1, source_target_pairs={{4,0},{8,4},{12,8},{16,12},{20,16},{24,20},{28,24},{5,1},{9,5},{13... | collective-permute-start | bytes 98312 | tf_op jit(solution)/shard_map/ppermute | solution.py:474
  34.9 0.8 copy-start.3
  35.6 0.8 copy-start.5
  37.1 36.6 %all-to-all-start.1 = ((bf16[8,256,256]{2,1,0:T(8,128)(2,1)}), bf16[8,256,256]{2,1,0:T(8,128)(2,1)}, u32[]{:S(2)}, u32[]{:S(2)}) async-start(bf16[8,256,256]{2,1,0:T(8,128)(2,1)} %shard_map.100), calls=%async_computation.1 | async-start | bytes 2097152 | tf_op jit(solution)/shard_map/all_to_all | solution.py:454
  43.5 27.2 %collective-permute-start.7 = (bf16[256,2048]{1,0:T(8,128)(2,1)}, bf16[256,2048]{1,0:T(8,128)(2,1)S(1)}, u32[]{:S(2)}, u32[]{:S(2)}) collective-permute-start(bf16[256,2048]{1,0:T(8,128)(2,1)} %get-tuple-element.25), channel_id=1, source_target_pairs={{0,1},{1,0},{2,3},{3,2},{4,5},{5,4},{6,7},{7,6},{8,9},{9,8},{10,11... | collective-permute-start | bytes 3145736 | tf_op jit(solution)/shard_map/ppermute | solution.py:472
  43.5 17.1 %collective-permute-start.8 = (bf16[256,1024]{1,0:T(8,128)(2,1)}, bf16[256,1024]{1,0:T(8,128)(2,1)}, u32[]{:S(2)}, u32[]{:S(2)}) collective-permute-start(bf16[256,1024]{1,0:T(8,128)(2,1)} %get-tuple-element.26), channel_id=1, source_target_pairs={{0,2},{1,3},{2,0},{3,1},{4,6},{5,7},{6,4},{7,5},{8,10},{9,11},{10,... | collective-permute-start | bytes 1572872 | tf_op jit(solution)/shard_map/ppermute | solution.py:473
  45.0 24.0 %collective-permute-start.9 = (bf16[256,1024]{1,0:T(8,128)(2,1)}, bf16[256,1024]{1,0:T(8,128)(2,1)}, u32[]{:S(2)}, u32[]{:S(2)}) collective-permute-start(bf16[256,1024]{1,0:T(8,128)(2,1)} %get-tuple-element.27), channel_id=1, source_target_pairs={{0,3},{1,2},{2,1},{3,0},{4,7},{5,6},{6,5},{7,4},{8,11},{9,10},{10,... | collective-permute-start | bytes 1572872 | tf_op jit(solution)/shard_map/ppermute | solution.py:473
  45.4 15.1 %collective-permute-start.5 = (bf16[64,256]{1,0:T(8,128)(2,1)S(1)}, bf16[64,256]{1,0:T(8,128)(2,1)S(1)}, u32[]{:S(2)}, u32[]{:S(2)}) collective-permute-start(bf16[64,256]{1,0:T(8,128)(2,1)S(1)} %get-tuple-element.23), channel_id=1, source_target_pairs={{0,4},{4,8},{8,12},{12,16},{16,20},{20,24},{24,28},{1,5},{5,9},{9,... | collective-permute-start | bytes 98312 | tf_op jit(solution)/shard_map/ppermute | solution.py:477
  48.8 23.0 %copy-start = (bf16[256,2048]{1,0:T(8,128)(2,1)S(1)}, bf16[256,2048]{1,0:T(8,128)(2,1)}, u32[]{:S(2)}) copy-start(bf16[256,2048]{1,0:T(8,128)(2,1)} %get-tuple-element.18.refs_0_.own_ref) | copy-start | bytes 3145732
  60.5 11.2 %collective-permute-start.6 = (bf16[256,256]{1,0:T(8,128)(2,1)S(1)}, bf16[256,256]{1,0:T(8,128)(2,1)S(1)}, u32[]{:S(2)}, u32[]{:S(2)}) collective-permute-start(bf16[256,256]{1,0:T(8,128)(2,1)S(1)} %shard_map.103.one_ref), channel_id=1, source_target_pairs={{0,1},{1,0},{2,3},{3,2},{4,5},{5,4},{6,7},{7,6},{8,9},{9,8},{10,11... | collective-permute-start | bytes 393224 | tf_op jit(solution)/shard_map/ppermute | solution.py:480
  60.6 13.1 %collective-permute-start = (bf16[256,128]{1,0:T(8,128)(2,1)}, bf16[256,128]{1,0:T(8,128)(2,1)S(1)}, u32[]{:S(2)}, u32[]{:S(2)}) collective-permute-start(bf16[256,128]{1,0:T(8,128)(2,1)} %get-tuple-element.16.refs_1_), channel_id=1, source_target_pairs={{0,4},{4,0},{8,12},{12,8},{16,20},{20,16},{24,28},{28,24},{1,5},{5... | collective-permute-start | bytes 196616 | tf_op jit(solution)/shard_map/ppermute | solution.py:465
  60.7 22.5 %collective-permute-start.10 = (bf16[256,256]{1,0:T(8,128)(2,1)S(1)}, bf16[256,256]{1,0:T(8,128)(2,1)}, u32[]{:S(2)}, u32[]{:S(2)}) collective-permute-start(bf16[256,256]{1,0:T(8,128)(2,1)S(1)} %shard_map.103.one_ref), channel_id=1, source_target_pairs={{0,2},{1,3},{2,0},{3,1},{4,6},{5,7},{6,4},{7,5},{8,10},{9,11},{10,... | collective-permute-start | bytes 393224 | tf_op jit(solution)/shard_map/ppermute | solution.py:480
  69.0 14.1 %collective-permute-start.11 = (bf16[256,256]{1,0:T(8,128)(2,1)S(1)}, bf16[256,256]{1,0:T(8,128)(2,1)}, u32[]{:S(2)}, u32[]{:S(2)}) collective-permute-start(bf16[256,256]{1,0:T(8,128)(2,1)S(1)} %shard_map.103.one_ref), channel_id=1, source_target_pairs={{0,3},{1,2},{2,1},{3,0},{4,7},{5,6},{6,5},{7,4},{8,11},{9,10},{10,... | collective-permute-start | bytes 393224 | tf_op jit(solution)/shard_map/ppermute | solution.py:480
  70.7 1.0 %copy-start.1 = (bf16[256,2048]{1,0:T(8,128)(2,1)}, bf16[256,2048]{1,0:T(8,128)(2,1)S(1)}, u32[]{:S(2)}) copy-start(bf16[256,2048]{1,0:T(8,128)(2,1)S(1)} %collective-permute-done.7.beside_ref) | copy-start | bytes 3145732
  71.7 1.2 %copy-start.2 = (bf16[256,2048]{1,0:T(8,128)(2,1)S(1)}, bf16[256,2048]{1,0:T(8,128)(2,1)}, u32[]{:S(2)}) copy-start(bf16[256,2048]{1,0:T(8,128)(2,1)} %copy-done.1) | copy-start | bytes 3145732
  73.7 0.8 copy-start.8
  74.5 8.6 %copy-start.4 = (bf16[256,1024]{1,0:T(8,128)(2,1)S(1)}, bf16[256,1024]{1,0:T(8,128)(2,1)}, u32[]{:S(2)}) copy-start(bf16[256,1024]{1,0:T(8,128)(2,1)} %copy-done.3) | copy-start | bytes 1572868
  74.5 8.6 %copy-start.6 = (bf16[256,1024]{1,0:T(8,128)(2,1)S(1)}, bf16[256,1024]{1,0:T(8,128)(2,1)}, u32[]{:S(2)}) copy-start(bf16[256,1024]{1,0:T(8,128)(2,1)} %copy-done.5) | copy-start | bytes 1572868
  81.6 4.5 %collective-permute-start.4 = (bf16[256,128]{1,0:T(8,128)(2,1)S(1)}, bf16[256,128]{1,0:T(8,128)(2,1)S(1)}, u32[]{:S(2)}, u32[]{:S(2)}) collective-permute-start(bf16[256,128]{1,0:T(8,128)(2,1)S(1)} %get-tuple-element.22), channel_id=1, source_target_pairs={{0,4},{4,0},{8,12},{12,8},{16,20},{20,16},{24,28},{28,24},{1,5},{5... | collective-permute-start | bytes 196616 | tf_op jit(solution)/shard_map/ppermute | solution.py:485

commit v14 on v11

--- a/solution.py
+++ b/solution.py
@@ -17,6 +17,7 @@
 SMEM = pl.BlockSpec(memory_space=pltpu.SMEM)
 ANY = pl.BlockSpec(memory_space=pl.ANY)
 PARAMS = pltpu.CompilerParams(vmem_limit_bytes=16 * 1024 * 1024)
+WIDE = pltpu.CompilerParams(vmem_limit_bytes=40 * 1024 * 1024)
 
 
 def takes(microseconds):
@@ -205,7 +206,7 @@
     return [pltpu.SMEM((2 * rows // BLOCK,), jnp.int32)]
 
 
-def last_attend(queries, spill, incoming):
+def last_attend(queries, spill, incoming, before):
     rows, width = queries.shape
     return pl.pallas_call(
         last_kernel,
@@ -213,12 +214,12 @@
             jax.ShapeDtypeStruct((LEAD, width), queries.dtype),
             jax.ShapeDtypeStruct((BLOCK, width), queries.dtype),
         ),
-        in_specs=[VMEM] * 3,
+        in_specs=[VMEM] * 3 + [ANY] * len(before),
         out_specs=(VMEM, VMEM),
         scratch_shapes=order_scratch(rows),
         compiler_params=PARAMS,
         cost_estimate=takes(1),
-    )(queries, spill, incoming)
+    )(queries, spill, incoming, *before)
 
 
 def other_attend(queries, tail, incoming):
@@ -249,51 +250,80 @@
     )(back, answers)
 
 
+def touch_kernel(held_ref, mark_ref):
+    mark_ref[0] = 0
+
+
+def touch(held):
+    return pl.pallas_call(
+        touch_kernel,
+        out_shape=jax.ShapeDtypeStruct((1,), jnp.int32),
+        in_specs=[VMEM],
+        out_specs=SMEM,
+        compiler_params=PARAMS,
+    )(held)
+
+
 def self_kernel(pair_ref, side_ref, mark_ref, mine_ref, other_ref, incoming_ref, *refs):
-    ours_ref, theirs_ref, peak_ref, total_ref, accum_ref = refs[-5:]
+    ours_ref, theirs_ref, scores_ref, peak_ref, total_ref, accum_ref = refs
     pair, side = pair_ref[0], side_ref[0]
     tile = mine_ref.shape[0]
     rows = 2 * tile
     front = incoming_ref.shape[1] - tile
     chunk = min(128, tile)
-
-    def attend(at, fresh):
-        kv = incoming_ref[pl.ds(2 * at, 2), front:, :].reshape(rows, 2 * HD)
-        for start in range(0, rows, chunk):
-            here = slice(start, start + chunk)
+    chunks = [slice(start, start + chunk) for start in range(0, rows, chunk)]
+
+    def fold(function, block):
+        parts = [block[:, at : at + HD] for at in range(0, block.shape[1], HD)]
+        return functools.reduce(function, parts)
+
+    def score(at, fresh):
+        k = incoming_ref[pl.ds(2 * at, 2), front:, :HD].reshape(rows, HD)
+        for here in chunks:
+            start = here.start
             q_ref, offset = (mine_ref, start) if start < tile else (other_ref, start - tile)
-            s = dot_t(q_ref[offset : offset + chunk, :], kv[:, :HD])
+            s = dot_t(q_ref[offset : offset + chunk, :], k)
             if fresh:
                 row = lax.broadcasted_iota(jnp.int32, (chunk, rows), 0) + start
                 col = lax.broadcasted_iota(jnp.int32, (chunk, rows), 1)
                 turn = side * tile
                 row = row + turn if start < tile else row - turn
                 s = jnp.where(col <= row, s, NEGATIVE)
-            peak = jnp.max(s, axis=1, keepdims=True)
-            if not fresh:
-                old = peak_ref[here, :1]
-                peak = jnp.maximum(peak, old)
-                factor = jnp.exp2((old - peak) * SCALE)
-            p = jnp.exp2((s - peak) * SCALE)
-            total = jnp.sum(p, axis=1, keepdims=True)
-            accum = dot(p.astype(jnp.bfloat16), kv[:, HD:])
-            if not fresh:
-                total += total_ref[here, :1] * factor
-                accum += accum_ref[here, :] * factor
-            peak_ref[here, :] = jnp.broadcast_to(peak, (chunk, HD))
-            total_ref[here, :] = jnp.broadcast_to(total, (chunk, HD))
-            accum_ref[here, :] = accum
-
-    attend(pair, True)
-
-    def earlier(at, carry):
-        attend(at, False)
-        return carry
-
-    lax.fori_loop(0, pair, earlier, 0)
-    result = (accum_ref[...] / total_ref[...]).astype(jnp.bfloat16)
-    ours_ref[...] = result[:tile]
-    theirs_ref[...] = result[tile:]
+            scores_ref[at, here, :] = s
+            peak = fold(jnp.maximum, s)
+            peak_ref[here, :] = peak if fresh else jnp.maximum(peak, peak_ref[here, :])
+
+    def weigh(at, fresh):
+        v = incoming_ref[pl.ds(2 * at, 2), front:, HD:].reshape(rows, HD)
+        for here in chunks:
+            peak = jnp.concatenate([peak_ref[here, :]] * (rows // HD), axis=1)
+            p = jnp.exp2((scores_ref[at, here, :] - peak) * SCALE)
+            total = fold(jnp.add, p)
+            accum = dot(p.astype(jnp.bfloat16), v)
+            total_ref[here, :] = total if fresh else total + total_ref[here, :]
+            accum_ref[here, :] = accum if fresh else accum + accum_ref[here, :]
+
+    def earlier(work):
+        def step(at, carry):
+            work(at, False)
+            return carry
+
+        lax.fori_loop(0, pair, step, 0)
+
+    score(pair, True)
+    earlier(score)
+    for here in chunks:
+        peak = jnp.max(peak_ref[here, :], axis=1, keepdims=True)
+        peak_ref[here, :] = jnp.broadcast_to(peak, (chunk, HD))
+    weigh(pair, True)
+    earlier(weigh)
+    for here in chunks:
+        total = jnp.sum(total_ref[here, :], axis=1, keepdims=True)
+        result = (accum_ref[here, :] / total).astype(jnp.bfloat16)
+        if here.start < tile:
+            ours_ref[here, :] = result
+        else:
+            theirs_ref[here.start - tile : here.stop - tile, :] = result
 
 
 def self_attend(pair, side, mark, mine, other, incoming):
@@ -303,48 +333,26 @@
         out_shape=(jax.ShapeDtypeStruct((tile, HD), jnp.bfloat16),) * 2,
         in_specs=[SMEM] * 3 + [VMEM] * 3,
         out_specs=(VMEM, VMEM),
-        scratch_shapes=[pltpu.VMEM((2 * tile, HD), jnp.float32)] * 3,
-        compiler_params=PARAMS,
+        scratch_shapes=[
+            pltpu.VMEM((incoming.shape[0] // 2, 2 * tile, 2 * tile), jnp.float32)
+        ]
+        + [pltpu.VMEM((2 * tile, HD), jnp.float32)] * 3,
+        compiler_params=WIDE,
         cost_estimate=takes(6),
     )(pair, side, mark, mine, other, incoming)
 
 
-def near_kernel(one_ref, two_ref, own_ref, beside_ref, partial_ref, mark_ref):
-    mark_ref[0] = 0
-    width = partial_ref.shape[1]
-    term = jnp.concatenate([one_ref[...], two_ref[...]], axis=1)
-    tile = min(512, width)
-    for column in range(0, width, tile):
-        at = slice(column, column + tile)
-        partial_ref[:, at] = dot(
-            term, jnp.concatenate([own_ref[:, at], beside_ref[:, at]], axis=0)
-        )
-
-
-def project_near(terms, own, beside):
-    return pl.pallas_call(
-        near_kernel,
-        out_shape=(
-            jax.ShapeDtypeStruct((terms[0].shape[0], own.shape[1]), jnp.float32),
-            jax.ShapeDtypeStruct((1,), jnp.int32),
-        ),
-        in_specs=[VMEM] * 4,
-        out_specs=(VMEM, SMEM),
-        compiler_params=PARAMS,
-    )(*terms, own, beside)
-
-
-def far_kernel(count, partial_ref, *refs):
+def project_kernel(groups, *refs):
     crossed_ref, out_ref, sems = refs[-3:]
-    terms, direct = refs[:count], refs[count : 2 * count]
+    terms, blocks = refs[:groups], refs[groups:-3]
     width = crossed_ref.shape[1]
     tile = min(512, width)
     term = jnp.concatenate([held[...] for held in terms], axis=1)
     outs = []
     for column in range(0, width, tile):
         at = slice(column, column + tile)
-        total = dot(term, jnp.concatenate([block[:, at] for block in direct], axis=0))
-        out_ref[:, at] = (partial_ref[:, at] + total).astype(out_ref.dtype)
+        weight = jnp.concatenate([block[:, at] for block in blocks], axis=0)
+        out_ref[:, at] = dot(term, weight).astype(out_ref.dtype)
         out = pltpu.make_async_copy(
             out_ref.at[:, at], crossed_ref.at[:, at], sems.at[len(outs)]
         )
@@ -354,21 +362,21 @@
         out.wait()
 
 
-def project_far(partial, terms, direct):
-    rows, width = partial.shape
-    operands = (*terms, *direct)
-    return pl.pallas_call(
-        functools.partial(far_kernel, len(terms)),
+def project(terms, blocks):
+    rows, width = terms[0].shape[0], blocks[0].shape[1]
+    operands = (*terms, *blocks)
+    return pl.pallas_call(
+        functools.partial(project_kernel, len(terms)),
         out_shape=jax.ShapeDtypeStruct((rows, width), jnp.bfloat16),
-        in_specs=[VMEM] * (1 + len(operands)),
+        in_specs=[VMEM] * len(operands),
         out_specs=ANY,
         scratch_shapes=[
             pltpu.VMEM((rows, width), jnp.bfloat16),
             pltpu.SemaphoreType.DMA((width // min(512, width),)),
         ],
         compiler_params=PARAMS,
-        cost_estimate=takes(2),
-    )(partial, *operands)
+        cost_estimate=takes(3),
+    )(*operands)
 
 
 def shards(queries, keys, values, cross_queries, nbr_keys, nbr_values, nbr_slot, w_cross):
@@ -408,15 +416,14 @@
     ]
     spill = lax.ppermute(cross_queries[:BLOCK], "ctx", [(i + 1, i) for i in range(count - 1)])
 
-    tail, onward = last_attend(cross_queries, spill, incoming)
+    tail, onward = last_attend(cross_queries, spill, incoming, (q_other, beside))
     back = lax.ppermute(onward, "ctx", [(i, i + 1) for i in range(count - 1)])
     cca = merge(back, other_attend(cross_queries, tail, incoming))
     terms = [cca] + [lax.ppermute(cca, "tp", across[step]) for step in range(1, groups)]
-    partial, mark = project_near(terms[:2], own, beside)
-
-    ours, theirs = self_attend(pair, side, mark, q_mine, q_other, incoming)
+
+    ours, theirs = self_attend(pair, side, touch(terms[1]), q_mine, q_other, incoming)
     attended = both(ours, lax.ppermute(theirs, "ctx", swap), 1)
-    crossed = project_far(partial, terms[2:], direct)
+    crossed = project(terms, (own, beside, *direct))
     return (attended, crossed)
 
 

time: 82.7 us -> 80 us (0.967)
  the two profiles are of different devices: /device:TPU:25 before, /device:TPU:0 now
where the time goes in v14:
time: 80 us; the launch traced here: 79.5 us
  waiting for transfers between devices  41.5 us (52%)
  starting transfers between devices  19.7 us (25%)
  Pallas kernels  15.9 us (20%)
  local copies, waits for them, and re-layouts  0.85 us (1%)
    all_to_all x1, waiting for transfers between devices, exchange(): return lax.all_to_all(value, 'ctx', split_axis=0, concat_axis=0, tiled=True)  29.9 us
    ppermute x1, waiting for transfers between devices, shards(): lax.ppermute(cross_queries[:BLOCK], 'ctx', [(i + 1, i) for i in range(cou...  8.38 us
    all_to_all x1, starting transfers between devices, exchange(): return lax.all_to_all(value, 'ctx', split_axis=0, concat_axis=0, tiled=True)  7.29 us
    pallas_call x1, Pallas kernels, cut(): pl.pallas_call(functools.partial(cut_kernel, plan), out_shape=tuple(shape...  4.4 us
    pallas_call x1, Pallas kernels, arrange(): pl.pallas_call(arrange_kernel, out_shape=jax.ShapeDtypeStruct((indices, f...  3.64 us
    pallas_call x1, Pallas kernels, project(): pl.pallas_call(functools.partial(project_kernel, len(terms)), out_shape=j...  3.53 us
    ppermute x1, starting transfers between devices, shards(): back = lax.ppermute(onward, 'ctx', [(i, i + 1) for i in range(count - 1)])  3.02 us
    ppermute x1, starting transfers between devices, shards(): attended = both(ours, lax.ppermute(theirs, 'ctx', swap), 1)  2.29 us
  transfers between devices with their start and end apart: 11, of which 4 were waited for; matrix products, arithmetic and copies ran while one was open for 0% of the time, Pallas kernels for 15%

profile of v14, /device:TPU:0, one launch (start us, length us, event | category | flops | bytes accessed | tf_op | source)
XLA Modules:
  0.0 79.5 jit_solution(2838718045004596517)
XLA Ops:
  0.6 3.6 %shard_map.95 = bf16[8,528,256]{2,1,0:T(8,128)(2,1)} custom-call(s32[8]{0:T(128)} %slot_ref.1, bf16[8,128,256]{2,1,0:T(8,128)(2,1)} %keys_ref.1, bf16[8,128,256]{2,1,0:T(8,128)(2,1)} %values_ref.1, bf16[256,256]{1,0:T(8,128)(2,1)} %own_keys.1, bf16[256,256]{1,0:T(8,128)(2,1)} %own_values.1), custom_call_target="tpu_custom_call" | custom-call | flops 4000000000 | tf_op jit(solution)/shard_map/pallas_call | solution.py:129
  4.3 7.3 %all-to-all-start = ((bf16[8,528,256]{2,1,0:T(8,128)(2,1)}), bf16[8,528,256]{2,1,0:T(8,128)(2,1)S(1)}, u32[]{:S(2)}, u32[]{:S(2)}) async-start(bf16[8,528,256]{2,1,0:T(8,128)(2,1)} %shard_map.95), calls=%async_computation | async-start | bytes 4325376 | tf_op jit(solution)/shard_map/all_to_all | solution.py:405
  11.6 0.0 copy-start
  11.6 4.4 %shard_map.96 = (bf16[256,128]{1,0:T(8,128)(2,1)}, bf16[256,128]{1,0:T(8,128)(2,1)}, bf16[256,2048]{1,0:T(8,128)(2,1)}, bf16[256,2048]{1,0:T(8,128)(2,1)}, bf16[...) custom-call(s32[1]{0:T(128)} %bitcast.1.side_ref, s32[1]{0:T(128)} %bitcast.2.tp_ref, bf16[256,256]{1,0:T(8,128)(2,1)} %refs_0_.1, ...), custom_call_target="tpu_custom_call" | custom-call | flops 2000000000 | tf_op jit(solution)/shard_map/pallas_call | solution.py:68
  16.0 0.1 collective-permute-start.2
  16.1 1.6 %collective-permute-start.8 = (bf16[256,2048]{1,0:T(8,128)(2,1)}, bf16[256,2048]{1,0:T(8,128)(2,1)}, u32[]{:S(2)}, u32[]{:S(2)}) collective-permute-start(bf16[256,2048]{1,0:T(8,128)(2,1)} %get-tuple-element.20), channel_id=1, source_target_pairs={{0,2},{1,3},{2,0},{3,1},{4,6},{5,7},{6,4},{7,5},{8,10},{9,11},{10,... | collective-permute-start | bytes 3145736 | tf_op jit(solution)/shard_map/ppermute | solution.py:415
  17.6 0.3 collective-permute-start.9
  17.9 2.0 %collective-permute-start.1 = (bf16[256,128]{1,0:T(8,128)(2,1)}, bf16[256,128]{1,0:T(8,128)(2,1)S(1)}, u32[]{:S(2)}, u32[]{:S(2)}) collective-permute-start(bf16[256,128]{1,0:T(8,128)(2,1)} %get-tuple-element.12), channel_id=1, source_target_pairs={{0,4},{4,0},{8,12},{12,8},{16,20},{20,16},{24,28},{28,24},{1,5},{5... | collective-permute-start | bytes 196616 | tf_op jit(solution)/shard_map/ppermute | solution.py:413
  19.9 0.0 copy-done
  19.9 1.3 %collective-permute-start = (bf16[64,256]{1,0:T(8,128)(2,1)S(1)}, bf16[64,256]{1,0:T(8,128)(2,1)S(1)}, u32[]{:S(2)}, u32[]{:S(2)}) collective-permute-start(bf16[64,256]{1,0:T(8,128)(2,1)S(1)} %slice.3), channel_id=1, source_target_pairs={{4,0},{8,4},{12,8},{16,12},{20,16},{24,20},{28,24},{5,1},{9,5},{13... | collective-permute-start | bytes 98312 | tf_op jit(solution)/shard_map/ppermute | solution.py:417
  21.2 8.4 %collective-permute-done.spill_ref = bf16[64,256]{1,0:T(8,128)(2,1)S(1)} collective-permute-done((bf16[64,256]{1,0:T(8,128)(2,1)S(1)}, bf16[64,256]{1,0:T(8,128)(2,1)S(1)}, u32[]{:S(2)}, u32[]{:S(2)}) %collective-permute-start) | collective-permute-done | bytes 32800 | tf_op jit(solution)/shard_map/ppermute | solution.py:417
  29.6 2.0 %collective-permute-done.1.refs_0_.other_ref = bf16[256,128]{1,0:T(8,128)(2,1)S(1)} collective-permute-done((bf16[256,128]{1,0:T(8,128)(2,1)}, bf16[256,128]{1,0:T(8,128)(2,1)S(1)}, u32[]{:S(2)}, u32[]{:S(2)}) %collective-permute-start.1) | collective-permute-done | bytes 65568 | tf_op jit(solution)/shard_map/ppermute | solution.py:413
  31.6 0.0 collective-permute-done.2.refs_1_.refs_5_
  31.6 29.9 %all-to-all-done.incoming_ref = bf16[8,528,256]{2,1,0:T(8,128)(2,1)S(1)} async-done(((bf16[8,528,256]{2,1,0:T(8,128)(2,1)}), bf16[8,528,256]{2,1,0:T(8,128)(2,1)S(1)}, u32[]{:S(2)}, u32[]{:S(2)}) %all-to-all-start) | async-done | bytes 2162720 | tf_op jit(solution)/shard_map/all_to_all | solution.py:405
  61.6 0.6 shard_map.97
  62.2 3.0 %collective-permute-start.3 = (bf16[64,256]{1,0:T(8,128)(2,1)S(1)}, bf16[64,256]{1,0:T(8,128)(2,1)S(1)}, u32[]{:S(2)}, u32[]{:S(2)}) collective-permute-start(bf16[64,256]{1,0:T(8,128)(2,1)S(1)} %get-tuple-element.14), channel_id=1, source_target_pairs={{0,4},{4,8},{8,12},{12,16},{16,20},{20,24},{24,28},{1,5},{5,9},{9,... | collective-permute-start | bytes 98312 | tf_op jit(solution)/shard_map/ppermute | solution.py:420
  65.2 1.6 %shard_map.98.answers_ref = bf16[256,256]{1,0:T(8,128)(2,1)S(1)} custom-call(bf16[256,256]{1,0:T(8,128)(2,1)S(1)} %copy-done, bf16[16,256]{1,0:T(8,128)(2,1)S(1)} %get-tuple-element.15.tail_ref, bf16[8,528,256]{2,1,0:T(8,128)(2,1)S(1)} %all-to-all-done.incoming_ref), custom_call_target="tpu_custom_call" | custom-call | flops 2000000000 | tf_op jit(solution)/shard_map/pallas_call | solution.py:226
  66.8 0.0 collective-permute-done.3.back_ref
  66.9 0.1 collective-permute-start.4
  67.0 1.6 %collective-permute-start.6 = (bf16[256,256]{1,0:T(8,128)(2,1)S(1)}, bf16[256,256]{1,0:T(8,128)(2,1)S(1)}, u32[]{:S(2)}, u32[]{:S(2)}) collective-permute-start(bf16[256,256]{1,0:T(8,128)(2,1)S(1)} %shard_map.99.refs_0_), channel_id=1, source_target_pairs={{0,2},{1,3},{2,0},{3,1},{4,6},{5,7},{6,4},{7,5},{8,10},{9,11},{10,... | collective-permute-start | bytes 393224 | tf_op jit(solution)/shard_map/ppermute | solution.py:422
  68.5 0.3 collective-permute-start.7
  68.8 0.0 collective-permute-done.4.held_ref.refs_1_
  68.8 0.5 shard_map.100.mark_ref
  69.3 0.0 copy-start.2
  69.4 0.8 %copy-done.2 = bf16[256,128]{1,0:T(8,128)(2,1)S(1)} copy-done((bf16[256,128]{1,0:T(8,128)(2,1)S(1)}, bf16[256,128]{1,0:T(8,128)(2,1)}, u32[]{:S(2)}) %copy-start.2) | copy-done | bytes 65560
  70.2 0.0 copy-start.1
  70.2 1.6 %shard_map.101 = (bf16[256,128]{1,0:T(8,128)(2,1)S(1)}, bf16[256,128]{1,0:T(8,128)(2,1)S(1)}) custom-call(s32[1]{0:T(128)} %bitcast.pair_ref, s32[1]{0:T(128)} %bitcast.1.side_ref, s32[1]{0:T(128)} %shard_map.100.mark_ref, bf16[256,128]{1,0:T(8,128)(2,1)S(1)} %copy-done.2, bf16[256,128]{1,0:T(8,128)(2,1)S(1)} %collective-permute-done.1.refs_0_.other_ref, ...), custom_call_target="tpu_custom_call" | custom-call | flops 6000000000 | tf_op jit(solution)/shard_map/pallas_call | solution.py:331
  71.8 2.3 %collective-permute-start.5 = (bf16[256,128]{1,0:T(8,128)(2,1)S(1)}, bf16[256,128]{1,0:T(8,128)(2,1)S(1)}, u32[]{:S(2)}, u32[]{:S(2)}) collective-permute-start(bf16[256,128]{1,0:T(8,128)(2,1)S(1)} %get-tuple-element.18), channel_id=1, source_target_pairs={{0,4},{4,0},{8,12},{12,8},{16,20},{20,16},{24,28},{28,24},{1,5},{5... | collective-permute-start | bytes 196616 | tf_op jit(solution)/shard_map/ppermute | solution.py:425
  74.1 0.0 collective-permute-done.8.refs_6_
  74.1 0.0 collective-permute-done.9.refs_7_
  74.1 0.0 collective-permute-done.6.refs_2_
  74.1 1.1 %collective-permute-done.7.refs_3_ = bf16[256,256]{1,0:T(8,128)(2,1)S(1)} collective-permute-done((bf16[256,256]{1,0:T(8,128)(2,1)S(1)}, bf16[256,256]{1,0:T(8,128)(2,1)S(1)}, u32[]{:S(2)}, u32[]{:S(2)}) %collective-permute-start.7) | collective-permute-done | bytes 131104 | tf_op jit(solution)/shard_map/ppermute | solution.py:422
  75.2 0.0 copy-done.1
  75.2 3.5 %shard_map.102 = bf16[256,2048]{1,0:T(8,128)(2,1)} custom-call(bf16[256,256]{1,0:T(8,128)(2,1)S(1)} %shard_map.99.refs_0_, bf16[256,256]{1,0:T(8,128)(2,1)S(1)} %collective-permute-done.4.held_ref.refs_1_, bf16[256,256]{1,0:T(8,128)(2,1)S(1)} %collective-permute-done.6.refs_2_, bf16[256,256]{1,0:T(8,128)(2,1)S(1)} %collective-permute-done.7.refs_3_, ...), custom_call_target="tpu_custom_call" | custom-call | flops 3000000000 | tf_op jit(solution)/shard_map/pallas_call | solution.py:368
  78.7 0.0 collective-permute-done.5
  78.8 0.7 maximum_select_fusion
  (2 shorter events, 0.0 us)
Async XLA Ops:
  4.3 57.3 %all-to-all-start = ((bf16[8,528,256]{2,1,0:T(8,128)(2,1)}), bf16[8,528,256]{2,1,0:T(8,128)(2,1)S(1)}, u32[]{:S(2)}, u32[]{:S(2)}) async-start(bf16[8,528,256]{2,1,0:T(8,128)(2,1)} %shard_map.95), calls=%async_computation | async-start | bytes 4325376 | tf_op jit(solution)/shard_map/all_to_all | solution.py:405
  11.6 8.4 %copy-start = (bf16[256,256]{1,0:T(8,128)(2,1)S(1)}, bf16[256,256]{1,0:T(8,128)(2,1)}, u32[]{:S(2)}) copy-start(bf16[256,256]{1,0:T(8,128)(2,1)} %queries_ref.3) | copy-start | bytes 393220
  16.0 15.6 %collective-permute-start.2 = (bf16[256,2048]{1,0:T(8,128)(2,1)}, bf16[256,2048]{1,0:T(8,128)(2,1)S(1)}, u32[]{:S(2)}, u32[]{:S(2)}) collective-permute-start(bf16[256,2048]{1,0:T(8,128)(2,1)} %get-tuple-element.13), channel_id=1, source_target_pairs={{0,1},{1,0},{2,3},{3,2},{4,5},{5,4},{6,7},{7,6},{8,9},{9,8},{10,11... | collective-permute-start | bytes 3145736 | tf_op jit(solution)/shard_map/ppermute | solution.py:415
  16.1 58.0 %collective-permute-start.8 = (bf16[256,2048]{1,0:T(8,128)(2,1)}, bf16[256,2048]{1,0:T(8,128)(2,1)}, u32[]{:S(2)}, u32[]{:S(2)}) collective-permute-start(bf16[256,2048]{1,0:T(8,128)(2,1)} %get-tuple-element.20), channel_id=1, source_target_pairs={{0,2},{1,3},{2,0},{3,1},{4,6},{5,7},{6,4},{7,5},{8,10},{9,11},{10,... | collective-permute-start | bytes 3145736 | tf_op jit(solution)/shard_map/ppermute | solution.py:415
  17.6 56.5 %collective-permute-start.9 = (bf16[256,2048]{1,0:T(8,128)(2,1)}, bf16[256,2048]{1,0:T(8,128)(2,1)}, u32[]{:S(2)}, u32[]{:S(2)}) collective-permute-start(bf16[256,2048]{1,0:T(8,128)(2,1)} %get-tuple-element.21), channel_id=1, source_target_pairs={{0,3},{1,2},{2,1},{3,0},{4,7},{5,6},{6,5},{7,4},{8,11},{9,10},{10,... | collective-permute-start | bytes 3145736 | tf_op jit(solution)/shard_map/ppermute | solution.py:415
  17.9 13.7 %collective-permute-start.1 = (bf16[256,128]{1,0:T(8,128)(2,1)}, bf16[256,128]{1,0:T(8,128)(2,1)S(1)}, u32[]{:S(2)}, u32[]{:S(2)}) collective-permute-start(bf16[256,128]{1,0:T(8,128)(2,1)} %get-tuple-element.12), channel_id=1, source_target_pairs={{0,4},{4,0},{8,12},{12,8},{16,20},{20,16},{24,28},{28,24},{1,5},{5... | collective-permute-start | bytes 196616 | tf_op jit(solution)/shard_map/ppermute | solution.py:413
  19.9 9.7 %collective-permute-start = (bf16[64,256]{1,0:T(8,128)(2,1)S(1)}, bf16[64,256]{1,0:T(8,128)(2,1)S(1)}, u32[]{:S(2)}, u32[]{:S(2)}) collective-permute-start(bf16[64,256]{1,0:T(8,128)(2,1)S(1)} %slice.3), channel_id=1, source_target_pairs={{4,0},{8,4},{12,8},{16,12},{20,16},{24,20},{28,24},{5,1},{9,5},{13... | collective-permute-start | bytes 98312 | tf_op jit(solution)/shard_map/ppermute | solution.py:417
  62.2 4.7 %collective-permute-start.3 = (bf16[64,256]{1,0:T(8,128)(2,1)S(1)}, bf16[64,256]{1,0:T(8,128)(2,1)S(1)}, u32[]{:S(2)}, u32[]{:S(2)}) collective-permute-start(bf16[64,256]{1,0:T(8,128)(2,1)S(1)} %get-tuple-element.14), channel_id=1, source_target_pairs={{0,4},{4,8},{8,12},{12,16},{16,20},{20,24},{24,28},{1,5},{5,9},{9,... | collective-permute-start | bytes 98312 | tf_op jit(solution)/shard_map/ppermute | solution.py:420
  66.9 1.9 %collective-permute-start.4 = (bf16[256,256]{1,0:T(8,128)(2,1)S(1)}, bf16[256,256]{1,0:T(8,128)(2,1)S(1)}, u32[]{:S(2)}, u32[]{:S(2)}) collective-permute-start(bf16[256,256]{1,0:T(8,128)(2,1)S(1)} %shard_map.99.refs_0_), channel_id=1, source_target_pairs={{0,1},{1,0},{2,3},{3,2},{4,5},{5,4},{6,7},{7,6},{8,9},{9,8},{10,11... | collective-permute-start | bytes 393224 | tf_op jit(solution)/shard_map/ppermute | solution.py:422
  67.0 7.1 %collective-permute-start.6 = (bf16[256,256]{1,0:T(8,128)(2,1)S(1)}, bf16[256,256]{1,0:T(8,128)(2,1)S(1)}, u32[]{:S(2)}, u32[]{:S(2)}) collective-permute-start(bf16[256,256]{1,0:T(8,128)(2,1)S(1)} %shard_map.99.refs_0_), channel_id=1, source_target_pairs={{0,2},{1,3},{2,0},{3,1},{4,6},{5,7},{6,4},{7,5},{8,10},{9,11},{10,... | collective-permute-start | bytes 393224 | tf_op jit(solution)/shard_map/ppermute | solution.py:422
  68.5 6.7 %collective-permute-start.7 = (bf16[256,256]{1,0:T(8,128)(2,1)S(1)}, bf16[256,256]{1,0:T(8,128)(2,1)S(1)}, u32[]{:S(2)}, u32[]{:S(2)}) collective-permute-start(bf16[256,256]{1,0:T(8,128)(2,1)S(1)} %shard_map.99.refs_0_), channel_id=1, source_target_pairs={{0,3},{1,2},{2,1},{3,0},{4,7},{5,6},{6,5},{7,4},{8,11},{9,10},{10,... | collective-permute-start | bytes 393224 | tf_op jit(solution)/shard_map/ppermute | solution.py:422
  69.3 0.8 %copy-start.2 = (bf16[256,128]{1,0:T(8,128)(2,1)S(1)}, bf16[256,128]{1,0:T(8,128)(2,1)}, u32[]{:S(2)}) copy-start(bf16[256,128]{1,0:T(8,128)(2,1)} %get-tuple-element.16.mine_ref) | copy-start | bytes 196612
  70.2 5.0 %copy-start.1 = (bf16[256,2048]{1,0:T(8,128)(2,1)S(1)}, bf16[256,2048]{1,0:T(8,128)(2,1)}, u32[]{:S(2)}) copy-start(bf16[256,2048]{1,0:T(8,128)(2,1)} %get-tuple-element.19.refs_4_) | copy-start | bytes 3145732
  71.8 7.0 %collective-permute-start.5 = (bf16[256,128]{1,0:T(8,128)(2,1)S(1)}, bf16[256,128]{1,0:T(8,128)(2,1)S(1)}, u32[]{:S(2)}, u32[]{:S(2)}) collective-permute-start(bf16[256,128]{1,0:T(8,128)(2,1)S(1)} %get-tuple-element.18), channel_id=1, source_target_pairs={{0,4},{4,0},{8,12},{12,8},{16,20},{20,16},{24,28},{28,24},{1,5},{5... | collective-permute-start | bytes 196616 | tf_op jit(solution)/shard_map/ppermute | solution.py:425

commit v15 on v14

--- a/solution.py
+++ b/solution.py
@@ -76,50 +76,58 @@
 
 
 def arrange_kernel(slot_ref, keys_ref, values_ref, own_keys, own_values, out_ref, *refs):
-    held_ref, own_ref, sems = refs
+    held_ref, own_ref, none_ref, slots, sems = refs
     count, length, width = keys_ref.shape
     indices = out_ref.shape[0]
     rows = own_keys.shape[0]
     front = 2 * length + LEAD
-    owners = [slot_ref[n] // count for n in range(count)]
-    at = 0
-    copies = []
-    for n, owner in enumerate(owners):
-        for half, source in enumerate((keys_ref, values_ref)):
-            target = held_ref.at[owner, pl.ds(half * length, length)]
-            copies.append(pltpu.make_async_copy(source.at[n], target, sems.at[at]))
-            at += 1
+    ins, outs = [], []
+
+    def copy(source, target):
+        return pltpu.make_async_copy(source, target, sems.at[len(ins) + len(outs)])
+
+    ins.append(copy(slot_ref, slots))
     for head in range(2):
         for half, source in enumerate((own_keys, own_values)):
             piece = source.at[:, pl.ds(head * HD, HD)]
-            target = own_ref.at[head, :, pl.ds(half * HD, HD)]
-            copies.append(pltpu.make_async_copy(piece, target, sems.at[at]))
-            at += 1
-    for copy in copies:
-        copy.start()
-    for index in range(indices):
-        held_ref[index, 2 * length :, :] = jnp.full((LEAD, width), -1, held_ref.dtype)
+            ins.append(copy(piece, own_ref.at[head, :, pl.ds(half * HD, HD)]))
+    for n in range(count):
+        for half, source in enumerate((keys_ref, values_ref)):
+            target = held_ref.at[n, pl.ds(half * length, length)]
+            ins.append(copy(source.at[n], target))
+    for each in ins:
+        each.start()
+    none_ref[...] = jnp.full((LEAD, width), -1, none_ref.dtype)
+    ins[0].wait()
+    owners = [slots[n] // count for n in range(count)]
     for n, owner in enumerate(owners):
-        place = (slot_ref[n] - owner * count).astype(jnp.float32)
-        held_ref[owner, 2 * length :, :] = jnp.full((LEAD, width), place).astype(held_ref.dtype)
-    outs = []
+        place = (slots[n] - owner * count).astype(jnp.float32)
+        held_ref[n, 2 * length :, :] = jnp.full((LEAD, width), place).astype(held_ref.dtype)
     for head in range(2):
-        copies[2 * count + 2 * head].wait()
-        copies[2 * count + 2 * head + 1].wait()
+        ins[1 + 2 * head].wait()
+        ins[2 + 2 * head].wait()
         for index in range(head, indices, 2):
-            target = out_ref.at[index, pl.ds(front, rows)]
-            outs.append(pltpu.make_async_copy(own_ref.at[head], target, sems.at[at]))
+            outs.append(copy(own_ref.at[head], out_ref.at[index, pl.ds(front, rows)]))
             outs[-1].start()
-            at += 1
-    for copy in copies[: 2 * count]:
-        copy.wait()
-    for index in range(indices):
-        source, target = held_ref.at[index], out_ref.at[index, pl.ds(0, front)]
-        outs.append(pltpu.make_async_copy(source, target, sems.at[at]))
+    for n, owner in enumerate(owners):
+        ins[5 + 2 * n].wait()
+        ins[6 + 2 * n].wait()
+        outs.append(copy(held_ref.at[n], out_ref.at[owner, pl.ds(0, front)]))
         outs[-1].start()
-        at += 1
-    for out in outs:
-        out.wait()
+    for each in outs:
+        each.wait()
+    if indices > count:
+        for index in range(indices):
+            taken = owners[0] == index
+            for owner in owners[1:]:
+                taken = taken | (owner == index)
+
+            @pl.when(jnp.logical_not(taken))
+            def _():
+                target = out_ref.at[index, pl.ds(2 * length, LEAD)]
+                empty = pltpu.make_async_copy(none_ref, target, sems.at[0])
+                empty.start()
+                empty.wait()
 
 
 def arrange(slots, keys, values, own_keys, own_values, indices):
@@ -129,12 +137,14 @@
     return pl.pallas_call(
         arrange_kernel,
         out_shape=jax.ShapeDtypeStruct((indices, front + rows, width), keys.dtype),
-        in_specs=[SMEM] + [ANY] * 4,
+        in_specs=[ANY] * 5,
         out_specs=ANY,
         scratch_shapes=[
-            pltpu.VMEM((indices, front, width), keys.dtype),
+            pltpu.VMEM((count, front, width), keys.dtype),
             pltpu.VMEM((2, rows, 2 * HD), keys.dtype),
-            pltpu.SemaphoreType.DMA((2 * count + 4 + 2 * indices,)),
+            pltpu.VMEM((LEAD, width), keys.dtype),
+            pltpu.SMEM((count,), jnp.int32),
+            pltpu.SemaphoreType.DMA((3 * count + 5 + indices,)),
         ],
         cost_estimate=takes(4),
     )(slots, keys, values, own_keys, own_values)
@@ -281,8 +291,12 @@
         k = incoming_ref[pl.ds(2 * at, 2), front:, :HD].reshape(rows, HD)
         for here in chunks:
             start = here.start
-            q_ref, offset = (mine_ref, start) if start < tile else (other_ref, start - tile)
-            s = dot_t(q_ref[offset : offset + chunk, :], k)
+            if start < tile:
+                lane = pl.multiple_of(side * HD, HD)
+                q = mine_ref[start : start + chunk, pl.ds(lane, HD)]
+            else:
+                q = other_ref[start - tile : start - tile + chunk, :]
+            s = dot_t(q, k)
             if fresh:
                 row = lax.broadcasted_iota(jnp.int32, (chunk, rows), 0) + start
                 col = lax.broadcasted_iota(jnp.int32, (chunk, rows), 1)
@@ -343,18 +357,27 @@
 
 
 def project_kernel(groups, *refs):
-    crossed_ref, out_ref, sems = refs[-3:]
-    terms, blocks = refs[:groups], refs[groups:-3]
+    crossed_ref, far_ref, out_ref, sems = refs[-4:]
+    terms, near, far = refs[:groups], refs[groups : groups + 2], refs[groups + 2 : -4]
     width = crossed_ref.shape[1]
+    depth = near[0].shape[0]
     tile = min(512, width)
+    columns = [slice(at, at + tile) for at in range(0, width, tile)]
+    copies = []
+    for turn, at in enumerate(columns):
+        for index, block in enumerate(far):
+            target = far_ref.at[turn, pl.ds(index * depth, depth)]
+            copies.append(pltpu.make_async_copy(block.at[:, at], target, sems.at[len(copies)]))
+            copies[-1].start()
     term = jnp.concatenate([held[...] for held in terms], axis=1)
     outs = []
-    for column in range(0, width, tile):
-        at = slice(column, column + tile)
-        weight = jnp.concatenate([block[:, at] for block in blocks], axis=0)
-        out_ref[:, at] = dot(term, weight).astype(out_ref.dtype)
+    for turn, at in enumerate(columns):
+        for copy in copies[turn * len(far) : (turn + 1) * len(far)]:
+            copy.wait()
+        weight = [block[:, at] for block in near] + [far_ref[turn]]
+        out_ref[:, at] = dot(term, jnp.concatenate(weight, axis=0)).astype(out_ref.dtype)
         out = pltpu.make_async_copy(
-            out_ref.at[:, at], crossed_ref.at[:, at], sems.at[len(outs)]
+            out_ref.at[:, at], crossed_ref.at[:, at], sems.at[len(copies) + turn]
         )
         out.start()
         outs.append(out)
@@ -362,21 +385,24 @@
         out.wait()
 
 
-def project(terms, blocks):
-    rows, width = terms[0].shape[0], blocks[0].shape[1]
-    operands = (*terms, *blocks)
+def project(terms, near, far):
+    rows, depth = terms[0].shape[0], near[0].shape[0]
+    width = near[0].shape[1]
+    tile = min(512, width)
+    turns = width // tile
     return pl.pallas_call(
         functools.partial(project_kernel, len(terms)),
         out_shape=jax.ShapeDtypeStruct((rows, width), jnp.bfloat16),
-        in_specs=[VMEM] * len(operands),
+        in_specs=[VMEM] * (len(terms) + 2) + [ANY] * len(far),
         out_specs=ANY,
         scratch_shapes=[
+            pltpu.VMEM((turns, len(far) * depth, tile), near[0].dtype),
             pltpu.VMEM((rows, width), jnp.bfloat16),
-            pltpu.SemaphoreType.DMA((width // min(512, width),)),
+            pltpu.SemaphoreType.DMA((turns * (len(far) + 1),)),
         ],
         compiler_params=PARAMS,
         cost_estimate=takes(3),
-    )(*operands)
+    )(*terms, *near, *far)
 
 
 def shards(queries, keys, values, cross_queries, nbr_keys, nbr_values, nbr_slot, w_cross):
@@ -405,9 +431,9 @@
         return lax.all_to_all(value, "ctx", split_axis=0, concat_axis=0, tiled=True)
 
     incoming = exchange(arrange(nbr_slot, nbr_keys, nbr_values, keys, values, count))
-    q_mine, q_away, own, *blocks = cut(
+    q_away, own, *blocks = cut(
         side, tp, (queries, w_cross),
-        [[(0, turn, 0, 0, HD, rows)] for turn in range(2)]
+        [[(0, 1, 0, 0, HD, rows)]]
         + [[(1, step, width, 0, width, depth)] for step in range(groups)],
     )
     q_other = lax.ppermute(q_away, "ctx", swap)
@@ -421,9 +447,9 @@
     cca = merge(back, other_attend(cross_queries, tail, incoming))
     terms = [cca] + [lax.ppermute(cca, "tp", across[step]) for step in range(1, groups)]
 
-    ours, theirs = self_attend(pair, side, touch(terms[1]), q_mine, q_other, incoming)
+    ours, theirs = self_attend(pair, side, touch(terms[1]), queries, q_other, incoming)
     attended = both(ours, lax.ppermute(theirs, "ctx", swap), 1)
-    crossed = project(terms, (own, beside, *direct))
+    crossed = project(terms, (own, beside), direct)
     return (attended, crossed)
 
 

time: 80 us -> 78.9 us (0.986)
  Pallas kernels: 15.9 us -> 14.7 us
    pallas_call x1, Pallas kernels: 3.64 us -> 2.53 us  [arrange(): pl.pallas_call(arrange_kernel, out_shape=jax.ShapeDtypeStruct((indices, f...]
  transfers between devices with their start and end apart: 11 -> 11, of which waited for: 4 -> 4; matrix products, arithmetic and copies ran while one was open for 0% -> 0% of each run, Pallas kernels for 15% -> 16%
where the time goes in v15:
time: 78.9 us; the launch traced here: 78.4 us
  waiting for transfers between devices  41.6 us (53%)
  starting transfers between devices  19.8 us (25%)
  Pallas kernels  14.7 us (19%)
  local copies, waits for them, and re-layouts  0.91 us (1%)
    all_to_all x1, waiting for transfers between devices, exchange(): return lax.all_to_all(value, 'ctx', split_axis=0, concat_axis=0, tiled=True)  29.9 us
    ppermute x1, waiting for transfers between devices, shards(): lax.ppermute(cross_queries[:BLOCK], 'ctx', [(i + 1, i) for i in range(cou...  8.42 us
    all_to_all x1, starting transfers between devices, exchange(): return lax.all_to_all(value, 'ctx', split_axis=0, concat_axis=0, tiled=True)  7.29 us
    pallas_call x1, Pallas kernels, cut(): pl.pallas_call(functools.partial(cut_kernel, plan), out_shape=tuple(shape...  4.33 us
    pallas_call x1, Pallas kernels, project(): pl.pallas_call(functools.partial(project_kernel, len(terms)), out_shape=j...  3.61 us
    ppermute x1, starting transfers between devices, shards(): back = lax.ppermute(onward, 'ctx', [(i, i + 1) for i in range(count - 1)])  3.02 us
    pallas_call x1, Pallas kernels, arrange(): pl.pallas_call(arrange_kernel, out_shape=jax.ShapeDtypeStruct((indices, f...  2.53 us
    ppermute x1, starting transfers between devices, shards(): attended = both(ours, lax.ppermute(theirs, 'ctx', swap), 1)  2.3 us
  transfers between devices with their start and end apart: 11, of which 4 were waited for; matrix products, arithmetic and copies ran while one was open for 0% of the time, Pallas kernels for 16%

profile of v15, /device:TPU:0, one launch (start us, length us, event | category | flops | bytes accessed | tf_op | source)
XLA Modules:
  0.0 78.4 jit_solution(3189961999688695501)
XLA Ops:
  0.6 2.5 %shard_map.95 = bf16[8,528,256]{2,1,0:T(8,128)(2,1)} custom-call(s32[8]{0:T(128)} %slot_ref.1, bf16[8,128,256]{2,1,0:T(8,128)(2,1)} %keys_ref.1, bf16[8,128,256]{2,1,0:T(8,128)(2,1)} %values_ref.1, bf16[256,256]{1,0:T(8,128)(2,1)} %own_keys.1, bf16[256,256]{1,0:T(8,128)(2,1)} %own_values.1), custom_call_target="tpu_custom_call" | custom-call | flops 4000000000 | tf_op jit(solution)/shard_map/pallas_call | solution.py:137
  3.2 7.3 %all-to-all-start = ((bf16[8,528,256]{2,1,0:T(8,128)(2,1)}), bf16[8,528,256]{2,1,0:T(8,128)(2,1)S(1)}, u32[]{:S(2)}, u32[]{:S(2)}) async-start(bf16[8,528,256]{2,1,0:T(8,128)(2,1)} %shard_map.95), calls=%async_computation | async-start | bytes 4325376 | tf_op jit(solution)/shard_map/all_to_all | solution.py:431
  10.5 0.0 copy-start
  10.5 4.3 %shard_map.96 = (bf16[256,128]{1,0:T(8,128)(2,1)}, bf16[256,2048]{1,0:T(8,128)(2,1)}, bf16[256,2048]{1,0:T(8,128)(2,1)}, bf16[256,2048]{1,0:T(8,128)(2,1)}, bf16[256,2048]{1,0:T(8,128)(2,1)}) custom-call(s32[1]{0:T(128)} %bitcast.1.side_ref, s32[1]{0:T(128)} %bitcast.2.tp_ref, bf16[256,256]{1,0:T(8,128)(2,1)} %mine_ref.1, bf16[256,8192]{1,0:T(8,128)(2,1)} %refs_1_.1), custom_call_target="tpu_custom_call" | custom-call | flops 2000000000 | tf_op jit(solution)/shard_map/pallas_call | solution.py:68
  14.8 0.1 collective-permute-start.2
  14.9 1.6 %collective-permute-start.8 = (bf16[256,2048]{1,0:T(8,128)(2,1)}, bf16[256,2048]{1,0:T(8,128)(2,1)}, u32[]{:S(2)}, u32[]{:S(2)}) collective-permute-start(bf16[256,2048]{1,0:T(8,128)(2,1)} %get-tuple-element.18), channel_id=1, source_target_pairs={{0,2},{1,3},{2,0},{3,1},{4,6},{5,7},{6,4},{7,5},{8,10},{9,11},{10,... | collective-permute-start | bytes 3145736 | tf_op jit(solution)/shard_map/ppermute | solution.py:441
  16.4 0.3 collective-permute-start.9
  16.7 2.0 %collective-permute-start.1 = (bf16[256,128]{1,0:T(8,128)(2,1)}, bf16[256,128]{1,0:T(8,128)(2,1)S(1)}, u32[]{:S(2)}, u32[]{:S(2)}) collective-permute-start(bf16[256,128]{1,0:T(8,128)(2,1)} %get-tuple-element.11), channel_id=1, source_target_pairs={{0,4},{4,0},{8,12},{12,8},{16,20},{20,16},{24,28},{28,24},{1,5},{5... | collective-permute-start | bytes 196616 | tf_op jit(solution)/shard_map/ppermute | solution.py:439
  18.8 0.0 copy-done
  18.8 1.3 %collective-permute-start = (bf16[64,256]{1,0:T(8,128)(2,1)S(1)}, bf16[64,256]{1,0:T(8,128)(2,1)S(1)}, u32[]{:S(2)}, u32[]{:S(2)}) collective-permute-start(bf16[64,256]{1,0:T(8,128)(2,1)S(1)} %slice.3), channel_id=1, source_target_pairs={{4,0},{8,4},{12,8},{16,12},{20,16},{24,20},{28,24},{5,1},{9,5},{13... | collective-permute-start | bytes 98312 | tf_op jit(solution)/shard_map/ppermute | solution.py:443
  20.1 8.4 %collective-permute-done.spill_ref = bf16[64,256]{1,0:T(8,128)(2,1)S(1)} collective-permute-done((bf16[64,256]{1,0:T(8,128)(2,1)S(1)}, bf16[64,256]{1,0:T(8,128)(2,1)S(1)}, u32[]{:S(2)}, u32[]{:S(2)}) %collective-permute-start) | collective-permute-done | bytes 32800 | tf_op jit(solution)/shard_map/ppermute | solution.py:443
  28.5 2.0 %collective-permute-done.1.refs_0_.other_ref = bf16[256,128]{1,0:T(8,128)(2,1)S(1)} collective-permute-done((bf16[256,128]{1,0:T(8,128)(2,1)}, bf16[256,128]{1,0:T(8,128)(2,1)S(1)}, u32[]{:S(2)}, u32[]{:S(2)}) %collective-permute-start.1) | collective-permute-done | bytes 65568 | tf_op jit(solution)/shard_map/ppermute | solution.py:439
  30.5 0.0 collective-permute-done.2.refs_1_.refs_5_
  30.5 29.9 %all-to-all-done.incoming_ref = bf16[8,528,256]{2,1,0:T(8,128)(2,1)S(1)} async-done(((bf16[8,528,256]{2,1,0:T(8,128)(2,1)}), bf16[8,528,256]{2,1,0:T(8,128)(2,1)S(1)}, u32[]{:S(2)}, u32[]{:S(2)}) %all-to-all-start) | async-done | bytes 2162720 | tf_op jit(solution)/shard_map/all_to_all | solution.py:431
  60.5 0.6 shard_map.97
  61.1 3.0 %collective-permute-start.3 = (bf16[64,256]{1,0:T(8,128)(2,1)S(1)}, bf16[64,256]{1,0:T(8,128)(2,1)S(1)}, u32[]{:S(2)}, u32[]{:S(2)}) collective-permute-start(bf16[64,256]{1,0:T(8,128)(2,1)S(1)} %get-tuple-element.13), channel_id=1, source_target_pairs={{0,4},{4,8},{8,12},{12,16},{16,20},{20,24},{24,28},{1,5},{5,9},{9,... | collective-permute-start | bytes 98312 | tf_op jit(solution)/shard_map/ppermute | solution.py:446
  64.1 1.6 %shard_map.98.answers_ref = bf16[256,256]{1,0:T(8,128)(2,1)S(1)} custom-call(bf16[256,256]{1,0:T(8,128)(2,1)S(1)} %copy-done, bf16[16,256]{1,0:T(8,128)(2,1)S(1)} %get-tuple-element.14.tail_ref, bf16[8,528,256]{2,1,0:T(8,128)(2,1)S(1)} %all-to-all-done.incoming_ref), custom_call_target="tpu_custom_call" | custom-call | flops 2000000000 | tf_op jit(solution)/shard_map/pallas_call | solution.py:236
  65.7 0.0 collective-permute-done.3.back_ref
  65.8 0.1 collective-permute-start.4
  65.9 1.6 %collective-permute-start.6 = (bf16[256,256]{1,0:T(8,128)(2,1)S(1)}, bf16[256,256]{1,0:T(8,128)(2,1)S(1)}, u32[]{:S(2)}, u32[]{:S(2)}) collective-permute-start(bf16[256,256]{1,0:T(8,128)(2,1)S(1)} %shard_map.99.refs_0_), channel_id=1, source_target_pairs={{0,2},{1,3},{2,0},{3,1},{4,6},{5,7},{6,4},{7,5},{8,10},{9,11},{10,... | collective-permute-start | bytes 393224 | tf_op jit(solution)/shard_map/ppermute | solution.py:448
  67.4 0.3 collective-permute-start.7
  67.7 0.0 collective-permute-done.4.held_ref.refs_1_
  67.7 0.5 shard_map.100.mark_ref
  68.2 0.0 copy-start.1
  68.3 0.9 %copy-done.1 = bf16[256,256]{1,0:T(8,128)(2,1)S(1)} copy-done((bf16[256,256]{1,0:T(8,128)(2,1)S(1)}, bf16[256,256]{1,0:T(8,128)(2,1)}, u32[]{:S(2)}) %copy-start.1) | copy-done | bytes 131096
  69.1 0.0 copy-start.2
  69.1 1.5 %shard_map.101 = (bf16[256,128]{1,0:T(8,128)(2,1)S(1)}, bf16[256,128]{1,0:T(8,128)(2,1)S(1)}) custom-call(s32[1]{0:T(128)} %bitcast.pair_ref, s32[1]{0:T(128)} %bitcast.1.side_ref, s32[1]{0:T(128)} %shard_map.100.mark_ref, bf16[256,256]{1,0:T(8,128)(2,1)S(1)} %copy-done.1, bf16[256,128]{1,0:T(8,128)(2,1)S(1)} %collective-permute-done.1.refs_0_.other_ref, ...), custom_call_target="tpu_custom_call" | custom-call | flops 6000000000 | tf_op jit(solution)/shard_map/pallas_call | solution.py:345
  70.6 2.3 %collective-permute-start.5 = (bf16[256,128]{1,0:T(8,128)(2,1)S(1)}, bf16[256,128]{1,0:T(8,128)(2,1)S(1)}, u32[]{:S(2)}, u32[]{:S(2)}) collective-permute-start(bf16[256,128]{1,0:T(8,128)(2,1)S(1)} %get-tuple-element.16), channel_id=1, source_target_pairs={{0,4},{4,0},{8,12},{12,8},{16,20},{20,16},{24,28},{28,24},{1,5},{5... | collective-permute-start | bytes 196616 | tf_op jit(solution)/shard_map/ppermute | solution.py:451
  72.9 0.0 collective-permute-done.8.refs_6_
  72.9 0.0 collective-permute-done.9.refs_7_
  72.9 0.0 collective-permute-done.6.refs_2_
  72.9 1.2 %collective-permute-done.7.refs_3_ = bf16[256,256]{1,0:T(8,128)(2,1)S(1)} collective-permute-done((bf16[256,256]{1,0:T(8,128)(2,1)S(1)}, bf16[256,256]{1,0:T(8,128)(2,1)S(1)}, u32[]{:S(2)}, u32[]{:S(2)}) %collective-permute-start.7) | collective-permute-done | bytes 131104 | tf_op jit(solution)/shard_map/ppermute | solution.py:448
  74.1 0.0 copy-done.2
  74.1 3.6 %shard_map.102 = bf16[256,2048]{1,0:T(8,128)(2,1)} custom-call(bf16[256,256]{1,0:T(8,128)(2,1)S(1)} %shard_map.99.refs_0_, bf16[256,256]{1,0:T(8,128)(2,1)S(1)} %collective-permute-done.4.held_ref.refs_1_, bf16[256,256]{1,0:T(8,128)(2,1)S(1)} %collective-permute-done.6.refs_2_, bf16[256,256]{1,0:T(8,128)(2,1)S(1)} %collective-permute-done.7.refs_3_, ...), custom_call_target="tpu_custom_call" | custom-call | flops 3000000000 | tf_op jit(solution)/shard_map/pallas_call | solution.py:393
  77.7 0.0 collective-permute-done.5
  77.7 0.7 maximum_select_fusion
  (2 shorter events, 0.0 us)
Async XLA Ops:
  3.2 57.3 %all-to-all-start = ((bf16[8,528,256]{2,1,0:T(8,128)(2,1)}), bf16[8,528,256]{2,1,0:T(8,128)(2,1)S(1)}, u32[]{:S(2)}, u32[]{:S(2)}) async-start(bf16[8,528,256]{2,1,0:T(8,128)(2,1)} %shard_map.95), calls=%async_computation | async-start | bytes 4325376 | tf_op jit(solution)/shard_map/all_to_all | solution.py:431
  10.5 8.3 %copy-start = (bf16[256,256]{1,0:T(8,128)(2,1)S(1)}, bf16[256,256]{1,0:T(8,128)(2,1)}, u32[]{:S(2)}) copy-start(bf16[256,256]{1,0:T(8,128)(2,1)} %queries_ref.3) | copy-start | bytes 393220
  14.8 15.7 %collective-permute-start.2 = (bf16[256,2048]{1,0:T(8,128)(2,1)}, bf16[256,2048]{1,0:T(8,128)(2,1)S(1)}, u32[]{:S(2)}, u32[]{:S(2)}) collective-permute-start(bf16[256,2048]{1,0:T(8,128)(2,1)} %get-tuple-element.12), channel_id=1, source_target_pairs={{0,1},{1,0},{2,3},{3,2},{4,5},{5,4},{6,7},{7,6},{8,9},{9,8},{10,11... | collective-permute-start | bytes 3145736 | tf_op jit(solution)/shard_map/ppermute | solution.py:441
  14.9 58.1 %collective-permute-start.8 = (bf16[256,2048]{1,0:T(8,128)(2,1)}, bf16[256,2048]{1,0:T(8,128)(2,1)}, u32[]{:S(2)}, u32[]{:S(2)}) collective-permute-start(bf16[256,2048]{1,0:T(8,128)(2,1)} %get-tuple-element.18), channel_id=1, source_target_pairs={{0,2},{1,3},{2,0},{3,1},{4,6},{5,7},{6,4},{7,5},{8,10},{9,11},{10,... | collective-permute-start | bytes 3145736 | tf_op jit(solution)/shard_map/ppermute | solution.py:441
  16.4 56.5 %collective-permute-start.9 = (bf16[256,2048]{1,0:T(8,128)(2,1)}, bf16[256,2048]{1,0:T(8,128)(2,1)}, u32[]{:S(2)}, u32[]{:S(2)}) collective-permute-start(bf16[256,2048]{1,0:T(8,128)(2,1)} %get-tuple-element.19), channel_id=1, source_target_pairs={{0,3},{1,2},{2,1},{3,0},{4,7},{5,6},{6,5},{7,4},{8,11},{9,10},{10,... | collective-permute-start | bytes 3145736 | tf_op jit(solution)/shard_map/ppermute | solution.py:441
  16.7 13.8 %collective-permute-start.1 = (bf16[256,128]{1,0:T(8,128)(2,1)}, bf16[256,128]{1,0:T(8,128)(2,1)S(1)}, u32[]{:S(2)}, u32[]{:S(2)}) collective-permute-start(bf16[256,128]{1,0:T(8,128)(2,1)} %get-tuple-element.11), channel_id=1, source_target_pairs={{0,4},{4,0},{8,12},{12,8},{16,20},{20,16},{24,28},{28,24},{1,5},{5... | collective-permute-start | bytes 196616 | tf_op jit(solution)/shard_map/ppermute | solution.py:439
  18.8 9.7 %collective-permute-start = (bf16[64,256]{1,0:T(8,128)(2,1)S(1)}, bf16[64,256]{1,0:T(8,128)(2,1)S(1)}, u32[]{:S(2)}, u32[]{:S(2)}) collective-permute-start(bf16[64,256]{1,0:T(8,128)(2,1)S(1)} %slice.3), channel_id=1, source_target_pairs={{4,0},{8,4},{12,8},{16,12},{20,16},{24,20},{28,24},{5,1},{9,5},{13... | collective-permute-start | bytes 98312 | tf_op jit(solution)/shard_map/ppermute | solution.py:443
  61.1 4.7 %collective-permute-start.3 = (bf16[64,256]{1,0:T(8,128)(2,1)S(1)}, bf16[64,256]{1,0:T(8,128)(2,1)S(1)}, u32[]{:S(2)}, u32[]{:S(2)}) collective-permute-start(bf16[64,256]{1,0:T(8,128)(2,1)S(1)} %get-tuple-element.13), channel_id=1, source_target_pairs={{0,4},{4,8},{8,12},{12,16},{16,20},{20,24},{24,28},{1,5},{5,9},{9,... | collective-permute-start | bytes 98312 | tf_op jit(solution)/shard_map/ppermute | solution.py:446
  65.8 1.9 %collective-permute-start.4 = (bf16[256,256]{1,0:T(8,128)(2,1)S(1)}, bf16[256,256]{1,0:T(8,128)(2,1)S(1)}, u32[]{:S(2)}, u32[]{:S(2)}) collective-permute-start(bf16[256,256]{1,0:T(8,128)(2,1)S(1)} %shard_map.99.refs_0_), channel_id=1, source_target_pairs={{0,1},{1,0},{2,3},{3,2},{4,5},{5,4},{6,7},{7,6},{8,9},{9,8},{10,11... | collective-permute-start | bytes 393224 | tf_op jit(solution)/shard_map/ppermute | solution.py:448
  65.9 7.1 %collective-permute-start.6 = (bf16[256,256]{1,0:T(8,128)(2,1)S(1)}, bf16[256,256]{1,0:T(8,128)(2,1)S(1)}, u32[]{:S(2)}, u32[]{:S(2)}) collective-permute-start(bf16[256,256]{1,0:T(8,128)(2,1)S(1)} %shard_map.99.refs_0_), channel_id=1, source_target_pairs={{0,2},{1,3},{2,0},{3,1},{4,6},{5,7},{6,4},{7,5},{8,10},{9,11},{10,... | collective-permute-start | bytes 393224 | tf_op jit(solution)/shard_map/ppermute | solution.py:448
  67.4 6.7 %collective-permute-start.7 = (bf16[256,256]{1,0:T(8,128)(2,1)S(1)}, bf16[256,256]{1,0:T(8,128)(2,1)S(1)}, u32[]{:S(2)}, u32[]{:S(2)}) collective-permute-start(bf16[256,256]{1,0:T(8,128)(2,1)S(1)} %shard_map.99.refs_0_), channel_id=1, source_target_pairs={{0,3},{1,2},{2,1},{3,0},{4,7},{5,6},{6,5},{7,4},{8,11},{9,10},{10,... | collective-permute-start | bytes 393224 | tf_op jit(solution)/shard_map/ppermute | solution.py:448
  68.2 0.9 %copy-start.1 = (bf16[256,256]{1,0:T(8,128)(2,1)S(1)}, bf16[256,256]{1,0:T(8,128)(2,1)}, u32[]{:S(2)}) copy-start(bf16[256,256]{1,0:T(8,128)(2,1)} %mine_ref.1) | copy-start | bytes 393220
  69.1 5.0 %copy-start.2 = (bf16[256,2048]{1,0:T(8,128)(2,1)S(1)}, bf16[256,2048]{1,0:T(8,128)(2,1)}, u32[]{:S(2)}) copy-start(bf16[256,2048]{1,0:T(8,128)(2,1)} %get-tuple-element.17.refs_4_) | copy-start | bytes 3145732
  70.6 7.1 %collective-permute-start.5 = (bf16[256,128]{1,0:T(8,128)(2,1)S(1)}, bf16[256,128]{1,0:T(8,128)(2,1)S(1)}, u32[]{:S(2)}, u32[]{:S(2)}) collective-permute-start(bf16[256,128]{1,0:T(8,128)(2,1)S(1)} %get-tuple-element.16), channel_id=1, source_target_pairs={{0,4},{4,0},{8,12},{12,8},{16,20},{20,16},{24,28},{28,24},{1,5},{5... | collective-permute-start | bytes 196616 | tf_op jit(solution)/shard_map/ppermute | solution.py:451

commit v16 on v15

--- a/solution.py
+++ b/solution.py
@@ -357,25 +357,24 @@
 
 
 def project_kernel(groups, *refs):
-    crossed_ref, far_ref, out_ref, sems = refs[-4:]
-    terms, near, far = refs[:groups], refs[groups : groups + 2], refs[groups + 2 : -4]
+    crossed_ref, weight_ref, out_ref, sems = refs[-4:]
+    terms, blocks = refs[:groups], refs[groups:-4]
     width = crossed_ref.shape[1]
-    depth = near[0].shape[0]
+    depth = blocks[0].shape[0]
     tile = min(512, width)
     columns = [slice(at, at + tile) for at in range(0, width, tile)]
     copies = []
     for turn, at in enumerate(columns):
-        for index, block in enumerate(far):
-            target = far_ref.at[turn, pl.ds(index * depth, depth)]
+        for index, block in enumerate(blocks):
+            target = weight_ref.at[turn, pl.ds(index * depth, depth)]
             copies.append(pltpu.make_async_copy(block.at[:, at], target, sems.at[len(copies)]))
             copies[-1].start()
     term = jnp.concatenate([held[...] for held in terms], axis=1)
     outs = []
     for turn, at in enumerate(columns):
-        for copy in copies[turn * len(far) : (turn + 1) * len(far)]:
+        for copy in copies[turn * groups : (turn + 1) * groups]:
             copy.wait()
-        weight = [block[:, at] for block in near] + [far_ref[turn]]
-        out_ref[:, at] = dot(term, jnp.concatenate(weight, axis=0)).astype(out_ref.dtype)
+        out_ref[:, at] = dot(term, weight_ref[turn]).astype(out_ref.dtype)
         out = pltpu.make_async_copy(
             out_ref.at[:, at], crossed_ref.at[:, at], sems.at[len(copies) + turn]
         )
@@ -385,24 +384,25 @@
         out.wait()
 
 
-def project(terms, near, far):
-    rows, depth = terms[0].shape[0], near[0].shape[0]
-    width = near[0].shape[1]
+def project(terms, blocks):
+    groups = len(terms)
+    rows = terms[0].shape[0]
+    depth, width = blocks[0].shape
     tile = min(512, width)
     turns = width // tile
     return pl.pallas_call(
-        functools.partial(project_kernel, len(terms)),
+        functools.partial(project_kernel, groups),
         out_shape=jax.ShapeDtypeStruct((rows, width), jnp.bfloat16),
-        in_specs=[VMEM] * (len(terms) + 2) + [ANY] * len(far),
+        in_specs=[VMEM] * groups + [ANY] * groups,
         out_specs=ANY,
         scratch_shapes=[
-            pltpu.VMEM((turns, len(far) * depth, tile), near[0].dtype),
+            pltpu.VMEM((turns, groups * depth, tile), blocks[0].dtype),
             pltpu.VMEM((rows, width), jnp.bfloat16),
-            pltpu.SemaphoreType.DMA((turns * (len(far) + 1),)),
+            pltpu.SemaphoreType.DMA((turns * (groups + 1),)),
         ],
         compiler_params=PARAMS,
         cost_estimate=takes(3),
-    )(*terms, *near, *far)
+    )(*terms, *blocks)
 
 
 def shards(queries, keys, values, cross_queries, nbr_keys, nbr_values, nbr_slot, w_cross):
@@ -449,7 +449,7 @@
 
     ours, theirs = self_attend(pair, side, touch(terms[1]), queries, q_other, incoming)
     attended = both(ours, lax.ppermute(theirs, "ctx", swap), 1)
-    crossed = project(terms, (own, beside), direct)
+    crossed = project(terms, (own, beside, *direct))
     return (attended, crossed)
 
 

time: 78.9 us -> 79 us (level)
  no operation moved by 1% of the time
where the time goes in v16:
time: 79 us; the launch traced here: 78.5 us
  waiting for transfers between devices  41.6 us (53%)
  starting transfers between devices  19.8 us (25%)
  Pallas kernels  14.8 us (19%)
  local copies, waits for them, and re-layouts  0.91 us (1%)
    all_to_all x1, waiting for transfers between devices, exchange(): return lax.all_to_all(value, 'ctx', split_axis=0, concat_axis=0, tiled=True)  29.9 us
    ppermute x1, waiting for transfers between devices, shards(): lax.ppermute(cross_queries[:BLOCK], 'ctx', [(i + 1, i) for i in range(cou...  8.42 us
    all_to_all x1, starting transfers between devices, exchange(): return lax.all_to_all(value, 'ctx', split_axis=0, concat_axis=0, tiled=True)  7.29 us
    pallas_call x1, Pallas kernels, cut(): pl.pallas_call(functools.partial(cut_kernel, plan), out_shape=tuple(shape...  4.33 us
    pallas_call x1, Pallas kernels, project(): pl.pallas_call(functools.partial(project_kernel, groups), out_shape=jax.S...  3.72 us
    ppermute x1, starting transfers between devices, shards(): back = lax.ppermute(onward, 'ctx', [(i, i + 1) for i in range(count - 1)])  3.02 us
    pallas_call x1, Pallas kernels, arrange(): pl.pallas_call(arrange_kernel, out_shape=jax.ShapeDtypeStruct((indices, f...  2.53 us
    ppermute x1, starting transfers between devices, shards(): attended = both(ours, lax.ppermute(theirs, 'ctx', swap), 1)  2.3 us
  transfers between devices with their start and end apart: 11, of which 4 were waited for; matrix products, arithmetic and copies ran while one was open for 0% of the time, Pallas kernels for 16%

profile of v16, /device:TPU:0, one launch (start us, length us, event | category | flops | bytes accessed | tf_op | source)
XLA Modules:
  0.0 78.5 jit_solution(337149203336365231)
XLA Ops:
  0.6 2.5 %shard_map.95 = bf16[8,528,256]{2,1,0:T(8,128)(2,1)} custom-call(s32[8]{0:T(128)} %slot_ref.1, bf16[8,128,256]{2,1,0:T(8,128)(2,1)} %keys_ref.1, bf16[8,128,256]{2,1,0:T(8,128)(2,1)} %values_ref.1, bf16[256,256]{1,0:T(8,128)(2,1)} %own_keys.1, bf16[256,256]{1,0:T(8,128)(2,1)} %own_values.1), custom_call_target="tpu_custom_call" | custom-call | flops 4000000000 | tf_op jit(solution)/shard_map/pallas_call | solution.py:137
  3.2 7.3 %all-to-all-start = ((bf16[8,528,256]{2,1,0:T(8,128)(2,1)}), bf16[8,528,256]{2,1,0:T(8,128)(2,1)S(1)}, u32[]{:S(2)}, u32[]{:S(2)}) async-start(bf16[8,528,256]{2,1,0:T(8,128)(2,1)} %shard_map.95), calls=%async_computation | async-start | bytes 4325376 | tf_op jit(solution)/shard_map/all_to_all | solution.py:431
  10.5 0.0 copy-start
  10.5 4.3 %shard_map.96 = (bf16[256,128]{1,0:T(8,128)(2,1)}, bf16[256,2048]{1,0:T(8,128)(2,1)}, bf16[256,2048]{1,0:T(8,128)(2,1)}, bf16[256,2048]{1,0:T(8,128)(2,1)}, bf16[256,2048]{1,0:T(8,128)(2,1)}) custom-call(s32[1]{0:T(128)} %bitcast.1.side_ref, s32[1]{0:T(128)} %bitcast.2.tp_ref, bf16[256,256]{1,0:T(8,128)(2,1)} %mine_ref.1, bf16[256,8192]{1,0:T(8,128)(2,1)} %refs_1_.1), custom_call_target="tpu_custom_call" | custom-call | flops 2000000000 | tf_op jit(solution)/shard_map/pallas_call | solution.py:68
  14.8 0.1 collective-permute-start.2
  14.9 1.6 %collective-permute-start.8 = (bf16[256,2048]{1,0:T(8,128)(2,1)}, bf16[256,2048]{1,0:T(8,128)(2,1)}, u32[]{:S(2)}, u32[]{:S(2)}) collective-permute-start(bf16[256,2048]{1,0:T(8,128)(2,1)} %get-tuple-element.18), channel_id=1, source_target_pairs={{0,2},{1,3},{2,0},{3,1},{4,6},{5,7},{6,4},{7,5},{8,10},{9,11},{10,... | collective-permute-start | bytes 3145736 | tf_op jit(solution)/shard_map/ppermute | solution.py:441
  16.4 0.3 collective-permute-start.9
  16.7 2.0 %collective-permute-start.1 = (bf16[256,128]{1,0:T(8,128)(2,1)}, bf16[256,128]{1,0:T(8,128)(2,1)S(1)}, u32[]{:S(2)}, u32[]{:S(2)}) collective-permute-start(bf16[256,128]{1,0:T(8,128)(2,1)} %get-tuple-element.11), channel_id=1, source_target_pairs={{0,4},{4,0},{8,12},{12,8},{16,20},{20,16},{24,28},{28,24},{1,5},{5... | collective-permute-start | bytes 196616 | tf_op jit(solution)/shard_map/ppermute | solution.py:439
  18.8 0.0 copy-done
  18.8 1.3 %collective-permute-start = (bf16[64,256]{1,0:T(8,128)(2,1)S(1)}, bf16[64,256]{1,0:T(8,128)(2,1)S(1)}, u32[]{:S(2)}, u32[]{:S(2)}) collective-permute-start(bf16[64,256]{1,0:T(8,128)(2,1)S(1)} %slice.3), channel_id=1, source_target_pairs={{4,0},{8,4},{12,8},{16,12},{20,16},{24,20},{28,24},{5,1},{9,5},{13... | collective-permute-start | bytes 98312 | tf_op jit(solution)/shard_map/ppermute | solution.py:443
  20.1 8.4 %collective-permute-done.spill_ref = bf16[64,256]{1,0:T(8,128)(2,1)S(1)} collective-permute-done((bf16[64,256]{1,0:T(8,128)(2,1)S(1)}, bf16[64,256]{1,0:T(8,128)(2,1)S(1)}, u32[]{:S(2)}, u32[]{:S(2)}) %collective-permute-start) | collective-permute-done | bytes 32800 | tf_op jit(solution)/shard_map/ppermute | solution.py:443
  28.5 2.0 %collective-permute-done.1.refs_0_.other_ref = bf16[256,128]{1,0:T(8,128)(2,1)S(1)} collective-permute-done((bf16[256,128]{1,0:T(8,128)(2,1)}, bf16[256,128]{1,0:T(8,128)(2,1)S(1)}, u32[]{:S(2)}, u32[]{:S(2)}) %collective-permute-start.1) | collective-permute-done | bytes 65568 | tf_op jit(solution)/shard_map/ppermute | solution.py:439
  30.5 0.0 collective-permute-done.2.refs_1_.refs_5_
  30.5 29.9 %all-to-all-done.incoming_ref = bf16[8,528,256]{2,1,0:T(8,128)(2,1)S(1)} async-done(((bf16[8,528,256]{2,1,0:T(8,128)(2,1)}), bf16[8,528,256]{2,1,0:T(8,128)(2,1)S(1)}, u32[]{:S(2)}, u32[]{:S(2)}) %all-to-all-start) | async-done | bytes 2162720 | tf_op jit(solution)/shard_map/all_to_all | solution.py:431
  60.5 0.6 shard_map.97
  61.1 3.0 %collective-permute-start.3 = (bf16[64,256]{1,0:T(8,128)(2,1)S(1)}, bf16[64,256]{1,0:T(8,128)(2,1)S(1)}, u32[]{:S(2)}, u32[]{:S(2)}) collective-permute-start(bf16[64,256]{1,0:T(8,128)(2,1)S(1)} %get-tuple-element.13), channel_id=1, source_target_pairs={{0,4},{4,8},{8,12},{12,16},{16,20},{20,24},{24,28},{1,5},{5,9},{9,... | collective-permute-start | bytes 98312 | tf_op jit(solution)/shard_map/ppermute | solution.py:446
  64.1 1.6 %shard_map.98.answers_ref = bf16[256,256]{1,0:T(8,128)(2,1)S(1)} custom-call(bf16[256,256]{1,0:T(8,128)(2,1)S(1)} %copy-done, bf16[16,256]{1,0:T(8,128)(2,1)S(1)} %get-tuple-element.14.tail_ref, bf16[8,528,256]{2,1,0:T(8,128)(2,1)S(1)} %all-to-all-done.incoming_ref), custom_call_target="tpu_custom_call" | custom-call | flops 2000000000 | tf_op jit(solution)/shard_map/pallas_call | solution.py:236
  65.7 0.0 collective-permute-done.3.back_ref
  65.8 0.1 collective-permute-start.4
  65.9 1.6 %collective-permute-start.6 = (bf16[256,256]{1,0:T(8,128)(2,1)S(1)}, bf16[256,256]{1,0:T(8,128)(2,1)S(1)}, u32[]{:S(2)}, u32[]{:S(2)}) collective-permute-start(bf16[256,256]{1,0:T(8,128)(2,1)S(1)} %shard_map.99.refs_0_), channel_id=1, source_target_pairs={{0,2},{1,3},{2,0},{3,1},{4,6},{5,7},{6,4},{7,5},{8,10},{9,11},{10,... | collective-permute-start | bytes 393224 | tf_op jit(solution)/shard_map/ppermute | solution.py:448
  67.4 0.3 collective-permute-start.7
  67.7 0.0 collective-permute-done.4.held_ref.refs_1_
  67.7 0.5 shard_map.100.mark_ref
  68.2 0.0 copy-start.1
  68.3 0.9 %copy-done.1 = bf16[256,256]{1,0:T(8,128)(2,1)S(1)} copy-done((bf16[256,256]{1,0:T(8,128)(2,1)S(1)}, bf16[256,256]{1,0:T(8,128)(2,1)}, u32[]{:S(2)}) %copy-start.1) | copy-done | bytes 131096
  69.1 0.0 copy-start.2
  69.1 1.5 %shard_map.101 = (bf16[256,128]{1,0:T(8,128)(2,1)S(1)}, bf16[256,128]{1,0:T(8,128)(2,1)S(1)}) custom-call(s32[1]{0:T(128)} %bitcast.pair_ref, s32[1]{0:T(128)} %bitcast.1.side_ref, s32[1]{0:T(128)} %shard_map.100.mark_ref, bf16[256,256]{1,0:T(8,128)(2,1)S(1)} %copy-done.1, bf16[256,128]{1,0:T(8,128)(2,1)S(1)} %collective-permute-done.1.refs_0_.other_ref, ...), custom_call_target="tpu_custom_call" | custom-call | flops 6000000000 | tf_op jit(solution)/shard_map/pallas_call | solution.py:345
  70.6 2.3 %collective-permute-start.5 = (bf16[256,128]{1,0:T(8,128)(2,1)S(1)}, bf16[256,128]{1,0:T(8,128)(2,1)S(1)}, u32[]{:S(2)}, u32[]{:S(2)}) collective-permute-start(bf16[256,128]{1,0:T(8,128)(2,1)S(1)} %get-tuple-element.16), channel_id=1, source_target_pairs={{0,4},{4,0},{8,12},{12,8},{16,20},{20,16},{24,28},{28,24},{1,5},{5... | collective-permute-start | bytes 196616 | tf_op jit(solution)/shard_map/ppermute | solution.py:451
  72.9 0.0 collective-permute-done.8.refs_6_
  72.9 0.0 collective-permute-done.9.refs_7_
  72.9 0.0 collective-permute-done.6.refs_2_
  72.9 1.2 %collective-permute-done.7.refs_3_ = bf16[256,256]{1,0:T(8,128)(2,1)S(1)} collective-permute-done((bf16[256,256]{1,0:T(8,128)(2,1)S(1)}, bf16[256,256]{1,0:T(8,128)(2,1)S(1)}, u32[]{:S(2)}, u32[]{:S(2)}) %collective-permute-start.7) | collective-permute-done | bytes 131104 | tf_op jit(solution)/shard_map/ppermute | solution.py:448
  74.1 0.0 copy-done.2
  74.1 3.7 %shard_map.102 = bf16[256,2048]{1,0:T(8,128)(2,1)} custom-call(bf16[256,256]{1,0:T(8,128)(2,1)S(1)} %shard_map.99.refs_0_, bf16[256,256]{1,0:T(8,128)(2,1)S(1)} %collective-permute-done.4.held_ref.refs_1_, bf16[256,256]{1,0:T(8,128)(2,1)S(1)} %collective-permute-done.6.refs_2_, bf16[256,256]{1,0:T(8,128)(2,1)S(1)} %collective-permute-done.7.refs_3_, ...), custom_call_target="tpu_custom_call" | custom-call | flops 3000000000 | tf_op jit(solution)/shard_map/pallas_call | solution.py:393
  77.8 0.0 collective-permute-done.5
  77.8 0.7 maximum_select_fusion
  (2 shorter events, 0.0 us)
Async XLA Ops:
  3.2 57.3 %all-to-all-start = ((bf16[8,528,256]{2,1,0:T(8,128)(2,1)}), bf16[8,528,256]{2,1,0:T(8,128)(2,1)S(1)}, u32[]{:S(2)}, u32[]{:S(2)}) async-start(bf16[8,528,256]{2,1,0:T(8,128)(2,1)} %shard_map.95), calls=%async_computation | async-start | bytes 4325376 | tf_op jit(solution)/shard_map/all_to_all | solution.py:431
  10.5 8.3 %copy-start = (bf16[256,256]{1,0:T(8,128)(2,1)S(1)}, bf16[256,256]{1,0:T(8,128)(2,1)}, u32[]{:S(2)}) copy-start(bf16[256,256]{1,0:T(8,128)(2,1)} %queries_ref.3) | copy-start | bytes 393220
  14.8 15.7 %collective-permute-start.2 = (bf16[256,2048]{1,0:T(8,128)(2,1)}, bf16[256,2048]{1,0:T(8,128)(2,1)S(1)}, u32[]{:S(2)}, u32[]{:S(2)}) collective-permute-start(bf16[256,2048]{1,0:T(8,128)(2,1)} %get-tuple-element.12), channel_id=1, source_target_pairs={{0,1},{1,0},{2,3},{3,2},{4,5},{5,4},{6,7},{7,6},{8,9},{9,8},{10,11... | collective-permute-start | bytes 3145736 | tf_op jit(solution)/shard_map/ppermute | solution.py:441
  14.9 58.1 %collective-permute-start.8 = (bf16[256,2048]{1,0:T(8,128)(2,1)}, bf16[256,2048]{1,0:T(8,128)(2,1)}, u32[]{:S(2)}, u32[]{:S(2)}) collective-permute-start(bf16[256,2048]{1,0:T(8,128)(2,1)} %get-tuple-element.18), channel_id=1, source_target_pairs={{0,2},{1,3},{2,0},{3,1},{4,6},{5,7},{6,4},{7,5},{8,10},{9,11},{10,... | collective-permute-start | bytes 3145736 | tf_op jit(solution)/shard_map/ppermute | solution.py:441
  16.4 56.5 %collective-permute-start.9 = (bf16[256,2048]{1,0:T(8,128)(2,1)}, bf16[256,2048]{1,0:T(8,128)(2,1)}, u32[]{:S(2)}, u32[]{:S(2)}) collective-permute-start(bf16[256,2048]{1,0:T(8,128)(2,1)} %get-tuple-element.19), channel_id=1, source_target_pairs={{0,3},{1,2},{2,1},{3,0},{4,7},{5,6},{6,5},{7,4},{8,11},{9,10},{10,... | collective-permute-start | bytes 3145736 | tf_op jit(solution)/shard_map/ppermute | solution.py:441
  16.7 13.8 %collective-permute-start.1 = (bf16[256,128]{1,0:T(8,128)(2,1)}, bf16[256,128]{1,0:T(8,128)(2,1)S(1)}, u32[]{:S(2)}, u32[]{:S(2)}) collective-permute-start(bf16[256,128]{1,0:T(8,128)(2,1)} %get-tuple-element.11), channel_id=1, source_target_pairs={{0,4},{4,0},{8,12},{12,8},{16,20},{20,16},{24,28},{28,24},{1,5},{5... | collective-permute-start | bytes 196616 | tf_op jit(solution)/shard_map/ppermute | solution.py:439
  18.8 9.7 %collective-permute-start = (bf16[64,256]{1,0:T(8,128)(2,1)S(1)}, bf16[64,256]{1,0:T(8,128)(2,1)S(1)}, u32[]{:S(2)}, u32[]{:S(2)}) collective-permute-start(bf16[64,256]{1,0:T(8,128)(2,1)S(1)} %slice.3), channel_id=1, source_target_pairs={{4,0},{8,4},{12,8},{16,12},{20,16},{24,20},{28,24},{5,1},{9,5},{13... | collective-permute-start | bytes 98312 | tf_op jit(solution)/shard_map/ppermute | solution.py:443
  61.1 4.7 %collective-permute-start.3 = (bf16[64,256]{1,0:T(8,128)(2,1)S(1)}, bf16[64,256]{1,0:T(8,128)(2,1)S(1)}, u32[]{:S(2)}, u32[]{:S(2)}) collective-permute-start(bf16[64,256]{1,0:T(8,128)(2,1)S(1)} %get-tuple-element.13), channel_id=1, source_target_pairs={{0,4},{4,8},{8,12},{12,16},{16,20},{20,24},{24,28},{1,5},{5,9},{9,... | collective-permute-start | bytes 98312 | tf_op jit(solution)/shard_map/ppermute | solution.py:446
  65.8 1.9 %collective-permute-start.4 = (bf16[256,256]{1,0:T(8,128)(2,1)S(1)}, bf16[256,256]{1,0:T(8,128)(2,1)S(1)}, u32[]{:S(2)}, u32[]{:S(2)}) collective-permute-start(bf16[256,256]{1,0:T(8,128)(2,1)S(1)} %shard_map.99.refs_0_), channel_id=1, source_target_pairs={{0,1},{1,0},{2,3},{3,2},{4,5},{5,4},{6,7},{7,6},{8,9},{9,8},{10,11... | collective-permute-start | bytes 393224 | tf_op jit(solution)/shard_map/ppermute | solution.py:448
  65.9 7.1 %collective-permute-start.6 = (bf16[256,256]{1,0:T(8,128)(2,1)S(1)}, bf16[256,256]{1,0:T(8,128)(2,1)S(1)}, u32[]{:S(2)}, u32[]{:S(2)}) collective-permute-start(bf16[256,256]{1,0:T(8,128)(2,1)S(1)} %shard_map.99.refs_0_), channel_id=1, source_target_pairs={{0,2},{1,3},{2,0},{3,1},{4,6},{5,7},{6,4},{7,5},{8,10},{9,11},{10,... | collective-permute-start | bytes 393224 | tf_op jit(solution)/shard_map/ppermute | solution.py:448
  67.4 6.7 %collective-permute-start.7 = (bf16[256,256]{1,0:T(8,128)(2,1)S(1)}, bf16[256,256]{1,0:T(8,128)(2,1)S(1)}, u32[]{:S(2)}, u32[]{:S(2)}) collective-permute-start(bf16[256,256]{1,0:T(8,128)(2,1)S(1)} %shard_map.99.refs_0_), channel_id=1, source_target_pairs={{0,3},{1,2},{2,1},{3,0},{4,7},{5,6},{6,5},{7,4},{8,11},{9,10},{10,... | collective-permute-start | bytes 393224 | tf_op jit(solution)/shard_map/ppermute | solution.py:448
  68.2 0.9 %copy-start.1 = (bf16[256,256]{1,0:T(8,128)(2,1)S(1)}, bf16[256,256]{1,0:T(8,128)(2,1)}, u32[]{:S(2)}) copy-start(bf16[256,256]{1,0:T(8,128)(2,1)} %mine_ref.1) | copy-start | bytes 393220
  69.1 5.0 %copy-start.2 = (bf16[256,2048]{1,0:T(8,128)(2,1)S(1)}, bf16[256,2048]{1,0:T(8,128)(2,1)}, u32[]{:S(2)}) copy-start(bf16[256,2048]{1,0:T(8,128)(2,1)} %get-tuple-element.17.refs_4_) | copy-start | bytes 3145732
  70.6 7.2 %collective-permute-start.5 = (bf16[256,128]{1,0:T(8,128)(2,1)S(1)}, bf16[256,128]{1,0:T(8,128)(2,1)S(1)}, u32[]{:S(2)}, u32[]{:S(2)}) collective-permute-start(bf16[256,128]{1,0:T(8,128)(2,1)S(1)} %get-tuple-element.16), channel_id=1, source_target_pairs={{0,4},{4,0},{8,12},{12,8},{16,20},{20,16},{24,28},{28,24},{1,5},{5... | collective-permute-start | bytes 196616 | tf_op jit(solution)/shard_map/ppermute | solution.py:451

commit v17 on v15

--- a/solution.py
+++ b/solution.py
@@ -260,21 +260,22 @@
     )(back, answers)
 
 
-def touch_kernel(held_ref, mark_ref):
-    mark_ref[0] = 0
-
-
-def touch(held):
+def touch_kernel(side_ref, held_ref, queries_ref, mine_ref):
+    lane = pl.multiple_of(side_ref[0] * HD, HD)
+    mine_ref[...] = queries_ref[:, pl.ds(lane, HD)]
+
+
+def touch(side, held, queries):
     return pl.pallas_call(
         touch_kernel,
-        out_shape=jax.ShapeDtypeStruct((1,), jnp.int32),
-        in_specs=[VMEM],
-        out_specs=SMEM,
+        out_shape=jax.ShapeDtypeStruct((queries.shape[0], HD), queries.dtype),
+        in_specs=[SMEM, VMEM, VMEM],
+        out_specs=VMEM,
         compiler_params=PARAMS,
-    )(held)
-
-
-def self_kernel(pair_ref, side_ref, mark_ref, mine_ref, other_ref, incoming_ref, *refs):
+    )(side, held, queries)
+
+
+def self_kernel(pair_ref, side_ref, mine_ref, other_ref, incoming_ref, *refs):
     ours_ref, theirs_ref, scores_ref, peak_ref, total_ref, accum_ref = refs
     pair, side = pair_ref[0], side_ref[0]
     tile = mine_ref.shape[0]
@@ -291,12 +292,8 @@
         k = incoming_ref[pl.ds(2 * at, 2), front:, :HD].reshape(rows, HD)
         for here in chunks:
             start = here.start
-            if start < tile:
-                lane = pl.multiple_of(side * HD, HD)
-                q = mine_ref[start : start + chunk, pl.ds(lane, HD)]
-            else:
-                q = other_ref[start - tile : start - tile + chunk, :]
-            s = dot_t(q, k)
+            q_ref, offset = (mine_ref, start) if start < tile else (other_ref, start - tile)
+            s = dot_t(q_ref[offset : offset + chunk, :], k)
             if fresh:
                 row = lax.broadcasted_iota(jnp.int32, (chunk, rows), 0) + start
                 col = lax.broadcasted_iota(jnp.int32, (chunk, rows), 1)
@@ -340,12 +337,12 @@
             theirs_ref[here.start - tile : here.stop - tile, :] = result
 
 
-def self_attend(pair, side, mark, mine, other, incoming):
+def self_attend(pair, side, mine, other, incoming):
     tile = mine.shape[0]
     return pl.pallas_call(
         self_kernel,
         out_shape=(jax.ShapeDtypeStruct((tile, HD), jnp.bfloat16),) * 2,
-        in_specs=[SMEM] * 3 + [VMEM] * 3,
+        in_specs=[SMEM] * 2 + [VMEM] * 3,
         out_specs=(VMEM, VMEM),
         scratch_shapes=[
             pltpu.VMEM((incoming.shape[0] // 2, 2 * tile, 2 * tile), jnp.float32)
@@ -353,7 +350,7 @@
         + [pltpu.VMEM((2 * tile, HD), jnp.float32)] * 3,
         compiler_params=WIDE,
         cost_estimate=takes(6),
-    )(pair, side, mark, mine, other, incoming)
+    )(pair, side, mine, other, incoming)
 
 
 def project_kernel(groups, *refs):
@@ -447,7 +444,8 @@
     cca = merge(back, other_attend(cross_queries, tail, incoming))
     terms = [cca] + [lax.ppermute(cca, "tp", across[step]) for step in range(1, groups)]
 
-    ours, theirs = self_attend(pair, side, touch(terms[1]), queries, q_other, incoming)
+    q_mine = touch(side, terms[1], queries)
+    ours, theirs = self_attend(pair, side, q_mine, q_other, incoming)
     attended = both(ours, lax.ppermute(theirs, "ctx", swap), 1)
     crossed = project(terms, (own, beside), direct)
     return (attended, crossed)

time: 78.9 us -> 80.4 us (1.019)
  local copies, waits for them, and re-layouts: 0.91 us -> 2.22 us
  waiting for transfers between devices: 41.6 us -> 42.7 us
  Pallas kernels: 14.7 us -> 13.6 us
    ppermute x3, waiting for transfers between devices: 1.16 us -> 3.22 us  [shards(): lax.ppermute(cca, 'tp', across[step])]
    unnamed x6 -> x12, local copies, waits for them, and re-layouts: 0.91 us -> 2.22 us
    all_to_all x1, waiting for transfers between devices: 29.9 us -> 29 us  [exchange(): return lax.all_to_all(value, 'ctx', split_axis=0, concat_axis=0, tiled=True)]
  transfers between devices with their start and end apart: 11 -> 11, of which waited for: 4 -> 5; matrix products, arithmetic and copies ran while one was open for 0% -> 0% of each run, Pallas kernels for 16% -> 14%
where the time goes in v17:
time: 80.4 us; the launch traced here: 79.7 us
  waiting for transfers between devices  42.7 us (53%)
  starting transfers between devices  19.7 us (25%)
  Pallas kernels  13.6 us (17%)
  local copies, waits for them, and re-layouts  2.22 us (3%)
    all_to_all x1, waiting for transfers between devices, exchange(): return lax.all_to_all(value, 'ctx', split_axis=0, concat_axis=0, tiled=True)  29 us
    ppermute x1, waiting for transfers between devices, shards(): lax.ppermute(cross_queries[:BLOCK], 'ctx', [(i + 1, i) for i in range(cou...  8.42 us
    all_to_all x1, starting transfers between devices, exchange(): return lax.all_to_all(value, 'ctx', split_axis=0, concat_axis=0, tiled=True)  7.29 us
    pallas_call x1, Pallas kernels, cut(): pl.pallas_call(functools.partial(cut_kernel, plan), out_shape=tuple(shape...  4.33 us
    pallas_call x1, Pallas kernels, project(): pl.pallas_call(functools.partial(project_kernel, len(terms)), out_shape=j...  3.61 us
    ppermute x3, waiting for transfers between devices, shards(): lax.ppermute(cca, 'tp', across[step])  3.22 us
    ppermute x1, starting transfers between devices, shards(): back = lax.ppermute(onward, 'ctx', [(i, i + 1) for i in range(count - 1)])  3.02 us
    pallas_call x1, Pallas kernels, arrange(): pl.pallas_call(arrange_kernel, out_shape=jax.ShapeDtypeStruct((indices, f...  2.57 us
  transfers between devices with their start and end apart: 11, of which 5 were waited for; matrix products, arithmetic and copies ran while one was open for 0% of the time, Pallas kernels for 14%

profile of v17, /device:TPU:0, one launch (start us, length us, event | category | flops | bytes accessed | tf_op | source)
XLA Modules:
  0.0 79.7 jit_solution(11586006851658485028)
XLA Ops:
  0.6 2.6 %shard_map.95 = bf16[8,528,256]{2,1,0:T(8,128)(2,1)} custom-call(s32[8]{0:T(128)} %slot_ref.1, bf16[8,128,256]{2,1,0:T(8,128)(2,1)} %keys_ref.1, bf16[8,128,256]{2,1,0:T(8,128)(2,1)} %values_ref.1, bf16[256,256]{1,0:T(8,128)(2,1)} %own_keys.1, bf16[256,256]{1,0:T(8,128)(2,1)} %own_values.1), custom_call_target="tpu_custom_call" | custom-call | flops 4000000000 | tf_op jit(solution)/shard_map/pallas_call | solution.py:137
  3.2 7.3 %all-to-all-start = ((bf16[8,528,256]{2,1,0:T(8,128)(2,1)}), bf16[8,528,256]{2,1,0:T(8,128)(2,1)S(1)}, u32[]{:S(2)}, u32[]{:S(2)}) async-start(bf16[8,528,256]{2,1,0:T(8,128)(2,1)} %shard_map.95), calls=%async_computation | async-start | bytes 4325376 | tf_op jit(solution)/shard_map/all_to_all | solution.py:428
  10.5 0.0 copy-start.1
  10.5 4.3 %shard_map.96 = (bf16[256,128]{1,0:T(8,128)(2,1)}, bf16[256,2048]{1,0:T(8,128)(2,1)}, bf16[256,2048]{1,0:T(8,128)(2,1)}, bf16[256,2048]{1,0:T(8,128)(2,1)}, bf16[256,2048]{1,0:T(8,128)(2,1)}) custom-call(s32[1]{0:T(128)} %bitcast.1.side_ref, s32[1]{0:T(128)} %bitcast.2.tp_ref, bf16[256,256]{1,0:T(8,128)(2,1)} %queries_ref.5, bf16[256,8192]{1,0:T(8,128)(2,1)} %refs_1_.1), custom_call_target="tpu_custom_call" | custom-call | flops 2000000000 | tf_op jit(solution)/shard_map/pallas_call | solution.py:68
  14.8 0.1 collective-permute-start.2
  14.9 1.6 %collective-permute-start.8 = (bf16[256,2048]{1,0:T(8,128)(2,1)}, bf16[256,2048]{1,0:T(8,128)(2,1)}, u32[]{:S(2)}, u32[]{:S(2)}) collective-permute-start(bf16[256,2048]{1,0:T(8,128)(2,1)} %get-tuple-element.18), channel_id=1, source_target_pairs={{0,2},{1,3},{2,0},{3,1},{4,6},{5,7},{6,4},{7,5},{8,10},{9,11},{10,... | collective-permute-start | bytes 3145736 | tf_op jit(solution)/shard_map/ppermute | solution.py:438
  16.5 0.3 collective-permute-start.9
  16.8 2.0 %collective-permute-start.1 = (bf16[256,128]{1,0:T(8,128)(2,1)}, bf16[256,128]{1,0:T(8,128)(2,1)S(1)}, u32[]{:S(2)}, u32[]{:S(2)}) collective-permute-start(bf16[256,128]{1,0:T(8,128)(2,1)} %get-tuple-element.11), channel_id=1, source_target_pairs={{0,4},{4,0},{8,12},{12,8},{16,20},{20,16},{24,28},{28,24},{1,5},{5... | collective-permute-start | bytes 196616 | tf_op jit(solution)/shard_map/ppermute | solution.py:436
  18.8 0.0 copy-done.1
  18.8 1.3 %collective-permute-start = (bf16[64,256]{1,0:T(8,128)(2,1)S(1)}, bf16[64,256]{1,0:T(8,128)(2,1)S(1)}, u32[]{:S(2)}, u32[]{:S(2)}) collective-permute-start(bf16[64,256]{1,0:T(8,128)(2,1)S(1)} %slice.3), channel_id=1, source_target_pairs={{4,0},{8,4},{12,8},{16,12},{20,16},{24,20},{28,24},{5,1},{9,5},{13... | collective-permute-start | bytes 98312 | tf_op jit(solution)/shard_map/ppermute | solution.py:440
  20.1 8.4 %collective-permute-done.spill_ref = bf16[64,256]{1,0:T(8,128)(2,1)S(1)} collective-permute-done((bf16[64,256]{1,0:T(8,128)(2,1)S(1)}, bf16[64,256]{1,0:T(8,128)(2,1)S(1)}, u32[]{:S(2)}, u32[]{:S(2)}) %collective-permute-start) | collective-permute-done | bytes 32800 | tf_op jit(solution)/shard_map/ppermute | solution.py:440
  28.5 2.0 %collective-permute-done.1.refs_0_.other_ref = bf16[256,128]{1,0:T(8,128)(2,1)S(1)} collective-permute-done((bf16[256,128]{1,0:T(8,128)(2,1)}, bf16[256,128]{1,0:T(8,128)(2,1)S(1)}, u32[]{:S(2)}, u32[]{:S(2)}) %collective-permute-start.1) | collective-permute-done | bytes 65568 | tf_op jit(solution)/shard_map/ppermute | solution.py:436
  30.6 0.0 collective-permute-done.2.refs_1_.refs_5_
  30.6 0.0 copy-start.2
  30.6 1.0 %copy-done.2 = bf16[256,2048]{1,0:T(8,128)(2,1)} copy-done((bf16[256,2048]{1,0:T(8,128)(2,1)}, bf16[256,2048]{1,0:T(8,128)(2,1)S(1)}, u32[]{:S(2)}) %copy-start.2) | copy-done | bytes 1048600
  31.5 29.0 %all-to-all-done.incoming_ref = bf16[8,528,256]{2,1,0:T(8,128)(2,1)S(1)} async-done(((bf16[8,528,256]{2,1,0:T(8,128)(2,1)}), bf16[8,528,256]{2,1,0:T(8,128)(2,1)S(1)}, u32[]{:S(2)}, u32[]{:S(2)}) %all-to-all-start) | async-done | bytes 2162720 | tf_op jit(solution)/shard_map/all_to_all | solution.py:428
  60.5 0.0 copy-start.3
  60.5 1.2 %copy-done.3 = bf16[256,2048]{1,0:T(8,128)(2,1)S(1)} copy-done((bf16[256,2048]{1,0:T(8,128)(2,1)S(1)}, bf16[256,2048]{1,0:T(8,128)(2,1)}, u32[]{:S(2)}) %copy-start.3) | copy-done | bytes 1048600
  61.7 0.6 shard_map.97
  62.3 3.0 %collective-permute-start.3 = (bf16[64,256]{1,0:T(8,128)(2,1)S(1)}, bf16[64,256]{1,0:T(8,128)(2,1)S(1)}, u32[]{:S(2)}, u32[]{:S(2)}) collective-permute-start(bf16[64,256]{1,0:T(8,128)(2,1)S(1)} %get-tuple-element.13), channel_id=1, source_target_pairs={{0,4},{4,8},{8,12},{12,16},{16,20},{20,24},{24,28},{1,5},{5,9},{9,... | collective-permute-start | bytes 98312 | tf_op jit(solution)/shard_map/ppermute | solution.py:443
  65.4 0.0 copy-start
  65.4 1.6 %shard_map.98.answers_ref = bf16[256,256]{1,0:T(8,128)(2,1)S(1)} custom-call(bf16[256,256]{1,0:T(8,128)(2,1)S(1)} %copy-done.1, bf16[16,256]{1,0:T(8,128)(2,1)S(1)} %get-tuple-element.14.tail_ref, bf16[8,528,256]{2,1,0:T(8,128)(2,1)S(1)} %all-to-all-done.incoming_ref), custom_call_target="tpu_custom_call" | custom-call | flops 2000000000 | tf_op jit(solution)/shard_map/pallas_call | solution.py:236
  67.0 0.0 collective-permute-done.3.back_ref
  67.0 0.1 collective-permute-start.4
  67.1 1.6 %collective-permute-start.6 = (bf16[256,256]{1,0:T(8,128)(2,1)S(1)}, bf16[256,256]{1,0:T(8,128)(2,1)S(1)}, u32[]{:S(2)}, u32[]{:S(2)}) collective-permute-start(bf16[256,256]{1,0:T(8,128)(2,1)S(1)} %shard_map.99.refs_0_), channel_id=1, source_target_pairs={{0,2},{1,3},{2,0},{3,1},{4,6},{5,7},{6,4},{7,5},{8,10},{9,11},{10,... | collective-permute-start | bytes 393224 | tf_op jit(solution)/shard_map/ppermute | solution.py:445
  68.7 0.3 collective-permute-start.7
  69.0 0.0 collective-permute-done.4.held_ref.refs_1_
  69.0 0.0 copy-done
  69.0 0.0 copy-start.4
  69.0 0.0 copy-start.5
  69.0 0.8 %shard_map.101 = (bf16[256,128]{1,0:T(8,128)(2,1)S(1)}, bf16[256,128]{1,0:T(8,128)(2,1)S(1)}) custom-call(s32[1]{0:T(128)} %bitcast.pair_ref, s32[1]{0:T(128)} %bitcast.1.side_ref, bf16[256,128]{1,0:T(8,128)(2,1)S(1)} %shard_map.100.mine_ref, bf16[256,128]{1,0:T(8,128)(2,1)S(1)} %collective-permute-done.1.refs_0_.other_ref, ...), custom_call_target="tpu_custom_call" | custom-call | flops 6000000000 | tf_op jit(solution)/shard_map/pallas_call | solution.py:342
  69.9 2.3 %collective-permute-start.5 = (bf16[256,128]{1,0:T(8,128)(2,1)S(1)}, bf16[256,128]{1,0:T(8,128)(2,1)S(1)}, u32[]{:S(2)}, u32[]{:S(2)}) collective-permute-start(bf16[256,128]{1,0:T(8,128)(2,1)S(1)} %get-tuple-element.16), channel_id=1, source_target_pairs={{0,4},{4,0},{8,12},{12,8},{16,20},{20,16},{24,28},{28,24},{1,5},{5... | collective-permute-start | bytes 196616 | tf_op jit(solution)/shard_map/ppermute | solution.py:449
  72.2 0.0 collective-permute-done.8.refs_6_
  72.2 0.0 collective-permute-done.9.refs_7_
  72.2 1.3 %collective-permute-done.6.refs_2_ = bf16[256,256]{1,0:T(8,128)(2,1)S(1)} collective-permute-done((bf16[256,256]{1,0:T(8,128)(2,1)S(1)}, bf16[256,256]{1,0:T(8,128)(2,1)S(1)}, u32[]{:S(2)}, u32[]{:S(2)}) %collective-permute-start.6) | collective-permute-done | bytes 131104 | tf_op jit(solution)/shard_map/ppermute | solution.py:445
  73.5 1.9 %collective-permute-done.7.refs_3_ = bf16[256,256]{1,0:T(8,128)(2,1)S(1)} collective-permute-done((bf16[256,256]{1,0:T(8,128)(2,1)S(1)}, bf16[256,256]{1,0:T(8,128)(2,1)S(1)}, u32[]{:S(2)}, u32[]{:S(2)}) %collective-permute-start.7) | collective-permute-done | bytes 131104 | tf_op jit(solution)/shard_map/ppermute | solution.py:445
  75.4 0.0 copy-done.4
  75.4 0.0 copy-done.5
  75.4 3.6 %shard_map.102 = bf16[256,2048]{1,0:T(8,128)(2,1)} custom-call(bf16[256,256]{1,0:T(8,128)(2,1)S(1)} %shard_map.99.refs_0_, bf16[256,256]{1,0:T(8,128)(2,1)S(1)} %collective-permute-done.4.held_ref.refs_1_, bf16[256,256]{1,0:T(8,128)(2,1)S(1)} %collective-permute-done.6.refs_2_, bf16[256,256]{1,0:T(8,128)(2,1)S(1)} %collective-permute-done.7.refs_3_, ...), custom_call_target="tpu_custom_call" | custom-call | flops 3000000000 | tf_op jit(solution)/shard_map/pallas_call | solution.py:390
  79.0 0.0 collective-permute-done.5
  79.0 0.7 maximum_select_fusion
  (3 shorter events, 0.0 us)
Async XLA Ops:
  3.2 57.3 %all-to-all-start = ((bf16[8,528,256]{2,1,0:T(8,128)(2,1)}), bf16[8,528,256]{2,1,0:T(8,128)(2,1)S(1)}, u32[]{:S(2)}, u32[]{:S(2)}) async-start(bf16[8,528,256]{2,1,0:T(8,128)(2,1)} %shard_map.95), calls=%async_computation | async-start | bytes 4325376 | tf_op jit(solution)/shard_map/all_to_all | solution.py:428
  10.5 8.3 %copy-start.1 = (bf16[256,256]{1,0:T(8,128)(2,1)S(1)}, bf16[256,256]{1,0:T(8,128)(2,1)}, u32[]{:S(2)}) copy-start(bf16[256,256]{1,0:T(8,128)(2,1)} %queries_ref.4) | copy-start | bytes 393220
  14.8 15.7 %collective-permute-start.2 = (bf16[256,2048]{1,0:T(8,128)(2,1)}, bf16[256,2048]{1,0:T(8,128)(2,1)S(1)}, u32[]{:S(2)}, u32[]{:S(2)}) collective-permute-start(bf16[256,2048]{1,0:T(8,128)(2,1)} %get-tuple-element.12), channel_id=1, source_target_pairs={{0,1},{1,0},{2,3},{3,2},{4,5},{5,4},{6,7},{7,6},{8,9},{9,8},{10,11... | collective-permute-start | bytes 3145736 | tf_op jit(solution)/shard_map/ppermute | solution.py:438
  14.9 57.2 %collective-permute-start.8 = (bf16[256,2048]{1,0:T(8,128)(2,1)}, bf16[256,2048]{1,0:T(8,128)(2,1)}, u32[]{:S(2)}, u32[]{:S(2)}) collective-permute-start(bf16[256,2048]{1,0:T(8,128)(2,1)} %get-tuple-element.18), channel_id=1, source_target_pairs={{0,2},{1,3},{2,0},{3,1},{4,6},{5,7},{6,4},{7,5},{8,10},{9,11},{10,... | collective-permute-start | bytes 3145736 | tf_op jit(solution)/shard_map/ppermute | solution.py:438
  16.5 55.7 %collective-permute-start.9 = (bf16[256,2048]{1,0:T(8,128)(2,1)}, bf16[256,2048]{1,0:T(8,128)(2,1)}, u32[]{:S(2)}, u32[]{:S(2)}) collective-permute-start(bf16[256,2048]{1,0:T(8,128)(2,1)} %get-tuple-element.19), channel_id=1, source_target_pairs={{0,3},{1,2},{2,1},{3,0},{4,7},{5,6},{6,5},{7,4},{8,11},{9,10},{10,... | collective-permute-start | bytes 3145736 | tf_op jit(solution)/shard_map/ppermute | solution.py:438
  16.8 13.8 %collective-permute-start.1 = (bf16[256,128]{1,0:T(8,128)(2,1)}, bf16[256,128]{1,0:T(8,128)(2,1)S(1)}, u32[]{:S(2)}, u32[]{:S(2)}) collective-permute-start(bf16[256,128]{1,0:T(8,128)(2,1)} %get-tuple-element.11), channel_id=1, source_target_pairs={{0,4},{4,0},{8,12},{12,8},{16,20},{20,16},{24,28},{28,24},{1,5},{5... | collective-permute-start | bytes 196616 | tf_op jit(solution)/shard_map/ppermute | solution.py:436
  18.8 9.7 %collective-permute-start = (bf16[64,256]{1,0:T(8,128)(2,1)S(1)}, bf16[64,256]{1,0:T(8,128)(2,1)S(1)}, u32[]{:S(2)}, u32[]{:S(2)}) collective-permute-start(bf16[64,256]{1,0:T(8,128)(2,1)S(1)} %slice.3), channel_id=1, source_target_pairs={{4,0},{8,4},{12,8},{16,12},{20,16},{24,20},{28,24},{5,1},{9,5},{13... | collective-permute-start | bytes 98312 | tf_op jit(solution)/shard_map/ppermute | solution.py:440
  30.6 1.0 %copy-start.2 = (bf16[256,2048]{1,0:T(8,128)(2,1)}, bf16[256,2048]{1,0:T(8,128)(2,1)S(1)}, u32[]{:S(2)}) copy-start(bf16[256,2048]{1,0:T(8,128)(2,1)S(1)} %collective-permute-done.2.refs_1_.refs_5_) | copy-start | bytes 3145732
  60.5 1.2 %copy-start.3 = (bf16[256,2048]{1,0:T(8,128)(2,1)S(1)}, bf16[256,2048]{1,0:T(8,128)(2,1)}, u32[]{:S(2)}) copy-start(bf16[256,2048]{1,0:T(8,128)(2,1)} %copy-done.2) | copy-start | bytes 3145732
  62.3 4.7 %collective-permute-start.3 = (bf16[64,256]{1,0:T(8,128)(2,1)S(1)}, bf16[64,256]{1,0:T(8,128)(2,1)S(1)}, u32[]{:S(2)}, u32[]{:S(2)}) collective-permute-start(bf16[64,256]{1,0:T(8,128)(2,1)S(1)} %get-tuple-element.13), channel_id=1, source_target_pairs={{0,4},{4,8},{8,12},{12,16},{16,20},{20,24},{24,28},{1,5},{5,9},{9,... | collective-permute-start | bytes 98312 | tf_op jit(solution)/shard_map/ppermute | solution.py:443
  65.4 3.6 %copy-start = (bf16[256,256]{1,0:T(8,128)(2,1)S(1)}, bf16[256,256]{1,0:T(8,128)(2,1)}, u32[]{:S(2)}) copy-start(bf16[256,256]{1,0:T(8,128)(2,1)} %queries_ref.5) | copy-start | bytes 393220
  67.0 1.9 %collective-permute-start.4 = (bf16[256,256]{1,0:T(8,128)(2,1)S(1)}, bf16[256,256]{1,0:T(8,128)(2,1)S(1)}, u32[]{:S(2)}, u32[]{:S(2)}) collective-permute-start(bf16[256,256]{1,0:T(8,128)(2,1)S(1)} %shard_map.99.refs_0_), channel_id=1, source_target_pairs={{0,1},{1,0},{2,3},{3,2},{4,5},{5,4},{6,7},{7,6},{8,9},{9,8},{10,11... | collective-permute-start | bytes 393224 | tf_op jit(solution)/shard_map/ppermute | solution.py:445
  67.1 6.4 %collective-permute-start.6 = (bf16[256,256]{1,0:T(8,128)(2,1)S(1)}, bf16[256,256]{1,0:T(8,128)(2,1)S(1)}, u32[]{:S(2)}, u32[]{:S(2)}) collective-permute-start(bf16[256,256]{1,0:T(8,128)(2,1)S(1)} %shard_map.99.refs_0_), channel_id=1, source_target_pairs={{0,2},{1,3},{2,0},{3,1},{4,6},{5,7},{6,4},{7,5},{8,10},{9,11},{10,... | collective-permute-start | bytes 393224 | tf_op jit(solution)/shard_map/ppermute | solution.py:445
  68.7 6.7 %collective-permute-start.7 = (bf16[256,256]{1,0:T(8,128)(2,1)S(1)}, bf16[256,256]{1,0:T(8,128)(2,1)S(1)}, u32[]{:S(2)}, u32[]{:S(2)}) collective-permute-start(bf16[256,256]{1,0:T(8,128)(2,1)S(1)} %shard_map.99.refs_0_), channel_id=1, source_target_pairs={{0,3},{1,2},{2,1},{3,0},{4,7},{5,6},{6,5},{7,4},{8,11},{9,10},{10,... | collective-permute-start | bytes 393224 | tf_op jit(solution)/shard_map/ppermute | solution.py:445
  69.0 6.4 %copy-start.4 = (bf16[256,2048]{1,0:T(8,128)(2,1)S(1)}, bf16[256,2048]{1,0:T(8,128)(2,1)}, u32[]{:S(2)}) copy-start(bf16[256,2048]{1,0:T(8,128)(2,1)} %copy-done.2) | copy-start | bytes 3145732
  69.0 6.4 %copy-start.5 = (bf16[256,2048]{1,0:T(8,128)(2,1)S(1)}, bf16[256,2048]{1,0:T(8,128)(2,1)}, u32[]{:S(2)}) copy-start(bf16[256,2048]{1,0:T(8,128)(2,1)} %get-tuple-element.17.refs_4_) | copy-start | bytes 3145732
  69.9 9.1 %collective-permute-start.5 = (bf16[256,128]{1,0:T(8,128)(2,1)S(1)}, bf16[256,128]{1,0:T(8,128)(2,1)S(1)}, u32[]{:S(2)}, u32[]{:S(2)}) collective-permute-start(bf16[256,128]{1,0:T(8,128)(2,1)S(1)} %get-tuple-element.16), channel_id=1, source_target_pairs={{0,4},{4,0},{8,12},{12,8},{16,20},{20,16},{24,28},{28,24},{1,5},{5... | collective-permute-start | bytes 196616 | tf_op jit(solution)/shard_map/ppermute | solution.py:449

commit v18 on v15

--- a/solution.py
+++ b/solution.py
@@ -361,7 +361,7 @@
     terms, near, far = refs[:groups], refs[groups : groups + 2], refs[groups + 2 : -4]
     width = crossed_ref.shape[1]
     depth = near[0].shape[0]
-    tile = min(512, width)
+    tile = min(1024, width)
     columns = [slice(at, at + tile) for at in range(0, width, tile)]
     copies = []
     for turn, at in enumerate(columns):
@@ -388,7 +388,7 @@
 def project(terms, near, far):
     rows, depth = terms[0].shape[0], near[0].shape[0]
     width = near[0].shape[1]
-    tile = min(512, width)
+    tile = min(1024, width)
     turns = width // tile
     return pl.pallas_call(
         functools.partial(project_kernel, len(terms)),

time: 78.9 us -> 78.8 us (level)
  transfers between devices with their start and end apart: 11 -> 11, of which waited for: 4 -> 4; matrix products, arithmetic and copies ran while one was open for 0% -> 0% of each run, Pallas kernels for 16% -> 15%
where the time goes in v18:
time: 78.8 us; the launch traced here: 78.3 us
  waiting for transfers between devices  41.6 us (53%)
  starting transfers between devices  19.8 us (25%)
  Pallas kernels  14.6 us (19%)
  local copies, waits for them, and re-layouts  0.91 us (1%)
    all_to_all x1, waiting for transfers between devices, exchange(): return lax.all_to_all(value, 'ctx', split_axis=0, concat_axis=0, tiled=True)  29.9 us
    ppermute x1, waiting for transfers between devices, shards(): lax.ppermute(cross_queries[:BLOCK], 'ctx', [(i + 1, i) for i in range(cou...  8.42 us
    all_to_all x1, starting transfers between devices, exchange(): return lax.all_to_all(value, 'ctx', split_axis=0, concat_axis=0, tiled=True)  7.29 us
    pallas_call x1, Pallas kernels, cut(): pl.pallas_call(functools.partial(cut_kernel, plan), out_shape=tuple(shape...  4.33 us
    pallas_call x1, Pallas kernels, project(): pl.pallas_call(functools.partial(project_kernel, len(terms)), out_shape=j...  3.47 us
    ppermute x1, starting transfers between devices, shards(): back = lax.ppermute(onward, 'ctx', [(i, i + 1) for i in range(count - 1)])  3.02 us
    pallas_call x1, Pallas kernels, arrange(): pl.pallas_call(arrange_kernel, out_shape=jax.ShapeDtypeStruct((indices, f...  2.53 us
    ppermute x1, starting transfers between devices, shards(): attended = both(ours, lax.ppermute(theirs, 'ctx', swap), 1)  2.3 us
  transfers between devices with their start and end apart: 11, of which 4 were waited for; matrix products, arithmetic and copies ran while one was open for 0% of the time, Pallas kernels for 15%

profile of v18, /device:TPU:0, one launch (start us, length us, event | category | flops | bytes accessed | tf_op | source)
XLA Modules:
  0.0 78.3 jit_solution(13009681036014841731)
XLA Ops:
  0.6 2.5 %shard_map.95 = bf16[8,528,256]{2,1,0:T(8,128)(2,1)} custom-call(s32[8]{0:T(128)} %slot_ref.1, bf16[8,128,256]{2,1,0:T(8,128)(2,1)} %keys_ref.1, bf16[8,128,256]{2,1,0:T(8,128)(2,1)} %values_ref.1, bf16[256,256]{1,0:T(8,128)(2,1)} %own_keys.1, bf16[256,256]{1,0:T(8,128)(2,1)} %own_values.1), custom_call_target="tpu_custom_call" | custom-call | flops 4000000000 | tf_op jit(solution)/shard_map/pallas_call | solution.py:137
  3.2 7.3 %all-to-all-start = ((bf16[8,528,256]{2,1,0:T(8,128)(2,1)}), bf16[8,528,256]{2,1,0:T(8,128)(2,1)S(1)}, u32[]{:S(2)}, u32[]{:S(2)}) async-start(bf16[8,528,256]{2,1,0:T(8,128)(2,1)} %shard_map.95), calls=%async_computation | async-start | bytes 4325376 | tf_op jit(solution)/shard_map/all_to_all | solution.py:431
  10.5 0.0 copy-start
  10.5 4.3 %shard_map.96 = (bf16[256,128]{1,0:T(8,128)(2,1)}, bf16[256,2048]{1,0:T(8,128)(2,1)}, bf16[256,2048]{1,0:T(8,128)(2,1)}, bf16[256,2048]{1,0:T(8,128)(2,1)}, bf16[256,2048]{1,0:T(8,128)(2,1)}) custom-call(s32[1]{0:T(128)} %bitcast.1.side_ref, s32[1]{0:T(128)} %bitcast.2.tp_ref, bf16[256,256]{1,0:T(8,128)(2,1)} %mine_ref.1, bf16[256,8192]{1,0:T(8,128)(2,1)} %refs_1_.1), custom_call_target="tpu_custom_call" | custom-call | flops 2000000000 | tf_op jit(solution)/shard_map/pallas_call | solution.py:68
  14.8 0.1 collective-permute-start.2
  14.9 1.6 %collective-permute-start.8 = (bf16[256,2048]{1,0:T(8,128)(2,1)}, bf16[256,2048]{1,0:T(8,128)(2,1)}, u32[]{:S(2)}, u32[]{:S(2)}) collective-permute-start(bf16[256,2048]{1,0:T(8,128)(2,1)} %get-tuple-element.18), channel_id=1, source_target_pairs={{0,2},{1,3},{2,0},{3,1},{4,6},{5,7},{6,4},{7,5},{8,10},{9,11},{10,... | collective-permute-start | bytes 3145736 | tf_op jit(solution)/shard_map/ppermute | solution.py:441
  16.4 0.3 collective-permute-start.9
  16.7 2.0 %collective-permute-start.1 = (bf16[256,128]{1,0:T(8,128)(2,1)}, bf16[256,128]{1,0:T(8,128)(2,1)S(1)}, u32[]{:S(2)}, u32[]{:S(2)}) collective-permute-start(bf16[256,128]{1,0:T(8,128)(2,1)} %get-tuple-element.11), channel_id=1, source_target_pairs={{0,4},{4,0},{8,12},{12,8},{16,20},{20,16},{24,28},{28,24},{1,5},{5... | collective-permute-start | bytes 196616 | tf_op jit(solution)/shard_map/ppermute | solution.py:439
  18.8 0.0 copy-done
  18.8 1.3 %collective-permute-start = (bf16[64,256]{1,0:T(8,128)(2,1)S(1)}, bf16[64,256]{1,0:T(8,128)(2,1)S(1)}, u32[]{:S(2)}, u32[]{:S(2)}) collective-permute-start(bf16[64,256]{1,0:T(8,128)(2,1)S(1)} %slice.3), channel_id=1, source_target_pairs={{4,0},{8,4},{12,8},{16,12},{20,16},{24,20},{28,24},{5,1},{9,5},{13... | collective-permute-start | bytes 98312 | tf_op jit(solution)/shard_map/ppermute | solution.py:443
  20.1 8.4 %collective-permute-done.spill_ref = bf16[64,256]{1,0:T(8,128)(2,1)S(1)} collective-permute-done((bf16[64,256]{1,0:T(8,128)(2,1)S(1)}, bf16[64,256]{1,0:T(8,128)(2,1)S(1)}, u32[]{:S(2)}, u32[]{:S(2)}) %collective-permute-start) | collective-permute-done | bytes 32800 | tf_op jit(solution)/shard_map/ppermute | solution.py:443
  28.5 2.0 %collective-permute-done.1.refs_0_.other_ref = bf16[256,128]{1,0:T(8,128)(2,1)S(1)} collective-permute-done((bf16[256,128]{1,0:T(8,128)(2,1)}, bf16[256,128]{1,0:T(8,128)(2,1)S(1)}, u32[]{:S(2)}, u32[]{:S(2)}) %collective-permute-start.1) | collective-permute-done | bytes 65568 | tf_op jit(solution)/shard_map/ppermute | solution.py:439
  30.5 0.0 collective-permute-done.2.refs_1_.refs_5_
  30.5 29.9 %all-to-all-done.incoming_ref = bf16[8,528,256]{2,1,0:T(8,128)(2,1)S(1)} async-done(((bf16[8,528,256]{2,1,0:T(8,128)(2,1)}), bf16[8,528,256]{2,1,0:T(8,128)(2,1)S(1)}, u32[]{:S(2)}, u32[]{:S(2)}) %all-to-all-start) | async-done | bytes 2162720 | tf_op jit(solution)/shard_map/all_to_all | solution.py:431
  60.5 0.6 shard_map.97
  61.1 3.0 %collective-permute-start.3 = (bf16[64,256]{1,0:T(8,128)(2,1)S(1)}, bf16[64,256]{1,0:T(8,128)(2,1)S(1)}, u32[]{:S(2)}, u32[]{:S(2)}) collective-permute-start(bf16[64,256]{1,0:T(8,128)(2,1)S(1)} %get-tuple-element.13), channel_id=1, source_target_pairs={{0,4},{4,8},{8,12},{12,16},{16,20},{20,24},{24,28},{1,5},{5,9},{9,... | collective-permute-start | bytes 98312 | tf_op jit(solution)/shard_map/ppermute | solution.py:446
  64.1 1.6 %shard_map.98.answers_ref = bf16[256,256]{1,0:T(8,128)(2,1)S(1)} custom-call(bf16[256,256]{1,0:T(8,128)(2,1)S(1)} %copy-done, bf16[16,256]{1,0:T(8,128)(2,1)S(1)} %get-tuple-element.14.tail_ref, bf16[8,528,256]{2,1,0:T(8,128)(2,1)S(1)} %all-to-all-done.incoming_ref), custom_call_target="tpu_custom_call" | custom-call | flops 2000000000 | tf_op jit(solution)/shard_map/pallas_call | solution.py:236
  65.7 0.0 collective-permute-done.3.back_ref
  65.8 0.1 collective-permute-start.4
  65.9 1.6 %collective-permute-start.6 = (bf16[256,256]{1,0:T(8,128)(2,1)S(1)}, bf16[256,256]{1,0:T(8,128)(2,1)S(1)}, u32[]{:S(2)}, u32[]{:S(2)}) collective-permute-start(bf16[256,256]{1,0:T(8,128)(2,1)S(1)} %shard_map.99.refs_0_), channel_id=1, source_target_pairs={{0,2},{1,3},{2,0},{3,1},{4,6},{5,7},{6,4},{7,5},{8,10},{9,11},{10,... | collective-permute-start | bytes 393224 | tf_op jit(solution)/shard_map/ppermute | solution.py:448
  67.4 0.3 collective-permute-start.7
  67.7 0.0 collective-permute-done.4.held_ref.refs_1_
  67.7 0.5 shard_map.100.mark_ref
  68.2 0.0 copy-start.1
  68.3 0.9 %copy-done.1 = bf16[256,256]{1,0:T(8,128)(2,1)S(1)} copy-done((bf16[256,256]{1,0:T(8,128)(2,1)S(1)}, bf16[256,256]{1,0:T(8,128)(2,1)}, u32[]{:S(2)}) %copy-start.1) | copy-done | bytes 131096
  69.1 0.0 copy-start.2
  69.1 1.5 %shard_map.101 = (bf16[256,128]{1,0:T(8,128)(2,1)S(1)}, bf16[256,128]{1,0:T(8,128)(2,1)S(1)}) custom-call(s32[1]{0:T(128)} %bitcast.pair_ref, s32[1]{0:T(128)} %bitcast.1.side_ref, s32[1]{0:T(128)} %shard_map.100.mark_ref, bf16[256,256]{1,0:T(8,128)(2,1)S(1)} %copy-done.1, bf16[256,128]{1,0:T(8,128)(2,1)S(1)} %collective-permute-done.1.refs_0_.other_ref, ...), custom_call_target="tpu_custom_call" | custom-call | flops 6000000000 | tf_op jit(solution)/shard_map/pallas_call | solution.py:345
  70.6 2.3 %collective-permute-start.5 = (bf16[256,128]{1,0:T(8,128)(2,1)S(1)}, bf16[256,128]{1,0:T(8,128)(2,1)S(1)}, u32[]{:S(2)}, u32[]{:S(2)}) collective-permute-start(bf16[256,128]{1,0:T(8,128)(2,1)S(1)} %get-tuple-element.16), channel_id=1, source_target_pairs={{0,4},{4,0},{8,12},{12,8},{16,20},{20,16},{24,28},{28,24},{1,5},{5... | collective-permute-start | bytes 196616 | tf_op jit(solution)/shard_map/ppermute | solution.py:451
  72.9 0.0 collective-permute-done.8.refs_6_
  72.9 0.0 collective-permute-done.9.refs_7_
  72.9 0.0 collective-permute-done.6.refs_2_
  72.9 1.2 %collective-permute-done.7.refs_3_ = bf16[256,256]{1,0:T(8,128)(2,1)S(1)} collective-permute-done((bf16[256,256]{1,0:T(8,128)(2,1)S(1)}, bf16[256,256]{1,0:T(8,128)(2,1)S(1)}, u32[]{:S(2)}, u32[]{:S(2)}) %collective-permute-start.7) | collective-permute-done | bytes 131104 | tf_op jit(solution)/shard_map/ppermute | solution.py:448
  74.1 0.0 copy-done.2
  74.1 3.5 %shard_map.102 = bf16[256,2048]{1,0:T(8,128)(2,1)} custom-call(bf16[256,256]{1,0:T(8,128)(2,1)S(1)} %shard_map.99.refs_0_, bf16[256,256]{1,0:T(8,128)(2,1)S(1)} %collective-permute-done.4.held_ref.refs_1_, bf16[256,256]{1,0:T(8,128)(2,1)S(1)} %collective-permute-done.6.refs_2_, bf16[256,256]{1,0:T(8,128)(2,1)S(1)} %collective-permute-done.7.refs_3_, ...), custom_call_target="tpu_custom_call" | custom-call | flops 3000000000 | tf_op jit(solution)/shard_map/pallas_call | solution.py:393
  77.6 0.0 collective-permute-done.5
  77.6 0.7 maximum_select_fusion
  (2 shorter events, 0.0 us)
Async XLA Ops:
  3.2 57.3 %all-to-all-start = ((bf16[8,528,256]{2,1,0:T(8,128)(2,1)}), bf16[8,528,256]{2,1,0:T(8,128)(2,1)S(1)}, u32[]{:S(2)}, u32[]{:S(2)}) async-start(bf16[8,528,256]{2,1,0:T(8,128)(2,1)} %shard_map.95), calls=%async_computation | async-start | bytes 4325376 | tf_op jit(solution)/shard_map/all_to_all | solution.py:431
  10.5 8.3 %copy-start = (bf16[256,256]{1,0:T(8,128)(2,1)S(1)}, bf16[256,256]{1,0:T(8,128)(2,1)}, u32[]{:S(2)}) copy-start(bf16[256,256]{1,0:T(8,128)(2,1)} %queries_ref.3) | copy-start | bytes 393220
  14.8 15.7 %collective-permute-start.2 = (bf16[256,2048]{1,0:T(8,128)(2,1)}, bf16[256,2048]{1,0:T(8,128)(2,1)S(1)}, u32[]{:S(2)}, u32[]{:S(2)}) collective-permute-start(bf16[256,2048]{1,0:T(8,128)(2,1)} %get-tuple-element.12), channel_id=1, source_target_pairs={{0,1},{1,0},{2,3},{3,2},{4,5},{5,4},{6,7},{7,6},{8,9},{9,8},{10,11... | collective-permute-start | bytes 3145736 | tf_op jit(solution)/shard_map/ppermute | solution.py:441
  14.9 58.1 %collective-permute-start.8 = (bf16[256,2048]{1,0:T(8,128)(2,1)}, bf16[256,2048]{1,0:T(8,128)(2,1)}, u32[]{:S(2)}, u32[]{:S(2)}) collective-permute-start(bf16[256,2048]{1,0:T(8,128)(2,1)} %get-tuple-element.18), channel_id=1, source_target_pairs={{0,2},{1,3},{2,0},{3,1},{4,6},{5,7},{6,4},{7,5},{8,10},{9,11},{10,... | collective-permute-start | bytes 3145736 | tf_op jit(solution)/shard_map/ppermute | solution.py:441
  16.4 56.5 %collective-permute-start.9 = (bf16[256,2048]{1,0:T(8,128)(2,1)}, bf16[256,2048]{1,0:T(8,128)(2,1)}, u32[]{:S(2)}, u32[]{:S(2)}) collective-permute-start(bf16[256,2048]{1,0:T(8,128)(2,1)} %get-tuple-element.19), channel_id=1, source_target_pairs={{0,3},{1,2},{2,1},{3,0},{4,7},{5,6},{6,5},{7,4},{8,11},{9,10},{10,... | collective-permute-start | bytes 3145736 | tf_op jit(solution)/shard_map/ppermute | solution.py:441
  16.7 13.8 %collective-permute-start.1 = (bf16[256,128]{1,0:T(8,128)(2,1)}, bf16[256,128]{1,0:T(8,128)(2,1)S(1)}, u32[]{:S(2)}, u32[]{:S(2)}) collective-permute-start(bf16[256,128]{1,0:T(8,128)(2,1)} %get-tuple-element.11), channel_id=1, source_target_pairs={{0,4},{4,0},{8,12},{12,8},{16,20},{20,16},{24,28},{28,24},{1,5},{5... | collective-permute-start | bytes 196616 | tf_op jit(solution)/shard_map/ppermute | solution.py:439
  18.8 9.7 %collective-permute-start = (bf16[64,256]{1,0:T(8,128)(2,1)S(1)}, bf16[64,256]{1,0:T(8,128)(2,1)S(1)}, u32[]{:S(2)}, u32[]{:S(2)}) collective-permute-start(bf16[64,256]{1,0:T(8,128)(2,1)S(1)} %slice.3), channel_id=1, source_target_pairs={{4,0},{8,4},{12,8},{16,12},{20,16},{24,20},{28,24},{5,1},{9,5},{13... | collective-permute-start | bytes 98312 | tf_op jit(solution)/shard_map/ppermute | solution.py:443
  61.1 4.7 %collective-permute-start.3 = (bf16[64,256]{1,0:T(8,128)(2,1)S(1)}, bf16[64,256]{1,0:T(8,128)(2,1)S(1)}, u32[]{:S(2)}, u32[]{:S(2)}) collective-permute-start(bf16[64,256]{1,0:T(8,128)(2,1)S(1)} %get-tuple-element.13), channel_id=1, source_target_pairs={{0,4},{4,8},{8,12},{12,16},{16,20},{20,24},{24,28},{1,5},{5,9},{9,... | collective-permute-start | bytes 98312 | tf_op jit(solution)/shard_map/ppermute | solution.py:446
  65.8 1.9 %collective-permute-start.4 = (bf16[256,256]{1,0:T(8,128)(2,1)S(1)}, bf16[256,256]{1,0:T(8,128)(2,1)S(1)}, u32[]{:S(2)}, u32[]{:S(2)}) collective-permute-start(bf16[256,256]{1,0:T(8,128)(2,1)S(1)} %shard_map.99.refs_0_), channel_id=1, source_target_pairs={{0,1},{1,0},{2,3},{3,2},{4,5},{5,4},{6,7},{7,6},{8,9},{9,8},{10,11... | collective-permute-start | bytes 393224 | tf_op jit(solution)/shard_map/ppermute | solution.py:448
  65.9 7.1 %collective-permute-start.6 = (bf16[256,256]{1,0:T(8,128)(2,1)S(1)}, bf16[256,256]{1,0:T(8,128)(2,1)S(1)}, u32[]{:S(2)}, u32[]{:S(2)}) collective-permute-start(bf16[256,256]{1,0:T(8,128)(2,1)S(1)} %shard_map.99.refs_0_), channel_id=1, source_target_pairs={{0,2},{1,3},{2,0},{3,1},{4,6},{5,7},{6,4},{7,5},{8,10},{9,11},{10,... | collective-permute-start | bytes 393224 | tf_op jit(solution)/shard_map/ppermute | solution.py:448
  67.4 6.7 %collective-permute-start.7 = (bf16[256,256]{1,0:T(8,128)(2,1)S(1)}, bf16[256,256]{1,0:T(8,128)(2,1)S(1)}, u32[]{:S(2)}, u32[]{:S(2)}) collective-permute-start(bf16[256,256]{1,0:T(8,128)(2,1)S(1)} %shard_map.99.refs_0_), channel_id=1, source_target_pairs={{0,3},{1,2},{2,1},{3,0},{4,7},{5,6},{6,5},{7,4},{8,11},{9,10},{10,... | collective-permute-start | bytes 393224 | tf_op jit(solution)/shard_map/ppermute | solution.py:448
  68.2 0.9 %copy-start.1 = (bf16[256,256]{1,0:T(8,128)(2,1)S(1)}, bf16[256,256]{1,0:T(8,128)(2,1)}, u32[]{:S(2)}) copy-start(bf16[256,256]{1,0:T(8,128)(2,1)} %mine_ref.1) | copy-start | bytes 393220
  69.1 5.0 %copy-start.2 = (bf16[256,2048]{1,0:T(8,128)(2,1)S(1)}, bf16[256,2048]{1,0:T(8,128)(2,1)}, u32[]{:S(2)}) copy-start(bf16[256,2048]{1,0:T(8,128)(2,1)} %get-tuple-element.17.refs_4_) | copy-start | bytes 3145732
  70.6 6.9 %collective-permute-start.5 = (bf16[256,128]{1,0:T(8,128)(2,1)S(1)}, bf16[256,128]{1,0:T(8,128)(2,1)S(1)}, u32[]{:S(2)}, u32[]{:S(2)}) collective-permute-start(bf16[256,128]{1,0:T(8,128)(2,1)S(1)} %get-tuple-element.16), channel_id=1, source_target_pairs={{0,4},{4,0},{8,12},{12,8},{16,20},{20,16},{24,28},{28,24},{1,5},{5... | collective-permute-start | bytes 196616 | tf_op jit(solution)/shard_map/ppermute | solution.py:451
